TPU v7x, 32 devices: a whole 2x2x4 slice. The times are simulated.
32 devices in a mesh: pitch: 8 (over y, x, core), span: 4 (over z).
Axes of the slice: x: 2, y: 2, z: 4, core: 2. Of those that a mesh axis runs over, the one named last changes fastest.
Arguments:
- state: float32 [5, 5, 5, 5, 16, 4, 128], P(None, None, None, None, 'pitch', 'span'), may hold values from -6 to 6
- wake_planes: float32 [5, 5, 5, 16, 4], P(None, None, None, 'pitch', 'span'), may hold values from -6 to 6
- bar_offsets: int32 [3], replicated, may hold values from 0 to 1, as said below
Outputs:
- advanced: float32 [5, 5, 5, 5, 16, 4, 128], P(None, None, None, None, 'pitch', 'span')
Inputs may be any that keep to these rules, and one draw needn't show every extreme that they name: `bar_offsets`: some section has offset 1 and some section offset 0.
All inputs are finite; a program needn't handle non-finite values.
Results may differ from a plain program's by a relative error of at most 0.0001.
Values sent between devices are 32-bit elements; how exact they have to be, the bound alone decides.
No kernel may reach another device: no remote copies, remote signals or barrier semaphores. Data moves between devices by JAX's collectives and lax.ppermute only.
A program may use at most 64 MiB of HBM per device.

v0:
```python
import functools

import jax
import jax.numpy as jnp
import ml_dtypes
import numpy as np
from jax import lax
from jax.experimental import pallas as pl
from jax.experimental.pallas import tpu as pltpu
from jax.sharding import PartitionSpec as P

MEAN_FLOW = (0.5, 0.3, 0.0)
WAVE_SPEED = (1.5, 1.3, 1.0)
ELEM_SIZE = (1.0, 0.8, 1.2)
END_WEIGHT = 0.1
TIME_STEP = 0.01
KEEP = (0.0, 0.75, 1.0 / 3.0)
GAIN = (1.0, 0.25, 2.0 / 3.0)

PLANE = 32
PER_VAR = 144
ROWS = 5 * PER_VAR
BLOCK = 128
SPAN_ROWS = 104
TRACES = 4 * BLOCK
HALO = 5 * BLOCK
WAKE_ROW = 125
LANES = 128
VMEM_LIMIT = 24 * 1024 * 1024


def derivative_table():
    points = np.array([-1.0, -np.sqrt(3.0 / 7.0), 0.0, np.sqrt(3.0 / 7.0), 1.0])
    products = np.array(
        [np.prod([points[j] - points[k] for k in range(5) if k != j]) for j in range(5)]
    )
    matrix = np.zeros((5, 5))
    for i in range(5):
        for j in range(5):
            if i != j:
                matrix[i, j] = products[i] / (products[j] * (points[i] - points[j]))
        matrix[i, i] = sum((1.0 / (points[i] - points[k]) for k in range(5) if k != i))
    return matrix


def flux_matrix(direction):
    flux = MEAN_FLOW[direction] * np.eye(5)
    flux[0, 1 + direction] += 1.0
    flux[4, 1 + direction] += 1.0
    flux[1 + direction, 4] += 1.0
    return flux


def half_flux(direction, sign):
    return 0.5 * (flux_matrix(direction) + sign * WAVE_SPEED[direction] * np.eye(5))


def lift_factor(direction):
    return TIME_STEP * 2.0 / (ELEM_SIZE[direction] * END_WEIGHT)


def node_row(v, a, p, s):
    start = {0: 0, 4: PLANE}.get(a, 2 * PLANE + (a - 1) * 25)
    return v * PER_VAR + start + p * 5 + s


def operator_tables():
    deriv = derivative_table()
    volume = np.zeros((ROWS, ROWS))
    lift = np.zeros((ROWS, HALO))
    trace = np.zeros((TRACES, ROWS))
    fluxes = [flux_matrix(d) for d in range(3)]
    plus = [half_flux(d, 1.0) for d in range(3)]
    minus = [half_flux(d, -1.0) for d in range(3)]
    plus_sent, minus_sent = (plus[2][:4], minus[2][:4])
    back_plus = np.vstack([np.eye(4), [[0.0, 0.0, 0.0, 1.0]]])
    back_minus = np.vstack([np.eye(4), [[0.0, 0.0, 0.0, -1.0]]])
    assert np.allclose(back_plus @ plus_sent, plus[2])
    assert np.allclose(back_minus @ minus_sent, minus[2])
    for a in range(5):
        for p in range(5):
            for s in range(5):
                here = [node_row(v, a, p, s) for v in range(5)]
                place = (a, p, s)
                for d in range(3):
                    for j in range(5):
                        there = list(place)
                        there[d] = j
                        cols = [node_row(v, *there) for v in range(5)]
                        coeff = -TIME_STEP * (2.0 / ELEM_SIZE[d]) * deriv[place[d], j]
                        volume[np.ix_(here, cols)] += coeff * fluxes[d]
                for d in (1, 2):
                    if place[d] == 4:
                        volume[np.ix_(here, here)] += lift_factor(d) * minus[d]
                    if place[d] == 0:
                        volume[np.ix_(here, here)] -= lift_factor(d) * plus[d]
                if p == 0:
                    cols = [v * 25 + a * 5 + s for v in range(5)]
                    lift[np.ix_(here, cols)] += lift_factor(1) * plus[1]
                    for v in range(5):
                        trace[BLOCK + v * 25 + a * 5 + s, here[v]] = 1.0
                if p == 4:
                    cols = [BLOCK + v * 25 + a * 5 + s for v in range(5)]
                    lift[np.ix_(here, cols)] -= lift_factor(1) * minus[1]
                    for v in range(5):
                        trace[v * 25 + a * 5 + s, here[v]] = 1.0
                if s == 0:
                    cols = [2 * BLOCK + c * 25 + a * 5 + p for c in range(4)]
                    lift[np.ix_(here, cols)] += lift_factor(2) * back_plus
                    rows = [3 * BLOCK + c * 25 + a * 5 + p for c in range(4)]
                    trace[np.ix_(rows, here)] += minus_sent
                if s == 4:
                    cols = [3 * BLOCK + c * 25 + a * 5 + p for c in range(4)]
                    lift[np.ix_(here, cols)] -= lift_factor(2) * back_minus
                    rows = [2 * BLOCK + c * 25 + a * 5 + p for c in range(4)]
                    trace[np.ix_(rows, here)] += plus_sent
                if a == 0:
                    cols = [4 * BLOCK + v * 25 + p * 5 + s for v in range(5)]
                    lift[np.ix_(here, cols)] += lift_factor(0) * plus[0]
    return volume, lift, trace, trace @ lift


def split_table(table):
    high = table.astype(ml_dtypes.bfloat16)
    low = (table - high.astype(np.float64)).astype(ml_dtypes.bfloat16)
    return high, low


def split(values):
    high = values.astype(jnp.bfloat16)
    low = (values - high.astype(jnp.float32)).astype(jnp.bfloat16)
    return high, low


def product(high, low, values_high, values_low):
    dot = functools.partial(jnp.dot, preferred_element_type=jnp.float32)
    total = dot(high, values_high) + dot(high, values_low)
    return total if low is None else total + dot(low, values_high)


def emit_faces(traces, wake, pitch_odd, span_odd, outs):
    pitch_a, pitch_b, span_a, span_b, inner = outs
    upper, lower = traces[0:BLOCK], traces[BLOCK : 2 * BLOCK]
    rows = lax.broadcasted_iota(jnp.int32, (BLOCK, LANES), 0)
    up = upper[:, LANES:]
    for k in range(2):
        up = jnp.where(rows == WAKE_ROW + k, wake[k : k + 1], up)
    down = lower[:, :LANES]
    pitch_a[...] = jnp.where(pitch_odd, down, up)
    pitch_b[...] = jnp.where(pitch_odd, up, down)
    inner[0:BLOCK] = upper[:, :LANES]
    inner[BLOCK:] = lower[:, LANES:]
    above = traces[2 * BLOCK : 2 * BLOCK + SPAN_ROWS]
    below = traces[3 * BLOCK : 3 * BLOCK + SPAN_ROWS]
    span_a[...] = jnp.where(span_odd, below, above)
    span_b[...] = jnp.where(span_odd, above, below)


def parities():
    return lax.axis_index("pitch") % 2 == 1, lax.axis_index("span") % 2 == 1


def begin_kernel(x, wake, trace, state, pitch_a, pitch_b, span_a, span_b, inner):
    for e in range(2):
        lanes = slice(e * LANES, (e + 1) * LANES)
        for v in range(5):
            base = v * PER_VAR
            first = v * 250 + e
            for start, count, room, at in (
                (first, 25, PLANE, base),
                (first + 200, 25, PLANE, base + PLANE),
                (first + 50, 75, 80, base + 2 * PLANE),
            ):
                state[at + room - 8 : at + room, lanes] = jnp.zeros((8, LANES), jnp.float32)
                state[at : at + count, lanes] = x[pl.ds(start, count, stride=2), :]
    planes = wake[...]
    rows = lax.broadcasted_iota(jnp.int32, (50, LANES), 0)
    cols = lax.broadcasted_iota(jnp.int32, (50, LANES), 1)
    spread = jnp.zeros((50, LANES), jnp.float32)
    for s in range(5):
        mine = (cols - s) == 5 * (rows // 2)
        spread = jnp.where(mine, planes[:, s : s + 1], spread)
    own = [
        jnp.sum(jnp.where(rows % 2 == k, spread, 0.0), axis=0, keepdims=True) for k in range(2)
    ]
    traces = product(trace[...], None, *split(state[...]))
    pitch_odd, span_odd = parities()
    emit_faces(
        traces,
        jnp.concatenate(own, axis=0),
        pitch_odd,
        span_odd,
        (pitch_a, pitch_b, span_a, span_b, inner),
    )


def axial_terms(state):
    lanes = lax.broadcasted_iota(jnp.int32, (PLANE, LANES), 1)
    upper_parts, lower_parts = ([], [])
    for e in range(2):
        own = slice(e * LANES, (e + 1) * LANES)
        upper_gap, lower_gap = ([], [])
        for v in range(5):
            base = v * PER_VAR
            lower = state[base : base + PLANE, own]
            upper = state[base + PLANE : base + 2 * PLANE, own]
            after = jnp.where(lanes == LANES - 1, upper, pltpu.roll(lower, LANES - 1, 1))
            before = jnp.where(lanes == 0, 0.0, pltpu.roll(upper, 1, 1))
            upper_gap.append(upper - after)
            lower_gap.append(before - lower)
        mixed = []
        for gap, sign in ((upper_gap, -1.0), (lower_gap, 1.0)):
            table = lift_factor(0) * half_flux(0, sign)
            mixed.append(
                [
                    sum(float(table[i, j]) * gap[j] for j in range(5) if table[i, j] != 0.0)
                    for i in range(5)
                ]
            )
        upper_parts.append(mixed[0])
        lower_parts.append(mixed[1])
    return upper_parts, lower_parts


def advance_body(section, base, state, volume_high, volume_low, trace, partial, faces):
    rate = product(volume_high[...], volume_low[...], *split(state[...]))
    gain, keep = GAIN[section], KEEP[section]
    if keep == 0.0:
        partial[...] = state[...] + rate
    else:
        partial[...] = keep * base[...] + gain * (state[...] + rate)
    upper_parts, lower_parts = axial_terms(state)
    for e in range(2):
        lanes = slice(e * LANES, (e + 1) * LANES)
        for v in range(5):
            at = v * PER_VAR
            partial[at : at + PLANE, lanes] += gain * lower_parts[e][v]
            partial[at + PLANE : at + 2 * PLANE, lanes] += gain * upper_parts[e][v]
    faces[...] = product(trace[...], None, *split(partial[...]))


def first_kernel(state, volume_high, volume_low, trace, partial, faces):
    advance_body(0, None, state, volume_high, volume_low, trace, partial, faces)


def later_kernel(
    section, base, before, halo_high, halo_low, lift_high, lift_low, volume_high, volume_low,
    trace, partial, faces, state,
):
    lifted = product(lift_high[...], lift_low[...], halo_high[...], halo_low[...])
    state[...] = before[...] + GAIN[section - 1] * lifted
    advance_body(section, base, state, volume_high, volume_low, trace, partial, faces)


def gather_halo(section, offsets, pitch_a, pitch_b, span_a, span_b, inner, halo):
    pitch_odd, span_odd = parities()
    after = jnp.where(pitch_odd, pitch_b[...], pitch_a[...])
    before = jnp.where(pitch_odd, pitch_a[...], pitch_b[...])
    halo[0:BLOCK, :LANES] = before
    halo[0:BLOCK, LANES:] = inner[0:BLOCK]
    halo[BLOCK : 2 * BLOCK, :LANES] = inner[BLOCK:]
    halo[BLOCK : 2 * BLOCK, LANES:] = after
    above = jnp.where(span_odd, span_b[...], span_a[...])
    below = jnp.where(span_odd, span_a[...], span_b[...])
    rest = jnp.zeros((BLOCK - SPAN_ROWS, 2 * LANES), jnp.float32)
    halo[2 * BLOCK : 2 * BLOCK + SPAN_ROWS] = below
    halo[2 * BLOCK + SPAN_ROWS : 3 * BLOCK] = rest
    halo[3 * BLOCK : 3 * BLOCK + SPAN_ROWS] = above
    halo[3 * BLOCK + SPAN_ROWS : 4 * BLOCK] = rest
    wake = before[WAKE_ROW : WAKE_ROW + 2]
    moved = offsets[section] % 2 == 1
    rows = lax.broadcasted_iota(jnp.int32, (BLOCK, LANES), 0)
    cols = lax.broadcasted_iota(jnp.int32, (BLOCK, LANES), 1)
    for e in range(2):
        row = jnp.where(moved, wake[1 - e : 2 - e], wake[e : e + 1])
        column = jnp.sum(jnp.where(rows == cols, row, 0.0), axis=1, keepdims=True)
        halo[4 * BLOCK :, e * LANES : (e + 1) * LANES] = jnp.where(cols == 0, column, 0.0)
    return wake


def exchange_kernel(
    section, offsets, pitch_a, pitch_b, span_a, span_b, inner, faces, link_high, link_low,
    next_pitch_a, next_pitch_b, next_span_a, next_span_b, next_inner, halo_high, halo_low, halo,
):
    wake = gather_halo(section, offsets, pitch_a, pitch_b, span_a, span_b, inner, halo)
    high, low = split(halo[...])
    halo_high[...] = high
    halo_low[...] = low
    traces = faces[...] + GAIN[section] * product(link_high[...], link_low[...], high, low)
    pitch_odd, span_odd = parities()
    emit_faces(
        traces,
        wake,
        pitch_odd,
        span_odd,
        (next_pitch_a, next_pitch_b, next_span_a, next_span_b, next_inner),
    )


def final_kernel(
    offsets, pitch_a, pitch_b, span_a, span_b, inner, before, lift_high, lift_low, out, halo
):
    gather_halo(2, offsets, pitch_a, pitch_b, span_a, span_b, inner, halo)
    high, low = split(halo[...])
    lifted = product(lift_high[...], lift_low[...], high, low)
    result = before[...] + GAIN[2] * lifted
    for e in range(2):
        lanes = slice(e * LANES, (e + 1) * LANES)
        for v in range(5):
            base = v * PER_VAR
            first = v * 250 + e
            out[pl.ds(first, 25, stride=2), :] = result[base : base + 25, lanes]
            out[pl.ds(first + 200, 25, stride=2), :] = result[base + PLANE : base + PLANE + 25, lanes]
            at = base + 2 * PLANE
            out[pl.ds(first + 50, 75, stride=2), :] = result[at : at + 75, lanes]


IN_VMEM = pl.BlockSpec(memory_space=pltpu.VMEM)
IN_SMEM = pl.BlockSpec(memory_space=pltpu.SMEM)


def call(kernel, name, outs, args, scalars=0, scratch=(), flops=0):
    return pl.pallas_call(
        kernel,
        name=name,
        out_shape=[jax.ShapeDtypeStruct(shape, dtype) for shape, dtype in outs],
        in_specs=[IN_SMEM] * scalars + [IN_VMEM] * (len(args) - scalars),
        out_specs=[IN_VMEM] * len(outs),
        scratch_shapes=list(scratch),
        compiler_params=pltpu.CompilerParams(vmem_limit_bytes=VMEM_LIMIT),
        cost_estimate=pl.CostEstimate(flops=flops, bytes_accessed=2**20, transcendentals=0),
    )(*args)


def swapped(value, axis, odd, wrap):
    size = lax.axis_size(axis)
    pairs = []
    for i in range(odd, size if wrap else size - 1, 2):
        j = (i + 1) % size
        pairs += [(i, j), (j, i)]
    return lax.ppermute(value, axis, pairs)


def exchanged(faces):
    pitch_a, pitch_b, span_a, span_b, inner = faces
    return (
        swapped(pitch_a, "pitch", 0, True),
        swapped(pitch_b, "pitch", 1, True),
        swapped(span_a, "span", 0, False),
        swapped(span_b, "span", 1, False),
        inner,
    )


F32 = jnp.float32
FACE_OUTS = [
    ((BLOCK, LANES), F32),
    ((BLOCK, LANES), F32),
    ((SPAN_ROWS, 2 * LANES), F32),
    ((SPAN_ROWS, 2 * LANES), F32),
    ((2 * BLOCK, LANES), F32),
]
HALO_OUTS = [((HALO, 2 * LANES), jnp.bfloat16)] * 2
PARTIAL_OUTS = [((ROWS, 2 * LANES), F32), ((TRACES, 2 * LANES), F32)]


def shards(tables, state, wake_planes, bar_offsets):
    volume, lift, trace, link = tables
    x = state.reshape(-1, LANES)
    wake = wake_planes.transpose(0, 1, 3, 4, 2).reshape(50, 5)
    base, *faces = call(
        begin_kernel, "begin", [((ROWS, 2 * LANES), F32)] + FACE_OUTS, [x, wake, trace], flops=10**8
    )
    arrived = exchanged(faces)
    partial, traces = call(
        first_kernel, "first", PARTIAL_OUTS, [base, *volume, trace], flops=2 * 10**9
    )
    for section in range(2):
        *faces, high, low = call(
            functools.partial(exchange_kernel, section),
            "exchange",
            FACE_OUTS + HALO_OUTS,
            [bar_offsets, *arrived, traces, *link],
            scalars=1,
            scratch=[pltpu.VMEM((HALO, 2 * LANES), F32)],
            flops=10**8,
        )
        arrived = exchanged(faces)
        partial, traces = call(
            functools.partial(later_kernel, section + 1),
            "later",
            PARTIAL_OUTS,
            [base, partial, high, low, *lift, *volume, trace],
            scratch=[pltpu.VMEM((ROWS, 2 * LANES), F32)],
            flops=3 * 10**9,
        )
    (out,) = call(
        final_kernel,
        "final",
        [(x.shape, F32)],
        [bar_offsets, *arrived, partial, *lift],
        scalars=1,
        scratch=[pltpu.VMEM((HALO, 2 * LANES), F32)],
        flops=10**8,
    )
    return out.reshape(state.shape)


def solution(mesh):
    volume, lift, trace, link = operator_tables()
    tables = (
        split_table(volume),
        split_table(lift),
        trace.astype(ml_dtypes.bfloat16),
        split_table(link),
    )
    tables = jax.tree.map(jnp.asarray, tables)
    in_specs = (
        P(None, None, None, None, "pitch", "span", None),
        P(None, None, None, "pitch", "span"),
        P(),
    )
    out_specs = P(None, None, None, None, "pitch", "span", None)
    return jax.shard_map(
        functools.partial(shards, tables),
        mesh=mesh,
        in_specs=in_specs,
        out_specs=out_specs,
        check_vma=False,
    )
```

profile of v0, /device:TPU:0, one launch (start us, length us, event | category | flops | bytes accessed | tf_op | source)
XLA Modules:
  0.0 38.0 jit_solution(12825356979881379914)
XLA Ops:
  0.0 0.0 copy-start
  0.0 1.5 %pad = f32[1256,1,128]{2,1,0:T(1,128)S(1)} pad(f32[1250,1,128]{2,1,0:T(1,128)} %bitcast.12, f32[]{:T(128)} %constant.29), padding=0_6x0_0x0_0 | pad | bytes 1283076
  1.6 0.0 copy-done
  1.6 0.0 copy-start.7
  1.6 0.1 bitcast_reduce_fusion
  1.7 0.0 copy-done.5
  1.7 0.6 %begin.1 = (f32[720,256]{1,0:T(8,128)S(1)}, f32[128,128]{1,0:T(8,128)S(1)}, f32[128,128]{1,0:T(8,128)S(1)}, f32[104,256]{1,0:T(8,128)S(1)}, f32[104,256]{1,0:T(8,128)S(1)}, /*index=5*/f32[256,128]{1,0:T(8,128)S(1)}) custom-call(f32[1250,128]{1,0:T(8,128)S(1)} %bitcast.10, f32[50,5]{1,0:T(8,128)S(1)} %reshape.10.wake, bf16[512,720]{1,0:T(8,128)(2,1)S(1)} %copy-done.5), custom_call_target="tpu_custom_call" | custom-call | flops 100000000 | bytes 1048576 | tf_op jit(solution)/shard_map/begin/pallas_call | solution.py:323
  2.4 0.5 %collective-permute-start = (f32[128,128]{1,0:T(8,128)S(1)}, f32[128,128]{1,0:T(8,128)S(1)}, u32[]{:S(2)}, u32[]{:S(2)}) collective-permute-start(f32[128,128]{1,0:T(8,128)S(1)} %get-tuple-element.30), channel_id=1, source_target_pairs={{0,4},{4,0},{8,12},{12,8},{16,20},{20,16},{24,28},{28,24},{1,5},{5... | collective-permute-start | bytes 196616 | tf_op jit(solution)/shard_map/ppermute | solution.py:341
  2.9 3.6 %collective-permute-start.1 = (f32[128,128]{1,0:T(8,128)S(1)}, f32[128,128]{1,0:T(8,128)S(1)}, u32[]{:S(2)}, u32[]{:S(2)}) collective-permute-start(f32[128,128]{1,0:T(8,128)S(1)} %get-tuple-element.31), channel_id=1, source_target_pairs={{4,8},{8,4},{12,16},{16,12},{20,24},{24,20},{28,0},{0,28},{5,9},{9... | collective-permute-start | bytes 196616 | tf_op jit(solution)/shard_map/ppermute | solution.py:341
  6.5 1.6 %collective-permute-start.2 = (f32[104,256]{1,0:T(8,128)S(1)}, f32[104,256]{1,0:T(8,128)S(1)}, u32[]{:S(2)}, u32[]{:S(2)}) collective-permute-start(f32[104,256]{1,0:T(8,128)S(1)} %get-tuple-element.32), channel_id=1, source_target_pairs={{0,1},{1,0},{2,3},{3,2},{4,5},{5,4},{6,7},{7,6},{8,9},{9,8},{10,11... | collective-permute-start | bytes 319496 | tf_op jit(solution)/shard_map/ppermute | solution.py:341
  8.0 0.7 %collective-permute-start.3 = (f32[104,256]{1,0:T(8,128)S(1)}, f32[104,256]{1,0:T(8,128)S(1)}, u32[]{:S(2)}, u32[]{:S(2)}) collective-permute-start(f32[104,256]{1,0:T(8,128)S(1)} %get-tuple-element.33), channel_id=1, source_target_pairs={{1,2},{2,1},{5,6},{6,5},{9,10},{10,9},{13,14},{14,13},{17,18},{18,... | collective-permute-start | bytes 319496 | tf_op jit(solution)/shard_map/ppermute | solution.py:341
  8.7 0.0 copy-done.7
  8.7 0.0 copy-start.8
  8.7 1.2 %copy-done.8 = bf16[720,720]{1,0:T(8,128)(2,1)S(1)} copy-done((bf16[720,720]{1,0:T(8,128)(2,1)S(1)}, bf16[720,720]{1,0:T(8,128)(2,1)}, u32[]{:S(2)}) %copy-start.8) | copy-done | bytes 1036824
  10.0 2.2 %first.1 = (f32[720,256]{1,0:T(8,128)S(1)}, f32[512,256]{1,0:T(8,128)S(1)}) custom-call(f32[720,256]{1,0:T(8,128)S(1)} %get-tuple-element.35.state.base, bf16[720,720]{1,0:T(8,128)(2,1)S(1)} %copy-done.7, bf16[720,720]{1,0:T(8,128)(2,1)S(1)} %copy-done.8, bf16[512,720]{1,0:T(8,128)(2,1)S(1)} %copy-done.5), custom_call_target="tpu_custom_call" | custom-call | flops 2000000000 | bytes 1048576 | tf_op jit(solution)/shard_map/first/pallas_call | solution.py:323
  12.2 0.0 collective-permute-done.pitch_a
  12.2 0.0 collective-permute-done.1.pitch_b
  12.2 0.0 collective-permute-done.2.span_a
  12.2 0.0 collective-permute-done.3.span_b
  12.3 0.0 copy-done.1
  12.3 0.0 copy-done.2
  12.3 0.0 copy-done.6
  12.3 0.0 copy-start.3
  12.3 0.0 copy-start.4
  12.3 1.4 %exchange.2 = (f32[128,128]{1,0:T(8,128)S(1)}, f32[128,128]{1,0:T(8,128)S(1)}, f32[104,256]{1,0:T(8,128)S(1)}, f32[104,256]{1,0:T(8,128)S(1)}, f32[256,128]{1,0:...) custom-call(s32[3]{0:T(128)S(1)} %copy-done.6, f32[128,128]{1,0:T(8,128)S(1)} %collective-permute-done.pitch_a, ...), custom_call_target="tpu_custom_call" | custom-call | flops 100000000 | bytes 1048576 | tf_op jit(solution)/shard_map/exchange/pallas_call | solution.py:323
  13.7 0.1 collective-permute-start.4
  13.8 0.6 %collective-permute-start.5 = (f32[128,128]{1,0:T(8,128)S(1)}, f32[128,128]{1,0:T(8,128)S(1)}, u32[]{:S(2)}, u32[]{:S(2)}) collective-permute-start(f32[128,128]{1,0:T(8,128)S(1)} %get-tuple-element.38), channel_id=1, source_target_pairs={{4,8},{8,4},{12,16},{16,12},{20,24},{24,20},{28,0},{0,28},{5,9},{9... | collective-permute-start | bytes 196616 | tf_op jit(solution)/shard_map/ppermute | solution.py:341
  14.5 4.4 %collective-permute-start.6 = (f32[104,256]{1,0:T(8,128)S(1)}, f32[104,256]{1,0:T(8,128)S(1)}, u32[]{:S(2)}, u32[]{:S(2)}) collective-permute-start(f32[104,256]{1,0:T(8,128)S(1)} %get-tuple-element.39), channel_id=1, source_target_pairs={{0,1},{1,0},{2,3},{3,2},{4,5},{5,4},{6,7},{7,6},{8,9},{9,8},{10,11... | collective-permute-start | bytes 319496 | tf_op jit(solution)/shard_map/ppermute | solution.py:341
  18.9 0.7 %collective-permute-start.7 = (f32[104,256]{1,0:T(8,128)S(1)}, f32[104,256]{1,0:T(8,128)S(1)}, u32[]{:S(2)}, u32[]{:S(2)}) collective-permute-start(f32[104,256]{1,0:T(8,128)S(1)} %get-tuple-element.40), channel_id=1, source_target_pairs={{1,2},{2,1},{5,6},{6,5},{9,10},{10,9},{13,14},{14,13},{17,18},{18,... | collective-permute-start | bytes 319496 | tf_op jit(solution)/shard_map/ppermute | solution.py:341
  19.5 0.0 copy-done.9
  19.5 0.0 copy-done.3
  19.6 4.0 %later.2 = (f32[720,256]{1,0:T(8,128)S(1)}, f32[512,256]{1,0:T(8,128)S(1)}) custom-call(f32[720,256]{1,0:T(8,128)S(1)} %get-tuple-element.35.state.base, f32[720,256]{1,0:T(8,128)S(1)} %get-tuple-element.42.before, bf16[640,256]{1,0:T(8,128)(2,1)S(1)} %get-tuple-element.43.halo_high, bf16[640,256]{1,0:T(8,128)(2,1)S(1)} %get-tuple-element.44.halo_low, ...), custom_call_target="tpu_custom_call" | custom-call | flops 3000000000 | bytes 1048576 | tf_op jit(solution)/shard_map/later/pallas_call | solution.py:323
  23.6 0.0 collective-permute-done.4.pitch_a
  23.6 0.0 collective-permute-done.5.pitch_b
  23.6 0.0 collective-permute-done.6.span_a
  23.6 0.0 collective-permute-done.7.span_b
  23.6 1.4 %exchange.3 = (f32[128,128]{1,0:T(8,128)S(1)}, f32[128,128]{1,0:T(8,128)S(1)}, f32[104,256]{1,0:T(8,128)S(1)}, f32[104,256]{1,0:T(8,128)S(1)}, f32[256,128]{1,0:...) custom-call(s32[3]{0:T(128)S(1)} %copy-done.6, f32[128,128]{1,0:T(8,128)S(1)} %collective-permute-done.4.pitch_a, ...), custom_call_target="tpu_custom_call" | custom-call | flops 100000000 | bytes 1048576 | tf_op jit(solution)/shard_map/exchange/pallas_call | solution.py:323
  25.0 0.1 collective-permute-start.8
  25.1 1.9 %collective-permute-start.9 = (f32[128,128]{1,0:T(8,128)S(1)}, f32[128,128]{1,0:T(8,128)S(1)}, u32[]{:S(2)}, u32[]{:S(2)}) collective-permute-start(f32[128,128]{1,0:T(8,128)S(1)} %get-tuple-element.47), channel_id=1, source_target_pairs={{4,8},{8,4},{12,16},{16,12},{20,24},{24,20},{28,0},{0,28},{5,9},{9... | collective-permute-start | bytes 196616 | tf_op jit(solution)/shard_map/ppermute | solution.py:341
  27.0 2.6 %collective-permute-start.10 = (f32[104,256]{1,0:T(8,128)S(1)}, f32[104,256]{1,0:T(8,128)S(1)}, u32[]{:S(2)}, u32[]{:S(2)}) collective-permute-start(f32[104,256]{1,0:T(8,128)S(1)} %get-tuple-element.48), channel_id=1, source_target_pairs={{0,1},{1,0},{2,3},{3,2},{4,5},{5,4},{6,7},{7,6},{8,9},{9,8},{10,11... | collective-permute-start | bytes 319496 | tf_op jit(solution)/shard_map/ppermute | solution.py:341
  29.6 0.7 %collective-permute-start.11 = (f32[104,256]{1,0:T(8,128)S(1)}, f32[104,256]{1,0:T(8,128)S(1)}, u32[]{:S(2)}, u32[]{:S(2)}) collective-permute-start(f32[104,256]{1,0:T(8,128)S(1)} %get-tuple-element.49), channel_id=1, source_target_pairs={{1,2},{2,1},{5,6},{6,5},{9,10},{10,9},{13,14},{14,13},{17,18},{18,... | collective-permute-start | bytes 319496 | tf_op jit(solution)/shard_map/ppermute | solution.py:341
  30.2 4.8 %later.3 = (f32[720,256]{1,0:T(8,128)S(1)}, f32[512,256]{1,0:T(8,128)}) custom-call(f32[720,256]{1,0:T(8,128)S(1)} %get-tuple-element.35.state.base, f32[720,256]{1,0:T(8,128)S(1)} %get-tuple-element.51.before, bf16[640,256]{1,0:T(8,128)(2,1)S(1)} %get-tuple-element.52.halo_high, bf16[640,256]{1,0:T(8,128)(2,1)S(1)} %get-tuple-element.53.halo_low, ...), custom_call_target="tpu_custom_call" | custom-call | flops 3000000000 | bytes 1048576 | tf_op jit(solution)/shard_map/later/pallas_call | solution.py:323
  35.0 0.0 collective-permute-done.8.pitch_a
  35.0 0.0 collective-permute-done.9.pitch_b
  35.0 0.0 collective-permute-done.10.span_a
  35.0 0.0 collective-permute-done.11.span_b
  35.1 1.7 %final.1 = f32[1250,128]{1,0:T(8,128)S(1)} custom-call(s32[3]{0:T(128)S(1)} %copy-done.6, f32[128,128]{1,0:T(8,128)S(1)} %collective-permute-done.8.pitch_a, f32[128,128]{1,0:T(8,128)S(1)} %collective-permute-done.9.pitch_b, f32[104,256]{1,0:T(8,128)S(1)} %collective-permute-done.10.span_a, f32[104,256]{1,0:T(8,128)S(1)} %collective-permute-done.11.span_b, ...), custom_call_target="tpu_custom_call" | custom-call | flops 100000000 | bytes 1048576 | tf_op jit(solution)/shard_map/final/pallas_call | solution.py:323
  36.7 1.2 %reshape.11 = f32[5,5,5,5,2,1,128]{6,4,3,2,1,0,5:T(2,128)} reshape(f32[1250,128]{1,0:T(8,128)S(1)} %final.1) | data formatting | bytes 1280000 | tf_op jit(solution)/shard_map/reshape | solution.py:406
  (8 shorter events, 0.1 us)
Async XLA Ops:
  0.0 1.6 %copy-start = (f32[5,5,5,2,1]{2,4,3,1,0:T(1,128)S(1)}, f32[5,5,5,2,1]{2,4,3,1,0:T(1,128)}, u32[]{:S(2)}) copy-start(f32[5,5,5,2,1]{2,4,3,1,0:T(1,128)} %param.11) | copy-start | bytes 3004
  0.0 1.7 %copy-start.5 = (bf16[512,720]{1,0:T(8,128)(2,1)S(1)}, bf16[512,720]{1,0:T(8,128)(2,1)}, u32[]{:S(2)}) copy-start(bf16[512,720]{1,0:T(8,128)(2,1)} %constant.14.clone.trace) | copy-start | bytes 2211844
  1.6 7.1 %copy-start.7 = (bf16[720,720]{1,0:T(8,128)(2,1)S(1)}, bf16[720,720]{1,0:T(8,128)(2,1)}, u32[]{:S(2)}) copy-start(bf16[720,720]{1,0:T(8,128)(2,1)} %constant.15.clone.volume_high) | copy-start | bytes 3110404
  2.4 9.8 %collective-permute-start = (f32[128,128]{1,0:T(8,128)S(1)}, f32[128,128]{1,0:T(8,128)S(1)}, u32[]{:S(2)}, u32[]{:S(2)}) collective-permute-start(f32[128,128]{1,0:T(8,128)S(1)} %get-tuple-element.30), channel_id=1, source_target_pairs={{0,4},{4,0},{8,12},{12,8},{16,20},{20,16},{24,28},{28,24},{1,5},{5... | collective-permute-start | bytes 196616 | tf_op jit(solution)/shard_map/ppermute | solution.py:341
  2.9 9.3 %collective-permute-start.1 = (f32[128,128]{1,0:T(8,128)S(1)}, f32[128,128]{1,0:T(8,128)S(1)}, u32[]{:S(2)}, u32[]{:S(2)}) collective-permute-start(f32[128,128]{1,0:T(8,128)S(1)} %get-tuple-element.31), channel_id=1, source_target_pairs={{4,8},{8,4},{12,16},{16,12},{20,24},{24,20},{28,0},{0,28},{5,9},{9... | collective-permute-start | bytes 196616 | tf_op jit(solution)/shard_map/ppermute | solution.py:341
  6.5 5.8 %collective-permute-start.2 = (f32[104,256]{1,0:T(8,128)S(1)}, f32[104,256]{1,0:T(8,128)S(1)}, u32[]{:S(2)}, u32[]{:S(2)}) collective-permute-start(f32[104,256]{1,0:T(8,128)S(1)} %get-tuple-element.32), channel_id=1, source_target_pairs={{0,1},{1,0},{2,3},{3,2},{4,5},{5,4},{6,7},{7,6},{8,9},{9,8},{10,11... | collective-permute-start | bytes 319496 | tf_op jit(solution)/shard_map/ppermute | solution.py:341
  8.0 4.2 %collective-permute-start.3 = (f32[104,256]{1,0:T(8,128)S(1)}, f32[104,256]{1,0:T(8,128)S(1)}, u32[]{:S(2)}, u32[]{:S(2)}) collective-permute-start(f32[104,256]{1,0:T(8,128)S(1)} %get-tuple-element.33), channel_id=1, source_target_pairs={{1,2},{2,1},{5,6},{6,5},{9,10},{10,9},{13,14},{14,13},{17,18},{18,... | collective-permute-start | bytes 319496 | tf_op jit(solution)/shard_map/ppermute | solution.py:341
  8.7 1.2 %copy-start.8 = (bf16[720,720]{1,0:T(8,128)(2,1)S(1)}, bf16[720,720]{1,0:T(8,128)(2,1)}, u32[]{:S(2)}) copy-start(bf16[720,720]{1,0:T(8,128)(2,1)} %constant.16.clone.volume_low) | copy-start | bytes 3110404
  10.0 2.3 %copy-start.1 = (bf16[512,640]{1,0:T(8,128)(2,1)S(1)}, bf16[512,640]{1,0:T(8,128)(2,1)}, u32[]{:S(2)}) copy-start(bf16[512,640]{1,0:T(8,128)(2,1)} %constant.17.clone.link_high) | copy-start | bytes 1966084
  10.0 2.3 %copy-start.2 = (bf16[512,640]{1,0:T(8,128)(2,1)S(1)}, bf16[512,640]{1,0:T(8,128)(2,1)}, u32[]{:S(2)}) copy-start(bf16[512,640]{1,0:T(8,128)(2,1)} %constant.18.clone.link_low) | copy-start | bytes 1966084
  10.0 2.3 %copy-start.6 = (s32[3]{0:T(128)S(1)}, s32[3]{0:T(128)}, u32[]{:S(2)}) copy-start(s32[3]{0:T(128)} %offsets.5) | copy-start | bytes 40
  10.0 9.6 %copy-start.9 = (bf16[720,720]{1,0:T(8,128)(2,1)S(1)}, bf16[720,720]{1,0:T(8,128)(2,1)}, u32[]{:S(2)}) copy-start(bf16[720,720]{1,0:T(8,128)(2,1)} %constant.16.clone.volume_low) | copy-start | bytes 3110404
  12.3 7.2 %copy-start.3 = (bf16[720,640]{1,0:T(8,128)(2,1)S(1)}, bf16[720,640]{1,0:T(8,128)(2,1)}, u32[]{:S(2)}) copy-start(bf16[720,640]{1,0:T(8,128)(2,1)} %constant.19.clone.lift_high) | copy-start | bytes 2764804
  12.3 7.2 %copy-start.4 = (bf16[720,640]{1,0:T(8,128)(2,1)S(1)}, bf16[720,640]{1,0:T(8,128)(2,1)}, u32[]{:S(2)}) copy-start(bf16[720,640]{1,0:T(8,128)(2,1)} %constant.20.clone.lift_low) | copy-start | bytes 2764804
  13.7 9.8 %collective-permute-start.4 = (f32[128,128]{1,0:T(8,128)S(1)}, f32[128,128]{1,0:T(8,128)S(1)}, u32[]{:S(2)}, u32[]{:S(2)}) collective-permute-start(f32[128,128]{1,0:T(8,128)S(1)} %get-tuple-element.37), channel_id=1, source_target_pairs={{0,4},{4,0},{8,12},{12,8},{16,20},{20,16},{24,28},{28,24},{1,5},{5... | collective-permute-start | bytes 196616 | tf_op jit(solution)/shard_map/ppermute | solution.py:341
  13.8 9.7 %collective-permute-start.5 = (f32[128,128]{1,0:T(8,128)S(1)}, f32[128,128]{1,0:T(8,128)S(1)}, u32[]{:S(2)}, u32[]{:S(2)}) collective-permute-start(f32[128,128]{1,0:T(8,128)S(1)} %get-tuple-element.38), channel_id=1, source_target_pairs={{4,8},{8,4},{12,16},{16,12},{20,24},{24,20},{28,0},{0,28},{5,9},{9... | collective-permute-start | bytes 196616 | tf_op jit(solution)/shard_map/ppermute | solution.py:341
  14.5 9.1 %collective-permute-start.6 = (f32[104,256]{1,0:T(8,128)S(1)}, f32[104,256]{1,0:T(8,128)S(1)}, u32[]{:S(2)}, u32[]{:S(2)}) collective-permute-start(f32[104,256]{1,0:T(8,128)S(1)} %get-tuple-element.39), channel_id=1, source_target_pairs={{0,1},{1,0},{2,3},{3,2},{4,5},{5,4},{6,7},{7,6},{8,9},{9,8},{10,11... | collective-permute-start | bytes 319496 | tf_op jit(solution)/shard_map/ppermute | solution.py:341
  18.9 4.7 %collective-permute-start.7 = (f32[104,256]{1,0:T(8,128)S(1)}, f32[104,256]{1,0:T(8,128)S(1)}, u32[]{:S(2)}, u32[]{:S(2)}) collective-permute-start(f32[104,256]{1,0:T(8,128)S(1)} %get-tuple-element.40), channel_id=1, source_target_pairs={{1,2},{2,1},{5,6},{6,5},{9,10},{10,9},{13,14},{14,13},{17,18},{18,... | collective-permute-start | bytes 319496 | tf_op jit(solution)/shard_map/ppermute | solution.py:341
  25.0 10.0 %collective-permute-start.8 = (f32[128,128]{1,0:T(8,128)S(1)}, f32[128,128]{1,0:T(8,128)S(1)}, u32[]{:S(2)}, u32[]{:S(2)}) collective-permute-start(f32[128,128]{1,0:T(8,128)S(1)} %get-tuple-element.46), channel_id=1, source_target_pairs={{0,4},{4,0},{8,12},{12,8},{16,20},{20,16},{24,28},{28,24},{1,5},{5... | collective-permute-start | bytes 196616 | tf_op jit(solution)/shard_map/ppermute | solution.py:341
  25.1 9.9 %collective-permute-start.9 = (f32[128,128]{1,0:T(8,128)S(1)}, f32[128,128]{1,0:T(8,128)S(1)}, u32[]{:S(2)}, u32[]{:S(2)}) collective-permute-start(f32[128,128]{1,0:T(8,128)S(1)} %get-tuple-element.47), channel_id=1, source_target_pairs={{4,8},{8,4},{12,16},{16,12},{20,24},{24,20},{28,0},{0,28},{5,9},{9... | collective-permute-start | bytes 196616 | tf_op jit(solution)/shard_map/ppermute | solution.py:341
  27.0 8.1 %collective-permute-start.10 = (f32[104,256]{1,0:T(8,128)S(1)}, f32[104,256]{1,0:T(8,128)S(1)}, u32[]{:S(2)}, u32[]{:S(2)}) collective-permute-start(f32[104,256]{1,0:T(8,128)S(1)} %get-tuple-element.48), channel_id=1, source_target_pairs={{0,1},{1,0},{2,3},{3,2},{4,5},{5,4},{6,7},{7,6},{8,9},{9,8},{10,11... | collective-permute-start | bytes 319496 | tf_op jit(solution)/shard_map/ppermute | solution.py:341
  29.6 5.5 %collective-permute-start.11 = (f32[104,256]{1,0:T(8,128)S(1)}, f32[104,256]{1,0:T(8,128)S(1)}, u32[]{:S(2)}, u32[]{:S(2)}) collective-permute-start(f32[104,256]{1,0:T(8,128)S(1)} %get-tuple-element.49), channel_id=1, source_target_pairs={{1,2},{2,1},{5,6},{6,5},{9,10},{10,9},{13,14},{14,13},{17,18},{18,... | collective-permute-start | bytes 319496 | tf_op jit(solution)/shard_map/ppermute | solution.py:341
where the time goes:
time: 38.2 us; the launch traced here: 38 us
  starting transfers between devices  17.2 us (45%)
  Pallas kernels  16.2 us (42%)
  local copies, waits for them, and re-layouts  4.17 us (11%)
    ppermute x12, starting transfers between devices, swapped(): return lax.ppermute(value, axis, pairs)  17.2 us
    pallas_call x7, Pallas kernels, call(): pl.pallas_call(kernel, name=name, out_shape=[jax.ShapeDtypeStruct(shape,...  16.2 us
    unnamed x22, local copies, waits for them, and re-layouts  2.86 us
    reshape x1, local copies, waits for them, and re-layouts, shards(): return out.reshape(state.shape)  1.21 us
  transfers between devices with their start and end apart: 12, of which 0 were waited for; matrix products, arithmetic and copies ran while one was open for 0% of the time, Pallas kernels for 29%

commit v1 on v0

--- a/solution.py
+++ b/solution.py
@@ -17,9 +17,12 @@
 KEEP = (0.0, 0.75, 1.0 / 3.0)
 GAIN = (1.0, 0.25, 2.0 / 3.0)
 
-PLANE = 32
-PER_VAR = 144
+ORDER = (1, 4, 2, 3, 0)
+MAIN = 24
+TAIL = 5 * MAIN
+PER_VAR = 128
 ROWS = 5 * PER_VAR
+TILES = ((0, 0, 2), (1, 2, 4), (4, 4, 5))
 BLOCK = 128
 SPAN_ROWS = 104
 TRACES = 4 * BLOCK
@@ -59,9 +62,17 @@
     return TIME_STEP * 2.0 / (ELEM_SIZE[direction] * END_WEIGHT)
 
 
+def half_scales():
+    return (lift_factor(1) / 10.0, lift_factor(1), lift_factor(2), lift_factor(2), lift_factor(0))
+
+
+def var_start(v):
+    return ORDER.index(v) * PER_VAR
+
+
 def node_row(v, a, p, s):
-    start = {0: 0, 4: PLANE}.get(a, 2 * PLANE + (a - 1) * 25)
-    return v * PER_VAR + start + p * 5 + s
+    node = p * 5 + s
+    return var_start(v) + (a * MAIN + node if node < MAIN else TAIL + a)
 
 
 def operator_tables():
@@ -117,7 +128,14 @@
                 if a == 0:
                     cols = [4 * BLOCK + v * 25 + p * 5 + s for v in range(5)]
                     lift[np.ix_(here, cols)] += lift_factor(0) * plus[0]
+    lift = lift / np.repeat(half_scales(), BLOCK)
     return volume, lift, trace, trace @ lift
+
+
+def exact_table(table):
+    exact = table.astype(ml_dtypes.bfloat16)
+    assert np.allclose(exact.astype(np.float64), table, rtol=1e-12, atol=1e-12)
+    return exact
 
 
 def split_table(table):
@@ -132,10 +150,12 @@
     return high, low
 
 
-def product(high, low, values_high, values_low):
-    dot = functools.partial(jnp.dot, preferred_element_type=jnp.float32)
-    total = dot(high, values_high) + dot(high, values_low)
-    return total if low is None else total + dot(low, values_high)
+def dot(left, right):
+    return jnp.dot(left, right, preferred_element_type=jnp.float32)
+
+
+def product(table, high, low):
+    return dot(table, high) + dot(table, low)
 
 
 def emit_faces(traces, wake, pitch_odd, span_odd, outs):
@@ -161,18 +181,18 @@
 
 
 def begin_kernel(x, wake, trace, state, pitch_a, pitch_b, span_a, span_b, inner):
+    flat = x.reshape(x.shape[0], LANES)
     for e in range(2):
         lanes = slice(e * LANES, (e + 1) * LANES)
         for v in range(5):
-            base = v * PER_VAR
+            base = var_start(v)
             first = v * 250 + e
-            for start, count, room, at in (
-                (first, 25, PLANE, base),
-                (first + 200, 25, PLANE, base + PLANE),
-                (first + 50, 75, 80, base + 2 * PLANE),
-            ):
-                state[at + room - 8 : at + room, lanes] = jnp.zeros((8, LANES), jnp.float32)
-                state[at : at + count, lanes] = x[pl.ds(start, count, stride=2), :]
+            for a in range(5):
+                at = base + a * MAIN
+                state[at : at + MAIN, lanes] = flat[pl.ds(first + a * 50, MAIN, stride=2), :]
+            tail = base + TAIL
+            state[tail : tail + 8, lanes] = jnp.zeros((8, LANES), jnp.float32)
+            state[tail : tail + 5, lanes] = flat[pl.ds(first + 2 * MAIN, 5, stride=50), :]
     planes = wake[...]
     rows = lax.broadcasted_iota(jnp.int32, (50, LANES), 0)
     cols = lax.broadcasted_iota(jnp.int32, (50, LANES), 1)
@@ -183,7 +203,7 @@
     own = [
         jnp.sum(jnp.where(rows % 2 == k, spread, 0.0), axis=0, keepdims=True) for k in range(2)
     ]
-    traces = product(trace[...], None, *split(state[...]))
+    traces = product(trace[...], *split(state[...]))
     pitch_odd, span_odd = parities()
     emit_faces(
         traces,
@@ -194,78 +214,97 @@
     )
 
 
-def axial_terms(state):
-    lanes = lax.broadcasted_iota(jnp.int32, (PLANE, LANES), 1)
-    upper_parts, lower_parts = ([], [])
+def add_axial_terms(gain, state, partial):
+    lanes = lax.broadcasted_iota(jnp.int32, (MAIN + 8, LANES), 1)
+    rows = lax.broadcasted_iota(jnp.int32, (8, LANES), 0)
     for e in range(2):
         own = slice(e * LANES, (e + 1) * LANES)
         upper_gap, lower_gap = ([], [])
         for v in range(5):
-            base = v * PER_VAR
-            lower = state[base : base + PLANE, own]
-            upper = state[base + PLANE : base + 2 * PLANE, own]
-            after = jnp.where(lanes == LANES - 1, upper, pltpu.roll(lower, LANES - 1, 1))
-            before = jnp.where(lanes == 0, 0.0, pltpu.roll(upper, 1, 1))
-            upper_gap.append(upper - after)
-            lower_gap.append(before - lower)
+            base = var_start(v)
+            lower = state[base : base + MAIN, own]
+            upper = state[base + 4 * MAIN : base + TAIL, own]
+            tail = state[base + TAIL : base + PER_VAR, own]
+            turned = pltpu.roll(tail, 4, 0)
+            join = lambda main, end: jnp.concatenate([main, end], axis=0)
+            after = pltpu.roll(join(lower, turned), LANES - 1, 1)
+            before = pltpu.roll(join(upper, turned), 1, 1)
+            upper = join(upper, tail)
+            upper_gap.append(jnp.where(lanes == LANES - 1, 0.0, upper - after))
+            lower_gap.append(jnp.where(lanes == 0, 0.0, before) - join(lower, tail))
         mixed = []
         for gap, sign in ((upper_gap, -1.0), (lower_gap, 1.0)):
-            table = lift_factor(0) * half_flux(0, sign)
+            table = gain * lift_factor(0) * half_flux(0, sign)
             mixed.append(
                 [
                     sum(float(table[i, j]) * gap[j] for j in range(5) if table[i, j] != 0.0)
                     for i in range(5)
                 ]
             )
-        upper_parts.append(mixed[0])
-        lower_parts.append(mixed[1])
-    return upper_parts, lower_parts
-
-
-def advance_body(section, base, state, volume_high, volume_low, trace, partial, faces):
-    rate = product(volume_high[...], volume_low[...], *split(state[...]))
+        for v in range(5):
+            base = var_start(v)
+            upper, lower = (mixed[0][v], mixed[1][v])
+            partial[base : base + MAIN, own] += lower[:MAIN]
+            partial[base + 4 * MAIN : base + TAIL, own] += upper[:MAIN]
+            ends = jnp.where(rows == 0, lower[MAIN:], jnp.where(rows == 4, upper[MAIN:], 0.0))
+            partial[base + TAIL : base + PER_VAR, own] += ends
+
+
+def volume_rate(tables, high, low):
+    rate = [None] * 5
+    for (first, start, stop), table_high, table_low in zip(TILES, tables[:3], tables[3:]):
+        part = slice(start * PER_VAR, stop * PER_VAR)
+        term = product(table_high[...], high[part], low[part]) + dot(table_low[...], high[part])
+        for v in range(first, 5):
+            block = term[(v - first) * PER_VAR : (v - first + 1) * PER_VAR]
+            rate[v] = block if rate[v] is None else rate[v] + block
+    return jnp.concatenate(rate, axis=0)
+
+
+def advance_body(section, base, state, volume, partial):
+    rate = volume_rate(volume, *split(state[...]))
     gain, keep = GAIN[section], KEEP[section]
     if keep == 0.0:
         partial[...] = state[...] + rate
     else:
         partial[...] = keep * base[...] + gain * (state[...] + rate)
-    upper_parts, lower_parts = axial_terms(state)
-    for e in range(2):
-        lanes = slice(e * LANES, (e + 1) * LANES)
-        for v in range(5):
-            at = v * PER_VAR
-            partial[at : at + PLANE, lanes] += gain * lower_parts[e][v]
-            partial[at + PLANE : at + 2 * PLANE, lanes] += gain * upper_parts[e][v]
-    faces[...] = product(trace[...], None, *split(partial[...]))
-
-
-def first_kernel(state, volume_high, volume_low, trace, partial, faces):
-    advance_body(0, None, state, volume_high, volume_low, trace, partial, faces)
-
-
-def later_kernel(
-    section, base, before, halo_high, halo_low, lift_high, lift_low, volume_high, volume_low,
-    trace, partial, faces, state,
-):
-    lifted = product(lift_high[...], lift_low[...], halo_high[...], halo_low[...])
-    state[...] = before[...] + GAIN[section - 1] * lifted
-    advance_body(section, base, state, volume_high, volume_low, trace, partial, faces)
+    add_axial_terms(gain, state, partial)
+
+
+def first_kernel(state, trace, *refs):
+    *volume, partial, faces = refs
+    advance_body(0, None, state, volume, partial)
+    faces[...] = product(trace[...], *split(partial[...]))
+
+
+def later_kernel(section, base, before, halo_high, halo_low, lift, trace, *refs):
+    *volume, partial, faces, state = refs
+    state[...] = before[...] + GAIN[section - 1] * product(lift[...], halo_high[...], halo_low[...])
+    advance_body(section, base, state, volume, partial)
+    faces[...] = product(trace[...], *split(partial[...]))
+
+
+def last_kernel(section, base, before, halo_high, halo_low, lift, *refs):
+    *volume, partial, state = refs
+    state[...] = before[...] + GAIN[section - 1] * product(lift[...], halo_high[...], halo_low[...])
+    advance_body(section, base, state, volume, partial)
 
 
 def gather_halo(section, offsets, pitch_a, pitch_b, span_a, span_b, inner, halo):
     pitch_odd, span_odd = parities()
     after = jnp.where(pitch_odd, pitch_b[...], pitch_a[...])
     before = jnp.where(pitch_odd, pitch_a[...], pitch_b[...])
-    halo[0:BLOCK, :LANES] = before
-    halo[0:BLOCK, LANES:] = inner[0:BLOCK]
-    halo[BLOCK : 2 * BLOCK, :LANES] = inner[BLOCK:]
-    halo[BLOCK : 2 * BLOCK, LANES:] = after
+    scales = half_scales()
+    halo[0:BLOCK, :LANES] = scales[0] * before
+    halo[0:BLOCK, LANES:] = scales[0] * inner[0:BLOCK]
+    halo[BLOCK : 2 * BLOCK, :LANES] = scales[1] * inner[BLOCK:]
+    halo[BLOCK : 2 * BLOCK, LANES:] = scales[1] * after
     above = jnp.where(span_odd, span_b[...], span_a[...])
     below = jnp.where(span_odd, span_a[...], span_b[...])
     rest = jnp.zeros((BLOCK - SPAN_ROWS, 2 * LANES), jnp.float32)
-    halo[2 * BLOCK : 2 * BLOCK + SPAN_ROWS] = below
+    halo[2 * BLOCK : 2 * BLOCK + SPAN_ROWS] = scales[2] * below
     halo[2 * BLOCK + SPAN_ROWS : 3 * BLOCK] = rest
-    halo[3 * BLOCK : 3 * BLOCK + SPAN_ROWS] = above
+    halo[3 * BLOCK : 3 * BLOCK + SPAN_ROWS] = scales[3] * above
     halo[3 * BLOCK + SPAN_ROWS : 4 * BLOCK] = rest
     wake = before[WAKE_ROW : WAKE_ROW + 2]
     moved = offsets[section] % 2 == 1
@@ -274,19 +313,21 @@
     for e in range(2):
         row = jnp.where(moved, wake[1 - e : 2 - e], wake[e : e + 1])
         column = jnp.sum(jnp.where(rows == cols, row, 0.0), axis=1, keepdims=True)
-        halo[4 * BLOCK :, e * LANES : (e + 1) * LANES] = jnp.where(cols == 0, column, 0.0)
+        halo[4 * BLOCK :, e * LANES : (e + 1) * LANES] = jnp.where(
+            cols == 0, scales[4] * column, 0.0
+        )
     return wake
 
 
 def exchange_kernel(
-    section, offsets, pitch_a, pitch_b, span_a, span_b, inner, faces, link_high, link_low,
+    section, offsets, pitch_a, pitch_b, span_a, span_b, inner, faces, link,
     next_pitch_a, next_pitch_b, next_span_a, next_span_b, next_inner, halo_high, halo_low, halo,
 ):
     wake = gather_halo(section, offsets, pitch_a, pitch_b, span_a, span_b, inner, halo)
     high, low = split(halo[...])
     halo_high[...] = high
     halo_low[...] = low
-    traces = faces[...] + GAIN[section] * product(link_high[...], link_low[...], high, low)
+    traces = faces[...] + GAIN[section] * product(link[...], high, low)
     pitch_odd, span_odd = parities()
     emit_faces(
         traces,
@@ -298,21 +339,22 @@
 
 
 def final_kernel(
-    offsets, pitch_a, pitch_b, span_a, span_b, inner, before, lift_high, lift_low, out, halo
+    offsets, pitch_a, pitch_b, span_a, span_b, inner, before, lift, out, halo
 ):
     gather_halo(2, offsets, pitch_a, pitch_b, span_a, span_b, inner, halo)
     high, low = split(halo[...])
-    lifted = product(lift_high[...], lift_low[...], high, low)
-    result = before[...] + GAIN[2] * lifted
+    result = before[...] + GAIN[2] * product(lift[...], high, low)
+    flat = out.reshape(out.shape[0], LANES)
     for e in range(2):
         lanes = slice(e * LANES, (e + 1) * LANES)
         for v in range(5):
-            base = v * PER_VAR
+            base = var_start(v)
             first = v * 250 + e
-            out[pl.ds(first, 25, stride=2), :] = result[base : base + 25, lanes]
-            out[pl.ds(first + 200, 25, stride=2), :] = result[base + PLANE : base + PLANE + 25, lanes]
-            at = base + 2 * PLANE
-            out[pl.ds(first + 50, 75, stride=2), :] = result[at : at + 75, lanes]
+            for a in range(5):
+                at = base + a * MAIN
+                flat[pl.ds(first + a * 50, MAIN, stride=2), :] = result[at : at + MAIN, lanes]
+            tail = base + TAIL
+            flat[pl.ds(first + 2 * MAIN, 5, stride=50), :] = result[tail : tail + 5, lanes]
 
 
 IN_VMEM = pl.BlockSpec(memory_space=pltpu.VMEM)
@@ -366,39 +408,41 @@
 
 def shards(tables, state, wake_planes, bar_offsets):
     volume, lift, trace, link = tables
-    x = state.reshape(-1, LANES)
+    x = state.reshape(-1, 1, LANES)
     wake = wake_planes.transpose(0, 1, 3, 4, 2).reshape(50, 5)
     base, *faces = call(
         begin_kernel, "begin", [((ROWS, 2 * LANES), F32)] + FACE_OUTS, [x, wake, trace], flops=10**8
     )
     arrived = exchanged(faces)
     partial, traces = call(
-        first_kernel, "first", PARTIAL_OUTS, [base, *volume, trace], flops=2 * 10**9
+        first_kernel, "first", PARTIAL_OUTS, [base, trace, *volume], flops=2 * 10**9
     )
     for section in range(2):
         *faces, high, low = call(
             functools.partial(exchange_kernel, section),
             "exchange",
             FACE_OUTS + HALO_OUTS,
-            [bar_offsets, *arrived, traces, *link],
+            [bar_offsets, *arrived, traces, link],
             scalars=1,
             scratch=[pltpu.VMEM((HALO, 2 * LANES), F32)],
             flops=10**8,
         )
         arrived = exchanged(faces)
-        partial, traces = call(
-            functools.partial(later_kernel, section + 1),
-            "later",
-            PARTIAL_OUTS,
-            [base, partial, high, low, *lift, *volume, trace],
+        last = section == 1
+        partial, *traces = call(
+            functools.partial(last_kernel if last else later_kernel, section + 1),
+            "last" if last else "later",
+            PARTIAL_OUTS[:1] if last else PARTIAL_OUTS,
+            [base, partial, high, low, lift] + ([] if last else [trace]) + [*volume],
             scratch=[pltpu.VMEM((ROWS, 2 * LANES), F32)],
-            flops=3 * 10**9,
+            flops=2 * 10**9,
         )
+        traces = None if last else traces[0]
     (out,) = call(
         final_kernel,
         "final",
         [(x.shape, F32)],
-        [bar_offsets, *arrived, partial, *lift],
+        [bar_offsets, *arrived, partial, lift],
         scalars=1,
         scratch=[pltpu.VMEM((HALO, 2 * LANES), F32)],
         flops=10**8,
@@ -408,11 +452,17 @@
 
 def solution(mesh):
     volume, lift, trace, link = operator_tables()
+    blocks = []
+    for first, start, stop in TILES:
+        blocks.append(volume[first * PER_VAR :, start * PER_VAR : stop * PER_VAR].copy())
+        volume[first * PER_VAR :, start * PER_VAR : stop * PER_VAR] = 0.0
+    assert not volume.any()
+    halves = [split_table(block) for block in blocks]
     tables = (
-        split_table(volume),
-        split_table(lift),
-        trace.astype(ml_dtypes.bfloat16),
-        split_table(link),
+        [high for high, _ in halves] + [low for _, low in halves],
+        exact_table(lift),
+        exact_table(trace),
+        exact_table(link),
     )
     tables = jax.tree.map(jnp.asarray, tables)
     in_specs = (

time: 38.2 us -> 37.4 us (0.979)
  the two profiles are of different devices: /device:TPU:0 before, /device:TPU:8 now
where the time goes in v1:
time: 37.4 us; the launch traced here: 37 us
  starting transfers between devices  16.6 us (44%)
  Pallas kernels  11.8 us (32%)
  local copies, waits for them, and re-layouts  5.58 us (15%)
  waiting for transfers between devices  2.76 us (7%)
    ppermute x12, starting transfers between devices, swapped(): return lax.ppermute(value, axis, pairs)  16.6 us
    pallas_call x7, Pallas kernels, call(): pl.pallas_call(kernel, name=name, out_shape=[jax.ShapeDtypeStruct(shape,...  11.8 us
    unnamed x30, local copies, waits for them, and re-layouts  5.48 us
    ppermute x12, waiting for transfers between devices, swapped(): return lax.ppermute(value, axis, pairs)  2.76 us
  transfers between devices with their start and end apart: 12, of which 2 were waited for; matrix products, arithmetic and copies ran while one was open for 0% of the time, Pallas kernels for 18%

profile of v1, /device:TPU:8, one launch (start us, length us, event | category | flops | bytes accessed | tf_op | source)
XLA Modules:
  0.0 37.0 jit_solution(17083229155896716457)
XLA Ops:
  0.0 0.0 copy-start
  0.0 0.7 %copy-done = f32[5,5,5,2,1]{2,4,3,1,0:T(1,128)S(1)} copy-done((f32[5,5,5,2,1]{2,4,3,1,0:T(1,128)S(1)}, f32[5,5,5,2,1]{2,4,3,1,0:T(1,128)}, u32[]{:S(2)}) %copy-start) | copy-done | bytes 1024
  0.7 0.1 bitcast_reduce_fusion
  0.8 0.0 copy-start.13
  0.9 0.0 copy-start.3
  0.9 1.1 %copy-done.3 = bf16[512,640]{1,0:T(8,128)(2,1)S(1)} copy-done((bf16[512,640]{1,0:T(8,128)(2,1)S(1)}, bf16[512,640]{1,0:T(8,128)(2,1)}, u32[]{:S(2)}) %copy-start.3) | copy-done | bytes 655384
  2.0 1.1 %copy-done.5 = f32[5,5,5,5,2,1,128]{6,5,4,3,2,1,0:T(1,128)S(1)} copy-done((f32[5,5,5,5,2,1,128]{6,5,4,3,2,1,0:T(1,128)S(1)}, f32[5,5,5,5,2,1,128]{6,5,4,3,2,1,0:T(1,128)}, u32[]{:S(2)}) %copy-start.5) | copy-done | bytes 640024
  3.0 0.6 %begin.1 = (f32[640,256]{1,0:T(8,128)S(1)}, f32[128,128]{1,0:T(8,128)S(1)}, f32[128,128]{1,0:T(8,128)S(1)}, f32[104,256]{1,0:T(8,128)S(1)}, f32[104,256]{1,0:T(8,128)S(1)}, /*index=5*/f32[256,128]{1,0:T(8,128)S(1)}) custom-call(f32[1250,1,128]{2,1,0:T(1,128)S(1)} %bitcast.8, f32[50,5]{1,0:T(8,128)S(1)} %reshape.10.wake, bf16[512,640]{1,0:T(8,128)(2,1)S(1)} %copy-done.3), custom_call_target="tpu_custom_call" | custom-call | flops 100000000 | bytes 1048576 | tf_op jit(solution)/shard_map/begin/pallas_call | solution.py:365
  3.7 0.1 collective-permute-start
  3.7 2.5 %collective-permute-start.1 = (f32[128,128]{1,0:T(8,128)S(1)}, f32[128,128]{1,0:T(8,128)S(1)}, u32[]{:S(2)}, u32[]{:S(2)}) collective-permute-start(f32[128,128]{1,0:T(8,128)S(1)} %get-tuple-element.30), channel_id=1, source_target_pairs={{4,8},{8,4},{12,16},{16,12},{20,24},{24,20},{28,0},{0,28},{5,9},{9... | collective-permute-start | bytes 196616 | tf_op jit(solution)/shard_map/ppermute | solution.py:383
  6.3 0.4 %collective-permute-start.2 = (f32[104,256]{1,0:T(8,128)S(1)}, f32[104,256]{1,0:T(8,128)S(1)}, u32[]{:S(2)}, u32[]{:S(2)}) collective-permute-start(f32[104,256]{1,0:T(8,128)S(1)} %get-tuple-element.31), channel_id=1, source_target_pairs={{0,1},{1,0},{2,3},{3,2},{4,5},{5,4},{6,7},{7,6},{8,9},{9,8},{10,11... | collective-permute-start | bytes 319496 | tf_op jit(solution)/shard_map/ppermute | solution.py:383
  6.7 4.6 %collective-permute-start.3 = (f32[104,256]{1,0:T(8,128)S(1)}, f32[104,256]{1,0:T(8,128)S(1)}, u32[]{:S(2)}, u32[]{:S(2)}) collective-permute-start(f32[104,256]{1,0:T(8,128)S(1)} %get-tuple-element.32), channel_id=1, source_target_pairs={{1,2},{2,1},{5,6},{6,5},{9,10},{10,9},{13,14},{14,13},{17,18},{18,... | collective-permute-start | bytes 319496 | tf_op jit(solution)/shard_map/ppermute | solution.py:383
  11.3 0.0 copy-done.14
  11.3 0.0 copy-done.13
  11.4 0.0 copy-done.4
  11.4 0.0 copy-done.7
  11.4 0.0 copy-done.8
  11.4 0.0 copy-start.9
  11.4 0.9 %copy-done.9 = bf16[512,256]{1,0:T(8,128)(2,1)S(1)} copy-done((bf16[512,256]{1,0:T(8,128)(2,1)S(1)}, bf16[512,256]{1,0:T(8,128)(2,1)}, u32[]{:S(2)}) %copy-start.9) | copy-done | bytes 262168
  12.3 0.9 %copy-done.11 = bf16[512,256]{1,0:T(8,128)(2,1)S(1)} copy-done((bf16[512,256]{1,0:T(8,128)(2,1)S(1)}, bf16[512,256]{1,0:T(8,128)(2,1)}, u32[]{:S(2)}) %copy-start.11) | copy-done | bytes 262168
  13.3 1.8 %first.1 = (f32[640,256]{1,0:T(8,128)S(1)}, f32[512,256]{1,0:T(8,128)S(1)}) custom-call(f32[640,256]{1,0:T(8,128)S(1)} %get-tuple-element.34.state.base, bf16[512,640]{1,0:T(8,128)(2,1)S(1)} %copy-done.4, bf16[640,256]{1,0:T(8,128)(2,1)S(1)} %copy-done.8, bf16[512,256]{1,0:T(8,128)(2,1)S(1)} %copy-done.11, bf16[128,128]{1,0:T(8,128)(2,1)S(1)} %copy-done.14, ...), custom_call_target="tpu_custom_call" | custom-call | flops 2000000000 | bytes 1048576 | tf_op jit(solution)/shard_map/first/pallas_call | solution.py:365
  15.1 0.0 collective-permute-done.pitch_a
  15.1 0.0 collective-permute-done.1.pitch_b
  15.1 0.0 collective-permute-done.2.span_a
  15.1 0.0 collective-permute-done.3.span_b
  15.1 0.0 copy-start.6
  15.2 0.6 %copy-done.6 = s32[3]{0:T(128)S(1)} copy-done((s32[3]{0:T(128)S(1)}, s32[3]{0:T(128)}, u32[]{:S(2)}) %copy-start.6) | copy-done | bytes 36
  15.8 1.2 %exchange.2 = (f32[128,128]{1,0:T(8,128)S(1)}, f32[128,128]{1,0:T(8,128)S(1)}, f32[104,256]{1,0:T(8,128)S(1)}, f32[104,256]{1,0:T(8,128)S(1)}, f32[256,128]{1,0:...) custom-call(s32[3]{0:T(128)S(1)} %copy-done.6, f32[128,128]{1,0:T(8,128)S(1)} %collective-permute-done.pitch_a, ...), custom_call_target="tpu_custom_call" | custom-call | flops 100000000 | bytes 1048576 | tf_op jit(solution)/shard_map/exchange/pallas_call | solution.py:365
  17.0 0.1 collective-permute-start.4
  17.1 0.6 %collective-permute-start.5 = (f32[128,128]{1,0:T(8,128)S(1)}, f32[128,128]{1,0:T(8,128)S(1)}, u32[]{:S(2)}, u32[]{:S(2)}) collective-permute-start(f32[128,128]{1,0:T(8,128)S(1)} %get-tuple-element.37), channel_id=1, source_target_pairs={{4,8},{8,4},{12,16},{16,12},{20,24},{24,20},{28,0},{0,28},{5,9},{9... | collective-permute-start | bytes 196616 | tf_op jit(solution)/shard_map/ppermute | solution.py:383
  17.7 0.0 collective-permute-start.6
  17.7 2.8 %collective-permute-start.7 = (f32[104,256]{1,0:T(8,128)S(1)}, f32[104,256]{1,0:T(8,128)S(1)}, u32[]{:S(2)}, u32[]{:S(2)}) collective-permute-start(f32[104,256]{1,0:T(8,128)S(1)} %get-tuple-element.39), channel_id=1, source_target_pairs={{1,2},{2,1},{5,6},{6,5},{9,10},{10,9},{13,14},{14,13},{17,18},{18,... | collective-permute-start | bytes 319496 | tf_op jit(solution)/shard_map/ppermute | solution.py:383
  20.5 2.5 %later.1 = (f32[640,256]{1,0:T(8,128)S(1)}, f32[512,256]{1,0:T(8,128)S(1)}) custom-call(f32[640,256]{1,0:T(8,128)S(1)} %get-tuple-element.34.state.base, f32[640,256]{1,0:T(8,128)S(1)} %get-tuple-element.41.before, bf16[640,256]{1,0:T(8,128)(2,1)S(1)} %get-tuple-element.42.halo_high, bf16[640,256]{1,0:T(8,128)(2,1)S(1)} %get-tuple-element.43.halo_low, ...), custom_call_target="tpu_custom_call" | custom-call | flops 2000000000 | bytes 1048576 | tf_op jit(solution)/shard_map/later/pallas_call | solution.py:365
  23.1 0.0 collective-permute-done.4.pitch_a
  23.1 0.0 collective-permute-done.5.pitch_b
  23.1 0.0 collective-permute-done.6.span_a
  23.1 1.3 %collective-permute-done.7.span_b = f32[104,256]{1,0:T(8,128)S(1)} collective-permute-done((f32[104,256]{1,0:T(8,128)S(1)}, f32[104,256]{1,0:T(8,128)S(1)}, u32[]{:S(2)}, u32[]{:S(2)}) %collective-permute-start.7) | collective-permute-done | bytes 106528 | tf_op jit(solution)/shard_map/ppermute | solution.py:383
  24.4 1.2 %exchange.3 = (f32[128,128]{1,0:T(8,128)S(1)}, f32[128,128]{1,0:T(8,128)S(1)}, f32[104,256]{1,0:T(8,128)S(1)}, f32[104,256]{1,0:T(8,128)S(1)}, f32[256,128]{1,0:...) custom-call(s32[3]{0:T(128)S(1)} %copy-done.6, f32[128,128]{1,0:T(8,128)S(1)} %collective-permute-done.4.pitch_a, ...), custom_call_target="tpu_custom_call" | custom-call | flops 100000000 | bytes 1048576 | tf_op jit(solution)/shard_map/exchange/pallas_call | solution.py:365
  25.6 0.1 collective-permute-start.8
  25.7 2.6 %collective-permute-start.9 = (f32[128,128]{1,0:T(8,128)S(1)}, f32[128,128]{1,0:T(8,128)S(1)}, u32[]{:S(2)}, u32[]{:S(2)}) collective-permute-start(f32[128,128]{1,0:T(8,128)S(1)} %get-tuple-element.46), channel_id=1, source_target_pairs={{4,8},{8,4},{12,16},{16,12},{20,24},{24,20},{28,0},{0,28},{5,9},{9... | collective-permute-start | bytes 196616 | tf_op jit(solution)/shard_map/ppermute | solution.py:383
  28.3 0.0 collective-permute-start.10
  28.3 2.8 %collective-permute-start.11 = (f32[104,256]{1,0:T(8,128)S(1)}, f32[104,256]{1,0:T(8,128)S(1)}, u32[]{:S(2)}, u32[]{:S(2)}) collective-permute-start(f32[104,256]{1,0:T(8,128)S(1)} %get-tuple-element.48), channel_id=1, source_target_pairs={{1,2},{2,1},{5,6},{6,5},{9,10},{10,9},{13,14},{14,13},{17,18},{18,... | collective-permute-start | bytes 319496 | tf_op jit(solution)/shard_map/ppermute | solution.py:383
  31.1 2.2 %last.1.before = f32[640,256]{1,0:T(8,128)S(1)} custom-call(f32[640,256]{1,0:T(8,128)S(1)} %get-tuple-element.34.state.base, f32[640,256]{1,0:T(8,128)S(1)} %get-tuple-element.50.before, bf16[640,256]{1,0:T(8,128)(2,1)S(1)} %get-tuple-element.51.halo_high, bf16[640,256]{1,0:T(8,128)(2,1)S(1)} %get-tuple-element.52.halo_low, bf16[640,640]{1,0:T(8,128)(2,1)S(1)} %copy-done.2, ...), custom_call_target="tpu_custom_call" | custom-call | flops 2000000000 | bytes 1048576 | tf_op jit(solution)/shard_map/last/pallas_call | solution.py:365
  33.3 0.0 collective-permute-done.8.pitch_a
  33.4 0.0 collective-permute-done.9.pitch_b
  33.4 0.0 collective-permute-done.10.span_a
  33.4 1.5 %collective-permute-done.11.span_b = f32[104,256]{1,0:T(8,128)S(1)} collective-permute-done((f32[104,256]{1,0:T(8,128)S(1)}, f32[104,256]{1,0:T(8,128)S(1)}, u32[]{:S(2)}, u32[]{:S(2)}) %collective-permute-start.11) | collective-permute-done | bytes 106528 | tf_op jit(solution)/shard_map/ppermute | solution.py:383
  34.8 2.2 %final.1 = f32[1250,1,128]{2,1,0:T(1,128)} custom-call(s32[3]{0:T(128)S(1)} %copy-done.6, f32[128,128]{1,0:T(8,128)S(1)} %collective-permute-done.8.pitch_a, f32[128,128]{1,0:T(8,128)S(1)} %collective-permute-done.9.pitch_b, f32[104,256]{1,0:T(8,128)S(1)} %collective-permute-done.10.span_a, f32[104,256]{1,0:T(8,128)S(1)} %collective-permute-done.11.span_b, ...), custom_call_target="tpu_custom_call" | custom-call | flops 100000000 | bytes 1048576 | tf_op jit(solution)/shard_map/final/pallas_call | solution.py:365
  (15 shorter events, 0.0 us)
Async XLA Ops:
  0.0 0.7 %copy-start = (f32[5,5,5,2,1]{2,4,3,1,0:T(1,128)S(1)}, f32[5,5,5,2,1]{2,4,3,1,0:T(1,128)}, u32[]{:S(2)}) copy-start(f32[5,5,5,2,1]{2,4,3,1,0:T(1,128)} %param.13) | copy-start | bytes 3004
  0.7 10.6 %copy-start.14 = (bf16[128,128]{1,0:T(8,128)(2,1)S(1)}, bf16[128,128]{1,0:T(8,128)(2,1)}, u32[]{:S(2)}) copy-start(bf16[128,128]{1,0:T(8,128)(2,1)} %constant.21.clone.refs_2_) | copy-start | bytes 98308
  0.8 10.5 %copy-start.13 = (bf16[128,128]{1,0:T(8,128)(2,1)S(1)}, bf16[128,128]{1,0:T(8,128)(2,1)}, u32[]{:S(2)}) copy-start(bf16[128,128]{1,0:T(8,128)(2,1)} %constant.24.clone.refs_5_) | copy-start | bytes 98308
  0.9 1.1 %copy-start.3 = (bf16[512,640]{1,0:T(8,128)(2,1)S(1)}, bf16[512,640]{1,0:T(8,128)(2,1)}, u32[]{:S(2)}) copy-start(bf16[512,640]{1,0:T(8,128)(2,1)} %constant.18.clone.trace) | copy-start | bytes 1966084
  2.0 1.1 %copy-start.5 = (f32[5,5,5,5,2,1,128]{6,5,4,3,2,1,0:T(1,128)S(1)}, f32[5,5,5,5,2,1,128]{6,5,4,3,2,1,0:T(1,128)}, u32[]{:S(2)}) copy-start(f32[5,5,5,5,2,1,128]{6,5,4,3,2,1,0:T(1,128)} %param.12) | copy-start | bytes 1920004
  3.0 8.3 %copy-start.4 = (bf16[512,640]{1,0:T(8,128)(2,1)S(1)}, bf16[512,640]{1,0:T(8,128)(2,1)}, u32[]{:S(2)}) copy-start(bf16[512,640]{1,0:T(8,128)(2,1)} %constant.18.clone.trace) | copy-start | bytes 1966084
  3.0 8.3 %copy-start.7 = (bf16[640,256]{1,0:T(8,128)(2,1)S(1)}, bf16[640,256]{1,0:T(8,128)(2,1)}, u32[]{:S(2)}) copy-start(bf16[640,256]{1,0:T(8,128)(2,1)} %constant.22.clone.refs_3_) | copy-start | bytes 983044
  3.0 8.3 %copy-start.8 = (bf16[640,256]{1,0:T(8,128)(2,1)S(1)}, bf16[640,256]{1,0:T(8,128)(2,1)}, u32[]{:S(2)}) copy-start(bf16[640,256]{1,0:T(8,128)(2,1)} %constant.19.clone.refs_0_) | copy-start | bytes 983044
  3.7 11.4 %collective-permute-start = (f32[128,128]{1,0:T(8,128)S(1)}, f32[128,128]{1,0:T(8,128)S(1)}, u32[]{:S(2)}, u32[]{:S(2)}) collective-permute-start(f32[128,128]{1,0:T(8,128)S(1)} %get-tuple-element.29), channel_id=1, source_target_pairs={{0,4},{4,0},{8,12},{12,8},{16,20},{20,16},{24,28},{28,24},{1,5},{5... | collective-permute-start | bytes 196616 | tf_op jit(solution)/shard_map/ppermute | solution.py:383
  3.7 11.4 %collective-permute-start.1 = (f32[128,128]{1,0:T(8,128)S(1)}, f32[128,128]{1,0:T(8,128)S(1)}, u32[]{:S(2)}, u32[]{:S(2)}) collective-permute-start(f32[128,128]{1,0:T(8,128)S(1)} %get-tuple-element.30), channel_id=1, source_target_pairs={{4,8},{8,4},{12,16},{16,12},{20,24},{24,20},{28,0},{0,28},{5,9},{9... | collective-permute-start | bytes 196616 | tf_op jit(solution)/shard_map/ppermute | solution.py:383
  6.3 8.8 %collective-permute-start.2 = (f32[104,256]{1,0:T(8,128)S(1)}, f32[104,256]{1,0:T(8,128)S(1)}, u32[]{:S(2)}, u32[]{:S(2)}) collective-permute-start(f32[104,256]{1,0:T(8,128)S(1)} %get-tuple-element.31), channel_id=1, source_target_pairs={{0,1},{1,0},{2,3},{3,2},{4,5},{5,4},{6,7},{7,6},{8,9},{9,8},{10,11... | collective-permute-start | bytes 319496 | tf_op jit(solution)/shard_map/ppermute | solution.py:383
  6.7 8.4 %collective-permute-start.3 = (f32[104,256]{1,0:T(8,128)S(1)}, f32[104,256]{1,0:T(8,128)S(1)}, u32[]{:S(2)}, u32[]{:S(2)}) collective-permute-start(f32[104,256]{1,0:T(8,128)S(1)} %get-tuple-element.32), channel_id=1, source_target_pairs={{1,2},{2,1},{5,6},{6,5},{9,10},{10,9},{13,14},{14,13},{17,18},{18,... | collective-permute-start | bytes 319496 | tf_op jit(solution)/shard_map/ppermute | solution.py:383
  11.4 1.0 %copy-start.9 = (bf16[512,256]{1,0:T(8,128)(2,1)S(1)}, bf16[512,256]{1,0:T(8,128)(2,1)}, u32[]{:S(2)}) copy-start(bf16[512,256]{1,0:T(8,128)(2,1)} %constant.23.clone.refs_4_) | copy-start | bytes 786436
  12.3 0.9 %copy-start.11 = (bf16[512,256]{1,0:T(8,128)(2,1)S(1)}, bf16[512,256]{1,0:T(8,128)(2,1)}, u32[]{:S(2)}) copy-start(bf16[512,256]{1,0:T(8,128)(2,1)} %constant.20.clone.refs_1_) | copy-start | bytes 786436
  13.3 1.9 %copy-start.1 = (bf16[512,640]{1,0:T(8,128)(2,1)S(1)}, bf16[512,640]{1,0:T(8,128)(2,1)}, u32[]{:S(2)}) copy-start(bf16[512,640]{1,0:T(8,128)(2,1)} %constant.25.clone.link) | copy-start | bytes 1966084
  15.1 0.7 %copy-start.6 = (s32[3]{0:T(128)S(1)}, s32[3]{0:T(128)}, u32[]{:S(2)}) copy-start(s32[3]{0:T(128)} %offsets.5) | copy-start | bytes 40
  15.8 4.7 %copy-start.2 = (bf16[640,640]{1,0:T(8,128)(2,1)S(1)}, bf16[640,640]{1,0:T(8,128)(2,1)}, u32[]{:S(2)}) copy-start(bf16[640,640]{1,0:T(8,128)(2,1)} %constant.26.clone.lift) | copy-start | bytes 2457604
  17.0 6.1 %collective-permute-start.4 = (f32[128,128]{1,0:T(8,128)S(1)}, f32[128,128]{1,0:T(8,128)S(1)}, u32[]{:S(2)}, u32[]{:S(2)}) collective-permute-start(f32[128,128]{1,0:T(8,128)S(1)} %get-tuple-element.36), channel_id=1, source_target_pairs={{0,4},{4,0},{8,12},{12,8},{16,20},{20,16},{24,28},{28,24},{1,5},{5... | collective-permute-start | bytes 196616 | tf_op jit(solution)/shard_map/ppermute | solution.py:383
  17.1 6.0 %collective-permute-start.5 = (f32[128,128]{1,0:T(8,128)S(1)}, f32[128,128]{1,0:T(8,128)S(1)}, u32[]{:S(2)}, u32[]{:S(2)}) collective-permute-start(f32[128,128]{1,0:T(8,128)S(1)} %get-tuple-element.37), channel_id=1, source_target_pairs={{4,8},{8,4},{12,16},{16,12},{20,24},{24,20},{28,0},{0,28},{5,9},{9... | collective-permute-start | bytes 196616 | tf_op jit(solution)/shard_map/ppermute | solution.py:383
  17.7 5.4 %collective-permute-start.6 = (f32[104,256]{1,0:T(8,128)S(1)}, f32[104,256]{1,0:T(8,128)S(1)}, u32[]{:S(2)}, u32[]{:S(2)}) collective-permute-start(f32[104,256]{1,0:T(8,128)S(1)} %get-tuple-element.38), channel_id=1, source_target_pairs={{0,1},{1,0},{2,3},{3,2},{4,5},{5,4},{6,7},{7,6},{8,9},{9,8},{10,11... | collective-permute-start | bytes 319496 | tf_op jit(solution)/shard_map/ppermute | solution.py:383
  17.7 6.6 %collective-permute-start.7 = (f32[104,256]{1,0:T(8,128)S(1)}, f32[104,256]{1,0:T(8,128)S(1)}, u32[]{:S(2)}, u32[]{:S(2)}) collective-permute-start(f32[104,256]{1,0:T(8,128)S(1)} %get-tuple-element.39), channel_id=1, source_target_pairs={{1,2},{2,1},{5,6},{6,5},{9,10},{10,9},{13,14},{14,13},{17,18},{18,... | collective-permute-start | bytes 319496 | tf_op jit(solution)/shard_map/ppermute | solution.py:383
  24.4 6.7 %copy-start.10 = (bf16[512,256]{1,0:T(8,128)(2,1)S(1)}, bf16[512,256]{1,0:T(8,128)(2,1)}, u32[]{:S(2)}) copy-start(bf16[512,256]{1,0:T(8,128)(2,1)} %constant.23.clone.refs_4_) | copy-start | bytes 786436
  24.4 6.7 %copy-start.12 = (bf16[512,256]{1,0:T(8,128)(2,1)S(1)}, bf16[512,256]{1,0:T(8,128)(2,1)}, u32[]{:S(2)}) copy-start(bf16[512,256]{1,0:T(8,128)(2,1)} %constant.20.clone.refs_1_) | copy-start | bytes 786436
  25.6 7.7 %collective-permute-start.8 = (f32[128,128]{1,0:T(8,128)S(1)}, f32[128,128]{1,0:T(8,128)S(1)}, u32[]{:S(2)}, u32[]{:S(2)}) collective-permute-start(f32[128,128]{1,0:T(8,128)S(1)} %get-tuple-element.45), channel_id=1, source_target_pairs={{0,4},{4,0},{8,12},{12,8},{16,20},{20,16},{24,28},{28,24},{1,5},{5... | collective-permute-start | bytes 196616 | tf_op jit(solution)/shard_map/ppermute | solution.py:383
  25.7 7.7 %collective-permute-start.9 = (f32[128,128]{1,0:T(8,128)S(1)}, f32[128,128]{1,0:T(8,128)S(1)}, u32[]{:S(2)}, u32[]{:S(2)}) collective-permute-start(f32[128,128]{1,0:T(8,128)S(1)} %get-tuple-element.46), channel_id=1, source_target_pairs={{4,8},{8,4},{12,16},{16,12},{20,24},{24,20},{28,0},{0,28},{5,9},{9... | collective-permute-start | bytes 196616 | tf_op jit(solution)/shard_map/ppermute | solution.py:383
  28.3 5.1 %collective-permute-start.10 = (f32[104,256]{1,0:T(8,128)S(1)}, f32[104,256]{1,0:T(8,128)S(1)}, u32[]{:S(2)}, u32[]{:S(2)}) collective-permute-start(f32[104,256]{1,0:T(8,128)S(1)} %get-tuple-element.47), channel_id=1, source_target_pairs={{0,1},{1,0},{2,3},{3,2},{4,5},{5,4},{6,7},{7,6},{8,9},{9,8},{10,11... | collective-permute-start | bytes 319496 | tf_op jit(solution)/shard_map/ppermute | solution.py:383
  28.3 6.6 %collective-permute-start.11 = (f32[104,256]{1,0:T(8,128)S(1)}, f32[104,256]{1,0:T(8,128)S(1)}, u32[]{:S(2)}, u32[]{:S(2)}) collective-permute-start(f32[104,256]{1,0:T(8,128)S(1)} %get-tuple-element.48), channel_id=1, source_target_pairs={{1,2},{2,1},{5,6},{6,5},{9,10},{10,9},{13,14},{14,13},{17,18},{18,... | collective-permute-start | bytes 319496 | tf_op jit(solution)/shard_map/ppermute | solution.py:383

commit v2 on v1

v2 whole, which is shorter than its diff:
```python
import functools

import jax
import jax.numpy as jnp
import ml_dtypes
import numpy as np
from jax import lax
from jax.experimental import pallas as pl
from jax.experimental.pallas import tpu as pltpu
from jax.sharding import PartitionSpec as P

MEAN_FLOW = (0.5, 0.3, 0.0)
WAVE_SPEED = (1.5, 1.3, 1.0)
ELEM_SIZE = (1.0, 0.8, 1.2)
END_WEIGHT = 0.1
TIME_STEP = 0.01
KEEP = (0.0, 0.75, 1.0 / 3.0)
GAIN = (1.0, 0.25, 2.0 / 3.0)

ORDER = (1, 4, 2, 3, 0)
MAIN = 24
TAIL = 5 * MAIN
PER_VAR = 128
ROWS = 5 * PER_VAR
TILES = ((0, 0, 2), (1, 2, 4), (4, 4, 5))
BLOCK = 128
SPAN_ROWS = 104
TRACES = 4 * BLOCK
HALO = 5 * BLOCK
WAKE_ROW = 125
TRACE_AT, LINK_AT, LIFT_AT = (0, TRACES, 2 * TRACES)
HIGH_AT = LIFT_AT + ROWS
LOW_AT = HIGH_AT + ROWS
TABLE_ROWS = LOW_AT + ROWS
LANES = 128
VMEM_LIMIT = 24 * 1024 * 1024


def derivative_table():
    points = np.array([-1.0, -np.sqrt(3.0 / 7.0), 0.0, np.sqrt(3.0 / 7.0), 1.0])
    products = np.array(
        [np.prod([points[j] - points[k] for k in range(5) if k != j]) for j in range(5)]
    )
    matrix = np.zeros((5, 5))
    for i in range(5):
        for j in range(5):
            if i != j:
                matrix[i, j] = products[i] / (products[j] * (points[i] - points[j]))
        matrix[i, i] = sum((1.0 / (points[i] - points[k]) for k in range(5) if k != i))
    return matrix


def flux_matrix(direction):
    flux = MEAN_FLOW[direction] * np.eye(5)
    flux[0, 1 + direction] += 1.0
    flux[4, 1 + direction] += 1.0
    flux[1 + direction, 4] += 1.0
    return flux


def half_flux(direction, sign):
    return 0.5 * (flux_matrix(direction) + sign * WAVE_SPEED[direction] * np.eye(5))


def lift_factor(direction):
    return TIME_STEP * 2.0 / (ELEM_SIZE[direction] * END_WEIGHT)


def half_scales():
    return (lift_factor(1) / 10.0, lift_factor(1), lift_factor(2), lift_factor(2), lift_factor(0))


def var_start(v):
    return ORDER.index(v) * PER_VAR


def node_row(v, a, p, s):
    node = p * 5 + s
    return var_start(v) + (a * MAIN + node if node < MAIN else TAIL + a)


def operator_tables():
    deriv = derivative_table()
    volume = np.zeros((ROWS, ROWS))
    lift = np.zeros((ROWS, HALO))
    trace = np.zeros((TRACES, ROWS))
    fluxes = [flux_matrix(d) for d in range(3)]
    plus = [half_flux(d, 1.0) for d in range(3)]
    minus = [half_flux(d, -1.0) for d in range(3)]
    plus_sent, minus_sent = (plus[2][:4], minus[2][:4])
    back_plus = np.vstack([np.eye(4), [[0.0, 0.0, 0.0, 1.0]]])
    back_minus = np.vstack([np.eye(4), [[0.0, 0.0, 0.0, -1.0]]])
    assert np.allclose(back_plus @ plus_sent, plus[2])
    assert np.allclose(back_minus @ minus_sent, minus[2])
    for a in range(5):
        for p in range(5):
            for s in range(5):
                here = [node_row(v, a, p, s) for v in range(5)]
                place = (a, p, s)
                for d in range(3):
                    for j in range(5):
                        there = list(place)
                        there[d] = j
                        cols = [node_row(v, *there) for v in range(5)]
                        coeff = -TIME_STEP * (2.0 / ELEM_SIZE[d]) * deriv[place[d], j]
                        volume[np.ix_(here, cols)] += coeff * fluxes[d]
                for d in (1, 2):
                    if place[d] == 4:
                        volume[np.ix_(here, here)] += lift_factor(d) * minus[d]
                    if place[d] == 0:
                        volume[np.ix_(here, here)] -= lift_factor(d) * plus[d]
                if p == 0:
                    cols = [s * 25 + v * 5 + a for v in range(5)]
                    lift[np.ix_(here, cols)] += lift_factor(1) * plus[1]
                    for v in range(5):
                        trace[BLOCK + s * 25 + v * 5 + a, here[v]] = 1.0
                if p == 4:
                    cols = [BLOCK + s * 25 + v * 5 + a for v in range(5)]
                    lift[np.ix_(here, cols)] -= lift_factor(1) * minus[1]
                    for v in range(5):
                        trace[s * 25 + v * 5 + a, here[v]] = 1.0
                if s == 0:
                    cols = [2 * BLOCK + c * 25 + a * 5 + p for c in range(4)]
                    lift[np.ix_(here, cols)] += lift_factor(2) * back_plus
                    rows = [3 * BLOCK + c * 25 + a * 5 + p for c in range(4)]
                    trace[np.ix_(rows, here)] += minus_sent
                if s == 4:
                    cols = [3 * BLOCK + c * 25 + a * 5 + p for c in range(4)]
                    lift[np.ix_(here, cols)] -= lift_factor(2) * back_minus
                    rows = [2 * BLOCK + c * 25 + a * 5 + p for c in range(4)]
                    trace[np.ix_(rows, here)] += plus_sent
                if a == 0:
                    cols = [4 * BLOCK + v * 25 + p * 5 + s for v in range(5)]
                    lift[np.ix_(here, cols)] += lift_factor(0) * plus[0]
    lift = lift / np.repeat(half_scales(), BLOCK)
    return volume, lift, trace, trace @ lift


def exact_table(table):
    exact = table.astype(ml_dtypes.bfloat16)
    assert np.allclose(exact.astype(np.float64), table, rtol=1e-12, atol=1e-12)
    return exact


def split_table(table):
    high = table.astype(ml_dtypes.bfloat16)
    low = (table - high.astype(np.float64)).astype(ml_dtypes.bfloat16)
    return high, low


def split(values):
    high = values.astype(jnp.bfloat16)
    low = (values - high.astype(jnp.float32)).astype(jnp.bfloat16)
    return high, low


def dot(left, right):
    return jnp.dot(left, right, preferred_element_type=jnp.float32)


def product(table, high, low):
    return dot(table, high) + dot(table, low)


def with_rows(values, first, extra):
    rows = lax.broadcasted_iota(jnp.int32, values.shape, 0)
    for k, row in enumerate(extra):
        values = jnp.where(rows == first + k, row, values)
    return values


def emit_pitch_faces(traces, wake, pitch_odd, pitch_a, pitch_b, inner):
    upper, lower = traces[0:BLOCK], traces[BLOCK : 2 * BLOCK]
    up = with_rows(upper[:, LANES:], WAKE_ROW, wake)
    down = lower[:, :LANES]
    pitch_a[...] = jnp.where(pitch_odd, down, up)
    pitch_b[...] = jnp.where(pitch_odd, up, down)
    inner[0:BLOCK] = upper[:, :LANES]
    inner[BLOCK:] = lower[:, LANES:]


def emit_span_faces(traces, span_odd, span_a, span_b):
    above, below = traces[0:SPAN_ROWS], traces[BLOCK : BLOCK + SPAN_ROWS]
    span_a[...] = jnp.where(span_odd, below, above)
    span_b[...] = jnp.where(span_odd, above, below)


def parities():
    return lax.axis_index("pitch") % 2 == 1, lax.axis_index("span") % 2 == 1


def combine(table, values):
    return [
        sum(float(table[i, j]) * values[j] for j in range(5) if table[i, j] != 0.0)
        for i in range(table.shape[0])
    ]


def begin_span_kernel(x, span_a, span_b):
    flat = x.reshape(x.shape[0], LANES)
    _, span_odd = parities()
    rest = jnp.zeros((SPAN_ROWS - 96, LANES), jnp.float32)
    for e in range(2):
        lanes = slice(e * LANES, (e + 1) * LANES)
        sides = []
        for s, sign in ((4, 1.0), (0, -1.0)):
            faces = [flat[pl.ds(v * 250 + 2 * s + e, 25, stride=10), :] for v in range(5)]
            sides.append(combine(half_flux(2, sign)[:4], faces))
        span_a[96:SPAN_ROWS, lanes] = rest
        span_b[96:SPAN_ROWS, lanes] = rest
        for c in range(4):
            above, below = (sides[0][c], sides[1][c])
            span_a[c * 25 : c * 25 + 25, lanes] = jnp.where(span_odd, below, above)
            span_b[c * 25 : c * 25 + 25, lanes] = jnp.where(span_odd, above, below)


def begin_pitch_kernel(x, wake, pitch_a, pitch_b, inner):
    flat = x.reshape(x.shape[0], LANES)
    pitch_odd, _ = parities()
    planes = wake.reshape(50, 5)[...]
    rows = lax.broadcasted_iota(jnp.int32, (50, LANES), 0)
    cols = lax.broadcasted_iota(jnp.int32, (50, LANES), 1)
    spread = jnp.zeros((50, LANES), jnp.float32)
    for s in range(5):
        mine = (cols - s) == 5 * (rows // 2)
        spread = jnp.where(mine, planes[:, s : s + 1], spread)
    own = [
        jnp.sum(jnp.where(rows % 2 == k, spread, 0.0), axis=0, keepdims=True) for k in range(2)
    ]
    tail = jnp.zeros((8, LANES), jnp.float32)
    up_tail = with_rows(tail, WAKE_ROW - 120, own)
    pitch_a[120:BLOCK] = jnp.where(pitch_odd, tail, up_tail)
    pitch_b[120:BLOCK] = jnp.where(pitch_odd, up_tail, tail)
    inner[120:BLOCK] = tail
    inner[BLOCK + 120 :] = tail
    for s in range(5):
        at = slice(s * 25, s * 25 + 25)
        upper, lower = (
            [flat[pl.ds(p * 10 + 2 * s + e, 25, stride=50), :] for e in range(2)] for p in (4, 0)
        )
        pitch_a[at] = jnp.where(pitch_odd, lower[0], upper[1])
        pitch_b[at] = jnp.where(pitch_odd, upper[1], lower[0])
        inner[at] = upper[0]
        inner[BLOCK + s * 25 : BLOCK + s * 25 + 25] = lower[1]


def load_state(x, state):
    flat = x.reshape(x.shape[0], LANES)
    for e in range(2):
        lanes = slice(e * LANES, (e + 1) * LANES)
        for v in range(5):
            base = var_start(v)
            first = v * 250 + e
            for a in range(5):
                at = base + a * MAIN
                state[at : at + MAIN, lanes] = flat[pl.ds(first + a * 50, MAIN, stride=2), :]
            tail = base + TAIL
            state[tail : tail + 8, lanes] = jnp.zeros((8, LANES), jnp.float32)
            state[tail : tail + 5, lanes] = flat[pl.ds(first + 2 * MAIN, 5, stride=50), :]


def add_axial_terms(gain, state, partial):
    lanes = lax.broadcasted_iota(jnp.int32, (MAIN + 8, LANES), 1)
    rows = lax.broadcasted_iota(jnp.int32, (8, LANES), 0)
    for e in range(2):
        own = slice(e * LANES, (e + 1) * LANES)
        upper_gap, lower_gap = ([], [])
        for v in range(5):
            base = var_start(v)
            lower = state[base : base + MAIN, own]
            upper = state[base + 4 * MAIN : base + TAIL, own]
            tail = state[base + TAIL : base + PER_VAR, own]
            turned = pltpu.roll(tail, 4, 0)
            join = lambda main, end: jnp.concatenate([main, end], axis=0)
            after = pltpu.roll(join(lower, turned), LANES - 1, 1)
            before = pltpu.roll(join(upper, turned), 1, 1)
            upper = join(upper, tail)
            upper_gap.append(jnp.where(lanes == LANES - 1, 0.0, upper - after))
            lower_gap.append(jnp.where(lanes == 0, 0.0, before) - join(lower, tail))
        mixed = []
        for gap, sign in ((upper_gap, -1.0), (lower_gap, 1.0)):
            mixed.append(combine(gain * lift_factor(0) * half_flux(0, sign), gap))
        for v in range(5):
            base = var_start(v)
            upper, lower = (mixed[0][v], mixed[1][v])
            partial[base : base + MAIN, own] += lower[:MAIN]
            partial[base + 4 * MAIN : base + TAIL, own] += upper[:MAIN]
            ends = jnp.where(rows == 0, lower[MAIN:], jnp.where(rows == 4, upper[MAIN:], 0.0))
            partial[base + TAIL : base + PER_VAR, own] += ends


def volume_rate(table, high, low):
    rate = [None] * 5
    for first, start, stop in TILES:
        part = slice(start * PER_VAR, stop * PER_VAR)
        table_high, table_low = (
            table[at + first * PER_VAR : at + ROWS, part] for at in (HIGH_AT, LOW_AT)
        )
        term = product(table_high, high[part], low[part]) + dot(table_low, high[part])
        for v in range(first, 5):
            block = term[(v - first) * PER_VAR : (v - first + 1) * PER_VAR]
            rate[v] = block if rate[v] is None else rate[v] + block
    return jnp.concatenate(rate, axis=0)


def advance_body(section, base, state, table, partial, faces):
    rate = volume_rate(table, *split(state[...]))
    gain, keep = GAIN[section], KEEP[section]
    if keep == 0.0:
        partial[...] = state[...] + rate
    else:
        partial[...] = keep * base[...] + gain * (state[...] + rate)
    add_axial_terms(gain, state, partial)
    if faces is not None:
        faces[...] = product(table[TRACE_AT : TRACE_AT + TRACES], *split(partial[...]))


def lift_table(table):
    return table[LIFT_AT : LIFT_AT + ROWS]


def first_kernel(offsets, x, table, base, partial, faces, flags):
    cols = lax.broadcasted_iota(jnp.int32, flags.shape, 1)
    moved = jnp.zeros(flags.shape, jnp.float32)
    for k in range(3):
        moved = jnp.where((cols == k) & (offsets[k] % 2 == 1), 1.0, moved)
    flags[...] = moved
    load_state(x, base)
    advance_body(0, None, base, table, partial, faces)


def later_kernel(section, base, before, halo_high, halo_low, table, partial, *refs):
    *faces, state = refs
    lifted = product(lift_table(table), halo_high[...], halo_low[...])
    state[...] = before[...] + GAIN[section - 1] * lifted
    advance_body(section, base, state, table, partial, faces[0] if faces else None)


def gather_halo(section, flags, pitch_a, pitch_b, span_a, span_b, inner, halo):
    pitch_odd, span_odd = parities()
    after = jnp.where(pitch_odd, pitch_b[...], pitch_a[...])
    before = jnp.where(pitch_odd, pitch_a[...], pitch_b[...])
    scales = half_scales()
    halo[0:BLOCK, :LANES] = scales[0] * before
    halo[0:BLOCK, LANES:] = scales[0] * inner[0:BLOCK]
    halo[BLOCK : 2 * BLOCK, :LANES] = scales[1] * inner[BLOCK:]
    halo[BLOCK : 2 * BLOCK, LANES:] = scales[1] * after
    above = jnp.where(span_odd, span_b[...], span_a[...])
    below = jnp.where(span_odd, span_a[...], span_b[...])
    rest = jnp.zeros((BLOCK - SPAN_ROWS, 2 * LANES), jnp.float32)
    halo[2 * BLOCK : 2 * BLOCK + SPAN_ROWS] = scales[2] * below
    halo[2 * BLOCK + SPAN_ROWS : 3 * BLOCK] = rest
    halo[3 * BLOCK : 3 * BLOCK + SPAN_ROWS] = scales[3] * above
    halo[3 * BLOCK + SPAN_ROWS : 4 * BLOCK] = rest
    wake = before[WAKE_ROW : WAKE_ROW + 2]
    moved = flags[0:1, section : section + 1] > 0.5
    rows = lax.broadcasted_iota(jnp.int32, (BLOCK, LANES), 0)
    cols = lax.broadcasted_iota(jnp.int32, (BLOCK, LANES), 1)
    for e in range(2):
        row = jnp.where(moved, wake[1 - e : 2 - e], wake[e : e + 1])
        column = jnp.sum(jnp.where(rows == cols, row, 0.0), axis=1, keepdims=True)
        halo[4 * BLOCK :, e * LANES : (e + 1) * LANES] = jnp.where(
            cols == 0, scales[4] * column, 0.0
        )
    return wake


def next_traces(section, side, faces, table, high, low):
    at = LINK_AT + side * 2 * BLOCK
    rows = slice(side * 2 * BLOCK, (side + 1) * 2 * BLOCK)
    return faces[rows] + GAIN[section] * product(table[at : at + 2 * BLOCK], high, low)


def span_kernel(
    section, flags, pitch_a, pitch_b, span_a, span_b, inner, faces, table,
    next_span_a, next_span_b, halo_high, halo_low, wake, halo,
):
    arrived = gather_halo(section, flags, pitch_a, pitch_b, span_a, span_b, inner, halo)
    wake[...] = jnp.concatenate([arrived, jnp.zeros((6, LANES), jnp.float32)], axis=0)
    high, low = split(halo[...])
    halo_high[...] = high
    halo_low[...] = low
    _, span_odd = parities()
    traces = next_traces(section, 1, faces, table, high, low)
    emit_span_faces(traces, span_odd, next_span_a, next_span_b)


def pitch_kernel(
    section, faces, table, halo_high, halo_low, wake, next_pitch_a, next_pitch_b, next_inner
):
    pitch_odd, _ = parities()
    traces = next_traces(section, 0, faces, table, halo_high[...], halo_low[...])
    emit_pitch_faces(
        traces, [wake[0:1], wake[1:2]], pitch_odd, next_pitch_a, next_pitch_b, next_inner
    )


def final_kernel(
    flags, pitch_a, pitch_b, span_a, span_b, inner, before, table, out, halo, result, done
):
    gather_halo(2, flags, pitch_a, pitch_b, span_a, span_b, inner, halo)
    total = before[...] + GAIN[2] * product(lift_table(table), *split(halo[...]))
    flat = result.reshape(result.shape[0], LANES)
    copies = []
    for v in ORDER:
        base = var_start(v)
        for e in range(2):
            lanes = slice(e * LANES, (e + 1) * LANES)
            first = v * 250 + e
            for a in range(5):
                at = base + a * MAIN
                flat[pl.ds(first + a * 50, MAIN, stride=2), :] = total[at : at + MAIN, lanes]
            tail = base + TAIL
            flat[pl.ds(first + 2 * MAIN, 5, stride=50), :] = total[tail : tail + 5, lanes]
        part = pl.ds(v * 250, 250)
        copies.append(pltpu.make_async_copy(result.at[part], out.at[part], done.at[v]))
        copies[-1].start()
    for copy in copies:
        copy.wait()


IN_VMEM = pl.BlockSpec(memory_space=pltpu.VMEM)
IN_SMEM = pl.BlockSpec(memory_space=pltpu.SMEM)


def call(kernel, name, outs, args, in_specs=(), scratch=(), flops=0, out_spec=IN_VMEM):
    in_specs = list(in_specs)
    return pl.pallas_call(
        kernel,
        name=name,
        out_shape=[jax.ShapeDtypeStruct(shape, dtype) for shape, dtype in outs],
        in_specs=in_specs + [IN_VMEM] * (len(args) - len(in_specs)),
        out_specs=[out_spec] * len(outs),
        scratch_shapes=list(scratch),
        compiler_params=pltpu.CompilerParams(vmem_limit_bytes=VMEM_LIMIT),
        cost_estimate=pl.CostEstimate(flops=flops, bytes_accessed=2**20, transcendentals=0),
    )(*args)


def swapped(value, axis, odd, wrap):
    size = lax.axis_size(axis)
    pairs = []
    for i in range(odd, size if wrap else size - 1, 2):
        j = (i + 1) % size
        pairs += [(i, j), (j, i)]
    return lax.ppermute(value, axis, pairs)


def span_exchanged(faces):
    return swapped(faces[0], "span", 0, False), swapped(faces[1], "span", 1, False)


def pitch_exchanged(faces):
    return swapped(faces[0], "pitch", 0, True), swapped(faces[1], "pitch", 1, True)


F32 = jnp.float32
PITCH_OUTS = [((BLOCK, LANES), F32), ((BLOCK, LANES), F32), ((2 * BLOCK, LANES), F32)]
SPAN_OUTS = [((SPAN_ROWS, 2 * LANES), F32)] * 2
SMALL_OUT = ((8, LANES), F32)
HALO_OUTS = [((HALO, 2 * LANES), jnp.bfloat16)] * 2
STATE_OUT = ((ROWS, 2 * LANES), F32)
TRACE_OUT = ((TRACES, 2 * LANES), F32)


def shards(table, state, wake_planes, bar_offsets):
    x = state.reshape(-1, 1, LANES)
    wake = wake_planes.transpose(0, 1, 3, 4, 2).reshape(50, 1, 5)
    faces = call(begin_span_kernel, "begin_span", SPAN_OUTS, [x])
    span = span_exchanged(faces)
    *faces, inner = call(begin_pitch_kernel, "begin_pitch", PITCH_OUTS, [x, wake])
    pitch = pitch_exchanged(faces)
    base, partial, traces, flags = call(
        first_kernel,
        "first",
        [STATE_OUT, STATE_OUT, TRACE_OUT, SMALL_OUT],
        [bar_offsets, x, table],
        in_specs=[IN_SMEM],
        flops=10**9,
    )
    for section in range(2):
        *faces, high, low, carried = call(
            functools.partial(span_kernel, section),
            "span_faces",
            SPAN_OUTS + HALO_OUTS + [SMALL_OUT],
            [flags, *pitch, *span, inner, traces, table],
            scratch=[pltpu.VMEM((HALO, 2 * LANES), F32)],
            flops=10**8,
        )
        span = span_exchanged(faces)
        *faces, inner = call(
            functools.partial(pitch_kernel, section),
            "pitch_faces",
            PITCH_OUTS,
            [traces, table, high, low, carried],
            flops=10**8,
        )
        pitch = pitch_exchanged(faces)
        last = section == 1
        partial, *traces = call(
            functools.partial(later_kernel, section + 1),
            "last" if last else "later",
            [STATE_OUT] if last else [STATE_OUT, TRACE_OUT],
            [base, partial, high, low, table],
            scratch=[pltpu.VMEM((ROWS, 2 * LANES), F32)],
            flops=10**9,
        )
        traces = None if last else traces[0]
    (out,) = call(
        final_kernel,
        "final",
        [(x.shape, F32)],
        [flags, *pitch, *span, inner, partial, table],
        scratch=[
            pltpu.VMEM((HALO, 2 * LANES), F32),
            pltpu.VMEM(x.shape, F32),
            pltpu.SemaphoreType.DMA((5,)),
        ],
        flops=10**8,
        out_spec=pl.BlockSpec(memory_space=pl.ANY),
    )
    return out.reshape(state.shape)


def solution(mesh):
    volume, lift, trace, link = operator_tables()
    high, low = split_table(volume)
    table = np.concatenate([exact_table(t) for t in (trace, link, lift)] + [high, low])
    assert table.shape == (TABLE_ROWS, ROWS)
    in_specs = (
        P(None, None, None, None, "pitch", "span", None),
        P(None, None, None, "pitch", "span"),
        P(),
    )
    out_specs = P(None, None, None, None, "pitch", "span", None)
    return jax.shard_map(
        functools.partial(shards, jnp.asarray(table)),
        mesh=mesh,
        in_specs=in_specs,
        out_specs=out_specs,
        check_vma=False,
    )
```

time: 37.4 us -> 35.8 us (0.957)
  the two profiles are of different devices: /device:TPU:8 before, /device:TPU:0 now
where the time goes in v2:
time: 35.8 us; the launch traced here: 35.3 us
  starting transfers between devices  14.3 us (40%)
  Pallas kernels  10.8 us (30%)
  local copies, waits for them, and re-layouts  5.62 us (16%)
  waiting for transfers between devices  4.42 us (12%)
    ppermute x12, starting transfers between devices, swapped(): return lax.ppermute(value, axis, pairs)  14.3 us
    pallas_call x10, Pallas kernels, call(): pl.pallas_call(kernel, name=name, out_shape=[jax.ShapeDtypeStruct(shape,...  10.8 us
    unnamed x12, local copies, waits for them, and re-layouts  5.62 us
    ppermute x12, waiting for transfers between devices, swapped(): return lax.ppermute(value, axis, pairs)  4.42 us
  transfers between devices with their start and end apart: 12, of which 2 were waited for; matrix products, arithmetic and copies ran while one was open for 0% of the time, Pallas kernels for 22%

profile of v2, /device:TPU:0, one launch (start us, length us, event | category | flops | bytes accessed | tf_op | source)
XLA Modules:
  0.0 35.3 jit_solution(15813854025967839576)
XLA Ops:
  0.0 0.0 copy-start.2
  0.0 1.1 %copy-done.2 = f32[5,5,5,5,2,1,128]{6,5,4,3,2,1,0:T(1,128)S(1)} copy-done((f32[5,5,5,5,2,1,128]{6,5,4,3,2,1,0:T(1,128)S(1)}, f32[5,5,5,5,2,1,128]{6,5,4,3,2,1,0:T(1,128)}, u32[]{:S(2)}) %copy-start.2) | copy-done | bytes 640024
  1.1 3.1 %collective-permute-start.2 = (f32[104,256]{1,0:T(8,128)S(1)}, f32[104,256]{1,0:T(8,128)S(1)}, u32[]{:S(2)}, u32[]{:S(2)}) collective-permute-start(f32[104,256]{1,0:T(8,128)S(1)} %get-tuple-element.37), channel_id=1, source_target_pairs={{0,1},{1,0},{2,3},{3,2},{4,5},{5,4},{6,7},{7,6},{8,9},{9,8},{10,11... | collective-permute-start | bytes 319496 | tf_op jit(solution)/shard_map/ppermute | solution.py:446
  4.2 0.7 %collective-permute-start.3 = (f32[104,256]{1,0:T(8,128)S(1)}, f32[104,256]{1,0:T(8,128)S(1)}, u32[]{:S(2)}, u32[]{:S(2)}) collective-permute-start(f32[104,256]{1,0:T(8,128)S(1)} %get-tuple-element.38), channel_id=1, source_target_pairs={{1,2},{2,1},{5,6},{6,5},{9,10},{10,9},{13,14},{14,13},{17,18},{18,... | collective-permute-start | bytes 319496 | tf_op jit(solution)/shard_map/ppermute | solution.py:446
  4.9 0.0 copy-start.4
  4.9 0.7 %copy-done.4 = f32[5,5,5,2,1]{2,4,3,1,0:T(1,128)S(1)} copy-done((f32[5,5,5,2,1]{2,4,3,1,0:T(1,128)S(1)}, f32[5,5,5,2,1]{2,4,3,1,0:T(1,128)}, u32[]{:S(2)}) %copy-start.4) | copy-done | bytes 1024
  5.6 0.1 begin_pitch.1
  5.8 0.1 collective-permute-start
  5.8 2.5 %collective-permute-start.1 = (f32[128,128]{1,0:T(8,128)S(1)}, f32[128,128]{1,0:T(8,128)S(1)}, u32[]{:S(2)}, u32[]{:S(2)}) collective-permute-start(f32[128,128]{1,0:T(8,128)S(1)} %get-tuple-element.36), channel_id=1, source_target_pairs={{4,8},{8,4},{12,16},{16,12},{20,24},{24,20},{28,0},{0,28},{5,9},{9... | collective-permute-start | bytes 196616 | tf_op jit(solution)/shard_map/ppermute | solution.py:446
  8.4 0.0 copy-start
  8.4 2.1 %copy-done = bf16[2944,640]{1,0:T(8,128)(2,1)S(1)} copy-done((bf16[2944,640]{1,0:T(8,128)(2,1)S(1)}, bf16[2944,640]{1,0:T(8,128)(2,1)}, u32[]{:S(2)}) %copy-start) | copy-done | bytes 3768344
  10.5 0.0 copy-start.3
  10.5 1.1 %copy-done.3 = f32[5,5,5,5,2,1,128]{6,5,4,3,2,1,0:T(1,128)S(1)} copy-done((f32[5,5,5,5,2,1,128]{6,5,4,3,2,1,0:T(1,128)S(1)}, f32[5,5,5,5,2,1,128]{6,5,4,3,2,1,0:T(1,128)}, u32[]{:S(2)}) %copy-start.3) | copy-done | bytes 640024
  11.5 0.0 copy-start.5
  11.5 0.7 %copy-done.5 = s32[3]{0:T(128)S(1)} copy-done((s32[3]{0:T(128)S(1)}, s32[3]{0:T(128)}, u32[]{:S(2)}) %copy-start.5) | copy-done | bytes 36
  12.2 0.0 copy-start.1
  12.2 2.4 %first.1 = (f32[640,256]{1,0:T(8,128)S(1)}, f32[640,256]{1,0:T(8,128)S(1)}, f32[512,256]{1,0:T(8,128)S(1)}, f32[8,128]{1,0:T(8,128)S(1)}) custom-call(s32[3]{0:T(128)S(1)} %copy-done.5, f32[1250,1,128]{2,1,0:T(1,128)S(1)} %bitcast.9, bf16[2944,640]{1,0:T(8,128)(2,1)S(1)} %copy-done), custom_call_target="tpu_custom_call" | custom-call | flops 1000000000 | bytes 1048576 | tf_op jit(solution)/shard_map/first/pallas_call | solution.py:428
  14.6 0.0 collective-permute-done.pitch_a
  14.6 0.0 collective-permute-done.1.pitch_b
  14.6 0.0 collective-permute-done.2.span_a
  14.6 0.0 collective-permute-done.3.span_b
  14.6 0.0 copy-done.1
  14.6 0.5 %span_faces.2 = (f32[104,256]{1,0:T(8,128)S(1)}, f32[104,256]{1,0:T(8,128)S(1)}, bf16[640,256]{1,0:T(8,128)(2,1)S(1)}, bf16[640,256]{1,0:T(8,128)(2,1)S(1)}, f32[8,128]{1,0:T(8,128)S(1)}) custom-call(f32[8,128]{1,0:T(8,128)S(1)} %get-tuple-element.32.flags, f32[128,128]{1,0:T(8,128)S(1)} %collective-permute-done.pitch_a, ...), custom_call_target="tpu_custom_call" | custom-call | flops 100000000 | bytes 1048576 | tf_op jit(solution)/shard_map/span_faces/pallas_call | solution.py:428
  15.2 4.5 %collective-permute-start.6 = (f32[104,256]{1,0:T(8,128)S(1)}, f32[104,256]{1,0:T(8,128)S(1)}, u32[]{:S(2)}, u32[]{:S(2)}) collective-permute-start(f32[104,256]{1,0:T(8,128)S(1)} %get-tuple-element.47), channel_id=1, source_target_pairs={{0,1},{1,0},{2,3},{3,2},{4,5},{5,4},{6,7},{7,6},{8,9},{9,8},{10,11... | collective-permute-start | bytes 319496 | tf_op jit(solution)/shard_map/ppermute | solution.py:446
  19.6 0.7 %collective-permute-start.7 = (f32[104,256]{1,0:T(8,128)S(1)}, f32[104,256]{1,0:T(8,128)S(1)}, u32[]{:S(2)}, u32[]{:S(2)}) collective-permute-start(f32[104,256]{1,0:T(8,128)S(1)} %get-tuple-element.48), channel_id=1, source_target_pairs={{1,2},{2,1},{5,6},{6,5},{9,10},{10,9},{13,14},{14,13},{17,18},{18,... | collective-permute-start | bytes 319496 | tf_op jit(solution)/shard_map/ppermute | solution.py:446
  20.3 0.4 %pitch_faces.2 = (f32[128,128]{1,0:T(8,128)S(1)}, f32[128,128]{1,0:T(8,128)S(1)}, f32[256,128]{1,0:T(8,128)S(1)}) custom-call(f32[512,256]{1,0:T(8,128)S(1)} %get-tuple-element.40.faces, bf16[2944,640]{1,0:T(8,128)(2,1)S(1)} %copy-done.1, bf16[640,256]{1,0:T(8,128)(2,1)S(1)} %get-tuple-element.41.halo_high, bf16[640,256]{1,0:T(8,128)(2,1)S(1)} %get-tuple-element.42.halo_low, ...), custom_call_target="tpu_custom_call" | custom-call | flops 100000000 | bytes 1048576 | tf_op jit(solution)/shard_map/pitch_faces/pallas_call | solution.py:428
  20.7 0.1 collective-permute-start.4
  20.7 0.6 %collective-permute-start.5 = (f32[128,128]{1,0:T(8,128)S(1)}, f32[128,128]{1,0:T(8,128)S(1)}, u32[]{:S(2)}, u32[]{:S(2)}) collective-permute-start(f32[128,128]{1,0:T(8,128)S(1)} %get-tuple-element.46), channel_id=1, source_target_pairs={{4,8},{8,4},{12,16},{16,12},{20,24},{24,20},{28,0},{0,28},{5,9},{9... | collective-permute-start | bytes 196616 | tf_op jit(solution)/shard_map/ppermute | solution.py:446
  21.4 2.5 %later.1 = (f32[640,256]{1,0:T(8,128)S(1)}, f32[512,256]{1,0:T(8,128)S(1)}) custom-call(f32[640,256]{1,0:T(8,128)S(1)} %get-tuple-element.33.base, f32[640,256]{1,0:T(8,128)S(1)} %get-tuple-element.34.before, bf16[640,256]{1,0:T(8,128)(2,1)S(1)} %get-tuple-element.41.halo_high, bf16[640,256]{1,0:T(8,128)(2,1)S(1)} %get-tuple-element.42.halo_low, ...), custom_call_target="tpu_custom_call" | custom-call | flops 1000000000 | bytes 1048576 | tf_op jit(solution)/shard_map/later/pallas_call | solution.py:428
  23.9 0.0 collective-permute-done.4.pitch_a
  23.9 1.8 %collective-permute-done.5.pitch_b = f32[128,128]{1,0:T(8,128)S(1)} collective-permute-done((f32[128,128]{1,0:T(8,128)S(1)}, f32[128,128]{1,0:T(8,128)S(1)}, u32[]{:S(2)}, u32[]{:S(2)}) %collective-permute-start.5) | collective-permute-done | bytes 65568 | tf_op jit(solution)/shard_map/ppermute | solution.py:446
  25.7 0.0 collective-permute-done.6.span_a
  25.7 0.0 collective-permute-done.7.span_b
  25.8 0.5 %span_faces.3 = (f32[104,256]{1,0:T(8,128)S(1)}, f32[104,256]{1,0:T(8,128)S(1)}, bf16[640,256]{1,0:T(8,128)(2,1)S(1)}, bf16[640,256]{1,0:T(8,128)(2,1)S(1)}, f32[8,128]{1,0:T(8,128)S(1)}) custom-call(f32[8,128]{1,0:T(8,128)S(1)} %get-tuple-element.32.flags, f32[128,128]{1,0:T(8,128)S(1)} %collective-permute-done.4.pitch_a, ...), custom_call_target="tpu_custom_call" | custom-call | flops 100000000 | bytes 1048576 | tf_op jit(solution)/shard_map/span_faces/pallas_call | solution.py:428
  26.3 1.3 %collective-permute-start.10 = (f32[104,256]{1,0:T(8,128)S(1)}, f32[104,256]{1,0:T(8,128)S(1)}, u32[]{:S(2)}, u32[]{:S(2)}) collective-permute-start(f32[104,256]{1,0:T(8,128)S(1)} %get-tuple-element.55), channel_id=1, source_target_pairs={{0,1},{1,0},{2,3},{3,2},{4,5},{5,4},{6,7},{7,6},{8,9},{9,8},{10,11... | collective-permute-start | bytes 319496 | tf_op jit(solution)/shard_map/ppermute | solution.py:446
  27.6 0.7 %collective-permute-start.11 = (f32[104,256]{1,0:T(8,128)S(1)}, f32[104,256]{1,0:T(8,128)S(1)}, u32[]{:S(2)}, u32[]{:S(2)}) collective-permute-start(f32[104,256]{1,0:T(8,128)S(1)} %get-tuple-element.56), channel_id=1, source_target_pairs={{1,2},{2,1},{5,6},{6,5},{9,10},{10,9},{13,14},{14,13},{17,18},{18,... | collective-permute-start | bytes 319496 | tf_op jit(solution)/shard_map/ppermute | solution.py:446
  28.3 0.4 %pitch_faces.3 = (f32[128,128]{1,0:T(8,128)S(1)}, f32[128,128]{1,0:T(8,128)S(1)}, f32[256,128]{1,0:T(8,128)S(1)}) custom-call(f32[512,256]{1,0:T(8,128)S(1)} %get-tuple-element.43.faces, bf16[2944,640]{1,0:T(8,128)(2,1)S(1)} %copy-done.1, bf16[640,256]{1,0:T(8,128)(2,1)S(1)} %get-tuple-element.50.halo_high, bf16[640,256]{1,0:T(8,128)(2,1)S(1)} %get-tuple-element.51.halo_low, ...), custom_call_target="tpu_custom_call" | custom-call | flops 100000000 | bytes 1048576 | tf_op jit(solution)/shard_map/pitch_faces/pallas_call | solution.py:428
  28.7 0.1 collective-permute-start.8
  28.8 0.1 collective-permute-start.9
  28.9 2.2 %last.1.before = f32[640,256]{1,0:T(8,128)S(1)} custom-call(f32[640,256]{1,0:T(8,128)S(1)} %get-tuple-element.33.base, f32[640,256]{1,0:T(8,128)S(1)} %get-tuple-element.58.before, bf16[640,256]{1,0:T(8,128)(2,1)S(1)} %get-tuple-element.50.halo_high, bf16[640,256]{1,0:T(8,128)(2,1)S(1)} %get-tuple-element.51.halo_low, bf16[2944,640]{1,0:T(8,128)(2,1)S(1)} %copy-done.1), custom_call_target="tpu_custom_call" | custom-call | flops 1000000000 | bytes 1048576 | tf_op jit(solution)/shard_map/last/pallas_call | solution.py:428
  31.1 0.0 collective-permute-done.8.pitch_a
  31.1 2.6 %collective-permute-done.9.pitch_b = f32[128,128]{1,0:T(8,128)S(1)} collective-permute-done((f32[128,128]{1,0:T(8,128)S(1)}, f32[128,128]{1,0:T(8,128)S(1)}, u32[]{:S(2)}, u32[]{:S(2)}) %collective-permute-start.9) | collective-permute-done | bytes 65568 | tf_op jit(solution)/shard_map/ppermute | solution.py:446
  33.6 0.0 collective-permute-done.10.span_a
  33.6 0.0 collective-permute-done.11.span_b
  33.6 1.7 %final.1 = f32[1250,1,128]{2,1,0:T(1,128)} custom-call(f32[8,128]{1,0:T(8,128)S(1)} %get-tuple-element.32.flags, f32[128,128]{1,0:T(8,128)S(1)} %collective-permute-done.8.pitch_a, f32[128,128]{1,0:T(8,128)S(1)} %collective-permute-done.9.pitch_b, f32[104,256]{1,0:T(8,128)S(1)} %collective-permute-done.10.span_a, ...), custom_call_target="tpu_custom_call" | custom-call | flops 100000000 | bytes 1048576 | tf_op jit(solution)/shard_map/final/pallas_call | solution.py:428
  (1 shorter events, 0.0 us)
Async XLA Ops:
  0.0 1.1 %copy-start.2 = (f32[5,5,5,5,2,1,128]{6,5,4,3,2,1,0:T(1,128)S(1)}, f32[5,5,5,5,2,1,128]{6,5,4,3,2,1,0:T(1,128)}, u32[]{:S(2)}) copy-start(f32[5,5,5,5,2,1,128]{6,5,4,3,2,1,0:T(1,128)} %param.4) | copy-start | bytes 1920004
  1.1 13.5 %collective-permute-start.2 = (f32[104,256]{1,0:T(8,128)S(1)}, f32[104,256]{1,0:T(8,128)S(1)}, u32[]{:S(2)}, u32[]{:S(2)}) collective-permute-start(f32[104,256]{1,0:T(8,128)S(1)} %get-tuple-element.37), channel_id=1, source_target_pairs={{0,1},{1,0},{2,3},{3,2},{4,5},{5,4},{6,7},{7,6},{8,9},{9,8},{10,11... | collective-permute-start | bytes 319496 | tf_op jit(solution)/shard_map/ppermute | solution.py:446
  4.2 10.4 %collective-permute-start.3 = (f32[104,256]{1,0:T(8,128)S(1)}, f32[104,256]{1,0:T(8,128)S(1)}, u32[]{:S(2)}, u32[]{:S(2)}) collective-permute-start(f32[104,256]{1,0:T(8,128)S(1)} %get-tuple-element.38), channel_id=1, source_target_pairs={{1,2},{2,1},{5,6},{6,5},{9,10},{10,9},{13,14},{14,13},{17,18},{18,... | collective-permute-start | bytes 319496 | tf_op jit(solution)/shard_map/ppermute | solution.py:446
  4.9 0.7 %copy-start.4 = (f32[5,5,5,2,1]{2,4,3,1,0:T(1,128)S(1)}, f32[5,5,5,2,1]{2,4,3,1,0:T(1,128)}, u32[]{:S(2)}) copy-start(f32[5,5,5,2,1]{2,4,3,1,0:T(1,128)} %param.5) | copy-start | bytes 3004
  5.8 8.8 %collective-permute-start = (f32[128,128]{1,0:T(8,128)S(1)}, f32[128,128]{1,0:T(8,128)S(1)}, u32[]{:S(2)}, u32[]{:S(2)}) collective-permute-start(f32[128,128]{1,0:T(8,128)S(1)} %get-tuple-element.35), channel_id=1, source_target_pairs={{0,4},{4,0},{8,12},{12,8},{16,20},{20,16},{24,28},{28,24},{1,5},{5... | collective-permute-start | bytes 196616 | tf_op jit(solution)/shard_map/ppermute | solution.py:446
  5.8 8.7 %collective-permute-start.1 = (f32[128,128]{1,0:T(8,128)S(1)}, f32[128,128]{1,0:T(8,128)S(1)}, u32[]{:S(2)}, u32[]{:S(2)}) collective-permute-start(f32[128,128]{1,0:T(8,128)S(1)} %get-tuple-element.36), channel_id=1, source_target_pairs={{4,8},{8,4},{12,16},{16,12},{20,24},{24,20},{28,0},{0,28},{5,9},{9... | collective-permute-start | bytes 196616 | tf_op jit(solution)/shard_map/ppermute | solution.py:446
  8.4 2.1 %copy-start = (bf16[2944,640]{1,0:T(8,128)(2,1)S(1)}, bf16[2944,640]{1,0:T(8,128)(2,1)}, u32[]{:S(2)}) copy-start(bf16[2944,640]{1,0:T(8,128)(2,1)} %constant.2.clone.table) | copy-start | bytes 11304964
  10.5 1.1 %copy-start.3 = (f32[5,5,5,5,2,1,128]{6,5,4,3,2,1,0:T(1,128)S(1)}, f32[5,5,5,5,2,1,128]{6,5,4,3,2,1,0:T(1,128)}, u32[]{:S(2)}) copy-start(f32[5,5,5,5,2,1,128]{6,5,4,3,2,1,0:T(1,128)} %param.4) | copy-start | bytes 1920004
  11.5 0.7 %copy-start.5 = (s32[3]{0:T(128)S(1)}, s32[3]{0:T(128)}, u32[]{:S(2)}) copy-start(s32[3]{0:T(128)} %offsets.1) | copy-start | bytes 40
  12.2 2.4 %copy-start.1 = (bf16[2944,640]{1,0:T(8,128)(2,1)S(1)}, bf16[2944,640]{1,0:T(8,128)(2,1)}, u32[]{:S(2)}) copy-start(bf16[2944,640]{1,0:T(8,128)(2,1)} %constant.2.clone.table) | copy-start | bytes 11304964
  15.2 10.6 %collective-permute-start.6 = (f32[104,256]{1,0:T(8,128)S(1)}, f32[104,256]{1,0:T(8,128)S(1)}, u32[]{:S(2)}, u32[]{:S(2)}) collective-permute-start(f32[104,256]{1,0:T(8,128)S(1)} %get-tuple-element.47), channel_id=1, source_target_pairs={{0,1},{1,0},{2,3},{3,2},{4,5},{5,4},{6,7},{7,6},{8,9},{9,8},{10,11... | collective-permute-start | bytes 319496 | tf_op jit(solution)/shard_map/ppermute | solution.py:446
  19.6 6.1 %collective-permute-start.7 = (f32[104,256]{1,0:T(8,128)S(1)}, f32[104,256]{1,0:T(8,128)S(1)}, u32[]{:S(2)}, u32[]{:S(2)}) collective-permute-start(f32[104,256]{1,0:T(8,128)S(1)} %get-tuple-element.48), channel_id=1, source_target_pairs={{1,2},{2,1},{5,6},{6,5},{9,10},{10,9},{13,14},{14,13},{17,18},{18,... | collective-permute-start | bytes 319496 | tf_op jit(solution)/shard_map/ppermute | solution.py:446
  20.7 3.2 %collective-permute-start.4 = (f32[128,128]{1,0:T(8,128)S(1)}, f32[128,128]{1,0:T(8,128)S(1)}, u32[]{:S(2)}, u32[]{:S(2)}) collective-permute-start(f32[128,128]{1,0:T(8,128)S(1)} %get-tuple-element.45), channel_id=1, source_target_pairs={{0,4},{4,0},{8,12},{12,8},{16,20},{20,16},{24,28},{28,24},{1,5},{5... | collective-permute-start | bytes 196616 | tf_op jit(solution)/shard_map/ppermute | solution.py:446
  20.7 5.0 %collective-permute-start.5 = (f32[128,128]{1,0:T(8,128)S(1)}, f32[128,128]{1,0:T(8,128)S(1)}, u32[]{:S(2)}, u32[]{:S(2)}) collective-permute-start(f32[128,128]{1,0:T(8,128)S(1)} %get-tuple-element.46), channel_id=1, source_target_pairs={{4,8},{8,4},{12,16},{16,12},{20,24},{24,20},{28,0},{0,28},{5,9},{9... | collective-permute-start | bytes 196616 | tf_op jit(solution)/shard_map/ppermute | solution.py:446
  26.3 7.3 %collective-permute-start.10 = (f32[104,256]{1,0:T(8,128)S(1)}, f32[104,256]{1,0:T(8,128)S(1)}, u32[]{:S(2)}, u32[]{:S(2)}) collective-permute-start(f32[104,256]{1,0:T(8,128)S(1)} %get-tuple-element.55), channel_id=1, source_target_pairs={{0,1},{1,0},{2,3},{3,2},{4,5},{5,4},{6,7},{7,6},{8,9},{9,8},{10,11... | collective-permute-start | bytes 319496 | tf_op jit(solution)/shard_map/ppermute | solution.py:446
  27.6 6.0 %collective-permute-start.11 = (f32[104,256]{1,0:T(8,128)S(1)}, f32[104,256]{1,0:T(8,128)S(1)}, u32[]{:S(2)}, u32[]{:S(2)}) collective-permute-start(f32[104,256]{1,0:T(8,128)S(1)} %get-tuple-element.56), channel_id=1, source_target_pairs={{1,2},{2,1},{5,6},{6,5},{9,10},{10,9},{13,14},{14,13},{17,18},{18,... | collective-permute-start | bytes 319496 | tf_op jit(solution)/shard_map/ppermute | solution.py:446
  28.7 2.4 %collective-permute-start.8 = (f32[128,128]{1,0:T(8,128)S(1)}, f32[128,128]{1,0:T(8,128)S(1)}, u32[]{:S(2)}, u32[]{:S(2)}) collective-permute-start(f32[128,128]{1,0:T(8,128)S(1)} %get-tuple-element.53), channel_id=1, source_target_pairs={{0,4},{4,0},{8,12},{12,8},{16,20},{20,16},{24,28},{28,24},{1,5},{5... | collective-permute-start | bytes 196616 | tf_op jit(solution)/shard_map/ppermute | solution.py:446
  28.8 4.9 %collective-permute-start.9 = (f32[128,128]{1,0:T(8,128)S(1)}, f32[128,128]{1,0:T(8,128)S(1)}, u32[]{:S(2)}, u32[]{:S(2)}) collective-permute-start(f32[128,128]{1,0:T(8,128)S(1)} %get-tuple-element.54), channel_id=1, source_target_pairs={{4,8},{8,4},{12,16},{16,12},{20,24},{24,20},{28,0},{0,28},{5,9},{9... | collective-permute-start | bytes 196616 | tf_op jit(solution)/shard_map/ppermute | solution.py:446

commit v3 on v2

--- a/solution.py
+++ b/solution.py
@@ -466,9 +466,9 @@
 def shards(table, state, wake_planes, bar_offsets):
     x = state.reshape(-1, 1, LANES)
     wake = wake_planes.transpose(0, 1, 3, 4, 2).reshape(50, 1, 5)
-    faces = call(begin_span_kernel, "begin_span", SPAN_OUTS, [x])
+    faces = call(begin_span_kernel, "begin_span", SPAN_OUTS, [x], flops=10**10)
     span = span_exchanged(faces)
-    *faces, inner = call(begin_pitch_kernel, "begin_pitch", PITCH_OUTS, [x, wake])
+    *faces, inner = call(begin_pitch_kernel, "begin_pitch", PITCH_OUTS, [x, wake], flops=10**10)
     pitch = pitch_exchanged(faces)
     base, partial, traces, flags = call(
         first_kernel,

time: 35.8 us -> 31.2 us (0.87)
  the two profiles are of different devices: /device:TPU:0 before, /device:TPU:12 now
where the time goes in v3:
time: 31.2 us; the launch traced here: 30.9 us
  starting transfers between devices  15 us (48%)
  Pallas kernels  10.8 us (35%)
  waiting for transfers between devices  3.38 us (11%)
  local copies, waits for them, and re-layouts  1.53 us (5%)
    ppermute x12, starting transfers between devices, swapped(): return lax.ppermute(value, axis, pairs)  15 us
    pallas_call x10, Pallas kernels, call(): pl.pallas_call(kernel, name=name, out_shape=[jax.ShapeDtypeStruct(shape,...  10.8 us
    ppermute x12, waiting for transfers between devices, swapped(): return lax.ppermute(value, axis, pairs)  3.38 us
    unnamed x10, local copies, waits for them, and re-layouts  1.53 us
  transfers between devices with their start and end apart: 12, of which 3 were waited for; matrix products, arithmetic and copies ran while one was open for 0% of the time, Pallas kernels for 26%

profile of v3, /device:TPU:12, one launch (start us, length us, event | category | flops | bytes accessed | tf_op | source)
XLA Modules:
  0.0 30.9 jit_solution(15041180118961431621)
XLA Ops:
  0.0 0.0 copy-start.1
  0.0 1.1 %copy-done.1 = f32[5,5,5,5,2,1,128]{6,5,4,3,2,1,0:T(1,128)S(1)} copy-done((f32[5,5,5,5,2,1,128]{6,5,4,3,2,1,0:T(1,128)S(1)}, f32[5,5,5,5,2,1,128]{6,5,4,3,2,1,0:T(1,128)}, u32[]{:S(2)}) %copy-start.1) | copy-done | bytes 640024
  1.1 0.0 copy-start.4
  1.1 0.5 %collective-permute-start.2 = (f32[104,256]{1,0:T(8,128)S(1)}, f32[104,256]{1,0:T(8,128)S(1)}, u32[]{:S(2)}, u32[]{:S(2)}) collective-permute-start(f32[104,256]{1,0:T(8,128)S(1)} %get-tuple-element.37), channel_id=1, source_target_pairs={{0,1},{1,0},{2,3},{3,2},{4,5},{5,4},{6,7},{7,6},{8,9},{9,8},{10,11... | collective-permute-start | bytes 319496 | tf_op jit(solution)/shard_map/ppermute | solution.py:446
  1.7 4.6 %collective-permute-start.3 = (f32[104,256]{1,0:T(8,128)S(1)}, f32[104,256]{1,0:T(8,128)S(1)}, u32[]{:S(2)}, u32[]{:S(2)}) collective-permute-start(f32[104,256]{1,0:T(8,128)S(1)} %get-tuple-element.38), channel_id=1, source_target_pairs={{1,2},{2,1},{5,6},{6,5},{9,10},{10,9},{13,14},{14,13},{17,18},{18,... | collective-permute-start | bytes 319496 | tf_op jit(solution)/shard_map/ppermute | solution.py:446
  6.3 0.0 copy-done.4
  6.3 0.0 copy-start
  6.3 0.0 copy-start.2
  6.3 0.0 copy-start.3
  6.3 0.1 begin_pitch.1
  6.4 0.1 collective-permute-start
  6.5 1.5 %collective-permute-start.1 = (f32[128,128]{1,0:T(8,128)S(1)}, f32[128,128]{1,0:T(8,128)S(1)}, u32[]{:S(2)}, u32[]{:S(2)}) collective-permute-start(f32[128,128]{1,0:T(8,128)S(1)} %get-tuple-element.36), channel_id=1, source_target_pairs={{4,8},{8,4},{12,16},{16,12},{20,24},{24,20},{28,0},{0,28},{5,9},{9... | collective-permute-start | bytes 196616 | tf_op jit(solution)/shard_map/ppermute | solution.py:446
  8.1 0.3 copy-done
  8.3 0.1 copy-done.2
  8.5 0.0 copy-done.3
  8.5 2.4 %first.1 = (f32[640,256]{1,0:T(8,128)S(1)}, f32[640,256]{1,0:T(8,128)S(1)}, f32[512,256]{1,0:T(8,128)S(1)}, f32[8,128]{1,0:T(8,128)S(1)}) custom-call(s32[3]{0:T(128)S(1)} %copy-done.3, f32[1250,1,128]{2,1,0:T(1,128)S(1)} %bitcast.9, bf16[2944,640]{1,0:T(8,128)(2,1)S(1)} %copy-done), custom_call_target="tpu_custom_call" | custom-call | flops 1000000000 | bytes 1048576 | tf_op jit(solution)/shard_map/first/pallas_call | solution.py:428
  10.9 0.0 collective-permute-done.pitch_a
  10.9 0.7 %collective-permute-done.1.pitch_b = f32[128,128]{1,0:T(8,128)S(1)} collective-permute-done((f32[128,128]{1,0:T(8,128)S(1)}, f32[128,128]{1,0:T(8,128)S(1)}, u32[]{:S(2)}, u32[]{:S(2)}) %collective-permute-start.1) | collective-permute-done | bytes 65568 | tf_op jit(solution)/shard_map/ppermute | solution.py:446
  11.5 0.0 collective-permute-done.2.span_a
  11.5 0.0 collective-permute-done.3.span_b
  11.5 0.5 %span_faces.2 = (f32[104,256]{1,0:T(8,128)S(1)}, f32[104,256]{1,0:T(8,128)S(1)}, bf16[640,256]{1,0:T(8,128)(2,1)S(1)}, bf16[640,256]{1,0:T(8,128)(2,1)S(1)}, f32[8,128]{1,0:T(8,128)S(1)}) custom-call(f32[8,128]{1,0:T(8,128)S(1)} %get-tuple-element.32.flags, f32[128,128]{1,0:T(8,128)S(1)} %collective-permute-done.pitch_a, ...), custom_call_target="tpu_custom_call" | custom-call | flops 100000000 | bytes 1048576 | tf_op jit(solution)/shard_map/span_faces/pallas_call | solution.py:428
  12.1 0.1 collective-permute-start.6
  12.2 1.9 %collective-permute-start.7 = (f32[104,256]{1,0:T(8,128)S(1)}, f32[104,256]{1,0:T(8,128)S(1)}, u32[]{:S(2)}, u32[]{:S(2)}) collective-permute-start(f32[104,256]{1,0:T(8,128)S(1)} %get-tuple-element.48), channel_id=1, source_target_pairs={{1,2},{2,1},{5,6},{6,5},{9,10},{10,9},{13,14},{14,13},{17,18},{18,... | collective-permute-start | bytes 319496 | tf_op jit(solution)/shard_map/ppermute | solution.py:446
  14.1 0.4 %pitch_faces.2 = (f32[128,128]{1,0:T(8,128)S(1)}, f32[128,128]{1,0:T(8,128)S(1)}, f32[256,128]{1,0:T(8,128)S(1)}) custom-call(f32[512,256]{1,0:T(8,128)S(1)} %get-tuple-element.40.faces, bf16[2944,640]{1,0:T(8,128)(2,1)S(1)} %copy-done, bf16[640,256]{1,0:T(8,128)(2,1)S(1)} %get-tuple-element.41.halo_high, bf16[640,256]{1,0:T(8,128)(2,1)S(1)} %get-tuple-element.42.halo_low, ...), custom_call_target="tpu_custom_call" | custom-call | flops 100000000 | bytes 1048576 | tf_op jit(solution)/shard_map/pitch_faces/pallas_call | solution.py:428
  14.5 0.1 collective-permute-start.4
  14.6 1.3 %collective-permute-start.5 = (f32[128,128]{1,0:T(8,128)S(1)}, f32[128,128]{1,0:T(8,128)S(1)}, u32[]{:S(2)}, u32[]{:S(2)}) collective-permute-start(f32[128,128]{1,0:T(8,128)S(1)} %get-tuple-element.46), channel_id=1, source_target_pairs={{4,8},{8,4},{12,16},{16,12},{20,24},{24,20},{28,0},{0,28},{5,9},{9... | collective-permute-start | bytes 196616 | tf_op jit(solution)/shard_map/ppermute | solution.py:446
  15.9 2.5 %later.1 = (f32[640,256]{1,0:T(8,128)S(1)}, f32[512,256]{1,0:T(8,128)S(1)}) custom-call(f32[640,256]{1,0:T(8,128)S(1)} %get-tuple-element.33.base, f32[640,256]{1,0:T(8,128)S(1)} %get-tuple-element.34.before, bf16[640,256]{1,0:T(8,128)(2,1)S(1)} %get-tuple-element.41.halo_high, bf16[640,256]{1,0:T(8,128)(2,1)S(1)} %get-tuple-element.42.halo_low, ...), custom_call_target="tpu_custom_call" | custom-call | flops 1000000000 | bytes 1048576 | tf_op jit(solution)/shard_map/later/pallas_call | solution.py:428
  18.4 0.0 collective-permute-done.4.pitch_a
  18.4 1.1 %collective-permute-done.5.pitch_b = f32[128,128]{1,0:T(8,128)S(1)} collective-permute-done((f32[128,128]{1,0:T(8,128)S(1)}, f32[128,128]{1,0:T(8,128)S(1)}, u32[]{:S(2)}, u32[]{:S(2)}) %collective-permute-start.5) | collective-permute-done | bytes 65568 | tf_op jit(solution)/shard_map/ppermute | solution.py:446
  19.5 0.0 collective-permute-done.6.span_a
  19.5 0.0 collective-permute-done.7.span_b
  19.5 0.5 %span_faces.3 = (f32[104,256]{1,0:T(8,128)S(1)}, f32[104,256]{1,0:T(8,128)S(1)}, bf16[640,256]{1,0:T(8,128)(2,1)S(1)}, bf16[640,256]{1,0:T(8,128)(2,1)S(1)}, f32[8,128]{1,0:T(8,128)S(1)}) custom-call(f32[8,128]{1,0:T(8,128)S(1)} %get-tuple-element.32.flags, f32[128,128]{1,0:T(8,128)S(1)} %collective-permute-done.4.pitch_a, ...), custom_call_target="tpu_custom_call" | custom-call | flops 100000000 | bytes 1048576 | tf_op jit(solution)/shard_map/span_faces/pallas_call | solution.py:428
  20.1 0.8 %collective-permute-start.10 = (f32[104,256]{1,0:T(8,128)S(1)}, f32[104,256]{1,0:T(8,128)S(1)}, u32[]{:S(2)}, u32[]{:S(2)}) collective-permute-start(f32[104,256]{1,0:T(8,128)S(1)} %get-tuple-element.55), channel_id=1, source_target_pairs={{0,1},{1,0},{2,3},{3,2},{4,5},{5,4},{6,7},{7,6},{8,9},{9,8},{10,11... | collective-permute-start | bytes 319496 | tf_op jit(solution)/shard_map/ppermute | solution.py:446
  20.9 3.2 %collective-permute-start.11 = (f32[104,256]{1,0:T(8,128)S(1)}, f32[104,256]{1,0:T(8,128)S(1)}, u32[]{:S(2)}, u32[]{:S(2)}) collective-permute-start(f32[104,256]{1,0:T(8,128)S(1)} %get-tuple-element.56), channel_id=1, source_target_pairs={{1,2},{2,1},{5,6},{6,5},{9,10},{10,9},{13,14},{14,13},{17,18},{18,... | collective-permute-start | bytes 319496 | tf_op jit(solution)/shard_map/ppermute | solution.py:446
  24.1 0.4 %pitch_faces.3 = (f32[128,128]{1,0:T(8,128)S(1)}, f32[128,128]{1,0:T(8,128)S(1)}, f32[256,128]{1,0:T(8,128)S(1)}) custom-call(f32[512,256]{1,0:T(8,128)S(1)} %get-tuple-element.43.faces, bf16[2944,640]{1,0:T(8,128)(2,1)S(1)} %copy-done, bf16[640,256]{1,0:T(8,128)(2,1)S(1)} %get-tuple-element.50.halo_high, bf16[640,256]{1,0:T(8,128)(2,1)S(1)} %get-tuple-element.51.halo_low, ...), custom_call_target="tpu_custom_call" | custom-call | flops 100000000 | bytes 1048576 | tf_op jit(solution)/shard_map/pitch_faces/pallas_call | solution.py:428
  24.5 0.1 collective-permute-start.8
  24.5 0.8 %collective-permute-start.9 = (f32[128,128]{1,0:T(8,128)S(1)}, f32[128,128]{1,0:T(8,128)S(1)}, u32[]{:S(2)}, u32[]{:S(2)}) collective-permute-start(f32[128,128]{1,0:T(8,128)S(1)} %get-tuple-element.54), channel_id=1, source_target_pairs={{4,8},{8,4},{12,16},{16,12},{20,24},{24,20},{28,0},{0,28},{5,9},{9... | collective-permute-start | bytes 196616 | tf_op jit(solution)/shard_map/ppermute | solution.py:446
  25.3 2.2 %last.1.before = f32[640,256]{1,0:T(8,128)S(1)} custom-call(f32[640,256]{1,0:T(8,128)S(1)} %get-tuple-element.33.base, f32[640,256]{1,0:T(8,128)S(1)} %get-tuple-element.58.before, bf16[640,256]{1,0:T(8,128)(2,1)S(1)} %get-tuple-element.50.halo_high, bf16[640,256]{1,0:T(8,128)(2,1)S(1)} %get-tuple-element.51.halo_low, bf16[2944,640]{1,0:T(8,128)(2,1)S(1)} %copy-done), custom_call_target="tpu_custom_call" | custom-call | flops 1000000000 | bytes 1048576 | tf_op jit(solution)/shard_map/last/pallas_call | solution.py:428
  27.6 0.0 collective-permute-done.8.pitch_a
  27.6 1.6 %collective-permute-done.9.pitch_b = f32[128,128]{1,0:T(8,128)S(1)} collective-permute-done((f32[128,128]{1,0:T(8,128)S(1)}, f32[128,128]{1,0:T(8,128)S(1)}, u32[]{:S(2)}, u32[]{:S(2)}) %collective-permute-start.9) | collective-permute-done | bytes 65568 | tf_op jit(solution)/shard_map/ppermute | solution.py:446
  29.2 0.0 collective-permute-done.10.span_a
  29.2 0.0 collective-permute-done.11.span_b
  29.2 1.7 %final.1 = f32[1250,1,128]{2,1,0:T(1,128)} custom-call(f32[8,128]{1,0:T(8,128)S(1)} %get-tuple-element.32.flags, f32[128,128]{1,0:T(8,128)S(1)} %collective-permute-done.8.pitch_a, f32[128,128]{1,0:T(8,128)S(1)} %collective-permute-done.9.pitch_b, f32[104,256]{1,0:T(8,128)S(1)} %collective-permute-done.10.span_a, ...), custom_call_target="tpu_custom_call" | custom-call | flops 100000000 | bytes 1048576 | tf_op jit(solution)/shard_map/final/pallas_call | solution.py:428
  (1 shorter events, 0.0 us)
Async XLA Ops:
  0.0 1.1 %copy-start.1 = (f32[5,5,5,5,2,1,128]{6,5,4,3,2,1,0:T(1,128)S(1)}, f32[5,5,5,5,2,1,128]{6,5,4,3,2,1,0:T(1,128)}, u32[]{:S(2)}) copy-start(f32[5,5,5,5,2,1,128]{6,5,4,3,2,1,0:T(1,128)} %param.4) | copy-start | bytes 1920004
  1.1 5.2 %copy-start.4 = (f32[5,5,5,2,1]{2,4,3,1,0:T(1,128)S(1)}, f32[5,5,5,2,1]{2,4,3,1,0:T(1,128)}, u32[]{:S(2)}) copy-start(f32[5,5,5,2,1]{2,4,3,1,0:T(1,128)} %param.5) | copy-start | bytes 3004
  1.1 10.4 %collective-permute-start.2 = (f32[104,256]{1,0:T(8,128)S(1)}, f32[104,256]{1,0:T(8,128)S(1)}, u32[]{:S(2)}, u32[]{:S(2)}) collective-permute-start(f32[104,256]{1,0:T(8,128)S(1)} %get-tuple-element.37), channel_id=1, source_target_pairs={{0,1},{1,0},{2,3},{3,2},{4,5},{5,4},{6,7},{7,6},{8,9},{9,8},{10,11... | collective-permute-start | bytes 319496 | tf_op jit(solution)/shard_map/ppermute | solution.py:446
  1.7 9.9 %collective-permute-start.3 = (f32[104,256]{1,0:T(8,128)S(1)}, f32[104,256]{1,0:T(8,128)S(1)}, u32[]{:S(2)}, u32[]{:S(2)}) collective-permute-start(f32[104,256]{1,0:T(8,128)S(1)} %get-tuple-element.38), channel_id=1, source_target_pairs={{1,2},{2,1},{5,6},{6,5},{9,10},{10,9},{13,14},{14,13},{17,18},{18,... | collective-permute-start | bytes 319496 | tf_op jit(solution)/shard_map/ppermute | solution.py:446
  6.3 2.1 %copy-start = (bf16[2944,640]{1,0:T(8,128)(2,1)S(1)}, bf16[2944,640]{1,0:T(8,128)(2,1)}, u32[]{:S(2)}) copy-start(bf16[2944,640]{1,0:T(8,128)(2,1)} %constant.2.clone.table) | copy-start | bytes 11304964
  6.3 2.2 %copy-start.2 = (f32[5,5,5,5,2,1,128]{6,5,4,3,2,1,0:T(1,128)S(1)}, f32[5,5,5,5,2,1,128]{6,5,4,3,2,1,0:T(1,128)}, u32[]{:S(2)}) copy-start(f32[5,5,5,5,2,1,128]{6,5,4,3,2,1,0:T(1,128)} %param.4) | copy-start | bytes 1920004
  6.3 2.2 %copy-start.3 = (s32[3]{0:T(128)S(1)}, s32[3]{0:T(128)}, u32[]{:S(2)}) copy-start(s32[3]{0:T(128)} %offsets.1) | copy-start | bytes 40
  6.4 4.4 %collective-permute-start = (f32[128,128]{1,0:T(8,128)S(1)}, f32[128,128]{1,0:T(8,128)S(1)}, u32[]{:S(2)}, u32[]{:S(2)}) collective-permute-start(f32[128,128]{1,0:T(8,128)S(1)} %get-tuple-element.35), channel_id=1, source_target_pairs={{0,4},{4,0},{8,12},{12,8},{16,20},{20,16},{24,28},{28,24},{1,5},{5... | collective-permute-start | bytes 196616 | tf_op jit(solution)/shard_map/ppermute | solution.py:446
  6.5 5.0 %collective-permute-start.1 = (f32[128,128]{1,0:T(8,128)S(1)}, f32[128,128]{1,0:T(8,128)S(1)}, u32[]{:S(2)}, u32[]{:S(2)}) collective-permute-start(f32[128,128]{1,0:T(8,128)S(1)} %get-tuple-element.36), channel_id=1, source_target_pairs={{4,8},{8,4},{12,16},{16,12},{20,24},{24,20},{28,0},{0,28},{5,9},{9... | collective-permute-start | bytes 196616 | tf_op jit(solution)/shard_map/ppermute | solution.py:446
  12.1 7.4 %collective-permute-start.6 = (f32[104,256]{1,0:T(8,128)S(1)}, f32[104,256]{1,0:T(8,128)S(1)}, u32[]{:S(2)}, u32[]{:S(2)}) collective-permute-start(f32[104,256]{1,0:T(8,128)S(1)} %get-tuple-element.47), channel_id=1, source_target_pairs={{0,1},{1,0},{2,3},{3,2},{4,5},{5,4},{6,7},{7,6},{8,9},{9,8},{10,11... | collective-permute-start | bytes 319496 | tf_op jit(solution)/shard_map/ppermute | solution.py:446
  12.2 7.4 %collective-permute-start.7 = (f32[104,256]{1,0:T(8,128)S(1)}, f32[104,256]{1,0:T(8,128)S(1)}, u32[]{:S(2)}, u32[]{:S(2)}) collective-permute-start(f32[104,256]{1,0:T(8,128)S(1)} %get-tuple-element.48), channel_id=1, source_target_pairs={{1,2},{2,1},{5,6},{6,5},{9,10},{10,9},{13,14},{14,13},{17,18},{18,... | collective-permute-start | bytes 319496 | tf_op jit(solution)/shard_map/ppermute | solution.py:446
  14.5 4.0 %collective-permute-start.4 = (f32[128,128]{1,0:T(8,128)S(1)}, f32[128,128]{1,0:T(8,128)S(1)}, u32[]{:S(2)}, u32[]{:S(2)}) collective-permute-start(f32[128,128]{1,0:T(8,128)S(1)} %get-tuple-element.45), channel_id=1, source_target_pairs={{0,4},{4,0},{8,12},{12,8},{16,20},{20,16},{24,28},{28,24},{1,5},{5... | collective-permute-start | bytes 196616 | tf_op jit(solution)/shard_map/ppermute | solution.py:446
  14.6 5.0 %collective-permute-start.5 = (f32[128,128]{1,0:T(8,128)S(1)}, f32[128,128]{1,0:T(8,128)S(1)}, u32[]{:S(2)}, u32[]{:S(2)}) collective-permute-start(f32[128,128]{1,0:T(8,128)S(1)} %get-tuple-element.46), channel_id=1, source_target_pairs={{4,8},{8,4},{12,16},{16,12},{20,24},{24,20},{28,0},{0,28},{5,9},{9... | collective-permute-start | bytes 196616 | tf_op jit(solution)/shard_map/ppermute | solution.py:446
  20.1 9.1 %collective-permute-start.10 = (f32[104,256]{1,0:T(8,128)S(1)}, f32[104,256]{1,0:T(8,128)S(1)}, u32[]{:S(2)}, u32[]{:S(2)}) collective-permute-start(f32[104,256]{1,0:T(8,128)S(1)} %get-tuple-element.55), channel_id=1, source_target_pairs={{0,1},{1,0},{2,3},{3,2},{4,5},{5,4},{6,7},{7,6},{8,9},{9,8},{10,11... | collective-permute-start | bytes 319496 | tf_op jit(solution)/shard_map/ppermute | solution.py:446
  20.9 8.3 %collective-permute-start.11 = (f32[104,256]{1,0:T(8,128)S(1)}, f32[104,256]{1,0:T(8,128)S(1)}, u32[]{:S(2)}, u32[]{:S(2)}) collective-permute-start(f32[104,256]{1,0:T(8,128)S(1)} %get-tuple-element.56), channel_id=1, source_target_pairs={{1,2},{2,1},{5,6},{6,5},{9,10},{10,9},{13,14},{14,13},{17,18},{18,... | collective-permute-start | bytes 319496 | tf_op jit(solution)/shard_map/ppermute | solution.py:446
  24.5 3.1 %collective-permute-start.8 = (f32[128,128]{1,0:T(8,128)S(1)}, f32[128,128]{1,0:T(8,128)S(1)}, u32[]{:S(2)}, u32[]{:S(2)}) collective-permute-start(f32[128,128]{1,0:T(8,128)S(1)} %get-tuple-element.53), channel_id=1, source_target_pairs={{0,4},{4,0},{8,12},{12,8},{16,20},{20,16},{24,28},{28,24},{1,5},{5... | collective-permute-start | bytes 196616 | tf_op jit(solution)/shard_map/ppermute | solution.py:446
  24.5 4.7 %collective-permute-start.9 = (f32[128,128]{1,0:T(8,128)S(1)}, f32[128,128]{1,0:T(8,128)S(1)}, u32[]{:S(2)}, u32[]{:S(2)}) collective-permute-start(f32[128,128]{1,0:T(8,128)S(1)} %get-tuple-element.54), channel_id=1, source_target_pairs={{4,8},{8,4},{12,16},{16,12},{20,24},{24,20},{28,0},{0,28},{5,9},{9... | collective-permute-start | bytes 196616 | tf_op jit(solution)/shard_map/ppermute | solution.py:446

commit v4 on v3

--- a/solution.py
+++ b/solution.py
@@ -347,6 +347,9 @@
     halo[BLOCK : 2 * BLOCK, LANES:] = scales[1] * after
     above = jnp.where(span_odd, span_b[...], span_a[...])
     below = jnp.where(span_odd, span_a[...], span_b[...])
+    place = lax.axis_index("span")
+    above = jnp.where(place == lax.axis_size("span") - 1, 0.0, above)
+    below = jnp.where(place == 0, 0.0, below)
     rest = jnp.zeros((BLOCK - SPAN_ROWS, 2 * LANES), jnp.float32)
     halo[2 * BLOCK : 2 * BLOCK + SPAN_ROWS] = scales[2] * below
     halo[2 * BLOCK + SPAN_ROWS : 3 * BLOCK] = rest
@@ -437,21 +440,27 @@
     )(*args)
 
 
-def swapped(value, axis, odd, wrap):
-    size = lax.axis_size(axis)
+def swapped(value, axis, odd):
+    pitch, span = (lax.axis_size("pitch"), lax.axis_size("span"))
     pairs = []
-    for i in range(odd, size if wrap else size - 1, 2):
-        j = (i + 1) % size
-        pairs += [(i, j), (j, i)]
-    return lax.ppermute(value, axis, pairs)
+    for i in range(pitch):
+        for j in range(span):
+            if axis == "pitch":
+                other = ((i + (1 if i % 2 == odd else -1)) % pitch, j)
+            else:
+                other = (i, j + (1 if j % 2 == odd else -1))
+                if not 0 <= other[1] < span:
+                    other = (i ^ 1, j)
+            pairs.append((i * span + j, other[0] * span + other[1]))
+    return lax.ppermute(value, ("pitch", "span"), pairs)
 
 
 def span_exchanged(faces):
-    return swapped(faces[0], "span", 0, False), swapped(faces[1], "span", 1, False)
+    return swapped(faces[0], "span", 0), swapped(faces[1], "span", 1)
 
 
 def pitch_exchanged(faces):
-    return swapped(faces[0], "pitch", 0, True), swapped(faces[1], "pitch", 1, True)
+    return swapped(faces[0], "pitch", 0), swapped(faces[1], "pitch", 1)
 
 
 F32 = jnp.float32

time: 31.2 us -> 28.2 us (0.904)
  the two profiles are of different devices: /device:TPU:12 before, /device:TPU:0 now
where the time goes in v4:
time: 28.2 us; the launch traced here: 28 us
  starting transfers between devices  13.1 us (46%)
  Pallas kernels  10.9 us (39%)
  waiting for transfers between devices  2.81 us (10%)
  local copies, waits for them, and re-layouts  1.1 us (4%)
    ppermute x12, starting transfers between devices, swapped(): return lax.ppermute(value, ('pitch', 'span'), pairs)  13.1 us
    pallas_call x10, Pallas kernels, call(): pl.pallas_call(kernel, name=name, out_shape=[jax.ShapeDtypeStruct(shape,...  10.9 us
    ppermute x12, waiting for transfers between devices, swapped(): return lax.ppermute(value, ('pitch', 'span'), pairs)  2.81 us
    unnamed x10, local copies, waits for them, and re-layouts  1.1 us
  transfers between devices with their start and end apart: 12, of which 3 were waited for; matrix products, arithmetic and copies ran while one was open for 0% of the time, Pallas kernels for 29%

profile of v4, /device:TPU:0, one launch (start us, length us, event | category | flops | bytes accessed | tf_op | source)
XLA Modules:
  0.0 28.0 jit_solution(13435042151270545927)
XLA Ops:
  0.0 0.0 copy-start.1
  0.0 1.1 %copy-done.1 = f32[5,5,5,5,2,1,128]{6,5,4,3,2,1,0:T(1,128)S(1)} copy-done((f32[5,5,5,5,2,1,128]{6,5,4,3,2,1,0:T(1,128)S(1)}, f32[5,5,5,5,2,1,128]{6,5,4,3,2,1,0:T(1,128)}, u32[]{:S(2)}) %copy-start.1) | copy-done | bytes 640024
  1.1 0.0 copy-start.4
  1.1 3.1 %collective-permute-start.2 = (f32[104,256]{1,0:T(8,128)S(1)}, f32[104,256]{1,0:T(8,128)S(1)}, u32[]{:S(2)}, u32[]{:S(2)}) collective-permute-start(f32[104,256]{1,0:T(8,128)S(1)} %get-tuple-element.37), channel_id=1, source_target_pairs={{0,1},{1,0},{2,3},{3,2},{4,5},{5,4},{6,7},{7,6},{8,9},{9,8},{10,11... | collective-permute-start | bytes 319496 | tf_op jit(solution)/shard_map/ppermute | solution.py:455
  4.2 0.0 collective-permute-start.3
  4.2 0.0 copy-done.4
  4.2 0.0 copy-start
  4.2 0.0 copy-start.2
  4.2 0.0 copy-start.3
  4.3 0.1 begin_pitch.1
  4.4 0.6 %collective-permute-start = (f32[128,128]{1,0:T(8,128)S(1)}, f32[128,128]{1,0:T(8,128)S(1)}, u32[]{:S(2)}, u32[]{:S(2)}) collective-permute-start(f32[128,128]{1,0:T(8,128)S(1)} %get-tuple-element.35), channel_id=1, source_target_pairs={{0,4},{1,5},{2,6},{3,7},{4,0},{5,1},{6,2},{7,3},{8,12},{9,13},{10,... | collective-permute-start | bytes 196616 | tf_op jit(solution)/shard_map/ppermute | solution.py:455
  4.9 2.1 %collective-permute-start.1 = (f32[128,128]{1,0:T(8,128)S(1)}, f32[128,128]{1,0:T(8,128)S(1)}, u32[]{:S(2)}, u32[]{:S(2)}) collective-permute-start(f32[128,128]{1,0:T(8,128)S(1)} %get-tuple-element.36), channel_id=1, source_target_pairs={{0,28},{1,29},{2,30},{3,31},{4,8},{5,9},{6,10},{7,11},{8,4},{9,5},... | collective-permute-start | bytes 196616 | tf_op jit(solution)/shard_map/ppermute | solution.py:455
  7.1 0.0 copy-done
  7.1 0.0 copy-done.2
  7.1 0.0 copy-done.3
  7.1 2.4 %first.1 = (f32[640,256]{1,0:T(8,128)S(1)}, f32[640,256]{1,0:T(8,128)S(1)}, f32[512,256]{1,0:T(8,128)S(1)}, f32[8,128]{1,0:T(8,128)S(1)}) custom-call(s32[3]{0:T(128)S(1)} %copy-done.3, f32[1250,1,128]{2,1,0:T(1,128)S(1)} %bitcast.9, bf16[2944,640]{1,0:T(8,128)(2,1)S(1)} %copy-done), custom_call_target="tpu_custom_call" | custom-call | flops 1000000000 | bytes 1048576 | tf_op jit(solution)/shard_map/first/pallas_call | solution.py:431
  9.5 0.0 collective-permute-done.pitch_a
  9.5 0.5 %collective-permute-done.1.pitch_b = f32[128,128]{1,0:T(8,128)S(1)} collective-permute-done((f32[128,128]{1,0:T(8,128)S(1)}, f32[128,128]{1,0:T(8,128)S(1)}, u32[]{:S(2)}, u32[]{:S(2)}) %collective-permute-start.1) | collective-permute-done | bytes 65568 | tf_op jit(solution)/shard_map/ppermute | solution.py:455
  9.9 0.0 collective-permute-done.2.span_a
  9.9 0.0 collective-permute-done.3.span_b
  9.9 0.5 %span_faces.2 = (f32[104,256]{1,0:T(8,128)S(1)}, f32[104,256]{1,0:T(8,128)S(1)}, bf16[640,256]{1,0:T(8,128)(2,1)S(1)}, bf16[640,256]{1,0:T(8,128)(2,1)S(1)}, f32[8,128]{1,0:T(8,128)S(1)}) custom-call(f32[8,128]{1,0:T(8,128)S(1)} %get-tuple-element.32.flags, f32[128,128]{1,0:T(8,128)S(1)} %collective-permute-done.pitch_a, ...), custom_call_target="tpu_custom_call" | custom-call | flops 100000000 | bytes 1048576 | tf_op jit(solution)/shard_map/span_faces/pallas_call | solution.py:431
  10.5 2.7 %collective-permute-start.6 = (f32[104,256]{1,0:T(8,128)S(1)}, f32[104,256]{1,0:T(8,128)S(1)}, u32[]{:S(2)}, u32[]{:S(2)}) collective-permute-start(f32[104,256]{1,0:T(8,128)S(1)} %get-tuple-element.47), channel_id=1, source_target_pairs={{0,1},{1,0},{2,3},{3,2},{4,5},{5,4},{6,7},{7,6},{8,9},{9,8},{10,11... | collective-permute-start | bytes 319496 | tf_op jit(solution)/shard_map/ppermute | solution.py:455
  13.2 0.0 collective-permute-start.7
  13.2 0.4 %pitch_faces.2 = (f32[128,128]{1,0:T(8,128)S(1)}, f32[128,128]{1,0:T(8,128)S(1)}, f32[256,128]{1,0:T(8,128)S(1)}) custom-call(f32[512,256]{1,0:T(8,128)S(1)} %get-tuple-element.40.faces, bf16[2944,640]{1,0:T(8,128)(2,1)S(1)} %copy-done, bf16[640,256]{1,0:T(8,128)(2,1)S(1)} %get-tuple-element.41.halo_high, bf16[640,256]{1,0:T(8,128)(2,1)S(1)} %get-tuple-element.42.halo_low, ...), custom_call_target="tpu_custom_call" | custom-call | flops 100000000 | bytes 1048576 | tf_op jit(solution)/shard_map/pitch_faces/pallas_call | solution.py:431
  13.6 0.6 %collective-permute-start.4 = (f32[128,128]{1,0:T(8,128)S(1)}, f32[128,128]{1,0:T(8,128)S(1)}, u32[]{:S(2)}, u32[]{:S(2)}) collective-permute-start(f32[128,128]{1,0:T(8,128)S(1)} %get-tuple-element.45), channel_id=1, source_target_pairs={{0,4},{1,5},{2,6},{3,7},{4,0},{5,1},{6,2},{7,3},{8,12},{9,13},{10,... | collective-permute-start | bytes 196616 | tf_op jit(solution)/shard_map/ppermute | solution.py:455
  14.1 1.9 %collective-permute-start.5 = (f32[128,128]{1,0:T(8,128)S(1)}, f32[128,128]{1,0:T(8,128)S(1)}, u32[]{:S(2)}, u32[]{:S(2)}) collective-permute-start(f32[128,128]{1,0:T(8,128)S(1)} %get-tuple-element.46), channel_id=1, source_target_pairs={{0,28},{1,29},{2,30},{3,31},{4,8},{5,9},{6,10},{7,11},{8,4},{9,5},... | collective-permute-start | bytes 196616 | tf_op jit(solution)/shard_map/ppermute | solution.py:455
  16.0 2.5 %later.1 = (f32[640,256]{1,0:T(8,128)S(1)}, f32[512,256]{1,0:T(8,128)S(1)}) custom-call(f32[640,256]{1,0:T(8,128)S(1)} %get-tuple-element.33.base, f32[640,256]{1,0:T(8,128)S(1)} %get-tuple-element.34.before, bf16[640,256]{1,0:T(8,128)(2,1)S(1)} %get-tuple-element.41.halo_high, bf16[640,256]{1,0:T(8,128)(2,1)S(1)} %get-tuple-element.42.halo_low, ...), custom_call_target="tpu_custom_call" | custom-call | flops 1000000000 | bytes 1048576 | tf_op jit(solution)/shard_map/later/pallas_call | solution.py:431
  18.6 0.0 collective-permute-done.4.pitch_a
  18.6 0.6 %collective-permute-done.5.pitch_b = f32[128,128]{1,0:T(8,128)S(1)} collective-permute-done((f32[128,128]{1,0:T(8,128)S(1)}, f32[128,128]{1,0:T(8,128)S(1)}, u32[]{:S(2)}, u32[]{:S(2)}) %collective-permute-start.5) | collective-permute-done | bytes 65568 | tf_op jit(solution)/shard_map/ppermute | solution.py:455
  19.2 0.0 collective-permute-done.6.span_a
  19.2 0.0 collective-permute-done.7.span_b
  19.2 0.5 %span_faces.3 = (f32[104,256]{1,0:T(8,128)S(1)}, f32[104,256]{1,0:T(8,128)S(1)}, bf16[640,256]{1,0:T(8,128)(2,1)S(1)}, bf16[640,256]{1,0:T(8,128)(2,1)S(1)}, f32[8,128]{1,0:T(8,128)S(1)}) custom-call(f32[8,128]{1,0:T(8,128)S(1)} %get-tuple-element.32.flags, f32[128,128]{1,0:T(8,128)S(1)} %collective-permute-done.4.pitch_a, ...), custom_call_target="tpu_custom_call" | custom-call | flops 100000000 | bytes 1048576 | tf_op jit(solution)/shard_map/span_faces/pallas_call | solution.py:431
  19.7 0.6 %collective-permute-start.10 = (f32[104,256]{1,0:T(8,128)S(1)}, f32[104,256]{1,0:T(8,128)S(1)}, u32[]{:S(2)}, u32[]{:S(2)}) collective-permute-start(f32[104,256]{1,0:T(8,128)S(1)} %get-tuple-element.55), channel_id=1, source_target_pairs={{0,1},{1,0},{2,3},{3,2},{4,5},{5,4},{6,7},{7,6},{8,9},{9,8},{10,11... | collective-permute-start | bytes 319496 | tf_op jit(solution)/shard_map/ppermute | solution.py:455
  20.3 0.0 collective-permute-start.11
  20.3 0.4 %pitch_faces.3 = (f32[128,128]{1,0:T(8,128)S(1)}, f32[128,128]{1,0:T(8,128)S(1)}, f32[256,128]{1,0:T(8,128)S(1)}) custom-call(f32[512,256]{1,0:T(8,128)S(1)} %get-tuple-element.43.faces, bf16[2944,640]{1,0:T(8,128)(2,1)S(1)} %copy-done, bf16[640,256]{1,0:T(8,128)(2,1)S(1)} %get-tuple-element.50.halo_high, bf16[640,256]{1,0:T(8,128)(2,1)S(1)} %get-tuple-element.51.halo_low, ...), custom_call_target="tpu_custom_call" | custom-call | flops 100000000 | bytes 1048576 | tf_op jit(solution)/shard_map/pitch_faces/pallas_call | solution.py:431
  20.7 0.6 %collective-permute-start.8 = (f32[128,128]{1,0:T(8,128)S(1)}, f32[128,128]{1,0:T(8,128)S(1)}, u32[]{:S(2)}, u32[]{:S(2)}) collective-permute-start(f32[128,128]{1,0:T(8,128)S(1)} %get-tuple-element.53), channel_id=1, source_target_pairs={{0,4},{1,5},{2,6},{3,7},{4,0},{5,1},{6,2},{7,3},{8,12},{9,13},{10,... | collective-permute-start | bytes 196616 | tf_op jit(solution)/shard_map/ppermute | solution.py:455
  21.2 1.0 %collective-permute-start.9 = (f32[128,128]{1,0:T(8,128)S(1)}, f32[128,128]{1,0:T(8,128)S(1)}, u32[]{:S(2)}, u32[]{:S(2)}) collective-permute-start(f32[128,128]{1,0:T(8,128)S(1)} %get-tuple-element.54), channel_id=1, source_target_pairs={{0,28},{1,29},{2,30},{3,31},{4,8},{5,9},{6,10},{7,11},{8,4},{9,5},... | collective-permute-start | bytes 196616 | tf_op jit(solution)/shard_map/ppermute | solution.py:455
  22.3 2.2 %last.1.before = f32[640,256]{1,0:T(8,128)S(1)} custom-call(f32[640,256]{1,0:T(8,128)S(1)} %get-tuple-element.33.base, f32[640,256]{1,0:T(8,128)S(1)} %get-tuple-element.58.before, bf16[640,256]{1,0:T(8,128)(2,1)S(1)} %get-tuple-element.50.halo_high, bf16[640,256]{1,0:T(8,128)(2,1)S(1)} %get-tuple-element.51.halo_low, bf16[2944,640]{1,0:T(8,128)(2,1)S(1)} %copy-done), custom_call_target="tpu_custom_call" | custom-call | flops 1000000000 | bytes 1048576 | tf_op jit(solution)/shard_map/last/pallas_call | solution.py:431
  24.5 0.0 collective-permute-done.8.pitch_a
  24.5 1.8 %collective-permute-done.9.pitch_b = f32[128,128]{1,0:T(8,128)S(1)} collective-permute-done((f32[128,128]{1,0:T(8,128)S(1)}, f32[128,128]{1,0:T(8,128)S(1)}, u32[]{:S(2)}, u32[]{:S(2)}) %collective-permute-start.9) | collective-permute-done | bytes 65568 | tf_op jit(solution)/shard_map/ppermute | solution.py:455
  26.3 0.0 collective-permute-done.10.span_a
  26.3 0.0 collective-permute-done.11.span_b
  26.3 1.7 %final.1 = f32[1250,1,128]{2,1,0:T(1,128)} custom-call(f32[8,128]{1,0:T(8,128)S(1)} %get-tuple-element.32.flags, f32[128,128]{1,0:T(8,128)S(1)} %collective-permute-done.8.pitch_a, f32[128,128]{1,0:T(8,128)S(1)} %collective-permute-done.9.pitch_b, f32[104,256]{1,0:T(8,128)S(1)} %collective-permute-done.10.span_a, ...), custom_call_target="tpu_custom_call" | custom-call | flops 100000000 | bytes 1048576 | tf_op jit(solution)/shard_map/final/pallas_call | solution.py:431
  (1 shorter events, 0.0 us)
Async XLA Ops:
  0.0 1.1 %copy-start.1 = (f32[5,5,5,5,2,1,128]{6,5,4,3,2,1,0:T(1,128)S(1)}, f32[5,5,5,5,2,1,128]{6,5,4,3,2,1,0:T(1,128)}, u32[]{:S(2)}) copy-start(f32[5,5,5,5,2,1,128]{6,5,4,3,2,1,0:T(1,128)} %param.4) | copy-start | bytes 1920004
  1.1 3.1 %copy-start.4 = (f32[5,5,5,2,1]{2,4,3,1,0:T(1,128)S(1)}, f32[5,5,5,2,1]{2,4,3,1,0:T(1,128)}, u32[]{:S(2)}) copy-start(f32[5,5,5,2,1]{2,4,3,1,0:T(1,128)} %param.5) | copy-start | bytes 3004
  1.1 8.8 %collective-permute-start.2 = (f32[104,256]{1,0:T(8,128)S(1)}, f32[104,256]{1,0:T(8,128)S(1)}, u32[]{:S(2)}, u32[]{:S(2)}) collective-permute-start(f32[104,256]{1,0:T(8,128)S(1)} %get-tuple-element.37), channel_id=1, source_target_pairs={{0,1},{1,0},{2,3},{3,2},{4,5},{5,4},{6,7},{7,6},{8,9},{9,8},{10,11... | collective-permute-start | bytes 319496 | tf_op jit(solution)/shard_map/ppermute | solution.py:455
  4.2 5.7 %collective-permute-start.3 = (f32[104,256]{1,0:T(8,128)S(1)}, f32[104,256]{1,0:T(8,128)S(1)}, u32[]{:S(2)}, u32[]{:S(2)}) collective-permute-start(f32[104,256]{1,0:T(8,128)S(1)} %get-tuple-element.38), channel_id=1, source_target_pairs={{0,4},{1,2},{2,1},{3,7},{4,0},{5,6},{6,5},{7,3},{8,12},{9,10},{10,... | collective-permute-start | bytes 319496 | tf_op jit(solution)/shard_map/ppermute | solution.py:455
  4.2 2.8 %copy-start = (bf16[2944,640]{1,0:T(8,128)(2,1)S(1)}, bf16[2944,640]{1,0:T(8,128)(2,1)}, u32[]{:S(2)}) copy-start(bf16[2944,640]{1,0:T(8,128)(2,1)} %constant.2.clone.table) | copy-start | bytes 11304964
  4.2 2.8 %copy-start.2 = (f32[5,5,5,5,2,1,128]{6,5,4,3,2,1,0:T(1,128)S(1)}, f32[5,5,5,5,2,1,128]{6,5,4,3,2,1,0:T(1,128)}, u32[]{:S(2)}) copy-start(f32[5,5,5,5,2,1,128]{6,5,4,3,2,1,0:T(1,128)} %param.4) | copy-start | bytes 1920004
  4.2 2.8 %copy-start.3 = (s32[3]{0:T(128)S(1)}, s32[3]{0:T(128)}, u32[]{:S(2)}) copy-start(s32[3]{0:T(128)} %offsets.1) | copy-start | bytes 40
  4.4 5.1 %collective-permute-start = (f32[128,128]{1,0:T(8,128)S(1)}, f32[128,128]{1,0:T(8,128)S(1)}, u32[]{:S(2)}, u32[]{:S(2)}) collective-permute-start(f32[128,128]{1,0:T(8,128)S(1)} %get-tuple-element.35), channel_id=1, source_target_pairs={{0,4},{1,5},{2,6},{3,7},{4,0},{5,1},{6,2},{7,3},{8,12},{9,13},{10,... | collective-permute-start | bytes 196616 | tf_op jit(solution)/shard_map/ppermute | solution.py:455
  4.9 5.0 %collective-permute-start.1 = (f32[128,128]{1,0:T(8,128)S(1)}, f32[128,128]{1,0:T(8,128)S(1)}, u32[]{:S(2)}, u32[]{:S(2)}) collective-permute-start(f32[128,128]{1,0:T(8,128)S(1)} %get-tuple-element.36), channel_id=1, source_target_pairs={{0,28},{1,29},{2,30},{3,31},{4,8},{5,9},{6,10},{7,11},{8,4},{9,5},... | collective-permute-start | bytes 196616 | tf_op jit(solution)/shard_map/ppermute | solution.py:455
  10.5 8.7 %collective-permute-start.6 = (f32[104,256]{1,0:T(8,128)S(1)}, f32[104,256]{1,0:T(8,128)S(1)}, u32[]{:S(2)}, u32[]{:S(2)}) collective-permute-start(f32[104,256]{1,0:T(8,128)S(1)} %get-tuple-element.47), channel_id=1, source_target_pairs={{0,1},{1,0},{2,3},{3,2},{4,5},{5,4},{6,7},{7,6},{8,9},{9,8},{10,11... | collective-permute-start | bytes 319496 | tf_op jit(solution)/shard_map/ppermute | solution.py:455
  13.2 6.0 %collective-permute-start.7 = (f32[104,256]{1,0:T(8,128)S(1)}, f32[104,256]{1,0:T(8,128)S(1)}, u32[]{:S(2)}, u32[]{:S(2)}) collective-permute-start(f32[104,256]{1,0:T(8,128)S(1)} %get-tuple-element.48), channel_id=1, source_target_pairs={{0,4},{1,2},{2,1},{3,7},{4,0},{5,6},{6,5},{7,3},{8,12},{9,10},{10,... | collective-permute-start | bytes 319496 | tf_op jit(solution)/shard_map/ppermute | solution.py:455
  13.6 5.0 %collective-permute-start.4 = (f32[128,128]{1,0:T(8,128)S(1)}, f32[128,128]{1,0:T(8,128)S(1)}, u32[]{:S(2)}, u32[]{:S(2)}) collective-permute-start(f32[128,128]{1,0:T(8,128)S(1)} %get-tuple-element.45), channel_id=1, source_target_pairs={{0,4},{1,5},{2,6},{3,7},{4,0},{5,1},{6,2},{7,3},{8,12},{9,13},{10,... | collective-permute-start | bytes 196616 | tf_op jit(solution)/shard_map/ppermute | solution.py:455
  14.1 5.0 %collective-permute-start.5 = (f32[128,128]{1,0:T(8,128)S(1)}, f32[128,128]{1,0:T(8,128)S(1)}, u32[]{:S(2)}, u32[]{:S(2)}) collective-permute-start(f32[128,128]{1,0:T(8,128)S(1)} %get-tuple-element.46), channel_id=1, source_target_pairs={{0,28},{1,29},{2,30},{3,31},{4,8},{5,9},{6,10},{7,11},{8,4},{9,5},... | collective-permute-start | bytes 196616 | tf_op jit(solution)/shard_map/ppermute | solution.py:455
  19.7 6.5 %collective-permute-start.10 = (f32[104,256]{1,0:T(8,128)S(1)}, f32[104,256]{1,0:T(8,128)S(1)}, u32[]{:S(2)}, u32[]{:S(2)}) collective-permute-start(f32[104,256]{1,0:T(8,128)S(1)} %get-tuple-element.55), channel_id=1, source_target_pairs={{0,1},{1,0},{2,3},{3,2},{4,5},{5,4},{6,7},{7,6},{8,9},{9,8},{10,11... | collective-permute-start | bytes 319496 | tf_op jit(solution)/shard_map/ppermute | solution.py:455
  20.3 6.0 %collective-permute-start.11 = (f32[104,256]{1,0:T(8,128)S(1)}, f32[104,256]{1,0:T(8,128)S(1)}, u32[]{:S(2)}, u32[]{:S(2)}) collective-permute-start(f32[104,256]{1,0:T(8,128)S(1)} %get-tuple-element.56), channel_id=1, source_target_pairs={{0,4},{1,2},{2,1},{3,7},{4,0},{5,6},{6,5},{7,3},{8,12},{9,10},{10,... | collective-permute-start | bytes 319496 | tf_op jit(solution)/shard_map/ppermute | solution.py:455
  20.7 3.8 %collective-permute-start.8 = (f32[128,128]{1,0:T(8,128)S(1)}, f32[128,128]{1,0:T(8,128)S(1)}, u32[]{:S(2)}, u32[]{:S(2)}) collective-permute-start(f32[128,128]{1,0:T(8,128)S(1)} %get-tuple-element.53), channel_id=1, source_target_pairs={{0,4},{1,5},{2,6},{3,7},{4,0},{5,1},{6,2},{7,3},{8,12},{9,13},{10,... | collective-permute-start | bytes 196616 | tf_op jit(solution)/shard_map/ppermute | solution.py:455
  21.2 5.0 %collective-permute-start.9 = (f32[128,128]{1,0:T(8,128)S(1)}, f32[128,128]{1,0:T(8,128)S(1)}, u32[]{:S(2)}, u32[]{:S(2)}) collective-permute-start(f32[128,128]{1,0:T(8,128)S(1)} %get-tuple-element.54), channel_id=1, source_target_pairs={{0,28},{1,29},{2,30},{3,31},{4,8},{5,9},{6,10},{7,11},{8,4},{9,5},... | collective-permute-start | bytes 196616 | tf_op jit(solution)/shard_map/ppermute | solution.py:455

commit v5 on v4

--- a/solution.py
+++ b/solution.py
@@ -375,7 +375,7 @@
 
 
 def span_kernel(
-    section, flags, pitch_a, pitch_b, span_a, span_b, inner, faces, table,
+    section, flags, pitch_b, pitch_a, span_a, span_b, inner, faces, table,
     next_span_a, next_span_b, halo_high, halo_low, wake, halo,
 ):
     arrived = gather_halo(section, flags, pitch_a, pitch_b, span_a, span_b, inner, halo)
@@ -399,7 +399,7 @@
 
 
 def final_kernel(
-    flags, pitch_a, pitch_b, span_a, span_b, inner, before, table, out, halo, result, done
+    flags, pitch_b, pitch_a, span_a, span_b, inner, before, table, out, halo, result, done
 ):
     gather_halo(2, flags, pitch_a, pitch_b, span_a, span_b, inner, halo)
     total = before[...] + GAIN[2] * product(lift_table(table), *split(halo[...]))
@@ -460,7 +460,7 @@
 
 
 def pitch_exchanged(faces):
-    return swapped(faces[0], "pitch", 0), swapped(faces[1], "pitch", 1)
+    return swapped(faces[1], "pitch", 1), swapped(faces[0], "pitch", 0)
 
 
 F32 = jnp.float32

time: 28.2 us -> 27.1 us (0.961)
  starting transfers between devices: 13.1 us -> 12.4 us
  waiting for transfers between devices: 2.81 us -> 2.37 us
    ppermute x12, starting transfers between devices: 13.1 us -> 12.4 us  [swapped(): return lax.ppermute(value, ('pitch', 'span'), pairs)]
    ppermute x12, waiting for transfers between devices: 2.81 us -> 2.37 us  [swapped(): return lax.ppermute(value, ('pitch', 'span'), pairs)]
  transfers between devices with their start and end apart: 12 -> 12, of which waited for: 3 -> 2; matrix products, arithmetic and copies ran while one was open for 0% -> 0% of each run, Pallas kernels for 29% -> 30%
where the time goes in v5:
time: 27.1 us; the launch traced here: 26.9 us
  starting transfers between devices  12.4 us (46%)
  Pallas kernels  10.9 us (40%)
  waiting for transfers between devices  2.37 us (9%)
  local copies, waits for them, and re-layouts  1.1 us (4%)
    ppermute x12, starting transfers between devices, swapped(): return lax.ppermute(value, ('pitch', 'span'), pairs)  12.4 us
    pallas_call x10, Pallas kernels, call(): pl.pallas_call(kernel, name=name, out_shape=[jax.ShapeDtypeStruct(shape,...  10.9 us
    ppermute x12, waiting for transfers between devices, swapped(): return lax.ppermute(value, ('pitch', 'span'), pairs)  2.37 us
    unnamed x10, local copies, waits for them, and re-layouts  1.1 us
  transfers between devices with their start and end apart: 12, of which 2 were waited for; matrix products, arithmetic and copies ran while one was open for 0% of the time, Pallas kernels for 30%

profile of v5, /device:TPU:0, one launch (start us, length us, event | category | flops | bytes accessed | tf_op | source)
XLA Modules:
  0.0 26.9 jit_solution(11402119232385114063)
XLA Ops:
  0.0 0.0 copy-start.1
  0.0 1.1 %copy-done.1 = f32[5,5,5,5,2,1,128]{6,5,4,3,2,1,0:T(1,128)S(1)} copy-done((f32[5,5,5,5,2,1,128]{6,5,4,3,2,1,0:T(1,128)S(1)}, f32[5,5,5,5,2,1,128]{6,5,4,3,2,1,0:T(1,128)}, u32[]{:S(2)}) %copy-start.1) | copy-done | bytes 640024
  1.1 0.0 copy-start.4
  1.1 3.1 %collective-permute-start.2 = (f32[104,256]{1,0:T(8,128)S(1)}, f32[104,256]{1,0:T(8,128)S(1)}, u32[]{:S(2)}, u32[]{:S(2)}) collective-permute-start(f32[104,256]{1,0:T(8,128)S(1)} %get-tuple-element.37), channel_id=1, source_target_pairs={{0,1},{1,0},{2,3},{3,2},{4,5},{5,4},{6,7},{7,6},{8,9},{9,8},{10,11... | collective-permute-start | bytes 319496 | tf_op jit(solution)/shard_map/ppermute | solution.py:455
  4.2 0.0 collective-permute-start.3
  4.2 0.0 copy-done.4
  4.2 0.0 copy-start
  4.2 0.0 copy-start.2
  4.2 0.0 copy-start.3
  4.3 0.1 begin_pitch.1
  4.4 2.6 %collective-permute-start = (f32[128,128]{1,0:T(8,128)S(1)}, f32[128,128]{1,0:T(8,128)S(1)}, u32[]{:S(2)}, u32[]{:S(2)}) collective-permute-start(f32[128,128]{1,0:T(8,128)S(1)} %get-tuple-element.35), channel_id=1, source_target_pairs={{0,28},{1,29},{2,30},{3,31},{4,8},{5,9},{6,10},{7,11},{8,4},{9,5},... | collective-permute-start | bytes 196616 | tf_op jit(solution)/shard_map/ppermute | solution.py:455
  7.0 0.0 collective-permute-start.1
  7.0 0.0 copy-done
  7.0 0.0 copy-done.2
  7.0 0.0 copy-done.3
  7.0 2.4 %first.1 = (f32[640,256]{1,0:T(8,128)S(1)}, f32[640,256]{1,0:T(8,128)S(1)}, f32[512,256]{1,0:T(8,128)S(1)}, f32[8,128]{1,0:T(8,128)S(1)}) custom-call(s32[3]{0:T(128)S(1)} %copy-done.3, f32[1250,1,128]{2,1,0:T(1,128)S(1)} %bitcast.9, bf16[2944,640]{1,0:T(8,128)(2,1)S(1)} %copy-done), custom_call_target="tpu_custom_call" | custom-call | flops 1000000000 | bytes 1048576 | tf_op jit(solution)/shard_map/first/pallas_call | solution.py:431
  9.4 0.0 collective-permute-done.pitch_b
  9.4 0.0 collective-permute-done.1.pitch_a
  9.4 0.0 collective-permute-done.2.span_a
  9.4 0.0 collective-permute-done.3.span_b
  9.4 0.5 %span_faces.2 = (f32[104,256]{1,0:T(8,128)S(1)}, f32[104,256]{1,0:T(8,128)S(1)}, bf16[640,256]{1,0:T(8,128)(2,1)S(1)}, bf16[640,256]{1,0:T(8,128)(2,1)S(1)}, f32[8,128]{1,0:T(8,128)S(1)}) custom-call(f32[8,128]{1,0:T(8,128)S(1)} %get-tuple-element.32.flags, f32[128,128]{1,0:T(8,128)S(1)} %collective-permute-done.pitch_b, ...), custom_call_target="tpu_custom_call" | custom-call | flops 100000000 | bytes 1048576 | tf_op jit(solution)/shard_map/span_faces/pallas_call | solution.py:431
  10.0 3.4 %collective-permute-start.6 = (f32[104,256]{1,0:T(8,128)S(1)}, f32[104,256]{1,0:T(8,128)S(1)}, u32[]{:S(2)}, u32[]{:S(2)}) collective-permute-start(f32[104,256]{1,0:T(8,128)S(1)} %get-tuple-element.47), channel_id=1, source_target_pairs={{0,1},{1,0},{2,3},{3,2},{4,5},{5,4},{6,7},{7,6},{8,9},{9,8},{10,11... | collective-permute-start | bytes 319496 | tf_op jit(solution)/shard_map/ppermute | solution.py:455
  13.4 0.0 collective-permute-start.7
  13.4 0.4 %pitch_faces.2 = (f32[128,128]{1,0:T(8,128)S(1)}, f32[128,128]{1,0:T(8,128)S(1)}, f32[256,128]{1,0:T(8,128)S(1)}) custom-call(f32[512,256]{1,0:T(8,128)S(1)} %get-tuple-element.40.faces, bf16[2944,640]{1,0:T(8,128)(2,1)S(1)} %copy-done, bf16[640,256]{1,0:T(8,128)(2,1)S(1)} %get-tuple-element.41.halo_high, bf16[640,256]{1,0:T(8,128)(2,1)S(1)} %get-tuple-element.42.halo_low, ...), custom_call_target="tpu_custom_call" | custom-call | flops 100000000 | bytes 1048576 | tf_op jit(solution)/shard_map/pitch_faces/pallas_call | solution.py:431
  13.8 1.8 %collective-permute-start.4 = (f32[128,128]{1,0:T(8,128)S(1)}, f32[128,128]{1,0:T(8,128)S(1)}, u32[]{:S(2)}, u32[]{:S(2)}) collective-permute-start(f32[128,128]{1,0:T(8,128)S(1)} %get-tuple-element.45), channel_id=1, source_target_pairs={{0,28},{1,29},{2,30},{3,31},{4,8},{5,9},{6,10},{7,11},{8,4},{9,5},... | collective-permute-start | bytes 196616 | tf_op jit(solution)/shard_map/ppermute | solution.py:455
  15.6 0.0 collective-permute-start.5
  15.6 2.5 %later.1 = (f32[640,256]{1,0:T(8,128)S(1)}, f32[512,256]{1,0:T(8,128)S(1)}) custom-call(f32[640,256]{1,0:T(8,128)S(1)} %get-tuple-element.33.base, f32[640,256]{1,0:T(8,128)S(1)} %get-tuple-element.34.before, bf16[640,256]{1,0:T(8,128)(2,1)S(1)} %get-tuple-element.41.halo_high, bf16[640,256]{1,0:T(8,128)(2,1)S(1)} %get-tuple-element.42.halo_low, ...), custom_call_target="tpu_custom_call" | custom-call | flops 1000000000 | bytes 1048576 | tf_op jit(solution)/shard_map/later/pallas_call | solution.py:431
  18.2 0.8 %collective-permute-done.4.pitch_b = f32[128,128]{1,0:T(8,128)S(1)} collective-permute-done((f32[128,128]{1,0:T(8,128)S(1)}, f32[128,128]{1,0:T(8,128)S(1)}, u32[]{:S(2)}, u32[]{:S(2)}) %collective-permute-start.4) | collective-permute-done | bytes 65568 | tf_op jit(solution)/shard_map/ppermute | solution.py:455
  19.0 0.0 collective-permute-done.5.pitch_a
  19.0 0.0 collective-permute-done.6.span_a
  19.0 0.0 collective-permute-done.7.span_b
  19.0 0.5 %span_faces.3 = (f32[104,256]{1,0:T(8,128)S(1)}, f32[104,256]{1,0:T(8,128)S(1)}, bf16[640,256]{1,0:T(8,128)(2,1)S(1)}, bf16[640,256]{1,0:T(8,128)(2,1)S(1)}, f32[8,128]{1,0:T(8,128)S(1)}) custom-call(f32[8,128]{1,0:T(8,128)S(1)} %get-tuple-element.32.flags, f32[128,128]{1,0:T(8,128)S(1)} %collective-permute-done.4.pitch_b, ...), custom_call_target="tpu_custom_call" | custom-call | flops 100000000 | bytes 1048576 | tf_op jit(solution)/shard_map/span_faces/pallas_call | solution.py:431
  19.6 0.2 collective-permute-start.10
  19.7 0.0 collective-permute-start.11
  19.7 0.4 %pitch_faces.3 = (f32[128,128]{1,0:T(8,128)S(1)}, f32[128,128]{1,0:T(8,128)S(1)}, f32[256,128]{1,0:T(8,128)S(1)}) custom-call(f32[512,256]{1,0:T(8,128)S(1)} %get-tuple-element.43.faces, bf16[2944,640]{1,0:T(8,128)(2,1)S(1)} %copy-done, bf16[640,256]{1,0:T(8,128)(2,1)S(1)} %get-tuple-element.50.halo_high, bf16[640,256]{1,0:T(8,128)(2,1)S(1)} %get-tuple-element.51.halo_low, ...), custom_call_target="tpu_custom_call" | custom-call | flops 100000000 | bytes 1048576 | tf_op jit(solution)/shard_map/pitch_faces/pallas_call | solution.py:431
  20.1 1.3 %collective-permute-start.8 = (f32[128,128]{1,0:T(8,128)S(1)}, f32[128,128]{1,0:T(8,128)S(1)}, u32[]{:S(2)}, u32[]{:S(2)}) collective-permute-start(f32[128,128]{1,0:T(8,128)S(1)} %get-tuple-element.53), channel_id=1, source_target_pairs={{0,28},{1,29},{2,30},{3,31},{4,8},{5,9},{6,10},{7,11},{8,4},{9,5},... | collective-permute-start | bytes 196616 | tf_op jit(solution)/shard_map/ppermute | solution.py:455
  21.4 0.0 collective-permute-start.9
  21.4 2.2 %last.1.before = f32[640,256]{1,0:T(8,128)S(1)} custom-call(f32[640,256]{1,0:T(8,128)S(1)} %get-tuple-element.33.base, f32[640,256]{1,0:T(8,128)S(1)} %get-tuple-element.58.before, bf16[640,256]{1,0:T(8,128)(2,1)S(1)} %get-tuple-element.50.halo_high, bf16[640,256]{1,0:T(8,128)(2,1)S(1)} %get-tuple-element.51.halo_low, bf16[2944,640]{1,0:T(8,128)(2,1)S(1)} %copy-done), custom_call_target="tpu_custom_call" | custom-call | flops 1000000000 | bytes 1048576 | tf_op jit(solution)/shard_map/last/pallas_call | solution.py:431
  23.6 1.5 %collective-permute-done.8.pitch_b = f32[128,128]{1,0:T(8,128)S(1)} collective-permute-done((f32[128,128]{1,0:T(8,128)S(1)}, f32[128,128]{1,0:T(8,128)S(1)}, u32[]{:S(2)}, u32[]{:S(2)}) %collective-permute-start.8) | collective-permute-done | bytes 65568 | tf_op jit(solution)/shard_map/ppermute | solution.py:455
  25.2 0.0 collective-permute-done.9.pitch_a
  25.2 0.0 collective-permute-done.10.span_a
  25.2 0.0 collective-permute-done.11.span_b
  25.2 1.7 %final.1 = f32[1250,1,128]{2,1,0:T(1,128)} custom-call(f32[8,128]{1,0:T(8,128)S(1)} %get-tuple-element.32.flags, f32[128,128]{1,0:T(8,128)S(1)} %collective-permute-done.8.pitch_b, f32[128,128]{1,0:T(8,128)S(1)} %collective-permute-done.9.pitch_a, f32[104,256]{1,0:T(8,128)S(1)} %collective-permute-done.10.span_a, ...), custom_call_target="tpu_custom_call" | custom-call | flops 100000000 | bytes 1048576 | tf_op jit(solution)/shard_map/final/pallas_call | solution.py:431
  (1 shorter events, 0.0 us)
Async XLA Ops:
  0.0 1.1 %copy-start.1 = (f32[5,5,5,5,2,1,128]{6,5,4,3,2,1,0:T(1,128)S(1)}, f32[5,5,5,5,2,1,128]{6,5,4,3,2,1,0:T(1,128)}, u32[]{:S(2)}) copy-start(f32[5,5,5,5,2,1,128]{6,5,4,3,2,1,0:T(1,128)} %param.4) | copy-start | bytes 1920004
  1.1 3.1 %copy-start.4 = (f32[5,5,5,2,1]{2,4,3,1,0:T(1,128)S(1)}, f32[5,5,5,2,1]{2,4,3,1,0:T(1,128)}, u32[]{:S(2)}) copy-start(f32[5,5,5,2,1]{2,4,3,1,0:T(1,128)} %param.5) | copy-start | bytes 3004
  1.1 8.3 %collective-permute-start.2 = (f32[104,256]{1,0:T(8,128)S(1)}, f32[104,256]{1,0:T(8,128)S(1)}, u32[]{:S(2)}, u32[]{:S(2)}) collective-permute-start(f32[104,256]{1,0:T(8,128)S(1)} %get-tuple-element.37), channel_id=1, source_target_pairs={{0,1},{1,0},{2,3},{3,2},{4,5},{5,4},{6,7},{7,6},{8,9},{9,8},{10,11... | collective-permute-start | bytes 319496 | tf_op jit(solution)/shard_map/ppermute | solution.py:455
  4.2 5.2 %collective-permute-start.3 = (f32[104,256]{1,0:T(8,128)S(1)}, f32[104,256]{1,0:T(8,128)S(1)}, u32[]{:S(2)}, u32[]{:S(2)}) collective-permute-start(f32[104,256]{1,0:T(8,128)S(1)} %get-tuple-element.38), channel_id=1, source_target_pairs={{0,4},{1,2},{2,1},{3,7},{4,0},{5,6},{6,5},{7,3},{8,12},{9,10},{10,... | collective-permute-start | bytes 319496 | tf_op jit(solution)/shard_map/ppermute | solution.py:455
  4.2 2.8 %copy-start = (bf16[2944,640]{1,0:T(8,128)(2,1)S(1)}, bf16[2944,640]{1,0:T(8,128)(2,1)}, u32[]{:S(2)}) copy-start(bf16[2944,640]{1,0:T(8,128)(2,1)} %constant.2.clone.table) | copy-start | bytes 11304964
  4.2 2.8 %copy-start.2 = (f32[5,5,5,5,2,1,128]{6,5,4,3,2,1,0:T(1,128)S(1)}, f32[5,5,5,5,2,1,128]{6,5,4,3,2,1,0:T(1,128)}, u32[]{:S(2)}) copy-start(f32[5,5,5,5,2,1,128]{6,5,4,3,2,1,0:T(1,128)} %param.4) | copy-start | bytes 1920004
  4.2 2.8 %copy-start.3 = (s32[3]{0:T(128)S(1)}, s32[3]{0:T(128)}, u32[]{:S(2)}) copy-start(s32[3]{0:T(128)} %offsets.1) | copy-start | bytes 40
  4.4 5.0 %collective-permute-start = (f32[128,128]{1,0:T(8,128)S(1)}, f32[128,128]{1,0:T(8,128)S(1)}, u32[]{:S(2)}, u32[]{:S(2)}) collective-permute-start(f32[128,128]{1,0:T(8,128)S(1)} %get-tuple-element.35), channel_id=1, source_target_pairs={{0,28},{1,29},{2,30},{3,31},{4,8},{5,9},{6,10},{7,11},{8,4},{9,5},... | collective-permute-start | bytes 196616 | tf_op jit(solution)/shard_map/ppermute | solution.py:455
  7.0 2.4 %collective-permute-start.1 = (f32[128,128]{1,0:T(8,128)S(1)}, f32[128,128]{1,0:T(8,128)S(1)}, u32[]{:S(2)}, u32[]{:S(2)}) collective-permute-start(f32[128,128]{1,0:T(8,128)S(1)} %get-tuple-element.36), channel_id=1, source_target_pairs={{0,4},{1,5},{2,6},{3,7},{4,0},{5,1},{6,2},{7,3},{8,12},{9,13},{10,... | collective-permute-start | bytes 196616 | tf_op jit(solution)/shard_map/ppermute | solution.py:455
  10.0 9.0 %collective-permute-start.6 = (f32[104,256]{1,0:T(8,128)S(1)}, f32[104,256]{1,0:T(8,128)S(1)}, u32[]{:S(2)}, u32[]{:S(2)}) collective-permute-start(f32[104,256]{1,0:T(8,128)S(1)} %get-tuple-element.47), channel_id=1, source_target_pairs={{0,1},{1,0},{2,3},{3,2},{4,5},{5,4},{6,7},{7,6},{8,9},{9,8},{10,11... | collective-permute-start | bytes 319496 | tf_op jit(solution)/shard_map/ppermute | solution.py:455
  13.4 5.6 %collective-permute-start.7 = (f32[104,256]{1,0:T(8,128)S(1)}, f32[104,256]{1,0:T(8,128)S(1)}, u32[]{:S(2)}, u32[]{:S(2)}) collective-permute-start(f32[104,256]{1,0:T(8,128)S(1)} %get-tuple-element.48), channel_id=1, source_target_pairs={{0,4},{1,2},{2,1},{3,7},{4,0},{5,6},{6,5},{7,3},{8,12},{9,10},{10,... | collective-permute-start | bytes 319496 | tf_op jit(solution)/shard_map/ppermute | solution.py:455
  13.8 5.2 %collective-permute-start.4 = (f32[128,128]{1,0:T(8,128)S(1)}, f32[128,128]{1,0:T(8,128)S(1)}, u32[]{:S(2)}, u32[]{:S(2)}) collective-permute-start(f32[128,128]{1,0:T(8,128)S(1)} %get-tuple-element.45), channel_id=1, source_target_pairs={{0,28},{1,29},{2,30},{3,31},{4,8},{5,9},{6,10},{7,11},{8,4},{9,5},... | collective-permute-start | bytes 196616 | tf_op jit(solution)/shard_map/ppermute | solution.py:455
  15.6 3.4 %collective-permute-start.5 = (f32[128,128]{1,0:T(8,128)S(1)}, f32[128,128]{1,0:T(8,128)S(1)}, u32[]{:S(2)}, u32[]{:S(2)}) collective-permute-start(f32[128,128]{1,0:T(8,128)S(1)} %get-tuple-element.46), channel_id=1, source_target_pairs={{0,4},{1,5},{2,6},{3,7},{4,0},{5,1},{6,2},{7,3},{8,12},{9,13},{10,... | collective-permute-start | bytes 196616 | tf_op jit(solution)/shard_map/ppermute | solution.py:455
  19.6 5.6 %collective-permute-start.10 = (f32[104,256]{1,0:T(8,128)S(1)}, f32[104,256]{1,0:T(8,128)S(1)}, u32[]{:S(2)}, u32[]{:S(2)}) collective-permute-start(f32[104,256]{1,0:T(8,128)S(1)} %get-tuple-element.55), channel_id=1, source_target_pairs={{0,1},{1,0},{2,3},{3,2},{4,5},{5,4},{6,7},{7,6},{8,9},{9,8},{10,11... | collective-permute-start | bytes 319496 | tf_op jit(solution)/shard_map/ppermute | solution.py:455
  19.7 5.4 %collective-permute-start.11 = (f32[104,256]{1,0:T(8,128)S(1)}, f32[104,256]{1,0:T(8,128)S(1)}, u32[]{:S(2)}, u32[]{:S(2)}) collective-permute-start(f32[104,256]{1,0:T(8,128)S(1)} %get-tuple-element.56), channel_id=1, source_target_pairs={{0,4},{1,2},{2,1},{3,7},{4,0},{5,6},{6,5},{7,3},{8,12},{9,10},{10,... | collective-permute-start | bytes 319496 | tf_op jit(solution)/shard_map/ppermute | solution.py:455
  20.1 5.1 %collective-permute-start.8 = (f32[128,128]{1,0:T(8,128)S(1)}, f32[128,128]{1,0:T(8,128)S(1)}, u32[]{:S(2)}, u32[]{:S(2)}) collective-permute-start(f32[128,128]{1,0:T(8,128)S(1)} %get-tuple-element.53), channel_id=1, source_target_pairs={{0,28},{1,29},{2,30},{3,31},{4,8},{5,9},{6,10},{7,11},{8,4},{9,5},... | collective-permute-start | bytes 196616 | tf_op jit(solution)/shard_map/ppermute | solution.py:455
  21.4 3.8 %collective-permute-start.9 = (f32[128,128]{1,0:T(8,128)S(1)}, f32[128,128]{1,0:T(8,128)S(1)}, u32[]{:S(2)}, u32[]{:S(2)}) collective-permute-start(f32[128,128]{1,0:T(8,128)S(1)} %get-tuple-element.54), channel_id=1, source_target_pairs={{0,4},{1,5},{2,6},{3,7},{4,0},{5,1},{6,2},{7,3},{8,12},{9,13},{10,... | collective-permute-start | bytes 196616 | tf_op jit(solution)/shard_map/ppermute | solution.py:455

commit v6 on v5

--- a/solution.py
+++ b/solution.py
@@ -22,6 +22,7 @@
 TAIL = 5 * MAIN
 PER_VAR = 128
 ROWS = 5 * PER_VAR
+FINAL_GROUPS = ((0, 1), (2, 3, 4))
 TILES = ((0, 0, 2), (1, 2, 4), (4, 4, 5))
 BLOCK = 128
 SPAN_ROWS = 104
@@ -336,25 +337,26 @@
     advance_body(section, base, state, table, partial, faces[0] if faces else None)
 
 
-def gather_halo(section, flags, pitch_a, pitch_b, span_a, span_b, inner, halo):
+def gather_halo(section, flags, pitch_a, pitch_b, span_a, span_b, inner, halo_high, halo_low):
+    def put(block, first, values):
+        at = (slice(block * BLOCK, (block + 1) * BLOCK), slice(first, first + values.shape[1]))
+        halo_high[at], halo_low[at] = split(half_scales()[block] * values)
+
     pitch_odd, span_odd = parities()
     after = jnp.where(pitch_odd, pitch_b[...], pitch_a[...])
     before = jnp.where(pitch_odd, pitch_a[...], pitch_b[...])
-    scales = half_scales()
-    halo[0:BLOCK, :LANES] = scales[0] * before
-    halo[0:BLOCK, LANES:] = scales[0] * inner[0:BLOCK]
-    halo[BLOCK : 2 * BLOCK, :LANES] = scales[1] * inner[BLOCK:]
-    halo[BLOCK : 2 * BLOCK, LANES:] = scales[1] * after
+    put(0, 0, before)
+    put(0, LANES, inner[0:BLOCK])
+    put(1, 0, inner[BLOCK:])
+    put(1, LANES, after)
     above = jnp.where(span_odd, span_b[...], span_a[...])
     below = jnp.where(span_odd, span_a[...], span_b[...])
     place = lax.axis_index("span")
     above = jnp.where(place == lax.axis_size("span") - 1, 0.0, above)
     below = jnp.where(place == 0, 0.0, below)
     rest = jnp.zeros((BLOCK - SPAN_ROWS, 2 * LANES), jnp.float32)
-    halo[2 * BLOCK : 2 * BLOCK + SPAN_ROWS] = scales[2] * below
-    halo[2 * BLOCK + SPAN_ROWS : 3 * BLOCK] = rest
-    halo[3 * BLOCK : 3 * BLOCK + SPAN_ROWS] = scales[3] * above
-    halo[3 * BLOCK + SPAN_ROWS : 4 * BLOCK] = rest
+    put(2, 0, jnp.concatenate([below, rest], axis=0))
+    put(3, 0, jnp.concatenate([above, rest], axis=0))
     wake = before[WAKE_ROW : WAKE_ROW + 2]
     moved = flags[0:1, section : section + 1] > 0.5
     rows = lax.broadcasted_iota(jnp.int32, (BLOCK, LANES), 0)
@@ -362,62 +364,59 @@
     for e in range(2):
         row = jnp.where(moved, wake[1 - e : 2 - e], wake[e : e + 1])
         column = jnp.sum(jnp.where(rows == cols, row, 0.0), axis=1, keepdims=True)
-        halo[4 * BLOCK :, e * LANES : (e + 1) * LANES] = jnp.where(
-            cols == 0, scales[4] * column, 0.0
-        )
+        put(4, e * LANES, jnp.where(cols == 0, column, 0.0))
     return wake
 
 
 def next_traces(section, side, faces, table, high, low):
     at = LINK_AT + side * 2 * BLOCK
     rows = slice(side * 2 * BLOCK, (side + 1) * 2 * BLOCK)
-    return faces[rows] + GAIN[section] * product(table[at : at + 2 * BLOCK], high, low)
-
-
-def span_kernel(
-    section, flags, pitch_b, pitch_a, span_a, span_b, inner, faces, table,
-    next_span_a, next_span_b, halo_high, halo_low, wake, halo,
+    return faces[rows] + GAIN[section] * dot(table[at : at + 2 * BLOCK], high)
+
+
+def exchange_kernel(
+    section, flags, span_a, span_b, pitch_b, pitch_a, inner, faces, table,
+    next_pitch_a, next_pitch_b, next_inner, next_span_a, next_span_b, halo_high, halo_low,
 ):
-    arrived = gather_halo(section, flags, pitch_a, pitch_b, span_a, span_b, inner, halo)
-    wake[...] = jnp.concatenate([arrived, jnp.zeros((6, LANES), jnp.float32)], axis=0)
-    high, low = split(halo[...])
-    halo_high[...] = high
-    halo_low[...] = low
-    _, span_odd = parities()
-    traces = next_traces(section, 1, faces, table, high, low)
-    emit_span_faces(traces, span_odd, next_span_a, next_span_b)
-
-
-def pitch_kernel(
-    section, faces, table, halo_high, halo_low, wake, next_pitch_a, next_pitch_b, next_inner
-):
-    pitch_odd, _ = parities()
-    traces = next_traces(section, 0, faces, table, halo_high[...], halo_low[...])
+    wake = gather_halo(
+        section, flags, pitch_a, pitch_b, span_a, span_b, inner, halo_high, halo_low
+    )
+    pitch_odd, span_odd = parities()
+    traces = faces[...] + GAIN[section] * dot(
+        table[LINK_AT : LINK_AT + TRACES], halo_high[...]
+    )
+    emit_span_faces(traces[2 * BLOCK :], span_odd, next_span_a, next_span_b)
     emit_pitch_faces(
         traces, [wake[0:1], wake[1:2]], pitch_odd, next_pitch_a, next_pitch_b, next_inner
     )
 
 
 def final_kernel(
-    flags, pitch_b, pitch_a, span_a, span_b, inner, before, table, out, halo, result, done
+    flags, span_a, span_b, pitch_b, pitch_a, inner, before, table, out,
+    halo_high, halo_low, result, done,
 ):
-    gather_halo(2, flags, pitch_a, pitch_b, span_a, span_b, inner, halo)
-    total = before[...] + GAIN[2] * product(lift_table(table), *split(halo[...]))
+    gather_halo(2, flags, pitch_a, pitch_b, span_a, span_b, inner, halo_high, halo_low)
     flat = result.reshape(result.shape[0], LANES)
     copies = []
-    for v in ORDER:
-        base = var_start(v)
-        for e in range(2):
-            lanes = slice(e * LANES, (e + 1) * LANES)
-            first = v * 250 + e
-            for a in range(5):
-                at = base + a * MAIN
-                flat[pl.ds(first + a * 50, MAIN, stride=2), :] = total[at : at + MAIN, lanes]
-            tail = base + TAIL
-            flat[pl.ds(first + 2 * MAIN, 5, stride=50), :] = total[tail : tail + 5, lanes]
-        part = pl.ds(v * 250, 250)
-        copies.append(pltpu.make_async_copy(result.at[part], out.at[part], done.at[v]))
-        copies[-1].start()
+    for group in FINAL_GROUPS:
+        start, stop = (group[0] * PER_VAR, (group[-1] + 1) * PER_VAR)
+        lifted = product(
+            table[LIFT_AT + start : LIFT_AT + stop], halo_high[...], halo_low[...]
+        )
+        total = before[start:stop] + GAIN[2] * lifted
+        for place in group:
+            v, base = (ORDER[place], place * PER_VAR - start)
+            for e in range(2):
+                lanes = slice(e * LANES, (e + 1) * LANES)
+                first = v * 250 + e
+                for a in range(5):
+                    at = base + a * MAIN
+                    flat[pl.ds(first + a * 50, MAIN, stride=2), :] = total[at : at + MAIN, lanes]
+                tail = base + TAIL
+                flat[pl.ds(first + 2 * MAIN, 5, stride=50), :] = total[tail : tail + 5, lanes]
+            part = pl.ds(v * 250, 250)
+            copies.append(pltpu.make_async_copy(result.at[part], out.at[part], done.at[v]))
+            copies[-1].start()
     for copy in copies:
         copy.wait()
 
@@ -488,23 +487,15 @@
         flops=10**9,
     )
     for section in range(2):
-        *faces, high, low, carried = call(
-            functools.partial(span_kernel, section),
-            "span_faces",
-            SPAN_OUTS + HALO_OUTS + [SMALL_OUT],
-            [flags, *pitch, *span, inner, traces, table],
-            scratch=[pltpu.VMEM((HALO, 2 * LANES), F32)],
+        next_a, next_b, inner, *faces, high, low = call(
+            functools.partial(exchange_kernel, section),
+            "exchange",
+            PITCH_OUTS + SPAN_OUTS + HALO_OUTS,
+            [flags, span[0], span[1], pitch[0], pitch[1], inner, traces, table],
             flops=10**8,
         )
         span = span_exchanged(faces)
-        *faces, inner = call(
-            functools.partial(pitch_kernel, section),
-            "pitch_faces",
-            PITCH_OUTS,
-            [traces, table, high, low, carried],
-            flops=10**8,
-        )
-        pitch = pitch_exchanged(faces)
+        pitch = pitch_exchanged([next_a, next_b])
         last = section == 1
         partial, *traces = call(
             functools.partial(later_kernel, section + 1),
@@ -519,9 +510,9 @@
         final_kernel,
         "final",
         [(x.shape, F32)],
-        [flags, *pitch, *span, inner, partial, table],
+        [flags, span[0], span[1], pitch[0], pitch[1], inner, partial, table],
         scratch=[
-            pltpu.VMEM((HALO, 2 * LANES), F32),
+            *[pltpu.VMEM(shape, dtype) for shape, dtype in HALO_OUTS],
             pltpu.VMEM(x.shape, F32),
             pltpu.SemaphoreType.DMA((5,)),
         ],

time: 27.1 us -> 25.9 us (0.956)
  Pallas kernels: 10.9 us -> 9.77 us
    pallas_call x10 -> x8, Pallas kernels: 10.9 us -> 9.77 us  [call(): pl.pallas_call(kernel, name=name, out_shape=[jax.ShapeDtypeStruct(shape,...]
  transfers between devices with their start and end apart: 12 -> 12, of which waited for: 2 -> 2; matrix products, arithmetic and copies ran while one was open for 0% -> 0% of each run, Pallas kernels for 30% -> 28%
where the time goes in v6:
time: 25.9 us; the launch traced here: 25.7 us
  starting transfers between devices  12.4 us (48%)
  Pallas kernels  9.77 us (38%)
  waiting for transfers between devices  2.33 us (9%)
  local copies, waits for them, and re-layouts  1.1 us (4%)
    ppermute x12, starting transfers between devices, swapped(): return lax.ppermute(value, ('pitch', 'span'), pairs)  12.4 us
    pallas_call x8, Pallas kernels, call(): pl.pallas_call(kernel, name=name, out_shape=[jax.ShapeDtypeStruct(shape,...  9.77 us
    ppermute x12, waiting for transfers between devices, swapped(): return lax.ppermute(value, ('pitch', 'span'), pairs)  2.33 us
    unnamed x10, local copies, waits for them, and re-layouts  1.1 us
  transfers between devices with their start and end apart: 12, of which 2 were waited for; matrix products, arithmetic and copies ran while one was open for 0% of the time, Pallas kernels for 28%

profile of v6, /device:TPU:0, one launch (start us, length us, event | category | flops | bytes accessed | tf_op | source)
XLA Modules:
  0.0 25.7 jit_solution(14303577213027932492)
XLA Ops:
  0.0 0.0 copy-start.1
  0.0 1.1 %copy-done.1 = f32[5,5,5,5,2,1,128]{6,5,4,3,2,1,0:T(1,128)S(1)} copy-done((f32[5,5,5,5,2,1,128]{6,5,4,3,2,1,0:T(1,128)S(1)}, f32[5,5,5,5,2,1,128]{6,5,4,3,2,1,0:T(1,128)}, u32[]{:S(2)}) %copy-start.1) | copy-done | bytes 640024
  1.1 0.0 copy-start.4
  1.1 3.1 %collective-permute-start = (f32[104,256]{1,0:T(8,128)S(1)}, f32[104,256]{1,0:T(8,128)S(1)}, u32[]{:S(2)}, u32[]{:S(2)}) collective-permute-start(f32[104,256]{1,0:T(8,128)S(1)} %get-tuple-element.31), channel_id=1, source_target_pairs={{0,1},{1,0},{2,3},{3,2},{4,5},{5,4},{6,7},{7,6},{8,9},{9,8},{10,11... | collective-permute-start | bytes 319496 | tf_op jit(solution)/shard_map/ppermute | solution.py:454
  4.2 0.0 collective-permute-start.1
  4.2 0.0 copy-done.4
  4.2 0.0 copy-start
  4.2 0.0 copy-start.2
  4.2 0.0 copy-start.3
  4.3 0.1 begin_pitch.1
  4.4 2.6 %collective-permute-start.2 = (f32[128,128]{1,0:T(8,128)S(1)}, f32[128,128]{1,0:T(8,128)S(1)}, u32[]{:S(2)}, u32[]{:S(2)}) collective-permute-start(f32[128,128]{1,0:T(8,128)S(1)} %get-tuple-element.33), channel_id=1, source_target_pairs={{0,28},{1,29},{2,30},{3,31},{4,8},{5,9},{6,10},{7,11},{8,4},{9,5},... | collective-permute-start | bytes 196616 | tf_op jit(solution)/shard_map/ppermute | solution.py:454
  7.0 0.0 collective-permute-start.3
  7.0 0.0 copy-done
  7.0 0.0 copy-done.2
  7.0 0.0 copy-done.3
  7.0 2.4 %first.1 = (f32[640,256]{1,0:T(8,128)S(1)}, f32[640,256]{1,0:T(8,128)S(1)}, f32[512,256]{1,0:T(8,128)S(1)}, f32[8,128]{1,0:T(8,128)S(1)}) custom-call(s32[3]{0:T(128)S(1)} %copy-done.3, f32[1250,1,128]{2,1,0:T(1,128)S(1)} %bitcast.9, bf16[2944,640]{1,0:T(8,128)(2,1)S(1)} %copy-done), custom_call_target="tpu_custom_call" | custom-call | flops 1000000000 | bytes 1048576 | tf_op jit(solution)/shard_map/first/pallas_call | solution.py:430
  9.4 0.0 collective-permute-done.2.pitch_b
  9.4 0.0 collective-permute-done.3.pitch_a
  9.4 0.0 collective-permute-done.span_a
  9.4 0.0 collective-permute-done.1.span_b
  9.4 0.5 %exchange.2 = (f32[128,128]{1,0:T(8,128)S(1)}, f32[128,128]{1,0:T(8,128)S(1)}, f32[256,128]{1,0:T(8,128)S(1)}, f32[104,256]{1,0:T(8,128)S(1)}, f32[104,256]{1,0:...) custom-call(f32[8,128]{1,0:T(8,128)S(1)} %get-tuple-element.30.flags, ...), custom_call_target="tpu_custom_call" | custom-call | flops 100000000 | bytes 1048576 | tf_op jit(solution)/shard_map/exchange/pallas_call | solution.py:430
  9.9 3.4 %collective-permute-start.4 = (f32[104,256]{1,0:T(8,128)S(1)}, f32[104,256]{1,0:T(8,128)S(1)}, u32[]{:S(2)}, u32[]{:S(2)}) collective-permute-start(f32[104,256]{1,0:T(8,128)S(1)} %get-tuple-element.37), channel_id=1, source_target_pairs={{0,1},{1,0},{2,3},{3,2},{4,5},{5,4},{6,7},{7,6},{8,9},{9,8},{10,11... | collective-permute-start | bytes 319496 | tf_op jit(solution)/shard_map/ppermute | solution.py:454
  13.4 0.0 collective-permute-start.5
  13.4 1.8 %collective-permute-start.6 = (f32[128,128]{1,0:T(8,128)S(1)}, f32[128,128]{1,0:T(8,128)S(1)}, u32[]{:S(2)}, u32[]{:S(2)}) collective-permute-start(f32[128,128]{1,0:T(8,128)S(1)} %get-tuple-element.39), channel_id=1, source_target_pairs={{0,28},{1,29},{2,30},{3,31},{4,8},{5,9},{6,10},{7,11},{8,4},{9,5},... | collective-permute-start | bytes 196616 | tf_op jit(solution)/shard_map/ppermute | solution.py:454
  15.1 0.0 collective-permute-start.7
  15.1 2.5 %later.1 = (f32[640,256]{1,0:T(8,128)S(1)}, f32[512,256]{1,0:T(8,128)S(1)}) custom-call(f32[640,256]{1,0:T(8,128)S(1)} %get-tuple-element.42.base, f32[640,256]{1,0:T(8,128)S(1)} %get-tuple-element.43.before, bf16[640,256]{1,0:T(8,128)(2,1)S(1)} %get-tuple-element.44.halo_high, bf16[640,256]{1,0:T(8,128)(2,1)S(1)} %get-tuple-element.45.halo_low, ...), custom_call_target="tpu_custom_call" | custom-call | flops 1000000000 | bytes 1048576 | tf_op jit(solution)/shard_map/later/pallas_call | solution.py:430
  17.7 0.8 %collective-permute-done.6.pitch_b = f32[128,128]{1,0:T(8,128)S(1)} collective-permute-done((f32[128,128]{1,0:T(8,128)S(1)}, f32[128,128]{1,0:T(8,128)S(1)}, u32[]{:S(2)}, u32[]{:S(2)}) %collective-permute-start.6) | collective-permute-done | bytes 65568 | tf_op jit(solution)/shard_map/ppermute | solution.py:454
  18.5 0.0 collective-permute-done.7.pitch_a
  18.5 0.0 collective-permute-done.4.span_a
  18.5 0.0 collective-permute-done.5.span_b
  18.5 0.5 %exchange.3 = (f32[128,128]{1,0:T(8,128)S(1)}, f32[128,128]{1,0:T(8,128)S(1)}, f32[256,128]{1,0:T(8,128)S(1)}, f32[104,256]{1,0:T(8,128)S(1)}, f32[104,256]{1,0:...) custom-call(f32[8,128]{1,0:T(8,128)S(1)} %get-tuple-element.30.flags, ...), custom_call_target="tpu_custom_call" | custom-call | flops 100000000 | bytes 1048576 | tf_op jit(solution)/shard_map/exchange/pallas_call | solution.py:430
  19.0 0.1 collective-permute-start.8
  19.2 0.0 collective-permute-start.9
  19.2 1.3 %collective-permute-start.10 = (f32[128,128]{1,0:T(8,128)S(1)}, f32[128,128]{1,0:T(8,128)S(1)}, u32[]{:S(2)}, u32[]{:S(2)}) collective-permute-start(f32[128,128]{1,0:T(8,128)S(1)} %get-tuple-element.49), channel_id=1, source_target_pairs={{0,28},{1,29},{2,30},{3,31},{4,8},{5,9},{6,10},{7,11},{8,4},{9,5},... | collective-permute-start | bytes 196616 | tf_op jit(solution)/shard_map/ppermute | solution.py:454
  20.5 0.0 collective-permute-start.11
  20.5 2.2 %last.1.before = f32[640,256]{1,0:T(8,128)S(1)} custom-call(f32[640,256]{1,0:T(8,128)S(1)} %get-tuple-element.42.base, f32[640,256]{1,0:T(8,128)S(1)} %get-tuple-element.52.before, bf16[640,256]{1,0:T(8,128)(2,1)S(1)} %get-tuple-element.53.halo_high, bf16[640,256]{1,0:T(8,128)(2,1)S(1)} %get-tuple-element.54.halo_low, bf16[2944,640]{1,0:T(8,128)(2,1)S(1)} %copy-done), custom_call_target="tpu_custom_call" | custom-call | flops 1000000000 | bytes 1048576 | tf_op jit(solution)/shard_map/last/pallas_call | solution.py:430
  22.7 1.5 %collective-permute-done.10.pitch_b = f32[128,128]{1,0:T(8,128)S(1)} collective-permute-done((f32[128,128]{1,0:T(8,128)S(1)}, f32[128,128]{1,0:T(8,128)S(1)}, u32[]{:S(2)}, u32[]{:S(2)}) %collective-permute-start.10) | collective-permute-done | bytes 65568 | tf_op jit(solution)/shard_map/ppermute | solution.py:454
  24.2 0.0 collective-permute-done.11.pitch_a
  24.2 0.0 collective-permute-done.8.span_a
  24.2 0.0 collective-permute-done.9.span_b
  24.2 1.5 %final.1 = f32[1250,1,128]{2,1,0:T(1,128)} custom-call(f32[8,128]{1,0:T(8,128)S(1)} %get-tuple-element.30.flags, f32[104,256]{1,0:T(8,128)S(1)} %collective-permute-done.8.span_a, f32[104,256]{1,0:T(8,128)S(1)} %collective-permute-done.9.span_b, f32[128,128]{1,0:T(8,128)S(1)} %collective-permute-done.10.pitch_b, ...), custom_call_target="tpu_custom_call" | custom-call | flops 100000000 | bytes 1048576 | tf_op jit(solution)/shard_map/final/pallas_call | solution.py:430
  (1 shorter events, 0.0 us)
Async XLA Ops:
  0.0 1.1 %copy-start.1 = (f32[5,5,5,5,2,1,128]{6,5,4,3,2,1,0:T(1,128)S(1)}, f32[5,5,5,5,2,1,128]{6,5,4,3,2,1,0:T(1,128)}, u32[]{:S(2)}) copy-start(f32[5,5,5,5,2,1,128]{6,5,4,3,2,1,0:T(1,128)} %param.4) | copy-start | bytes 1920004
  1.1 3.1 %copy-start.4 = (f32[5,5,5,2,1]{2,4,3,1,0:T(1,128)S(1)}, f32[5,5,5,2,1]{2,4,3,1,0:T(1,128)}, u32[]{:S(2)}) copy-start(f32[5,5,5,2,1]{2,4,3,1,0:T(1,128)} %param.5) | copy-start | bytes 3004
  1.1 8.3 %collective-permute-start = (f32[104,256]{1,0:T(8,128)S(1)}, f32[104,256]{1,0:T(8,128)S(1)}, u32[]{:S(2)}, u32[]{:S(2)}) collective-permute-start(f32[104,256]{1,0:T(8,128)S(1)} %get-tuple-element.31), channel_id=1, source_target_pairs={{0,1},{1,0},{2,3},{3,2},{4,5},{5,4},{6,7},{7,6},{8,9},{9,8},{10,11... | collective-permute-start | bytes 319496 | tf_op jit(solution)/shard_map/ppermute | solution.py:454
  4.2 5.2 %collective-permute-start.1 = (f32[104,256]{1,0:T(8,128)S(1)}, f32[104,256]{1,0:T(8,128)S(1)}, u32[]{:S(2)}, u32[]{:S(2)}) collective-permute-start(f32[104,256]{1,0:T(8,128)S(1)} %get-tuple-element.32), channel_id=1, source_target_pairs={{0,4},{1,2},{2,1},{3,7},{4,0},{5,6},{6,5},{7,3},{8,12},{9,10},{10,... | collective-permute-start | bytes 319496 | tf_op jit(solution)/shard_map/ppermute | solution.py:454
  4.2 2.8 %copy-start = (bf16[2944,640]{1,0:T(8,128)(2,1)S(1)}, bf16[2944,640]{1,0:T(8,128)(2,1)}, u32[]{:S(2)}) copy-start(bf16[2944,640]{1,0:T(8,128)(2,1)} %constant.2.clone.table) | copy-start | bytes 11304964
  4.2 2.8 %copy-start.2 = (f32[5,5,5,5,2,1,128]{6,5,4,3,2,1,0:T(1,128)S(1)}, f32[5,5,5,5,2,1,128]{6,5,4,3,2,1,0:T(1,128)}, u32[]{:S(2)}) copy-start(f32[5,5,5,5,2,1,128]{6,5,4,3,2,1,0:T(1,128)} %param.4) | copy-start | bytes 1920004
  4.2 2.8 %copy-start.3 = (s32[3]{0:T(128)S(1)}, s32[3]{0:T(128)}, u32[]{:S(2)}) copy-start(s32[3]{0:T(128)} %offsets.1) | copy-start | bytes 40
  4.4 5.0 %collective-permute-start.2 = (f32[128,128]{1,0:T(8,128)S(1)}, f32[128,128]{1,0:T(8,128)S(1)}, u32[]{:S(2)}, u32[]{:S(2)}) collective-permute-start(f32[128,128]{1,0:T(8,128)S(1)} %get-tuple-element.33), channel_id=1, source_target_pairs={{0,28},{1,29},{2,30},{3,31},{4,8},{5,9},{6,10},{7,11},{8,4},{9,5},... | collective-permute-start | bytes 196616 | tf_op jit(solution)/shard_map/ppermute | solution.py:454
  7.0 2.4 %collective-permute-start.3 = (f32[128,128]{1,0:T(8,128)S(1)}, f32[128,128]{1,0:T(8,128)S(1)}, u32[]{:S(2)}, u32[]{:S(2)}) collective-permute-start(f32[128,128]{1,0:T(8,128)S(1)} %get-tuple-element.34), channel_id=1, source_target_pairs={{0,4},{1,5},{2,6},{3,7},{4,0},{5,1},{6,2},{7,3},{8,12},{9,13},{10,... | collective-permute-start | bytes 196616 | tf_op jit(solution)/shard_map/ppermute | solution.py:454
  9.9 8.6 %collective-permute-start.4 = (f32[104,256]{1,0:T(8,128)S(1)}, f32[104,256]{1,0:T(8,128)S(1)}, u32[]{:S(2)}, u32[]{:S(2)}) collective-permute-start(f32[104,256]{1,0:T(8,128)S(1)} %get-tuple-element.37), channel_id=1, source_target_pairs={{0,1},{1,0},{2,3},{3,2},{4,5},{5,4},{6,7},{7,6},{8,9},{9,8},{10,11... | collective-permute-start | bytes 319496 | tf_op jit(solution)/shard_map/ppermute | solution.py:454
  13.4 5.2 %collective-permute-start.5 = (f32[104,256]{1,0:T(8,128)S(1)}, f32[104,256]{1,0:T(8,128)S(1)}, u32[]{:S(2)}, u32[]{:S(2)}) collective-permute-start(f32[104,256]{1,0:T(8,128)S(1)} %get-tuple-element.38), channel_id=1, source_target_pairs={{0,4},{1,2},{2,1},{3,7},{4,0},{5,6},{6,5},{7,3},{8,12},{9,10},{10,... | collective-permute-start | bytes 319496 | tf_op jit(solution)/shard_map/ppermute | solution.py:454
  13.4 5.1 %collective-permute-start.6 = (f32[128,128]{1,0:T(8,128)S(1)}, f32[128,128]{1,0:T(8,128)S(1)}, u32[]{:S(2)}, u32[]{:S(2)}) collective-permute-start(f32[128,128]{1,0:T(8,128)S(1)} %get-tuple-element.39), channel_id=1, source_target_pairs={{0,28},{1,29},{2,30},{3,31},{4,8},{5,9},{6,10},{7,11},{8,4},{9,5},... | collective-permute-start | bytes 196616 | tf_op jit(solution)/shard_map/ppermute | solution.py:454
  15.1 3.4 %collective-permute-start.7 = (f32[128,128]{1,0:T(8,128)S(1)}, f32[128,128]{1,0:T(8,128)S(1)}, u32[]{:S(2)}, u32[]{:S(2)}) collective-permute-start(f32[128,128]{1,0:T(8,128)S(1)} %get-tuple-element.40), channel_id=1, source_target_pairs={{0,4},{1,5},{2,6},{3,7},{4,0},{5,1},{6,2},{7,3},{8,12},{9,13},{10,... | collective-permute-start | bytes 196616 | tf_op jit(solution)/shard_map/ppermute | solution.py:454
  19.0 5.2 %collective-permute-start.8 = (f32[104,256]{1,0:T(8,128)S(1)}, f32[104,256]{1,0:T(8,128)S(1)}, u32[]{:S(2)}, u32[]{:S(2)}) collective-permute-start(f32[104,256]{1,0:T(8,128)S(1)} %get-tuple-element.47), channel_id=1, source_target_pairs={{0,1},{1,0},{2,3},{3,2},{4,5},{5,4},{6,7},{7,6},{8,9},{9,8},{10,11... | collective-permute-start | bytes 319496 | tf_op jit(solution)/shard_map/ppermute | solution.py:454
  19.2 5.1 %collective-permute-start.9 = (f32[104,256]{1,0:T(8,128)S(1)}, f32[104,256]{1,0:T(8,128)S(1)}, u32[]{:S(2)}, u32[]{:S(2)}) collective-permute-start(f32[104,256]{1,0:T(8,128)S(1)} %get-tuple-element.48), channel_id=1, source_target_pairs={{0,4},{1,2},{2,1},{3,7},{4,0},{5,6},{6,5},{7,3},{8,12},{9,10},{10,... | collective-permute-start | bytes 319496 | tf_op jit(solution)/shard_map/ppermute | solution.py:454
  19.2 5.0 %collective-permute-start.10 = (f32[128,128]{1,0:T(8,128)S(1)}, f32[128,128]{1,0:T(8,128)S(1)}, u32[]{:S(2)}, u32[]{:S(2)}) collective-permute-start(f32[128,128]{1,0:T(8,128)S(1)} %get-tuple-element.49), channel_id=1, source_target_pairs={{0,28},{1,29},{2,30},{3,31},{4,8},{5,9},{6,10},{7,11},{8,4},{9,5},... | collective-permute-start | bytes 196616 | tf_op jit(solution)/shard_map/ppermute | solution.py:454
  20.5 3.7 %collective-permute-start.11 = (f32[128,128]{1,0:T(8,128)S(1)}, f32[128,128]{1,0:T(8,128)S(1)}, u32[]{:S(2)}, u32[]{:S(2)}) collective-permute-start(f32[128,128]{1,0:T(8,128)S(1)} %get-tuple-element.50), channel_id=1, source_target_pairs={{0,4},{1,5},{2,6},{3,7},{4,0},{5,1},{6,2},{7,3},{8,12},{9,13},{10,... | collective-permute-start | bytes 196616 | tf_op jit(solution)/shard_map/ppermute | solution.py:454

commit v7 on v6

--- a/solution.py
+++ b/solution.py
@@ -22,13 +22,13 @@
 TAIL = 5 * MAIN
 PER_VAR = 128
 ROWS = 5 * PER_VAR
-FINAL_GROUPS = ((0, 1), (2, 3, 4))
 TILES = ((0, 0, 2), (1, 2, 4), (4, 4, 5))
 BLOCK = 128
 SPAN_ROWS = 104
 TRACES = 4 * BLOCK
 HALO = 5 * BLOCK
 WAKE_ROW = 125
+FACE_PAD = 16
 TRACE_AT, LINK_AT, LIFT_AT = (0, TRACES, 2 * TRACES)
 HIGH_AT = LIFT_AT + ROWS
 LOW_AT = HIGH_AT + ROWS
@@ -331,10 +331,10 @@
 
 
 def later_kernel(section, base, before, halo_high, halo_low, table, partial, *refs):
-    *faces, state = refs
+    faces, state = refs
     lifted = product(lift_table(table), halo_high[...], halo_low[...])
     state[...] = before[...] + GAIN[section - 1] * lifted
-    advance_body(section, base, state, table, partial, faces[0] if faces else None)
+    advance_body(section, base, state, table, partial, faces)
 
 
 def gather_halo(section, flags, pitch_a, pitch_b, span_a, span_b, inner, halo_high, halo_low):
@@ -391,32 +391,100 @@
     )
 
 
+def last_kernel(base, before, halo_high, halo_low, table, rows, state, partial):
+    lifted = product(lift_table(table), halo_high[...], halo_low[...])
+    state[...] = before[...] + GAIN[1] * lifted
+    advance_body(2, base, state, table, partial, None)
+    flat = rows.reshape(rows.shape[0], LANES)
+    for e in range(2):
+        lanes = slice(e * LANES, (e + 1) * LANES)
+        for v in range(5):
+            start = var_start(v)
+            first = v * 250 + e
+            for a in range(5):
+                at = start + a * MAIN
+                flat[pl.ds(first + a * 50, MAIN, stride=2), :] = partial[at : at + MAIN, lanes]
+            tail = start + TAIL
+            flat[pl.ds(first + 2 * MAIN, 5, stride=50), :] = partial[tail : tail + 5, lanes]
+
+
+def mixed_faces(faces, s, lanes, direction, sign):
+    table = half_flux(direction, sign)
+    at = FACE_PAD + s * 25
+    rows = lax.broadcasted_iota(jnp.int32, (25, LANES), 0)
+    own = faces[at : at + 25, lanes]
+    total = float(table[0, 0]) * own
+    for i in range(5):
+        for j in range(5):
+            if i != j and table[i, j] != 0.0:
+                moved = faces[at + 5 * (j - i) : at + 5 * (j - i) + 25, lanes]
+                here = (rows >= 5 * i) & (rows < 5 * i + 5)
+                total = total + jnp.where(here, float(table[i, j]) * moved, 0.0)
+    return total
+
+
 def final_kernel(
-    flags, span_a, span_b, pitch_b, pitch_a, inner, before, table, out,
-    halo_high, halo_low, result, done,
+    flags, span_a, span_b, pitch_b, pitch_a, inner, before, out, result, after_faces,
+    before_faces, done,
 ):
-    gather_halo(2, flags, pitch_a, pitch_b, span_a, span_b, inner, halo_high, halo_low)
     flat = result.reshape(result.shape[0], LANES)
+    flat[...] = before.reshape(before.shape[0], LANES)[...]
+    pitch_odd, span_odd = parities()
+    gain = GAIN[2]
+
+    def add(start, stride, values):
+        at = pl.ds(start, values.shape[0], stride=stride)
+        flat[at, :] = flat[at, :] + values
+
+    place = lax.axis_index("span")
+    scale = gain * lift_factor(2)
+    up_scale = jnp.where(place == lax.axis_size("span") - 1, 0.0, -scale)
+    down_scale = jnp.where(place == 0, 0.0, scale)
+    for e in range(2):
+        lanes = slice(e * LANES, (e + 1) * LANES)
+        for c in range(4):
+            at = slice(c * 25, c * 25 + 25)
+            first, second = (span_a[at, lanes], span_b[at, lanes])
+            above = up_scale * jnp.where(span_odd, second, first)
+            below = down_scale * jnp.where(span_odd, first, second)
+            add(c * 250 + 8 + e, 10, above)
+            add(c * 250 + e, 10, below)
+            if c == 3:
+                add(4 * 250 + 8 + e, 10, -above)
+                add(4 * 250 + e, 10, below)
+
+    at = slice(FACE_PAD, FACE_PAD + BLOCK)
+    arrived = jnp.where(pitch_odd, pitch_a[...], pitch_b[...])
+    before_faces[at, :LANES] = arrived
+    before_faces[at, LANES:] = inner[0:BLOCK]
+    after_faces[at, :LANES] = inner[BLOCK:]
+    after_faces[at, LANES:] = jnp.where(pitch_odd, pitch_b[...], pitch_a[...])
+    scale = gain * lift_factor(1)
+    for e in range(2):
+        lanes = slice(e * LANES, (e + 1) * LANES)
+        for s in range(5):
+            add(40 + 2 * s + e, 50, -scale * mixed_faces(after_faces, s, lanes, 1, -1.0))
+            add(2 * s + e, 50, scale * mixed_faces(before_faces, s, lanes, 1, 1.0))
+
+    wake = arrived[WAKE_ROW : WAKE_ROW + 2]
+    moved = flags[0:1, 2:3] > 0.5
+    rows = lax.broadcasted_iota(jnp.int32, (25, LANES), 0)
+    cols = lax.broadcasted_iota(jnp.int32, (25, LANES), 1)
+    for e in range(2):
+        row = jnp.where(moved, wake[1 - e : 2 - e], wake[e : e + 1])
+        columns = [
+            jnp.sum(jnp.where(cols == rows + 25 * v, row, 0.0), axis=1, keepdims=True)
+            for v in range(5)
+        ]
+        inlet = combine(gain * lift_factor(0) * half_flux(0, 1.0), columns)
+        for v in range(5):
+            add(v * 250 + e, 2, jnp.where(cols == 0, inlet[v], 0.0))
+
     copies = []
-    for group in FINAL_GROUPS:
-        start, stop = (group[0] * PER_VAR, (group[-1] + 1) * PER_VAR)
-        lifted = product(
-            table[LIFT_AT + start : LIFT_AT + stop], halo_high[...], halo_low[...]
-        )
-        total = before[start:stop] + GAIN[2] * lifted
-        for place in group:
-            v, base = (ORDER[place], place * PER_VAR - start)
-            for e in range(2):
-                lanes = slice(e * LANES, (e + 1) * LANES)
-                first = v * 250 + e
-                for a in range(5):
-                    at = base + a * MAIN
-                    flat[pl.ds(first + a * 50, MAIN, stride=2), :] = total[at : at + MAIN, lanes]
-                tail = base + TAIL
-                flat[pl.ds(first + 2 * MAIN, 5, stride=50), :] = total[tail : tail + 5, lanes]
-            part = pl.ds(v * 250, 250)
-            copies.append(pltpu.make_async_copy(result.at[part], out.at[part], done.at[v]))
-            copies[-1].start()
+    for v in range(5):
+        part = pl.ds(v * 250, 250)
+        copies.append(pltpu.make_async_copy(result.at[part], out.at[part], done.at[v]))
+        copies[-1].start()
     for copy in copies:
         copy.wait()
 
@@ -496,24 +564,31 @@
         )
         span = span_exchanged(faces)
         pitch = pitch_exchanged([next_a, next_b])
-        last = section == 1
-        partial, *traces = call(
-            functools.partial(later_kernel, section + 1),
-            "last" if last else "later",
-            [STATE_OUT] if last else [STATE_OUT, TRACE_OUT],
-            [base, partial, high, low, table],
-            scratch=[pltpu.VMEM((ROWS, 2 * LANES), F32)],
-            flops=10**9,
-        )
-        traces = None if last else traces[0]
+        if section == 0:
+            partial, traces = call(
+                functools.partial(later_kernel, section + 1),
+                "later",
+                [STATE_OUT, TRACE_OUT],
+                [base, partial, high, low, table],
+                scratch=[pltpu.VMEM((ROWS, 2 * LANES), F32)],
+                flops=10**9,
+            )
+    (rows,) = call(
+        last_kernel,
+        "last",
+        [(x.shape, F32)],
+        [base, partial, high, low, table],
+        scratch=[pltpu.VMEM((ROWS, 2 * LANES), F32)] * 2,
+        flops=10**9,
+    )
     (out,) = call(
         final_kernel,
         "final",
         [(x.shape, F32)],
-        [flags, span[0], span[1], pitch[0], pitch[1], inner, partial, table],
+        [flags, span[0], span[1], pitch[0], pitch[1], inner, rows],
         scratch=[
-            *[pltpu.VMEM(shape, dtype) for shape, dtype in HALO_OUTS],
             pltpu.VMEM(x.shape, F32),
+            *[pltpu.VMEM((BLOCK + 2 * FACE_PAD, 2 * LANES), F32)] * 2,
             pltpu.SemaphoreType.DMA((5,)),
         ],
         flops=10**8,

time: 25.9 us -> 25.6 us (0.988)
  transfers between devices with their start and end apart: 12 -> 12, of which waited for: 2 -> 2; matrix products, arithmetic and copies ran while one was open for 0% -> 0% of each run, Pallas kernels for 28% -> 29%
where the time goes in v7:
time: 25.6 us; the launch traced here: 25.4 us
  starting transfers between devices  12.4 us (48%)
  Pallas kernels  9.53 us (37%)
  waiting for transfers between devices  2.33 us (9%)
  local copies, waits for them, and re-layouts  1.1 us (4%)
    ppermute x12, starting transfers between devices, swapped(): return lax.ppermute(value, ('pitch', 'span'), pairs)  12.4 us
    pallas_call x8, Pallas kernels, call(): pl.pallas_call(kernel, name=name, out_shape=[jax.ShapeDtypeStruct(shape,...  9.53 us
    ppermute x12, waiting for transfers between devices, swapped(): return lax.ppermute(value, ('pitch', 'span'), pairs)  2.33 us
    unnamed x10, local copies, waits for them, and re-layouts  1.1 us
  transfers between devices with their start and end apart: 12, of which 2 were waited for; matrix products, arithmetic and copies ran while one was open for 0% of the time, Pallas kernels for 29%

profile of v7, /device:TPU:0, one launch (start us, length us, event | category | flops | bytes accessed | tf_op | source)
XLA Modules:
  0.0 25.4 jit_solution(13131542957066885711)
XLA Ops:
  0.0 0.0 copy-start.1
  0.0 1.1 %copy-done.1 = f32[5,5,5,5,2,1,128]{6,5,4,3,2,1,0:T(1,128)S(1)} copy-done((f32[5,5,5,5,2,1,128]{6,5,4,3,2,1,0:T(1,128)S(1)}, f32[5,5,5,5,2,1,128]{6,5,4,3,2,1,0:T(1,128)}, u32[]{:S(2)}) %copy-start.1) | copy-done | bytes 640024
  1.1 0.0 copy-start.4
  1.1 3.1 %collective-permute-start = (f32[104,256]{1,0:T(8,128)S(1)}, f32[104,256]{1,0:T(8,128)S(1)}, u32[]{:S(2)}, u32[]{:S(2)}) collective-permute-start(f32[104,256]{1,0:T(8,128)S(1)} %get-tuple-element.31), channel_id=1, source_target_pairs={{0,1},{1,0},{2,3},{3,2},{4,5},{5,4},{6,7},{7,6},{8,9},{9,8},{10,11... | collective-permute-start | bytes 319496 | tf_op jit(solution)/shard_map/ppermute | solution.py:522
  4.2 0.0 collective-permute-start.1
  4.2 0.0 copy-done.4
  4.2 0.0 copy-start
  4.2 0.0 copy-start.2
  4.2 0.0 copy-start.3
  4.3 0.1 begin_pitch.1
  4.4 2.6 %collective-permute-start.2 = (f32[128,128]{1,0:T(8,128)S(1)}, f32[128,128]{1,0:T(8,128)S(1)}, u32[]{:S(2)}, u32[]{:S(2)}) collective-permute-start(f32[128,128]{1,0:T(8,128)S(1)} %get-tuple-element.33), channel_id=1, source_target_pairs={{0,28},{1,29},{2,30},{3,31},{4,8},{5,9},{6,10},{7,11},{8,4},{9,5},... | collective-permute-start | bytes 196616 | tf_op jit(solution)/shard_map/ppermute | solution.py:522
  7.0 0.0 collective-permute-start.3
  7.0 0.0 copy-done
  7.0 0.0 copy-done.2
  7.0 0.0 copy-done.3
  7.0 2.4 %first.1 = (f32[640,256]{1,0:T(8,128)S(1)}, f32[640,256]{1,0:T(8,128)S(1)}, f32[512,256]{1,0:T(8,128)S(1)}, f32[8,128]{1,0:T(8,128)S(1)}) custom-call(s32[3]{0:T(128)S(1)} %copy-done.3, f32[1250,1,128]{2,1,0:T(1,128)S(1)} %bitcast.9, bf16[2944,640]{1,0:T(8,128)(2,1)S(1)} %copy-done), custom_call_target="tpu_custom_call" | custom-call | flops 1000000000 | bytes 1048576 | tf_op jit(solution)/shard_map/first/pallas_call | solution.py:498
  9.4 0.0 collective-permute-done.2.pitch_b
  9.4 0.0 collective-permute-done.3.pitch_a
  9.4 0.0 collective-permute-done.span_a
  9.4 0.0 collective-permute-done.1.span_b
  9.4 0.5 %exchange.2 = (f32[128,128]{1,0:T(8,128)S(1)}, f32[128,128]{1,0:T(8,128)S(1)}, f32[256,128]{1,0:T(8,128)S(1)}, f32[104,256]{1,0:T(8,128)S(1)}, f32[104,256]{1,0:...) custom-call(f32[8,128]{1,0:T(8,128)S(1)} %get-tuple-element.30.flags, ...), custom_call_target="tpu_custom_call" | custom-call | flops 100000000 | bytes 1048576 | tf_op jit(solution)/shard_map/exchange/pallas_call | solution.py:498
  9.9 3.4 %collective-permute-start.4 = (f32[104,256]{1,0:T(8,128)S(1)}, f32[104,256]{1,0:T(8,128)S(1)}, u32[]{:S(2)}, u32[]{:S(2)}) collective-permute-start(f32[104,256]{1,0:T(8,128)S(1)} %get-tuple-element.37), channel_id=1, source_target_pairs={{0,1},{1,0},{2,3},{3,2},{4,5},{5,4},{6,7},{7,6},{8,9},{9,8},{10,11... | collective-permute-start | bytes 319496 | tf_op jit(solution)/shard_map/ppermute | solution.py:522
  13.4 0.0 collective-permute-start.5
  13.4 1.8 %collective-permute-start.6 = (f32[128,128]{1,0:T(8,128)S(1)}, f32[128,128]{1,0:T(8,128)S(1)}, u32[]{:S(2)}, u32[]{:S(2)}) collective-permute-start(f32[128,128]{1,0:T(8,128)S(1)} %get-tuple-element.39), channel_id=1, source_target_pairs={{0,28},{1,29},{2,30},{3,31},{4,8},{5,9},{6,10},{7,11},{8,4},{9,5},... | collective-permute-start | bytes 196616 | tf_op jit(solution)/shard_map/ppermute | solution.py:522
  15.1 0.0 collective-permute-start.7
  15.1 2.5 %later.1 = (f32[640,256]{1,0:T(8,128)S(1)}, f32[512,256]{1,0:T(8,128)S(1)}) custom-call(f32[640,256]{1,0:T(8,128)S(1)} %get-tuple-element.42.base, f32[640,256]{1,0:T(8,128)S(1)} %get-tuple-element.43.before, bf16[640,256]{1,0:T(8,128)(2,1)S(1)} %get-tuple-element.44.halo_high, bf16[640,256]{1,0:T(8,128)(2,1)S(1)} %get-tuple-element.45.halo_low, ...), custom_call_target="tpu_custom_call" | custom-call | flops 1000000000 | bytes 1048576 | tf_op jit(solution)/shard_map/later/pallas_call | solution.py:498
  17.7 0.8 %collective-permute-done.6.pitch_b = f32[128,128]{1,0:T(8,128)S(1)} collective-permute-done((f32[128,128]{1,0:T(8,128)S(1)}, f32[128,128]{1,0:T(8,128)S(1)}, u32[]{:S(2)}, u32[]{:S(2)}) %collective-permute-start.6) | collective-permute-done | bytes 65568 | tf_op jit(solution)/shard_map/ppermute | solution.py:522
  18.5 0.0 collective-permute-done.7.pitch_a
  18.5 0.0 collective-permute-done.4.span_a
  18.5 0.0 collective-permute-done.5.span_b
  18.5 0.5 %exchange.3 = (f32[128,128]{1,0:T(8,128)S(1)}, f32[128,128]{1,0:T(8,128)S(1)}, f32[256,128]{1,0:T(8,128)S(1)}, f32[104,256]{1,0:T(8,128)S(1)}, f32[104,256]{1,0:...) custom-call(f32[8,128]{1,0:T(8,128)S(1)} %get-tuple-element.30.flags, ...), custom_call_target="tpu_custom_call" | custom-call | flops 100000000 | bytes 1048576 | tf_op jit(solution)/shard_map/exchange/pallas_call | solution.py:498
  19.0 0.1 collective-permute-start.8
  19.2 0.0 collective-permute-start.9
  19.2 1.3 %collective-permute-start.10 = (f32[128,128]{1,0:T(8,128)S(1)}, f32[128,128]{1,0:T(8,128)S(1)}, u32[]{:S(2)}, u32[]{:S(2)}) collective-permute-start(f32[128,128]{1,0:T(8,128)S(1)} %get-tuple-element.49), channel_id=1, source_target_pairs={{0,28},{1,29},{2,30},{3,31},{4,8},{5,9},{6,10},{7,11},{8,4},{9,5},... | collective-permute-start | bytes 196616 | tf_op jit(solution)/shard_map/ppermute | solution.py:522
  20.5 0.0 collective-permute-start.11
  20.5 2.2 %last.1.before = f32[1250,1,128]{2,1,0:T(1,128)S(1)} custom-call(f32[640,256]{1,0:T(8,128)S(1)} %get-tuple-element.42.base, f32[640,256]{1,0:T(8,128)S(1)} %get-tuple-element.52.before, bf16[640,256]{1,0:T(8,128)(2,1)S(1)} %get-tuple-element.53.halo_high, bf16[640,256]{1,0:T(8,128)(2,1)S(1)} %get-tuple-element.54.halo_low, bf16[2944,640]{1,0:T(8,128)(2,1)S(1)} %copy-done), custom_call_target="tpu_custom_call" | custom-call | flops 1000000000 | bytes 1048576 | tf_op jit(solution)/shard_map/last/pallas_call | solution.py:498
  22.7 1.5 %collective-permute-done.10.pitch_b = f32[128,128]{1,0:T(8,128)S(1)} collective-permute-done((f32[128,128]{1,0:T(8,128)S(1)}, f32[128,128]{1,0:T(8,128)S(1)}, u32[]{:S(2)}, u32[]{:S(2)}) %collective-permute-start.10) | collective-permute-done | bytes 65568 | tf_op jit(solution)/shard_map/ppermute | solution.py:522
  24.2 0.0 collective-permute-done.11.pitch_a
  24.2 0.0 collective-permute-done.8.span_a
  24.2 0.0 collective-permute-done.9.span_b
  24.2 1.2 %final.1 = f32[1250,1,128]{2,1,0:T(1,128)} custom-call(f32[8,128]{1,0:T(8,128)S(1)} %get-tuple-element.30.flags, f32[104,256]{1,0:T(8,128)S(1)} %collective-permute-done.8.span_a, f32[104,256]{1,0:T(8,128)S(1)} %collective-permute-done.9.span_b, f32[128,128]{1,0:T(8,128)S(1)} %collective-permute-done.10.pitch_b, ...), custom_call_target="tpu_custom_call" | custom-call | flops 100000000 | bytes 1048576 | tf_op jit(solution)/shard_map/final/pallas_call | solution.py:498
  (1 shorter events, 0.0 us)
Async XLA Ops:
  0.0 1.1 %copy-start.1 = (f32[5,5,5,5,2,1,128]{6,5,4,3,2,1,0:T(1,128)S(1)}, f32[5,5,5,5,2,1,128]{6,5,4,3,2,1,0:T(1,128)}, u32[]{:S(2)}) copy-start(f32[5,5,5,5,2,1,128]{6,5,4,3,2,1,0:T(1,128)} %param.4) | copy-start | bytes 1920004
  1.1 3.1 %copy-start.4 = (f32[5,5,5,2,1]{2,4,3,1,0:T(1,128)S(1)}, f32[5,5,5,2,1]{2,4,3,1,0:T(1,128)}, u32[]{:S(2)}) copy-start(f32[5,5,5,2,1]{2,4,3,1,0:T(1,128)} %param.5) | copy-start | bytes 3004
  1.1 8.3 %collective-permute-start = (f32[104,256]{1,0:T(8,128)S(1)}, f32[104,256]{1,0:T(8,128)S(1)}, u32[]{:S(2)}, u32[]{:S(2)}) collective-permute-start(f32[104,256]{1,0:T(8,128)S(1)} %get-tuple-element.31), channel_id=1, source_target_pairs={{0,1},{1,0},{2,3},{3,2},{4,5},{5,4},{6,7},{7,6},{8,9},{9,8},{10,11... | collective-permute-start | bytes 319496 | tf_op jit(solution)/shard_map/ppermute | solution.py:522
  4.2 5.2 %collective-permute-start.1 = (f32[104,256]{1,0:T(8,128)S(1)}, f32[104,256]{1,0:T(8,128)S(1)}, u32[]{:S(2)}, u32[]{:S(2)}) collective-permute-start(f32[104,256]{1,0:T(8,128)S(1)} %get-tuple-element.32), channel_id=1, source_target_pairs={{0,4},{1,2},{2,1},{3,7},{4,0},{5,6},{6,5},{7,3},{8,12},{9,10},{10,... | collective-permute-start | bytes 319496 | tf_op jit(solution)/shard_map/ppermute | solution.py:522
  4.2 2.8 %copy-start = (bf16[2944,640]{1,0:T(8,128)(2,1)S(1)}, bf16[2944,640]{1,0:T(8,128)(2,1)}, u32[]{:S(2)}) copy-start(bf16[2944,640]{1,0:T(8,128)(2,1)} %constant.2.clone.table) | copy-start | bytes 11304964
  4.2 2.8 %copy-start.2 = (f32[5,5,5,5,2,1,128]{6,5,4,3,2,1,0:T(1,128)S(1)}, f32[5,5,5,5,2,1,128]{6,5,4,3,2,1,0:T(1,128)}, u32[]{:S(2)}) copy-start(f32[5,5,5,5,2,1,128]{6,5,4,3,2,1,0:T(1,128)} %param.4) | copy-start | bytes 1920004
  4.2 2.8 %copy-start.3 = (s32[3]{0:T(128)S(1)}, s32[3]{0:T(128)}, u32[]{:S(2)}) copy-start(s32[3]{0:T(128)} %offsets.1) | copy-start | bytes 40
  4.4 5.0 %collective-permute-start.2 = (f32[128,128]{1,0:T(8,128)S(1)}, f32[128,128]{1,0:T(8,128)S(1)}, u32[]{:S(2)}, u32[]{:S(2)}) collective-permute-start(f32[128,128]{1,0:T(8,128)S(1)} %get-tuple-element.33), channel_id=1, source_target_pairs={{0,28},{1,29},{2,30},{3,31},{4,8},{5,9},{6,10},{7,11},{8,4},{9,5},... | collective-permute-start | bytes 196616 | tf_op jit(solution)/shard_map/ppermute | solution.py:522
  7.0 2.4 %collective-permute-start.3 = (f32[128,128]{1,0:T(8,128)S(1)}, f32[128,128]{1,0:T(8,128)S(1)}, u32[]{:S(2)}, u32[]{:S(2)}) collective-permute-start(f32[128,128]{1,0:T(8,128)S(1)} %get-tuple-element.34), channel_id=1, source_target_pairs={{0,4},{1,5},{2,6},{3,7},{4,0},{5,1},{6,2},{7,3},{8,12},{9,13},{10,... | collective-permute-start | bytes 196616 | tf_op jit(solution)/shard_map/ppermute | solution.py:522
  9.9 8.6 %collective-permute-start.4 = (f32[104,256]{1,0:T(8,128)S(1)}, f32[104,256]{1,0:T(8,128)S(1)}, u32[]{:S(2)}, u32[]{:S(2)}) collective-permute-start(f32[104,256]{1,0:T(8,128)S(1)} %get-tuple-element.37), channel_id=1, source_target_pairs={{0,1},{1,0},{2,3},{3,2},{4,5},{5,4},{6,7},{7,6},{8,9},{9,8},{10,11... | collective-permute-start | bytes 319496 | tf_op jit(solution)/shard_map/ppermute | solution.py:522
  13.4 5.2 %collective-permute-start.5 = (f32[104,256]{1,0:T(8,128)S(1)}, f32[104,256]{1,0:T(8,128)S(1)}, u32[]{:S(2)}, u32[]{:S(2)}) collective-permute-start(f32[104,256]{1,0:T(8,128)S(1)} %get-tuple-element.38), channel_id=1, source_target_pairs={{0,4},{1,2},{2,1},{3,7},{4,0},{5,6},{6,5},{7,3},{8,12},{9,10},{10,... | collective-permute-start | bytes 319496 | tf_op jit(solution)/shard_map/ppermute | solution.py:522
  13.4 5.1 %collective-permute-start.6 = (f32[128,128]{1,0:T(8,128)S(1)}, f32[128,128]{1,0:T(8,128)S(1)}, u32[]{:S(2)}, u32[]{:S(2)}) collective-permute-start(f32[128,128]{1,0:T(8,128)S(1)} %get-tuple-element.39), channel_id=1, source_target_pairs={{0,28},{1,29},{2,30},{3,31},{4,8},{5,9},{6,10},{7,11},{8,4},{9,5},... | collective-permute-start | bytes 196616 | tf_op jit(solution)/shard_map/ppermute | solution.py:522
  15.1 3.4 %collective-permute-start.7 = (f32[128,128]{1,0:T(8,128)S(1)}, f32[128,128]{1,0:T(8,128)S(1)}, u32[]{:S(2)}, u32[]{:S(2)}) collective-permute-start(f32[128,128]{1,0:T(8,128)S(1)} %get-tuple-element.40), channel_id=1, source_target_pairs={{0,4},{1,5},{2,6},{3,7},{4,0},{5,1},{6,2},{7,3},{8,12},{9,13},{10,... | collective-permute-start | bytes 196616 | tf_op jit(solution)/shard_map/ppermute | solution.py:522
  19.0 5.2 %collective-permute-start.8 = (f32[104,256]{1,0:T(8,128)S(1)}, f32[104,256]{1,0:T(8,128)S(1)}, u32[]{:S(2)}, u32[]{:S(2)}) collective-permute-start(f32[104,256]{1,0:T(8,128)S(1)} %get-tuple-element.47), channel_id=1, source_target_pairs={{0,1},{1,0},{2,3},{3,2},{4,5},{5,4},{6,7},{7,6},{8,9},{9,8},{10,11... | collective-permute-start | bytes 319496 | tf_op jit(solution)/shard_map/ppermute | solution.py:522
  19.2 5.1 %collective-permute-start.9 = (f32[104,256]{1,0:T(8,128)S(1)}, f32[104,256]{1,0:T(8,128)S(1)}, u32[]{:S(2)}, u32[]{:S(2)}) collective-permute-start(f32[104,256]{1,0:T(8,128)S(1)} %get-tuple-element.48), channel_id=1, source_target_pairs={{0,4},{1,2},{2,1},{3,7},{4,0},{5,6},{6,5},{7,3},{8,12},{9,10},{10,... | collective-permute-start | bytes 319496 | tf_op jit(solution)/shard_map/ppermute | solution.py:522
  19.2 5.0 %collective-permute-start.10 = (f32[128,128]{1,0:T(8,128)S(1)}, f32[128,128]{1,0:T(8,128)S(1)}, u32[]{:S(2)}, u32[]{:S(2)}) collective-permute-start(f32[128,128]{1,0:T(8,128)S(1)} %get-tuple-element.49), channel_id=1, source_target_pairs={{0,28},{1,29},{2,30},{3,31},{4,8},{5,9},{6,10},{7,11},{8,4},{9,5},... | collective-permute-start | bytes 196616 | tf_op jit(solution)/shard_map/ppermute | solution.py:522
  20.5 3.7 %collective-permute-start.11 = (f32[128,128]{1,0:T(8,128)S(1)}, f32[128,128]{1,0:T(8,128)S(1)}, u32[]{:S(2)}, u32[]{:S(2)}) collective-permute-start(f32[128,128]{1,0:T(8,128)S(1)} %get-tuple-element.50), channel_id=1, source_target_pairs={{0,4},{1,5},{2,6},{3,7},{4,0},{5,1},{6,2},{7,3},{8,12},{9,13},{10,... | collective-permute-start | bytes 196616 | tf_op jit(solution)/shard_map/ppermute | solution.py:522

commit v8 on v7

--- a/solution.py
+++ b/solution.py
@@ -22,6 +22,7 @@
 TAIL = 5 * MAIN
 PER_VAR = 128
 ROWS = 5 * PER_VAR
+INLET_ROWS = 32
 TILES = ((0, 0, 2), (1, 2, 4), (4, 4, 5))
 BLOCK = 128
 SPAN_ROWS = 104
@@ -29,10 +30,10 @@
 HALO = 5 * BLOCK
 WAKE_ROW = 125
 FACE_PAD = 16
-TRACE_AT, LINK_AT, LIFT_AT = (0, TRACES, 2 * TRACES)
-HIGH_AT = LIFT_AT + ROWS
+HIGH_AT = TRACES
 LOW_AT = HIGH_AT + ROWS
-TABLE_ROWS = LOW_AT + ROWS
+LIFT_AT = TRACES
+INLET_AT = LIFT_AT + ROWS
 LANES = 128
 VMEM_LIMIT = 24 * 1024 * 1024
 
@@ -304,20 +305,46 @@
     return jnp.concatenate(rate, axis=0)
 
 
+def phase(run):
+    pl.when(lax.axis_index("span") >= 0)(run)
+
+
 def advance_body(section, base, state, table, partial, faces):
-    rate = volume_rate(table, *split(state[...]))
     gain, keep = GAIN[section], KEEP[section]
-    if keep == 0.0:
-        partial[...] = state[...] + rate
-    else:
-        partial[...] = keep * base[...] + gain * (state[...] + rate)
-    add_axial_terms(gain, state, partial)
+
+    @phase
+    def _():
+        rate = volume_rate(table, *split(state[...]))
+        if keep == 0.0:
+            partial[...] = state[...] + rate
+        else:
+            partial[...] = keep * base[...] + gain * (state[...] + rate)
+
+    @phase
+    def _():
+        add_axial_terms(gain, state, partial)
+
     if faces is not None:
-        faces[...] = product(table[TRACE_AT : TRACE_AT + TRACES], *split(partial[...]))
-
-
-def lift_table(table):
-    return table[LIFT_AT : LIFT_AT + ROWS]
+        faces[...] = product(table[0:TRACES], *split(partial[...]))
+
+
+def add_halo(section, before, near, far, links, state, far_high, far_low):
+    gain = GAIN[section]
+    gather_far(section, *far, far_high, far_low)
+    side = pl.multiple_of(lax.axis_index("pitch") % 2 * BLOCK, BLOCK)
+    rows = slice(LIFT_AT, LIFT_AT + ROWS)
+    near_high, near_low = near
+    state[...] = before[...] + gain * (
+        product(links[rows, : 4 * BLOCK], near_high[...], near_low[...])
+        + product(links[rows, pl.ds(side, BLOCK)], far_high[0:BLOCK], far_low[0:BLOCK])
+    )
+    added = gain * product(
+        links[INLET_AT : INLET_AT + 5 * INLET_ROWS, 0:BLOCK], far_high[BLOCK:], far_low[BLOCK:]
+    )
+    for k in range(5):
+        start, at = (k * PER_VAR, k * INLET_ROWS)
+        state[start : start + MAIN] += added[at : at + MAIN]
+        state[start + TAIL : start + PER_VAR] += added[at + MAIN : at + INLET_ROWS]
 
 
 def first_kernel(offsets, x, table, base, partial, faces, flags):
@@ -330,70 +357,171 @@
     advance_body(0, None, base, table, partial, faces)
 
 
-def later_kernel(section, base, before, halo_high, halo_low, table, partial, *refs):
-    faces, state = refs
-    lifted = product(lift_table(table), halo_high[...], halo_low[...])
-    state[...] = before[...] + GAIN[section - 1] * lifted
-    advance_body(section, base, state, table, partial, faces)
-
-
-def gather_halo(section, flags, pitch_a, pitch_b, span_a, span_b, inner, halo_high, halo_low):
-    def put(block, first, values):
-        at = (slice(block * BLOCK, (block + 1) * BLOCK), slice(first, first + values.shape[1]))
-        halo_high[at], halo_low[at] = split(half_scales()[block] * values)
-
+def later_kernel(
+    base, before, near_high, near_low, flags, pitch_b, pitch_a, table, links, partial, faces,
+    state, far_high, far_low,
+):
+    near, far = ((near_high, near_low), (flags, pitch_a, pitch_b))
+    add_halo(0, before, near, far, links, state, far_high, far_low)
+    advance_body(1, base, state, table, partial, faces)
+
+
+def put_halo(halo_high, halo_low, block, first, scale, values):
+    at = (slice(block * BLOCK, (block + 1) * BLOCK), slice(first, first + values.shape[1]))
+    halo_high[at], halo_low[at] = split(scale * values)
+
+
+def gather_near(pitch_a, span_a, span_b, inner, halo_high, halo_low):
+    put = functools.partial(put_halo, halo_high, halo_low)
+    scales = half_scales()
     pitch_odd, span_odd = parities()
-    after = jnp.where(pitch_odd, pitch_b[...], pitch_a[...])
-    before = jnp.where(pitch_odd, pitch_a[...], pitch_b[...])
-    put(0, 0, before)
-    put(0, LANES, inner[0:BLOCK])
-    put(1, 0, inner[BLOCK:])
-    put(1, LANES, after)
+    near = pitch_a[...]
+    put(0, 0, scales[0], jnp.where(pitch_odd, near, 0.0))
+    put(0, LANES, scales[0], inner[0:BLOCK])
+    put(1, 0, scales[1], inner[BLOCK:])
+    put(1, LANES, scales[1], jnp.where(pitch_odd, 0.0, near))
     above = jnp.where(span_odd, span_b[...], span_a[...])
     below = jnp.where(span_odd, span_a[...], span_b[...])
     place = lax.axis_index("span")
     above = jnp.where(place == lax.axis_size("span") - 1, 0.0, above)
     below = jnp.where(place == 0, 0.0, below)
     rest = jnp.zeros((BLOCK - SPAN_ROWS, 2 * LANES), jnp.float32)
-    put(2, 0, jnp.concatenate([below, rest], axis=0))
-    put(3, 0, jnp.concatenate([above, rest], axis=0))
-    wake = before[WAKE_ROW : WAKE_ROW + 2]
+    put(2, 0, scales[2], jnp.concatenate([below, rest], axis=0))
+    put(3, 0, scales[3], jnp.concatenate([above, rest], axis=0))
+
+
+def arrived_wake(pitch_a, pitch_b):
+    pitch_odd, _ = parities()
+    rows = slice(WAKE_ROW, WAKE_ROW + 2)
+    return jnp.where(pitch_odd, pitch_a[rows], pitch_b[rows])
+
+
+def inlet_row(section, flags, wake, e):
     moved = flags[0:1, section : section + 1] > 0.5
+    return jnp.where(moved, wake[1 - e : 2 - e], wake[e : e + 1])
+
+
+def gather_far(section, flags, pitch_a, pitch_b, halo_high, halo_low):
+    put = functools.partial(put_halo, halo_high, halo_low)
+    scales = half_scales()
+    pitch_odd, _ = parities()
+    far = jnp.where(pitch_odd, scales[1], scales[0]) * pitch_b[...]
+    put(0, 0, 1.0, jnp.where(pitch_odd, 0.0, far))
+    put(0, LANES, 1.0, jnp.where(pitch_odd, far, 0.0))
+    wake = arrived_wake(pitch_a, pitch_b)
     rows = lax.broadcasted_iota(jnp.int32, (BLOCK, LANES), 0)
     cols = lax.broadcasted_iota(jnp.int32, (BLOCK, LANES), 1)
     for e in range(2):
-        row = jnp.where(moved, wake[1 - e : 2 - e], wake[e : e + 1])
+        row = inlet_row(section, flags, wake, e)
         column = jnp.sum(jnp.where(rows == cols, row, 0.0), axis=1, keepdims=True)
-        put(4, e * LANES, jnp.where(cols == 0, column, 0.0))
-    return wake
-
-
-def next_traces(section, side, faces, table, high, low):
-    at = LINK_AT + side * 2 * BLOCK
-    rows = slice(side * 2 * BLOCK, (side + 1) * 2 * BLOCK)
-    return faces[rows] + GAIN[section] * dot(table[at : at + 2 * BLOCK], high)
-
-
-def exchange_kernel(
-    section, flags, span_a, span_b, pitch_b, pitch_a, inner, faces, table,
-    next_pitch_a, next_pitch_b, next_inner, next_span_a, next_span_b, halo_high, halo_low,
+        put(1, e * LANES, scales[4], jnp.where(cols == 0, column, 0.0))
+
+
+def near_kernel(
+    section, span_a, span_b, pitch_a, inner, faces, links, near_faces, halo_high, halo_low
 ):
-    wake = gather_halo(
-        section, flags, pitch_a, pitch_b, span_a, span_b, inner, halo_high, halo_low
-    )
+    gather_near(pitch_a, span_a, span_b, inner, halo_high, halo_low)
+    for half in range(2):
+        at = slice(half * 2 * BLOCK, (half + 1) * 2 * BLOCK)
+        near_faces[at] = faces[at] + GAIN[section] * dot(
+            links[at, : 4 * BLOCK], halo_high[...]
+        )
+
+
+def from_lanes(row, moves):
+    lanes = lax.broadcasted_iota(jnp.int32, row.shape, 1)
+    total = None
+    for factor, start, stop, distance in moves:
+        moved = pltpu.roll(row, distance % LANES, 1) if distance else row
+        term = jnp.where((lanes >= start) & (lanes < stop), factor * moved, 0.0)
+        total = term if total is None else total + term
+    return total
+
+
+def lane_moves(table):
+    return [
+        (float(table[i, j]), 25 * i, 25 * i + 25, 25 * (i - j))
+        for i in range(table.shape[0])
+        for j in range(table.shape[1])
+        if table[i, j] != 0.0
+    ]
+
+
+def far_kernel(
+    section, flags, pitch_b, pitch_a, near_faces,
+    next_pitch_a, next_pitch_b, next_inner, next_span_a, next_span_b, *refs
+):
+    *traces, faces, lifted = refs
     pitch_odd, span_odd = parities()
-    traces = faces[...] + GAIN[section] * dot(
-        table[LINK_AT : LINK_AT + TRACES], halo_high[...]
-    )
-    emit_span_faces(traces[2 * BLOCK :], span_odd, next_span_a, next_span_b)
+    gain = GAIN[section]
+    for e in range(2):
+        traces[e][...] = near_faces[:, e * LANES : (e + 1) * LANES]
+
+    def add(start, count, stride, e, values):
+        at = pl.ds(start, count, stride=stride) if stride > 1 else pl.ds(start, count)
+        traces[e][at, :] = traces[e][at, :] + values
+
+    faces[FACE_PAD : FACE_PAD + BLOCK] = pitch_b[...]
+    plus, minus = (half_flux(1, 1.0), half_flux(1, -1.0))
+    scale = gain * lift_factor(1)
+    assert np.allclose(plus - np.diag(np.diag(plus)), minus - np.diag(np.diag(minus)))
+    factor = lambda i, j: jnp.where(
+        pitch_odd, -scale * float(minus[i, j]), scale * float(plus[i, j])
+    )
+    rows = lax.broadcasted_iota(jnp.int32, (BLOCK, LANES), 0)
+    place = rows - 25 * sum((rows >= 25 * s).astype(jnp.int32) for s in range(1, 5))
+    total = factor(0, 0) * pitch_b[...]
+    for i in range(5):
+        for j in range(5):
+            if i != j and plus[i, j] != 0.0:
+                at = FACE_PAD + 5 * (j - i)
+                here = (place >= 5 * i) & (place < 5 * i + 5)
+                total = total + jnp.where(here, factor(i, j) * faces[at : at + BLOCK], 0.0)
+    total = jnp.where(rows < WAKE_ROW, total, 0.0)
+    lifted[...] = total
+    add(0, BLOCK, 1, 1, jnp.where(pitch_odd, total, 0.0))
+    add(BLOCK, BLOCK, 1, 0, jnp.where(pitch_odd, 0.0, total))
+    for block, s, sign in ((2, 4, 1.0), (3, 0, -1.0)):
+        edge = [lifted[s * 25 + 5 * v : s * 25 + 5 * v + 5] for v in range(5)]
+        for c, values in enumerate(combine(half_flux(2, sign)[:4], edge)):
+            start = block * BLOCK + c * 25
+            add(start + 4, 5, 5, 1, jnp.where(pitch_odd, values, 0.0))
+            add(start, 5, 5, 0, jnp.where(pitch_odd, 0.0, values))
+
+    wake = arrived_wake(pitch_a, pitch_b)
+    rows = lax.broadcasted_iota(jnp.int32, (5, LANES), 0)
+    cols = lax.broadcasted_iota(jnp.int32, (5, LANES), 1)
+    for e in range(2):
+
+        def add_column(start, stride, row, first, step):
+            picked = jnp.where(cols == first + step * rows, row, 0.0)
+            column = jnp.sum(picked, axis=1, keepdims=True)
+            add(start, 5, stride, e, jnp.where(cols == 0, column, 0.0))
+
+        row = jnp.broadcast_to(inlet_row(section, flags, wake, e), (8, LANES))
+        row = from_lanes(row, lane_moves(gain * lift_factor(0) * half_flux(0, 1.0)))
+        for block, p in ((0, 4), (1, 0)):
+            for s in range(5):
+                add_column(block * BLOCK + s * 25, 5, row[0:1], p * 5 + s, 25)
+        for block, s, sign in ((2, 4, 1.0), (3, 0, -1.0)):
+            sent = from_lanes(row, lane_moves(half_flux(2, sign)[:4]))
+            for c in range(4):
+                add_column(block * BLOCK + c * 25, 1, sent[0:1], c * 25 + s, 5)
+
+    both = jnp.concatenate([traces[0][...], traces[1][...]], axis=1)
+    emit_span_faces(both[2 * BLOCK :], span_odd, next_span_a, next_span_b)
     emit_pitch_faces(
-        traces, [wake[0:1], wake[1:2]], pitch_odd, next_pitch_a, next_pitch_b, next_inner
-    )
-
-
-def last_kernel(base, before, halo_high, halo_low, table, rows, state, partial):
-    lifted = product(lift_table(table), halo_high[...], halo_low[...])
-    state[...] = before[...] + GAIN[1] * lifted
+        both[: 2 * BLOCK], [wake[0:1], wake[1:2]], pitch_odd, next_pitch_a, next_pitch_b,
+        next_inner,
+    )
+
+
+def last_kernel(
+    base, before, near_high, near_low, flags, pitch_b, pitch_a, table, links, rows,
+    state, far_high, far_low, partial,
+):
+    near, far = ((near_high, near_low), (flags, pitch_a, pitch_b))
+    add_halo(1, before, near, far, links, state, far_high, far_low)
     advance_body(2, base, state, table, partial, None)
     flat = rows.reshape(rows.shape[0], LANES)
     for e in range(2):
@@ -534,12 +662,13 @@
 PITCH_OUTS = [((BLOCK, LANES), F32), ((BLOCK, LANES), F32), ((2 * BLOCK, LANES), F32)]
 SPAN_OUTS = [((SPAN_ROWS, 2 * LANES), F32)] * 2
 SMALL_OUT = ((8, LANES), F32)
-HALO_OUTS = [((HALO, 2 * LANES), jnp.bfloat16)] * 2
+NEAR_OUTS = [((4 * BLOCK, 2 * LANES), jnp.bfloat16)] * 2
+FAR_OUTS = [((2 * BLOCK, 2 * LANES), jnp.bfloat16)] * 2
 STATE_OUT = ((ROWS, 2 * LANES), F32)
 TRACE_OUT = ((TRACES, 2 * LANES), F32)
 
 
-def shards(table, state, wake_planes, bar_offsets):
+def shards(table, links, state, wake_planes, bar_offsets):
     x = state.reshape(-1, 1, LANES)
     wake = wake_planes.transpose(0, 1, 3, 4, 2).reshape(50, 1, 5)
     faces = call(begin_span_kernel, "begin_span", SPAN_OUTS, [x], flops=10**10)
@@ -554,31 +683,45 @@
         in_specs=[IN_SMEM],
         flops=10**9,
     )
+    buffers = [pltpu.VMEM(shape, dtype) for shape, dtype in [STATE_OUT] + FAR_OUTS]
     for section in range(2):
-        next_a, next_b, inner, *faces, high, low = call(
-            functools.partial(exchange_kernel, section),
-            "exchange",
-            PITCH_OUTS + SPAN_OUTS + HALO_OUTS,
-            [flags, span[0], span[1], pitch[0], pitch[1], inner, traces, table],
+        odd, even = pitch
+        near_faces, *near = call(
+            functools.partial(near_kernel, section),
+            "near",
+            [TRACE_OUT] + NEAR_OUTS,
+            [*span, even, inner, traces, links],
+            flops=10**8,
+        )
+        next_a, next_b, inner, *faces = call(
+            functools.partial(far_kernel, section),
+            "far",
+            PITCH_OUTS + SPAN_OUTS,
+            [flags, odd, even, near_faces],
+            scratch=[
+                pltpu.VMEM(shape, F32)
+                for shape in (
+                    (TRACES, LANES),
+                    (TRACES, LANES),
+                    (BLOCK + 2 * FACE_PAD, LANES),
+                    (BLOCK, LANES),
+                )
+            ],
             flops=10**8,
         )
         span = span_exchanged(faces)
         pitch = pitch_exchanged([next_a, next_b])
+        args = [base, partial, *near, flags, odd, even, table, links]
         if section == 0:
             partial, traces = call(
-                functools.partial(later_kernel, section + 1),
-                "later",
-                [STATE_OUT, TRACE_OUT],
-                [base, partial, high, low, table],
-                scratch=[pltpu.VMEM((ROWS, 2 * LANES), F32)],
-                flops=10**9,
+                later_kernel, "later", [STATE_OUT, TRACE_OUT], args, scratch=buffers, flops=10**9
             )
     (rows,) = call(
         last_kernel,
         "last",
         [(x.shape, F32)],
-        [base, partial, high, low, table],
-        scratch=[pltpu.VMEM((ROWS, 2 * LANES), F32)] * 2,
+        args,
+        scratch=buffers + buffers[:1],
         flops=10**9,
     )
     (out,) = call(
@@ -600,8 +743,15 @@
 def solution(mesh):
     volume, lift, trace, link = operator_tables()
     high, low = split_table(volume)
-    table = np.concatenate([exact_table(t) for t in (trace, link, lift)] + [high, low])
-    assert table.shape == (TABLE_ROWS, ROWS)
+    table = np.concatenate([exact_table(trace), high, low])
+    reached = [
+        v * PER_VAR + r for v in range(5) for r in (*range(MAIN), *range(TAIL, PER_VAR))
+    ]
+    inlet = np.zeros((5 * INLET_ROWS, HALO))
+    inlet[:, :BLOCK] = lift[reached, 4 * BLOCK :]
+    lift[reached, 4 * BLOCK :] = 0.0
+    assert not lift[:, 4 * BLOCK :].any()
+    links = np.concatenate([exact_table(t) for t in (link, lift, inlet)])
     in_specs = (
         P(None, None, None, None, "pitch", "span", None),
         P(None, None, None, "pitch", "span"),
@@ -609,7 +759,7 @@
     )
     out_specs = P(None, None, None, None, "pitch", "span", None)
     return jax.shard_map(
-        functools.partial(shards, jnp.asarray(table)),
+        functools.partial(shards, jnp.asarray(table), jnp.asarray(links)),
         mesh=mesh,
         in_specs=in_specs,
         out_specs=out_specs,

time: 25.6 us -> 25.3 us (0.988)
  Pallas kernels: 9.53 us -> 8.23 us
  waiting for transfers between devices: 2.33 us -> 3.38 us
    pallas_call x8 -> x10, Pallas kernels: 9.53 us -> 8.23 us  [call(): pl.pallas_call(kernel, name=name, out_shape=[jax.ShapeDtypeStruct(shape,...]
    ppermute x12, waiting for transfers between devices: 2.33 us -> 3.38 us  [swapped(): return lax.ppermute(value, ('pitch', 'span'), pairs)]
    unnamed x10 -> x12, local copies, waits for them, and re-layouts: 1.1 us -> 1.11 us
  transfers between devices with their start and end apart: 12 -> 12, of which waited for: 2 -> 2; matrix products, arithmetic and copies ran while one was open for 0% -> 0% of each run, Pallas kernels for 29% -> 25%
where the time goes in v8:
time: 25.3 us; the launch traced here: 25.1 us
  starting transfers between devices  12.2 us (48%)
  Pallas kernels  8.23 us (33%)
  waiting for transfers between devices  3.38 us (13%)
  local copies, waits for them, and re-layouts  1.11 us (4%)
    ppermute x12, starting transfers between devices, swapped(): return lax.ppermute(value, ('pitch', 'span'), pairs)  12.2 us
    pallas_call x10, Pallas kernels, call(): pl.pallas_call(kernel, name=name, out_shape=[jax.ShapeDtypeStruct(shape,...  8.23 us
    ppermute x12, waiting for transfers between devices, swapped(): return lax.ppermute(value, ('pitch', 'span'), pairs)  3.38 us
    unnamed x12, local copies, waits for them, and re-layouts  1.11 us
  transfers between devices with their start and end apart: 12, of which 2 were waited for; matrix products, arithmetic and copies ran while one was open for 0% of the time, Pallas kernels for 25%

profile of v8, /device:TPU:0, one launch (start us, length us, event | category | flops | bytes accessed | tf_op | source)
XLA Modules:
  0.0 25.1 jit_solution(8963136367701992344)
XLA Ops:
  0.0 0.0 copy-start.2
  0.0 1.1 %copy-done.2 = f32[5,5,5,5,2,1,128]{6,5,4,3,2,1,0:T(1,128)S(1)} copy-done((f32[5,5,5,5,2,1,128]{6,5,4,3,2,1,0:T(1,128)S(1)}, f32[5,5,5,5,2,1,128]{6,5,4,3,2,1,0:T(1,128)}, u32[]{:S(2)}) %copy-start.2) | copy-done | bytes 640024
  1.1 0.0 copy-start.4
  1.1 3.1 %collective-permute-start.2 = (f32[104,256]{1,0:T(8,128)S(1)}, f32[104,256]{1,0:T(8,128)S(1)}, u32[]{:S(2)}, u32[]{:S(2)}) collective-permute-start(f32[104,256]{1,0:T(8,128)S(1)} %get-tuple-element.35), channel_id=1, source_target_pairs={{0,1},{1,0},{2,3},{3,2},{4,5},{5,4},{6,7},{7,6},{8,9},{9,8},{10,11... | collective-permute-start | bytes 319496 | tf_op jit(solution)/shard_map/ppermute | solution.py:650
  4.2 0.0 collective-permute-start.3
  4.2 0.0 copy-done.4
  4.2 0.0 copy-start.1
  4.2 0.0 copy-start.3
  4.2 0.0 copy-start.5
  4.3 0.1 begin_pitch.1
  4.4 0.0 copy-start
  4.4 2.6 %collective-permute-start = (f32[128,128]{1,0:T(8,128)S(1)}, f32[128,128]{1,0:T(8,128)S(1)}, u32[]{:S(2)}, u32[]{:S(2)}) collective-permute-start(f32[128,128]{1,0:T(8,128)S(1)} %get-tuple-element.33), channel_id=1, source_target_pairs={{0,28},{1,29},{2,30},{3,31},{4,8},{5,9},{6,10},{7,11},{8,4},{9,5},... | collective-permute-start | bytes 196616 | tf_op jit(solution)/shard_map/ppermute | solution.py:650
  7.0 0.0 collective-permute-start.1
  7.0 0.0 copy-done.1
  7.0 0.0 copy-done.3
  7.0 0.0 copy-done.5
  7.0 1.9 %first.1 = (f32[640,256]{1,0:T(8,128)S(1)}, f32[640,256]{1,0:T(8,128)S(1)}, f32[512,256]{1,0:T(8,128)S(1)}, f32[8,128]{1,0:T(8,128)S(1)}) custom-call(s32[3]{0:T(128)S(1)} %copy-done.5, f32[1250,1,128]{2,1,0:T(1,128)S(1)} %bitcast.9, bf16[1792,640]{1,0:T(8,128)(2,1)S(1)} %copy-done.1), custom_call_target="tpu_custom_call" | custom-call | flops 1000000000 | bytes 1048576 | tf_op jit(solution)/shard_map/first/pallas_call | solution.py:626
  8.9 0.0 collective-permute-done.1.pitch_a
  8.9 0.0 collective-permute-done.2.span_a
  8.9 0.0 collective-permute-done.3.span_b
  9.0 0.0 copy-done
  9.0 0.3 %near.2 = (f32[512,256]{1,0:T(8,128)S(1)}, bf16[512,256]{1,0:T(8,128)(2,1)S(1)}, bf16[512,256]{1,0:T(8,128)(2,1)S(1)}) custom-call(f32[104,256]{1,0:T(8,128)S(1)} %collective-permute-done.2.span_a, f32[104,256]{1,0:T(8,128)S(1)} %collective-permute-done.3.span_b, f32[128,128]{1,0:T(8,128)S(1)} %collective-permute-done.1.pitch_a, ...), custom_call_target="tpu_custom_call" | custom-call | flops 100000000 | bytes 1048576 | tf_op jit(solution)/shard_map/near/pallas_call | solution.py:626
  9.3 0.0 collective-permute-done.pitch_b
  9.3 0.3 %far.2 = (f32[128,128]{1,0:T(8,128)S(1)}, f32[128,128]{1,0:T(8,128)S(1)}, f32[256,128]{1,0:T(8,128)S(1)}, f32[104,256]{1,0:T(8,128)S(1)}, f32[104,256]{1,0:T(8,128)S(1)}) custom-call(f32[8,128]{1,0:T(8,128)S(1)} %get-tuple-element.32.flags, f32[128,128]{1,0:T(8,128)S(1)} %collective-permute-done.pitch_b, f32[128,128]{1,0:T(8,128)S(1)} %collective-permute-done.1.pitch_a, ...), custom_call_target="tpu_custom_call" | custom-call | flops 100000000 | bytes 1048576 | tf_op jit(solution)/shard_map/far/pallas_call | solution.py:626
  9.7 3.5 %collective-permute-start.6 = (f32[104,256]{1,0:T(8,128)S(1)}, f32[104,256]{1,0:T(8,128)S(1)}, u32[]{:S(2)}, u32[]{:S(2)}) collective-permute-start(f32[104,256]{1,0:T(8,128)S(1)} %get-tuple-element.42), channel_id=1, source_target_pairs={{0,1},{1,0},{2,3},{3,2},{4,5},{5,4},{6,7},{7,6},{8,9},{9,8},{10,11... | collective-permute-start | bytes 319496 | tf_op jit(solution)/shard_map/ppermute | solution.py:650
  13.2 0.0 collective-permute-start.7
  13.2 1.2 %collective-permute-start.4 = (f32[128,128]{1,0:T(8,128)S(1)}, f32[128,128]{1,0:T(8,128)S(1)}, u32[]{:S(2)}, u32[]{:S(2)}) collective-permute-start(f32[128,128]{1,0:T(8,128)S(1)} %get-tuple-element.40), channel_id=1, source_target_pairs={{0,28},{1,29},{2,30},{3,31},{4,8},{5,9},{6,10},{7,11},{8,4},{9,5},... | collective-permute-start | bytes 196616 | tf_op jit(solution)/shard_map/ppermute | solution.py:650
  14.4 0.0 collective-permute-start.5
  14.4 2.0 %later.1 = (f32[640,256]{1,0:T(8,128)S(1)}, f32[512,256]{1,0:T(8,128)S(1)}) custom-call(f32[640,256]{1,0:T(8,128)S(1)} %get-tuple-element.45.base, f32[640,256]{1,0:T(8,128)S(1)} %get-tuple-element.46.before, bf16[512,256]{1,0:T(8,128)(2,1)S(1)} %get-tuple-element.47.near_high, bf16[512,256]{1,0:T(8,128)(2,1)S(1)} %get-tuple-element.48.near_low, ...), custom_call_target="tpu_custom_call" | custom-call | flops 1000000000 | bytes 1048576 | tf_op jit(solution)/shard_map/later/pallas_call | solution.py:626
  16.5 0.0 collective-permute-done.5.pitch_a
  16.5 0.0 collective-permute-done.6.span_a
  16.5 0.0 collective-permute-done.7.span_b
  16.5 0.3 %near.3 = (f32[512,256]{1,0:T(8,128)S(1)}, bf16[512,256]{1,0:T(8,128)(2,1)S(1)}, bf16[512,256]{1,0:T(8,128)(2,1)S(1)}) custom-call(f32[104,256]{1,0:T(8,128)S(1)} %collective-permute-done.6.span_a, f32[104,256]{1,0:T(8,128)S(1)} %collective-permute-done.7.span_b, f32[128,128]{1,0:T(8,128)S(1)} %collective-permute-done.5.pitch_a, ...), custom_call_target="tpu_custom_call" | custom-call | flops 100000000 | bytes 1048576 | tf_op jit(solution)/shard_map/near/pallas_call | solution.py:626
  16.9 1.5 %collective-permute-done.4.pitch_b = f32[128,128]{1,0:T(8,128)S(1)} collective-permute-done((f32[128,128]{1,0:T(8,128)S(1)}, f32[128,128]{1,0:T(8,128)S(1)}, u32[]{:S(2)}, u32[]{:S(2)}) %collective-permute-start.4) | collective-permute-done | bytes 65568 | tf_op jit(solution)/shard_map/ppermute | solution.py:650
  18.3 0.3 %far.3 = (f32[128,128]{1,0:T(8,128)S(1)}, f32[128,128]{1,0:T(8,128)S(1)}, f32[256,128]{1,0:T(8,128)S(1)}, f32[104,256]{1,0:T(8,128)S(1)}, f32[104,256]{1,0:T(8,128)S(1)}) custom-call(f32[8,128]{1,0:T(8,128)S(1)} %get-tuple-element.32.flags, f32[128,128]{1,0:T(8,128)S(1)} %collective-permute-done.4.pitch_b, f32[128,128]{1,0:T(8,128)S(1)} %collective-permute-done.5.pitch_a, ...), custom_call_target="tpu_custom_call" | custom-call | flops 100000000 | bytes 1048576 | tf_op jit(solution)/shard_map/far/pallas_call | solution.py:626
  18.7 0.1 collective-permute-start.8
  18.8 0.1 collective-permute-start.9
  18.8 1.6 %collective-permute-start.10 = (f32[128,128]{1,0:T(8,128)S(1)}, f32[128,128]{1,0:T(8,128)S(1)}, u32[]{:S(2)}, u32[]{:S(2)}) collective-permute-start(f32[128,128]{1,0:T(8,128)S(1)} %get-tuple-element.53), channel_id=1, source_target_pairs={{0,28},{1,29},{2,30},{3,31},{4,8},{5,9},{6,10},{7,11},{8,4},{9,5},... | collective-permute-start | bytes 196616 | tf_op jit(solution)/shard_map/ppermute | solution.py:650
  20.5 0.0 collective-permute-start.11
  20.5 1.5 %last.1.before = f32[1250,1,128]{2,1,0:T(1,128)S(1)} custom-call(f32[640,256]{1,0:T(8,128)S(1)} %get-tuple-element.45.base, f32[640,256]{1,0:T(8,128)S(1)} %get-tuple-element.56.before, bf16[512,256]{1,0:T(8,128)(2,1)S(1)} %get-tuple-element.57.near_high, bf16[512,256]{1,0:T(8,128)(2,1)S(1)} %get-tuple-element.58.near_low, ...), custom_call_target="tpu_custom_call" | custom-call | flops 1000000000 | bytes 1048576 | tf_op jit(solution)/shard_map/last/pallas_call | solution.py:626
  22.0 1.9 %collective-permute-done.10.pitch_b = f32[128,128]{1,0:T(8,128)S(1)} collective-permute-done((f32[128,128]{1,0:T(8,128)S(1)}, f32[128,128]{1,0:T(8,128)S(1)}, u32[]{:S(2)}, u32[]{:S(2)}) %collective-permute-start.10) | collective-permute-done | bytes 65568 | tf_op jit(solution)/shard_map/ppermute | solution.py:650
  23.9 0.0 collective-permute-done.11.pitch_a
  23.9 0.0 collective-permute-done.8.span_a
  23.9 0.0 collective-permute-done.9.span_b
  23.9 1.2 %final.1 = f32[1250,1,128]{2,1,0:T(1,128)} custom-call(f32[8,128]{1,0:T(8,128)S(1)} %get-tuple-element.32.flags, f32[104,256]{1,0:T(8,128)S(1)} %collective-permute-done.8.span_a, f32[104,256]{1,0:T(8,128)S(1)} %collective-permute-done.9.span_b, f32[128,128]{1,0:T(8,128)S(1)} %collective-permute-done.10.pitch_b, ...), custom_call_target="tpu_custom_call" | custom-call | flops 100000000 | bytes 1048576 | tf_op jit(solution)/shard_map/final/pallas_call | solution.py:626
  (1 shorter events, 0.0 us)
Async XLA Ops:
  0.0 1.1 %copy-start.2 = (f32[5,5,5,5,2,1,128]{6,5,4,3,2,1,0:T(1,128)S(1)}, f32[5,5,5,5,2,1,128]{6,5,4,3,2,1,0:T(1,128)}, u32[]{:S(2)}) copy-start(f32[5,5,5,5,2,1,128]{6,5,4,3,2,1,0:T(1,128)} %param.5) | copy-start | bytes 1920004
  1.1 3.1 %copy-start.4 = (f32[5,5,5,2,1]{2,4,3,1,0:T(1,128)S(1)}, f32[5,5,5,2,1]{2,4,3,1,0:T(1,128)}, u32[]{:S(2)}) copy-start(f32[5,5,5,2,1]{2,4,3,1,0:T(1,128)} %param.6) | copy-start | bytes 3004
  1.1 7.8 %collective-permute-start.2 = (f32[104,256]{1,0:T(8,128)S(1)}, f32[104,256]{1,0:T(8,128)S(1)}, u32[]{:S(2)}, u32[]{:S(2)}) collective-permute-start(f32[104,256]{1,0:T(8,128)S(1)} %get-tuple-element.35), channel_id=1, source_target_pairs={{0,1},{1,0},{2,3},{3,2},{4,5},{5,4},{6,7},{7,6},{8,9},{9,8},{10,11... | collective-permute-start | bytes 319496 | tf_op jit(solution)/shard_map/ppermute | solution.py:650
  4.2 4.7 %collective-permute-start.3 = (f32[104,256]{1,0:T(8,128)S(1)}, f32[104,256]{1,0:T(8,128)S(1)}, u32[]{:S(2)}, u32[]{:S(2)}) collective-permute-start(f32[104,256]{1,0:T(8,128)S(1)} %get-tuple-element.36), channel_id=1, source_target_pairs={{0,4},{1,2},{2,1},{3,7},{4,0},{5,6},{6,5},{7,3},{8,12},{9,10},{10,... | collective-permute-start | bytes 319496 | tf_op jit(solution)/shard_map/ppermute | solution.py:650
  4.2 2.8 %copy-start.1 = (bf16[1792,640]{1,0:T(8,128)(2,1)S(1)}, bf16[1792,640]{1,0:T(8,128)(2,1)}, u32[]{:S(2)}) copy-start(bf16[1792,640]{1,0:T(8,128)(2,1)} %constant.4.clone.table) | copy-start | bytes 6881284
  4.2 2.8 %copy-start.3 = (f32[5,5,5,5,2,1,128]{6,5,4,3,2,1,0:T(1,128)S(1)}, f32[5,5,5,5,2,1,128]{6,5,4,3,2,1,0:T(1,128)}, u32[]{:S(2)}) copy-start(f32[5,5,5,5,2,1,128]{6,5,4,3,2,1,0:T(1,128)} %param.5) | copy-start | bytes 1920004
  4.2 2.8 %copy-start.5 = (s32[3]{0:T(128)S(1)}, s32[3]{0:T(128)}, u32[]{:S(2)}) copy-start(s32[3]{0:T(128)} %offsets.1) | copy-start | bytes 40
  4.4 4.6 %copy-start = (bf16[1312,640]{1,0:T(8,128)(2,1)S(1)}, bf16[1312,640]{1,0:T(8,128)(2,1)}, u32[]{:S(2)}) copy-start(bf16[1312,640]{1,0:T(8,128)(2,1)} %constant.5.clone.links) | copy-start | bytes 5038084
  4.4 4.9 %collective-permute-start = (f32[128,128]{1,0:T(8,128)S(1)}, f32[128,128]{1,0:T(8,128)S(1)}, u32[]{:S(2)}, u32[]{:S(2)}) collective-permute-start(f32[128,128]{1,0:T(8,128)S(1)} %get-tuple-element.33), channel_id=1, source_target_pairs={{0,28},{1,29},{2,30},{3,31},{4,8},{5,9},{6,10},{7,11},{8,4},{9,5},... | collective-permute-start | bytes 196616 | tf_op jit(solution)/shard_map/ppermute | solution.py:650
  7.0 1.9 %collective-permute-start.1 = (f32[128,128]{1,0:T(8,128)S(1)}, f32[128,128]{1,0:T(8,128)S(1)}, u32[]{:S(2)}, u32[]{:S(2)}) collective-permute-start(f32[128,128]{1,0:T(8,128)S(1)} %get-tuple-element.34), channel_id=1, source_target_pairs={{0,4},{1,5},{2,6},{3,7},{4,0},{5,1},{6,2},{7,3},{8,12},{9,13},{10,... | collective-permute-start | bytes 196616 | tf_op jit(solution)/shard_map/ppermute | solution.py:650
  9.7 6.8 %collective-permute-start.6 = (f32[104,256]{1,0:T(8,128)S(1)}, f32[104,256]{1,0:T(8,128)S(1)}, u32[]{:S(2)}, u32[]{:S(2)}) collective-permute-start(f32[104,256]{1,0:T(8,128)S(1)} %get-tuple-element.42), channel_id=1, source_target_pairs={{0,1},{1,0},{2,3},{3,2},{4,5},{5,4},{6,7},{7,6},{8,9},{9,8},{10,11... | collective-permute-start | bytes 319496 | tf_op jit(solution)/shard_map/ppermute | solution.py:650
  13.2 3.3 %collective-permute-start.7 = (f32[104,256]{1,0:T(8,128)S(1)}, f32[104,256]{1,0:T(8,128)S(1)}, u32[]{:S(2)}, u32[]{:S(2)}) collective-permute-start(f32[104,256]{1,0:T(8,128)S(1)} %get-tuple-element.43), channel_id=1, source_target_pairs={{0,4},{1,2},{2,1},{3,7},{4,0},{5,6},{6,5},{7,3},{8,12},{9,10},{10,... | collective-permute-start | bytes 319496 | tf_op jit(solution)/shard_map/ppermute | solution.py:650
  13.2 5.1 %collective-permute-start.4 = (f32[128,128]{1,0:T(8,128)S(1)}, f32[128,128]{1,0:T(8,128)S(1)}, u32[]{:S(2)}, u32[]{:S(2)}) collective-permute-start(f32[128,128]{1,0:T(8,128)S(1)} %get-tuple-element.40), channel_id=1, source_target_pairs={{0,28},{1,29},{2,30},{3,31},{4,8},{5,9},{6,10},{7,11},{8,4},{9,5},... | collective-permute-start | bytes 196616 | tf_op jit(solution)/shard_map/ppermute | solution.py:650
  14.4 2.1 %collective-permute-start.5 = (f32[128,128]{1,0:T(8,128)S(1)}, f32[128,128]{1,0:T(8,128)S(1)}, u32[]{:S(2)}, u32[]{:S(2)}) collective-permute-start(f32[128,128]{1,0:T(8,128)S(1)} %get-tuple-element.41), channel_id=1, source_target_pairs={{0,4},{1,5},{2,6},{3,7},{4,0},{5,1},{6,2},{7,3},{8,12},{9,13},{10,... | collective-permute-start | bytes 196616 | tf_op jit(solution)/shard_map/ppermute | solution.py:650
  18.7 5.2 %collective-permute-start.8 = (f32[104,256]{1,0:T(8,128)S(1)}, f32[104,256]{1,0:T(8,128)S(1)}, u32[]{:S(2)}, u32[]{:S(2)}) collective-permute-start(f32[104,256]{1,0:T(8,128)S(1)} %get-tuple-element.51), channel_id=1, source_target_pairs={{0,1},{1,0},{2,3},{3,2},{4,5},{5,4},{6,7},{7,6},{8,9},{9,8},{10,11... | collective-permute-start | bytes 319496 | tf_op jit(solution)/shard_map/ppermute | solution.py:650
  18.8 5.1 %collective-permute-start.9 = (f32[104,256]{1,0:T(8,128)S(1)}, f32[104,256]{1,0:T(8,128)S(1)}, u32[]{:S(2)}, u32[]{:S(2)}) collective-permute-start(f32[104,256]{1,0:T(8,128)S(1)} %get-tuple-element.52), channel_id=1, source_target_pairs={{0,4},{1,2},{2,1},{3,7},{4,0},{5,6},{6,5},{7,3},{8,12},{9,10},{10,... | collective-permute-start | bytes 319496 | tf_op jit(solution)/shard_map/ppermute | solution.py:650
  18.8 5.0 %collective-permute-start.10 = (f32[128,128]{1,0:T(8,128)S(1)}, f32[128,128]{1,0:T(8,128)S(1)}, u32[]{:S(2)}, u32[]{:S(2)}) collective-permute-start(f32[128,128]{1,0:T(8,128)S(1)} %get-tuple-element.53), channel_id=1, source_target_pairs={{0,28},{1,29},{2,30},{3,31},{4,8},{5,9},{6,10},{7,11},{8,4},{9,5},... | collective-permute-start | bytes 196616 | tf_op jit(solution)/shard_map/ppermute | solution.py:650
  20.5 3.4 %collective-permute-start.11 = (f32[128,128]{1,0:T(8,128)S(1)}, f32[128,128]{1,0:T(8,128)S(1)}, u32[]{:S(2)}, u32[]{:S(2)}) collective-permute-start(f32[128,128]{1,0:T(8,128)S(1)} %get-tuple-element.54), channel_id=1, source_target_pairs={{0,4},{1,5},{2,6},{3,7},{4,0},{5,1},{6,2},{7,3},{8,12},{9,13},{10,... | collective-permute-start | bytes 196616 | tf_op jit(solution)/shard_map/ppermute | solution.py:650

commit v9 on v8

--- a/solution.py
+++ b/solution.py
@@ -447,20 +447,8 @@
     ]
 
 
-def far_kernel(
-    section, flags, pitch_b, pitch_a, near_faces,
-    next_pitch_a, next_pitch_b, next_inner, next_span_a, next_span_b, *refs
-):
-    *traces, faces, lifted = refs
-    pitch_odd, span_odd = parities()
-    gain = GAIN[section]
-    for e in range(2):
-        traces[e][...] = near_faces[:, e * LANES : (e + 1) * LANES]
-
-    def add(start, count, stride, e, values):
-        at = pl.ds(start, count, stride=stride) if stride > 1 else pl.ds(start, count)
-        traces[e][at, :] = traces[e][at, :] + values
-
+def far_lift(gain, pitch_b, faces):
+    pitch_odd, _ = parities()
     faces[FACE_PAD : FACE_PAD + BLOCK] = pitch_b[...]
     plus, minus = (half_flux(1, 1.0), half_flux(1, -1.0))
     scale = gain * lift_factor(1)
@@ -477,7 +465,24 @@
                 at = FACE_PAD + 5 * (j - i)
                 here = (place >= 5 * i) & (place < 5 * i + 5)
                 total = total + jnp.where(here, factor(i, j) * faces[at : at + BLOCK], 0.0)
-    total = jnp.where(rows < WAKE_ROW, total, 0.0)
+    return jnp.where(rows < WAKE_ROW, total, 0.0)
+
+
+def far_kernel(
+    section, flags, pitch_b, pitch_a, near_faces,
+    next_pitch_a, next_pitch_b, next_inner, next_span_a, next_span_b, *refs
+):
+    *traces, faces, lifted = refs
+    pitch_odd, span_odd = parities()
+    gain = GAIN[section]
+    for e in range(2):
+        traces[e][...] = near_faces[:, e * LANES : (e + 1) * LANES]
+
+    def add(start, count, stride, e, values):
+        at = pl.ds(start, count, stride=stride) if stride > 1 else pl.ds(start, count)
+        traces[e][at, :] = traces[e][at, :] + values
+
+    total = far_lift(gain, pitch_b, faces)
     lifted[...] = total
     add(0, BLOCK, 1, 1, jnp.where(pitch_odd, total, 0.0))
     add(BLOCK, BLOCK, 1, 0, jnp.where(pitch_odd, 0.0, total))
@@ -551,9 +556,8 @@
     return total
 
 
-def final_kernel(
-    flags, span_a, span_b, pitch_b, pitch_a, inner, before, out, result, after_faces,
-    before_faces, done,
+def final_near_kernel(
+    span_a, span_b, pitch_a, inner, before, result, after_faces, before_faces
 ):
     flat = result.reshape(result.shape[0], LANES)
     flat[...] = before.reshape(before.shape[0], LANES)[...]
@@ -582,11 +586,11 @@
                 add(4 * 250 + e, 10, below)
 
     at = slice(FACE_PAD, FACE_PAD + BLOCK)
-    arrived = jnp.where(pitch_odd, pitch_a[...], pitch_b[...])
-    before_faces[at, :LANES] = arrived
+    near = pitch_a[...]
+    before_faces[at, :LANES] = jnp.where(pitch_odd, near, 0.0)
     before_faces[at, LANES:] = inner[0:BLOCK]
     after_faces[at, :LANES] = inner[BLOCK:]
-    after_faces[at, LANES:] = jnp.where(pitch_odd, pitch_b[...], pitch_a[...])
+    after_faces[at, LANES:] = jnp.where(pitch_odd, 0.0, near)
     scale = gain * lift_factor(1)
     for e in range(2):
         lanes = slice(e * LANES, (e + 1) * LANES)
@@ -594,12 +598,28 @@
             add(40 + 2 * s + e, 50, -scale * mixed_faces(after_faces, s, lanes, 1, -1.0))
             add(2 * s + e, 50, scale * mixed_faces(before_faces, s, lanes, 1, 1.0))
 
-    wake = arrived[WAKE_ROW : WAKE_ROW + 2]
-    moved = flags[0:1, 2:3] > 0.5
+
+def final_kernel(flags, pitch_b, pitch_a, near, out, result, faces, lifted, done):
+    flat = result.reshape(result.shape[0], LANES)
+    flat[...] = near.reshape(near.shape[0], LANES)[...]
+    pitch_odd, _ = parities()
+    gain = GAIN[2]
+
+    def add(start, stride, values):
+        at = pl.ds(start, values.shape[0], stride=stride)
+        flat[at, :] = flat[at, :] + values
+
+    lifted[...] = far_lift(gain, pitch_b, faces)
+    for s in range(5):
+        values = lifted[s * 25 : s * 25 + 25]
+        add(40 + 2 * s + 1, 50, jnp.where(pitch_odd, values, 0.0))
+        add(2 * s, 50, jnp.where(pitch_odd, 0.0, values))
+
+    wake = arrived_wake(pitch_a, pitch_b)
     rows = lax.broadcasted_iota(jnp.int32, (25, LANES), 0)
     cols = lax.broadcasted_iota(jnp.int32, (25, LANES), 1)
     for e in range(2):
-        row = jnp.where(moved, wake[1 - e : 2 - e], wake[e : e + 1])
+        row = inlet_row(2, flags, wake, e)
         columns = [
             jnp.sum(jnp.where(cols == rows + 25 * v, row, 0.0), axis=1, keepdims=True)
             for v in range(5)
@@ -724,14 +744,24 @@
         scratch=buffers + buffers[:1],
         flops=10**9,
     )
+    odd, even = pitch
+    (near,) = call(
+        final_near_kernel,
+        "final_near",
+        [(x.shape, F32)],
+        [*span, even, inner, rows],
+        scratch=[pltpu.VMEM((BLOCK + 2 * FACE_PAD, 2 * LANES), F32)] * 2,
+        flops=10**8,
+    )
     (out,) = call(
         final_kernel,
         "final",
         [(x.shape, F32)],
-        [flags, span[0], span[1], pitch[0], pitch[1], inner, rows],
+        [flags, odd, even, near],
         scratch=[
             pltpu.VMEM(x.shape, F32),
-            *[pltpu.VMEM((BLOCK + 2 * FACE_PAD, 2 * LANES), F32)] * 2,
+            pltpu.VMEM((BLOCK + 2 * FACE_PAD, LANES), F32),
+            pltpu.VMEM((BLOCK, LANES), F32),
             pltpu.SemaphoreType.DMA((5,)),
         ],
         flops=10**8,

time: 25.3 us -> 25.1 us (level)
  waiting for transfers between devices: 3.38 us -> 3.11 us
    ppermute x12, waiting for transfers between devices: 3.38 us -> 3.11 us  [swapped(): return lax.ppermute(value, ('pitch', 'span'), pairs)]
    pallas_call x10 -> x11, Pallas kernels: 8.23 us -> 8.33 us  [call(): pl.pallas_call(kernel, name=name, out_shape=[jax.ShapeDtypeStruct(shape,...]
  transfers between devices with their start and end apart: 12 -> 12, of which waited for: 2 -> 3; matrix products, arithmetic and copies ran while one was open for 0% -> 0% of each run, Pallas kernels for 25% -> 26%
where the time goes in v9:
time: 25.1 us; the launch traced here: 25 us
  starting transfers between devices  12.2 us (49%)
  Pallas kernels  8.33 us (33%)
  waiting for transfers between devices  3.11 us (12%)
  local copies, waits for them, and re-layouts  1.11 us (4%)
    ppermute x12, starting transfers between devices, swapped(): return lax.ppermute(value, ('pitch', 'span'), pairs)  12.2 us
    pallas_call x11, Pallas kernels, call(): pl.pallas_call(kernel, name=name, out_shape=[jax.ShapeDtypeStruct(shape,...  8.33 us
    ppermute x12, waiting for transfers between devices, swapped(): return lax.ppermute(value, ('pitch', 'span'), pairs)  3.11 us
    unnamed x12, local copies, waits for them, and re-layouts  1.11 us
  transfers between devices with their start and end apart: 12, of which 3 were waited for; matrix products, arithmetic and copies ran while one was open for 0% of the time, Pallas kernels for 26%

profile of v9, /device:TPU:0, one launch (start us, length us, event | category | flops | bytes accessed | tf_op | source)
XLA Modules:
  0.0 25.0 jit_solution(14905244463689750650)
XLA Ops:
  0.0 0.0 copy-start.2
  0.0 1.1 %copy-done.2 = f32[5,5,5,5,2,1,128]{6,5,4,3,2,1,0:T(1,128)S(1)} copy-done((f32[5,5,5,5,2,1,128]{6,5,4,3,2,1,0:T(1,128)S(1)}, f32[5,5,5,5,2,1,128]{6,5,4,3,2,1,0:T(1,128)}, u32[]{:S(2)}) %copy-start.2) | copy-done | bytes 640024
  1.1 0.0 copy-start.4
  1.1 3.1 %collective-permute-start.2 = (f32[104,256]{1,0:T(8,128)S(1)}, f32[104,256]{1,0:T(8,128)S(1)}, u32[]{:S(2)}, u32[]{:S(2)}) collective-permute-start(f32[104,256]{1,0:T(8,128)S(1)} %get-tuple-element.35), channel_id=1, source_target_pairs={{0,1},{1,0},{2,3},{3,2},{4,5},{5,4},{6,7},{7,6},{8,9},{9,8},{10,11... | collective-permute-start | bytes 319496 | tf_op jit(solution)/shard_map/ppermute | solution.py:670
  4.2 0.0 collective-permute-start.3
  4.2 0.0 copy-done.4
  4.2 0.0 copy-start.1
  4.2 0.0 copy-start.3
  4.2 0.0 copy-start.5
  4.3 0.1 begin_pitch.1
  4.4 0.0 copy-start
  4.4 2.6 %collective-permute-start = (f32[128,128]{1,0:T(8,128)S(1)}, f32[128,128]{1,0:T(8,128)S(1)}, u32[]{:S(2)}, u32[]{:S(2)}) collective-permute-start(f32[128,128]{1,0:T(8,128)S(1)} %get-tuple-element.33), channel_id=1, source_target_pairs={{0,28},{1,29},{2,30},{3,31},{4,8},{5,9},{6,10},{7,11},{8,4},{9,5},... | collective-permute-start | bytes 196616 | tf_op jit(solution)/shard_map/ppermute | solution.py:670
  7.0 0.0 collective-permute-start.1
  7.0 0.0 copy-done.1
  7.0 0.0 copy-done.3
  7.0 0.0 copy-done.5
  7.0 1.9 %first.1 = (f32[640,256]{1,0:T(8,128)S(1)}, f32[640,256]{1,0:T(8,128)S(1)}, f32[512,256]{1,0:T(8,128)S(1)}, f32[8,128]{1,0:T(8,128)S(1)}) custom-call(s32[3]{0:T(128)S(1)} %copy-done.5, f32[1250,1,128]{2,1,0:T(1,128)S(1)} %bitcast.9, bf16[1792,640]{1,0:T(8,128)(2,1)S(1)} %copy-done.1), custom_call_target="tpu_custom_call" | custom-call | flops 1000000000 | bytes 1048576 | tf_op jit(solution)/shard_map/first/pallas_call | solution.py:646
  8.9 0.0 collective-permute-done.1.pitch_a
  8.9 0.0 collective-permute-done.2.span_a
  8.9 0.0 collective-permute-done.3.span_b
  9.0 0.0 copy-done
  9.0 0.3 %near.2 = (f32[512,256]{1,0:T(8,128)S(1)}, bf16[512,256]{1,0:T(8,128)(2,1)S(1)}, bf16[512,256]{1,0:T(8,128)(2,1)S(1)}) custom-call(f32[104,256]{1,0:T(8,128)S(1)} %collective-permute-done.2.span_a, f32[104,256]{1,0:T(8,128)S(1)} %collective-permute-done.3.span_b, f32[128,128]{1,0:T(8,128)S(1)} %collective-permute-done.1.pitch_a, ...), custom_call_target="tpu_custom_call" | custom-call | flops 100000000 | bytes 1048576 | tf_op jit(solution)/shard_map/near/pallas_call | solution.py:646
  9.3 0.0 collective-permute-done.pitch_b
  9.3 0.3 %far.2 = (f32[128,128]{1,0:T(8,128)S(1)}, f32[128,128]{1,0:T(8,128)S(1)}, f32[256,128]{1,0:T(8,128)S(1)}, f32[104,256]{1,0:T(8,128)S(1)}, f32[104,256]{1,0:T(8,128)S(1)}) custom-call(f32[8,128]{1,0:T(8,128)S(1)} %get-tuple-element.32.flags, f32[128,128]{1,0:T(8,128)S(1)} %collective-permute-done.pitch_b, f32[128,128]{1,0:T(8,128)S(1)} %collective-permute-done.1.pitch_a, ...), custom_call_target="tpu_custom_call" | custom-call | flops 100000000 | bytes 1048576 | tf_op jit(solution)/shard_map/far/pallas_call | solution.py:646
  9.7 3.5 %collective-permute-start.6 = (f32[104,256]{1,0:T(8,128)S(1)}, f32[104,256]{1,0:T(8,128)S(1)}, u32[]{:S(2)}, u32[]{:S(2)}) collective-permute-start(f32[104,256]{1,0:T(8,128)S(1)} %get-tuple-element.42), channel_id=1, source_target_pairs={{0,1},{1,0},{2,3},{3,2},{4,5},{5,4},{6,7},{7,6},{8,9},{9,8},{10,11... | collective-permute-start | bytes 319496 | tf_op jit(solution)/shard_map/ppermute | solution.py:670
  13.2 0.0 collective-permute-start.7
  13.2 1.2 %collective-permute-start.4 = (f32[128,128]{1,0:T(8,128)S(1)}, f32[128,128]{1,0:T(8,128)S(1)}, u32[]{:S(2)}, u32[]{:S(2)}) collective-permute-start(f32[128,128]{1,0:T(8,128)S(1)} %get-tuple-element.40), channel_id=1, source_target_pairs={{0,28},{1,29},{2,30},{3,31},{4,8},{5,9},{6,10},{7,11},{8,4},{9,5},... | collective-permute-start | bytes 196616 | tf_op jit(solution)/shard_map/ppermute | solution.py:670
  14.4 0.0 collective-permute-start.5
  14.4 2.0 %later.1 = (f32[640,256]{1,0:T(8,128)S(1)}, f32[512,256]{1,0:T(8,128)S(1)}) custom-call(f32[640,256]{1,0:T(8,128)S(1)} %get-tuple-element.45.base, f32[640,256]{1,0:T(8,128)S(1)} %get-tuple-element.46.before, bf16[512,256]{1,0:T(8,128)(2,1)S(1)} %get-tuple-element.47.near_high, bf16[512,256]{1,0:T(8,128)(2,1)S(1)} %get-tuple-element.48.near_low, ...), custom_call_target="tpu_custom_call" | custom-call | flops 1000000000 | bytes 1048576 | tf_op jit(solution)/shard_map/later/pallas_call | solution.py:646
  16.5 0.0 collective-permute-done.5.pitch_a
  16.5 0.0 collective-permute-done.6.span_a
  16.5 0.0 collective-permute-done.7.span_b
  16.5 0.3 %near.3 = (f32[512,256]{1,0:T(8,128)S(1)}, bf16[512,256]{1,0:T(8,128)(2,1)S(1)}, bf16[512,256]{1,0:T(8,128)(2,1)S(1)}) custom-call(f32[104,256]{1,0:T(8,128)S(1)} %collective-permute-done.6.span_a, f32[104,256]{1,0:T(8,128)S(1)} %collective-permute-done.7.span_b, f32[128,128]{1,0:T(8,128)S(1)} %collective-permute-done.5.pitch_a, ...), custom_call_target="tpu_custom_call" | custom-call | flops 100000000 | bytes 1048576 | tf_op jit(solution)/shard_map/near/pallas_call | solution.py:646
  16.9 1.5 %collective-permute-done.4.pitch_b = f32[128,128]{1,0:T(8,128)S(1)} collective-permute-done((f32[128,128]{1,0:T(8,128)S(1)}, f32[128,128]{1,0:T(8,128)S(1)}, u32[]{:S(2)}, u32[]{:S(2)}) %collective-permute-start.4) | collective-permute-done | bytes 65568 | tf_op jit(solution)/shard_map/ppermute | solution.py:670
  18.3 0.3 %far.3 = (f32[128,128]{1,0:T(8,128)S(1)}, f32[128,128]{1,0:T(8,128)S(1)}, f32[256,128]{1,0:T(8,128)S(1)}, f32[104,256]{1,0:T(8,128)S(1)}, f32[104,256]{1,0:T(8,128)S(1)}) custom-call(f32[8,128]{1,0:T(8,128)S(1)} %get-tuple-element.32.flags, f32[128,128]{1,0:T(8,128)S(1)} %collective-permute-done.4.pitch_b, f32[128,128]{1,0:T(8,128)S(1)} %collective-permute-done.5.pitch_a, ...), custom_call_target="tpu_custom_call" | custom-call | flops 100000000 | bytes 1048576 | tf_op jit(solution)/shard_map/far/pallas_call | solution.py:646
  18.7 0.1 collective-permute-start.10
  18.8 0.1 collective-permute-start.11
  18.8 1.6 %collective-permute-start.8 = (f32[128,128]{1,0:T(8,128)S(1)}, f32[128,128]{1,0:T(8,128)S(1)}, u32[]{:S(2)}, u32[]{:S(2)}) collective-permute-start(f32[128,128]{1,0:T(8,128)S(1)} %get-tuple-element.51), channel_id=1, source_target_pairs={{0,28},{1,29},{2,30},{3,31},{4,8},{5,9},{6,10},{7,11},{8,4},{9,5},... | collective-permute-start | bytes 196616 | tf_op jit(solution)/shard_map/ppermute | solution.py:670
  20.5 0.0 collective-permute-start.9
  20.5 1.5 %last.1.before = f32[1250,1,128]{2,1,0:T(1,128)S(1)} custom-call(f32[640,256]{1,0:T(8,128)S(1)} %get-tuple-element.45.base, f32[640,256]{1,0:T(8,128)S(1)} %get-tuple-element.56.before, bf16[512,256]{1,0:T(8,128)(2,1)S(1)} %get-tuple-element.57.near_high, bf16[512,256]{1,0:T(8,128)(2,1)S(1)} %get-tuple-element.58.near_low, ...), custom_call_target="tpu_custom_call" | custom-call | flops 1000000000 | bytes 1048576 | tf_op jit(solution)/shard_map/last/pallas_call | solution.py:646
  22.0 0.0 collective-permute-done.9.pitch_a
  22.0 1.5 %collective-permute-done.10.span_a = f32[104,256]{1,0:T(8,128)S(1)} collective-permute-done((f32[104,256]{1,0:T(8,128)S(1)}, f32[104,256]{1,0:T(8,128)S(1)}, u32[]{:S(2)}, u32[]{:S(2)}) %collective-permute-start.10) | collective-permute-done | bytes 106528 | tf_op jit(solution)/shard_map/ppermute | solution.py:670
  23.5 0.0 collective-permute-done.11.span_b
  23.5 0.3 %final_near.1.near = f32[1250,1,128]{2,1,0:T(1,128)S(1)} custom-call(f32[104,256]{1,0:T(8,128)S(1)} %collective-permute-done.10.span_a, f32[104,256]{1,0:T(8,128)S(1)} %collective-permute-done.11.span_b, f32[128,128]{1,0:T(8,128)S(1)} %collective-permute-done.9.pitch_a, f32[256,128]{1,0:T(8,128)S(1)} %get-tuple-element.55.inner, f32[1250,1,128]{2,1,0:T(1,128)S(1)} %last.1.before), custom_call_target="tpu_custom_call" | custom-call | flops 100000000 | bytes 1048576 | tf_op jit(solution)/shard_map/final_near/pallas_call | solution.py:646
  23.7 0.2 collective-permute-done.8.pitch_b
  23.9 1.1 %final.1 = f32[1250,1,128]{2,1,0:T(1,128)} custom-call(f32[8,128]{1,0:T(8,128)S(1)} %get-tuple-element.32.flags, f32[128,128]{1,0:T(8,128)S(1)} %collective-permute-done.8.pitch_b, f32[128,128]{1,0:T(8,128)S(1)} %collective-permute-done.9.pitch_a, f32[1250,1,128]{2,1,0:T(1,128)S(1)} %final_near.1.near), custom_call_target="tpu_custom_call" | custom-call | flops 100000000 | bytes 1048576 | tf_op jit(solution)/shard_map/final/pallas_call | solution.py:646
  (1 shorter events, 0.0 us)
Async XLA Ops:
  0.0 1.1 %copy-start.2 = (f32[5,5,5,5,2,1,128]{6,5,4,3,2,1,0:T(1,128)S(1)}, f32[5,5,5,5,2,1,128]{6,5,4,3,2,1,0:T(1,128)}, u32[]{:S(2)}) copy-start(f32[5,5,5,5,2,1,128]{6,5,4,3,2,1,0:T(1,128)} %param.5) | copy-start | bytes 1920004
  1.1 3.1 %copy-start.4 = (f32[5,5,5,2,1]{2,4,3,1,0:T(1,128)S(1)}, f32[5,5,5,2,1]{2,4,3,1,0:T(1,128)}, u32[]{:S(2)}) copy-start(f32[5,5,5,2,1]{2,4,3,1,0:T(1,128)} %param.6) | copy-start | bytes 3004
  1.1 7.8 %collective-permute-start.2 = (f32[104,256]{1,0:T(8,128)S(1)}, f32[104,256]{1,0:T(8,128)S(1)}, u32[]{:S(2)}, u32[]{:S(2)}) collective-permute-start(f32[104,256]{1,0:T(8,128)S(1)} %get-tuple-element.35), channel_id=1, source_target_pairs={{0,1},{1,0},{2,3},{3,2},{4,5},{5,4},{6,7},{7,6},{8,9},{9,8},{10,11... | collective-permute-start | bytes 319496 | tf_op jit(solution)/shard_map/ppermute | solution.py:670
  4.2 4.7 %collective-permute-start.3 = (f32[104,256]{1,0:T(8,128)S(1)}, f32[104,256]{1,0:T(8,128)S(1)}, u32[]{:S(2)}, u32[]{:S(2)}) collective-permute-start(f32[104,256]{1,0:T(8,128)S(1)} %get-tuple-element.36), channel_id=1, source_target_pairs={{0,4},{1,2},{2,1},{3,7},{4,0},{5,6},{6,5},{7,3},{8,12},{9,10},{10,... | collective-permute-start | bytes 319496 | tf_op jit(solution)/shard_map/ppermute | solution.py:670
  4.2 2.8 %copy-start.1 = (bf16[1792,640]{1,0:T(8,128)(2,1)S(1)}, bf16[1792,640]{1,0:T(8,128)(2,1)}, u32[]{:S(2)}) copy-start(bf16[1792,640]{1,0:T(8,128)(2,1)} %constant.4.clone.table) | copy-start | bytes 6881284
  4.2 2.8 %copy-start.3 = (f32[5,5,5,5,2,1,128]{6,5,4,3,2,1,0:T(1,128)S(1)}, f32[5,5,5,5,2,1,128]{6,5,4,3,2,1,0:T(1,128)}, u32[]{:S(2)}) copy-start(f32[5,5,5,5,2,1,128]{6,5,4,3,2,1,0:T(1,128)} %param.5) | copy-start | bytes 1920004
  4.2 2.8 %copy-start.5 = (s32[3]{0:T(128)S(1)}, s32[3]{0:T(128)}, u32[]{:S(2)}) copy-start(s32[3]{0:T(128)} %offsets.1) | copy-start | bytes 40
  4.4 4.6 %copy-start = (bf16[1312,640]{1,0:T(8,128)(2,1)S(1)}, bf16[1312,640]{1,0:T(8,128)(2,1)}, u32[]{:S(2)}) copy-start(bf16[1312,640]{1,0:T(8,128)(2,1)} %constant.5.clone.links) | copy-start | bytes 5038084
  4.4 4.9 %collective-permute-start = (f32[128,128]{1,0:T(8,128)S(1)}, f32[128,128]{1,0:T(8,128)S(1)}, u32[]{:S(2)}, u32[]{:S(2)}) collective-permute-start(f32[128,128]{1,0:T(8,128)S(1)} %get-tuple-element.33), channel_id=1, source_target_pairs={{0,28},{1,29},{2,30},{3,31},{4,8},{5,9},{6,10},{7,11},{8,4},{9,5},... | collective-permute-start | bytes 196616 | tf_op jit(solution)/shard_map/ppermute | solution.py:670
  7.0 1.9 %collective-permute-start.1 = (f32[128,128]{1,0:T(8,128)S(1)}, f32[128,128]{1,0:T(8,128)S(1)}, u32[]{:S(2)}, u32[]{:S(2)}) collective-permute-start(f32[128,128]{1,0:T(8,128)S(1)} %get-tuple-element.34), channel_id=1, source_target_pairs={{0,4},{1,5},{2,6},{3,7},{4,0},{5,1},{6,2},{7,3},{8,12},{9,13},{10,... | collective-permute-start | bytes 196616 | tf_op jit(solution)/shard_map/ppermute | solution.py:670
  9.7 6.8 %collective-permute-start.6 = (f32[104,256]{1,0:T(8,128)S(1)}, f32[104,256]{1,0:T(8,128)S(1)}, u32[]{:S(2)}, u32[]{:S(2)}) collective-permute-start(f32[104,256]{1,0:T(8,128)S(1)} %get-tuple-element.42), channel_id=1, source_target_pairs={{0,1},{1,0},{2,3},{3,2},{4,5},{5,4},{6,7},{7,6},{8,9},{9,8},{10,11... | collective-permute-start | bytes 319496 | tf_op jit(solution)/shard_map/ppermute | solution.py:670
  13.2 3.3 %collective-permute-start.7 = (f32[104,256]{1,0:T(8,128)S(1)}, f32[104,256]{1,0:T(8,128)S(1)}, u32[]{:S(2)}, u32[]{:S(2)}) collective-permute-start(f32[104,256]{1,0:T(8,128)S(1)} %get-tuple-element.43), channel_id=1, source_target_pairs={{0,4},{1,2},{2,1},{3,7},{4,0},{5,6},{6,5},{7,3},{8,12},{9,10},{10,... | collective-permute-start | bytes 319496 | tf_op jit(solution)/shard_map/ppermute | solution.py:670
  13.2 5.1 %collective-permute-start.4 = (f32[128,128]{1,0:T(8,128)S(1)}, f32[128,128]{1,0:T(8,128)S(1)}, u32[]{:S(2)}, u32[]{:S(2)}) collective-permute-start(f32[128,128]{1,0:T(8,128)S(1)} %get-tuple-element.40), channel_id=1, source_target_pairs={{0,28},{1,29},{2,30},{3,31},{4,8},{5,9},{6,10},{7,11},{8,4},{9,5},... | collective-permute-start | bytes 196616 | tf_op jit(solution)/shard_map/ppermute | solution.py:670
  14.4 2.1 %collective-permute-start.5 = (f32[128,128]{1,0:T(8,128)S(1)}, f32[128,128]{1,0:T(8,128)S(1)}, u32[]{:S(2)}, u32[]{:S(2)}) collective-permute-start(f32[128,128]{1,0:T(8,128)S(1)} %get-tuple-element.41), channel_id=1, source_target_pairs={{0,4},{1,5},{2,6},{3,7},{4,0},{5,1},{6,2},{7,3},{8,12},{9,13},{10,... | collective-permute-start | bytes 196616 | tf_op jit(solution)/shard_map/ppermute | solution.py:670
  18.7 4.8 %collective-permute-start.10 = (f32[104,256]{1,0:T(8,128)S(1)}, f32[104,256]{1,0:T(8,128)S(1)}, u32[]{:S(2)}, u32[]{:S(2)}) collective-permute-start(f32[104,256]{1,0:T(8,128)S(1)} %get-tuple-element.53), channel_id=1, source_target_pairs={{0,1},{1,0},{2,3},{3,2},{4,5},{5,4},{6,7},{7,6},{8,9},{9,8},{10,11... | collective-permute-start | bytes 319496 | tf_op jit(solution)/shard_map/ppermute | solution.py:670
  18.8 4.7 %collective-permute-start.11 = (f32[104,256]{1,0:T(8,128)S(1)}, f32[104,256]{1,0:T(8,128)S(1)}, u32[]{:S(2)}, u32[]{:S(2)}) collective-permute-start(f32[104,256]{1,0:T(8,128)S(1)} %get-tuple-element.54), channel_id=1, source_target_pairs={{0,4},{1,2},{2,1},{3,7},{4,0},{5,6},{6,5},{7,3},{8,12},{9,10},{10,... | collective-permute-start | bytes 319496 | tf_op jit(solution)/shard_map/ppermute | solution.py:670
  18.8 5.0 %collective-permute-start.8 = (f32[128,128]{1,0:T(8,128)S(1)}, f32[128,128]{1,0:T(8,128)S(1)}, u32[]{:S(2)}, u32[]{:S(2)}) collective-permute-start(f32[128,128]{1,0:T(8,128)S(1)} %get-tuple-element.51), channel_id=1, source_target_pairs={{0,28},{1,29},{2,30},{3,31},{4,8},{5,9},{6,10},{7,11},{8,4},{9,5},... | collective-permute-start | bytes 196616 | tf_op jit(solution)/shard_map/ppermute | solution.py:670
  20.5 1.5 %collective-permute-start.9 = (f32[128,128]{1,0:T(8,128)S(1)}, f32[128,128]{1,0:T(8,128)S(1)}, u32[]{:S(2)}, u32[]{:S(2)}) collective-permute-start(f32[128,128]{1,0:T(8,128)S(1)} %get-tuple-element.52), channel_id=1, source_target_pairs={{0,4},{1,5},{2,6},{3,7},{4,0},{5,1},{6,2},{7,3},{8,12},{9,13},{10,... | collective-permute-start | bytes 196616 | tf_op jit(solution)/shard_map/ppermute | solution.py:670

commit v10 on v9

--- a/solution.py
+++ b/solution.py
@@ -428,25 +428,6 @@
         )
 
 
-def from_lanes(row, moves):
-    lanes = lax.broadcasted_iota(jnp.int32, row.shape, 1)
-    total = None
-    for factor, start, stop, distance in moves:
-        moved = pltpu.roll(row, distance % LANES, 1) if distance else row
-        term = jnp.where((lanes >= start) & (lanes < stop), factor * moved, 0.0)
-        total = term if total is None else total + term
-    return total
-
-
-def lane_moves(table):
-    return [
-        (float(table[i, j]), 25 * i, 25 * i + 25, 25 * (i - j))
-        for i in range(table.shape[0])
-        for j in range(table.shape[1])
-        if table[i, j] != 0.0
-    ]
-
-
 def far_lift(gain, pitch_b, faces):
     pitch_odd, _ = parities()
     faces[FACE_PAD : FACE_PAD + BLOCK] = pitch_b[...]
@@ -472,11 +453,13 @@
     section, flags, pitch_b, pitch_a, near_faces,
     next_pitch_a, next_pitch_b, next_inner, next_span_a, next_span_b, *refs
 ):
-    *traces, faces, lifted = refs
+    *buffers, faces, lifted = refs
+    traces, inlets = (buffers[:2], buffers[2:])
     pitch_odd, span_odd = parities()
     gain = GAIN[section]
     for e in range(2):
         traces[e][...] = near_faces[:, e * LANES : (e + 1) * LANES]
+        inlets[e][...] = jnp.zeros((TRACES, LANES), jnp.float32)
 
     def add(start, count, stride, e, values):
         at = pl.ds(start, count, stride=stride) if stride > 1 else pl.ds(start, count)
@@ -494,26 +477,45 @@
             add(start, 5, 5, 0, jnp.where(pitch_odd, 0.0, values))
 
     wake = arrived_wake(pitch_a, pitch_b)
-    rows = lax.broadcasted_iota(jnp.int32, (5, LANES), 0)
-    cols = lax.broadcasted_iota(jnp.int32, (5, LANES), 1)
-    for e in range(2):
-
-        def add_column(start, stride, row, first, step):
-            picked = jnp.where(cols == first + step * rows, row, 0.0)
-            column = jnp.sum(picked, axis=1, keepdims=True)
-            add(start, 5, stride, e, jnp.where(cols == 0, column, 0.0))
-
-        row = jnp.broadcast_to(inlet_row(section, flags, wake, e), (8, LANES))
-        row = from_lanes(row, lane_moves(gain * lift_factor(0) * half_flux(0, 1.0)))
-        for block, p in ((0, 4), (1, 0)):
-            for s in range(5):
-                add_column(block * BLOCK + s * 25, 5, row[0:1], p * 5 + s, 25)
-        for block, s, sign in ((2, 4, 1.0), (3, 0, -1.0)):
-            sent = from_lanes(row, lane_moves(half_flux(2, sign)[:4]))
-            for c in range(4):
-                add_column(block * BLOCK + c * 25, 1, sent[0:1], c * 25 + s, 5)
-
-    both = jnp.concatenate([traces[0][...], traces[1][...]], axis=1)
+    rows = lax.broadcasted_iota(jnp.int32, (25, LANES), 0)
+    cols = lax.broadcasted_iota(jnp.int32, (25, LANES), 1)
+    node = sum((rows >= 5 * k).astype(jnp.int32) for k in range(1, 5))
+    variable = rows - 5 * node
+    scale = gain * lift_factor(0)
+    inflow = half_flux(0, 1.0)
+
+    def weights(table, choice, lane):
+        total = jnp.zeros(choice.shape, jnp.float32)
+        for v in range(5):
+            values = [float(scale * table[i, v]) for i in range(table.shape[0])]
+            if any(values):
+                factor = sum(
+                    jnp.where(choice == i, value, 0.0) for i, value in enumerate(values) if value
+                )
+                total = total + jnp.where(cols[: choice.shape[0]] == 25 * v + lane, factor, 0.0)
+        return total
+
+    def column(part, row):
+        total = jnp.sum(part * row, axis=1, keepdims=True)
+        return jnp.where(cols[: part.shape[0]] == 0, total, 0.0)
+
+    pitch_parts = [
+        (block, weights(inflow, variable, 5 * p + node)) for block, p in ((0, 4), (1, 0))
+    ]
+    span_parts = []
+    for block, s, sign in ((2, 4, 1.0), (3, 0, -1.0)):
+        sent = half_flux(2, sign)[:4] @ inflow
+        for c in range(4):
+            part = weights(sent[c : c + 1], rows[:5] * 0, 5 * rows[:5] + s)
+            span_parts.append((block * BLOCK + c * 25, part))
+    for e in range(2):
+        row = inlet_row(section, flags, wake, e)
+        for block, part in pitch_parts:
+            inlets[e][pl.ds(block * BLOCK, 25, stride=5), :] = column(part, row)
+        for start, part in span_parts:
+            inlets[e][start : start + 5] = column(part, row)
+
+    both = jnp.concatenate([traces[e][...] + inlets[e][...] for e in range(2)], axis=1)
     emit_span_faces(both[2 * BLOCK :], span_odd, next_span_a, next_span_b)
     emit_pitch_faces(
         both[: 2 * BLOCK], [wake[0:1], wake[1:2]], pitch_odd, next_pitch_a, next_pitch_b,
@@ -721,8 +723,7 @@
             scratch=[
                 pltpu.VMEM(shape, F32)
                 for shape in (
-                    (TRACES, LANES),
-                    (TRACES, LANES),
+                    *[(TRACES, LANES)] * 4,
                     (BLOCK + 2 * FACE_PAD, LANES),
                     (BLOCK, LANES),
                 )

time: 25.1 us -> 24.9 us (level)
  no operation moved by 1% of the time
where the time goes in v10:
time: 24.9 us; the launch traced here: 24.7 us
  starting transfers between devices  12.2 us (49%)
  Pallas kernels  8.09 us (32%)
  waiting for transfers between devices  3.11 us (12%)
  local copies, waits for them, and re-layouts  1.11 us (4%)
    ppermute x12, starting transfers between devices, swapped(): return lax.ppermute(value, ('pitch', 'span'), pairs)  12.2 us
    pallas_call x11, Pallas kernels, call(): pl.pallas_call(kernel, name=name, out_shape=[jax.ShapeDtypeStruct(shape,...  8.09 us
    ppermute x12, waiting for transfers between devices, swapped(): return lax.ppermute(value, ('pitch', 'span'), pairs)  3.11 us
    unnamed x12, local copies, waits for them, and re-layouts  1.11 us
  transfers between devices with their start and end apart: 12, of which 3 were waited for; matrix products, arithmetic and copies ran while one was open for 0% of the time, Pallas kernels for 26%

profile of v10, /device:TPU:0, one launch (start us, length us, event | category | flops | bytes accessed | tf_op | source)
XLA Modules:
  0.0 24.7 jit_solution(10730998819011397394)
XLA Ops:
  0.0 0.0 copy-start.2
  0.0 1.1 %copy-done.2 = f32[5,5,5,5,2,1,128]{6,5,4,3,2,1,0:T(1,128)S(1)} copy-done((f32[5,5,5,5,2,1,128]{6,5,4,3,2,1,0:T(1,128)S(1)}, f32[5,5,5,5,2,1,128]{6,5,4,3,2,1,0:T(1,128)}, u32[]{:S(2)}) %copy-start.2) | copy-done | bytes 640024
  1.1 0.0 copy-start.4
  1.1 3.1 %collective-permute-start.2 = (f32[104,256]{1,0:T(8,128)S(1)}, f32[104,256]{1,0:T(8,128)S(1)}, u32[]{:S(2)}, u32[]{:S(2)}) collective-permute-start(f32[104,256]{1,0:T(8,128)S(1)} %get-tuple-element.35), channel_id=1, source_target_pairs={{0,1},{1,0},{2,3},{3,2},{4,5},{5,4},{6,7},{7,6},{8,9},{9,8},{10,11... | collective-permute-start | bytes 319496 | tf_op jit(solution)/shard_map/ppermute | solution.py:672
  4.2 0.0 collective-permute-start.3
  4.2 0.0 copy-done.4
  4.2 0.0 copy-start.1
  4.2 0.0 copy-start.3
  4.2 0.0 copy-start.5
  4.3 0.1 begin_pitch.1
  4.4 0.0 copy-start
  4.4 2.6 %collective-permute-start = (f32[128,128]{1,0:T(8,128)S(1)}, f32[128,128]{1,0:T(8,128)S(1)}, u32[]{:S(2)}, u32[]{:S(2)}) collective-permute-start(f32[128,128]{1,0:T(8,128)S(1)} %get-tuple-element.33), channel_id=1, source_target_pairs={{0,28},{1,29},{2,30},{3,31},{4,8},{5,9},{6,10},{7,11},{8,4},{9,5},... | collective-permute-start | bytes 196616 | tf_op jit(solution)/shard_map/ppermute | solution.py:672
  7.0 0.0 collective-permute-start.1
  7.0 0.0 copy-done.1
  7.0 0.0 copy-done.3
  7.0 0.0 copy-done.5
  7.0 1.9 %first.1 = (f32[640,256]{1,0:T(8,128)S(1)}, f32[640,256]{1,0:T(8,128)S(1)}, f32[512,256]{1,0:T(8,128)S(1)}, f32[8,128]{1,0:T(8,128)S(1)}) custom-call(s32[3]{0:T(128)S(1)} %copy-done.5, f32[1250,1,128]{2,1,0:T(1,128)S(1)} %bitcast.9, bf16[1792,640]{1,0:T(8,128)(2,1)S(1)} %copy-done.1), custom_call_target="tpu_custom_call" | custom-call | flops 1000000000 | bytes 1048576 | tf_op jit(solution)/shard_map/first/pallas_call | solution.py:648
  8.9 0.0 collective-permute-done.1.pitch_a
  8.9 0.0 collective-permute-done.2.span_a
  8.9 0.0 collective-permute-done.3.span_b
  9.0 0.0 copy-done
  9.0 0.3 %near.2 = (f32[512,256]{1,0:T(8,128)S(1)}, bf16[512,256]{1,0:T(8,128)(2,1)S(1)}, bf16[512,256]{1,0:T(8,128)(2,1)S(1)}) custom-call(f32[104,256]{1,0:T(8,128)S(1)} %collective-permute-done.2.span_a, f32[104,256]{1,0:T(8,128)S(1)} %collective-permute-done.3.span_b, f32[128,128]{1,0:T(8,128)S(1)} %collective-permute-done.1.pitch_a, ...), custom_call_target="tpu_custom_call" | custom-call | flops 100000000 | bytes 1048576 | tf_op jit(solution)/shard_map/near/pallas_call | solution.py:648
  9.3 0.0 collective-permute-done.pitch_b
  9.3 0.2 far.2
  9.6 3.5 %collective-permute-start.6 = (f32[104,256]{1,0:T(8,128)S(1)}, f32[104,256]{1,0:T(8,128)S(1)}, u32[]{:S(2)}, u32[]{:S(2)}) collective-permute-start(f32[104,256]{1,0:T(8,128)S(1)} %get-tuple-element.42), channel_id=1, source_target_pairs={{0,1},{1,0},{2,3},{3,2},{4,5},{5,4},{6,7},{7,6},{8,9},{9,8},{10,11... | collective-permute-start | bytes 319496 | tf_op jit(solution)/shard_map/ppermute | solution.py:672
  13.1 0.0 collective-permute-start.7
  13.1 1.2 %collective-permute-start.4 = (f32[128,128]{1,0:T(8,128)S(1)}, f32[128,128]{1,0:T(8,128)S(1)}, u32[]{:S(2)}, u32[]{:S(2)}) collective-permute-start(f32[128,128]{1,0:T(8,128)S(1)} %get-tuple-element.40), channel_id=1, source_target_pairs={{0,28},{1,29},{2,30},{3,31},{4,8},{5,9},{6,10},{7,11},{8,4},{9,5},... | collective-permute-start | bytes 196616 | tf_op jit(solution)/shard_map/ppermute | solution.py:672
  14.3 0.0 collective-permute-start.5
  14.3 2.0 %later.1 = (f32[640,256]{1,0:T(8,128)S(1)}, f32[512,256]{1,0:T(8,128)S(1)}) custom-call(f32[640,256]{1,0:T(8,128)S(1)} %get-tuple-element.45.base, f32[640,256]{1,0:T(8,128)S(1)} %get-tuple-element.46.before, bf16[512,256]{1,0:T(8,128)(2,1)S(1)} %get-tuple-element.47.near_high, bf16[512,256]{1,0:T(8,128)(2,1)S(1)} %get-tuple-element.48.near_low, ...), custom_call_target="tpu_custom_call" | custom-call | flops 1000000000 | bytes 1048576 | tf_op jit(solution)/shard_map/later/pallas_call | solution.py:648
  16.4 0.0 collective-permute-done.5.pitch_a
  16.4 0.0 collective-permute-done.6.span_a
  16.4 0.0 collective-permute-done.7.span_b
  16.4 0.3 %near.3 = (f32[512,256]{1,0:T(8,128)S(1)}, bf16[512,256]{1,0:T(8,128)(2,1)S(1)}, bf16[512,256]{1,0:T(8,128)(2,1)S(1)}) custom-call(f32[104,256]{1,0:T(8,128)S(1)} %collective-permute-done.6.span_a, f32[104,256]{1,0:T(8,128)S(1)} %collective-permute-done.7.span_b, f32[128,128]{1,0:T(8,128)S(1)} %collective-permute-done.5.pitch_a, ...), custom_call_target="tpu_custom_call" | custom-call | flops 100000000 | bytes 1048576 | tf_op jit(solution)/shard_map/near/pallas_call | solution.py:648
  16.7 1.5 %collective-permute-done.4.pitch_b = f32[128,128]{1,0:T(8,128)S(1)} collective-permute-done((f32[128,128]{1,0:T(8,128)S(1)}, f32[128,128]{1,0:T(8,128)S(1)}, u32[]{:S(2)}, u32[]{:S(2)}) %collective-permute-start.4) | collective-permute-done | bytes 65568 | tf_op jit(solution)/shard_map/ppermute | solution.py:672
  18.2 0.2 far.3
  18.4 0.1 collective-permute-start.10
  18.5 0.1 collective-permute-start.11
  18.6 1.6 %collective-permute-start.8 = (f32[128,128]{1,0:T(8,128)S(1)}, f32[128,128]{1,0:T(8,128)S(1)}, u32[]{:S(2)}, u32[]{:S(2)}) collective-permute-start(f32[128,128]{1,0:T(8,128)S(1)} %get-tuple-element.51), channel_id=1, source_target_pairs={{0,28},{1,29},{2,30},{3,31},{4,8},{5,9},{6,10},{7,11},{8,4},{9,5},... | collective-permute-start | bytes 196616 | tf_op jit(solution)/shard_map/ppermute | solution.py:672
  20.2 0.0 collective-permute-start.9
  20.2 1.5 %last.1.before = f32[1250,1,128]{2,1,0:T(1,128)S(1)} custom-call(f32[640,256]{1,0:T(8,128)S(1)} %get-tuple-element.45.base, f32[640,256]{1,0:T(8,128)S(1)} %get-tuple-element.56.before, bf16[512,256]{1,0:T(8,128)(2,1)S(1)} %get-tuple-element.57.near_high, bf16[512,256]{1,0:T(8,128)(2,1)S(1)} %get-tuple-element.58.near_low, ...), custom_call_target="tpu_custom_call" | custom-call | flops 1000000000 | bytes 1048576 | tf_op jit(solution)/shard_map/last/pallas_call | solution.py:648
  21.7 0.0 collective-permute-done.9.pitch_a
  21.8 1.5 %collective-permute-done.10.span_a = f32[104,256]{1,0:T(8,128)S(1)} collective-permute-done((f32[104,256]{1,0:T(8,128)S(1)}, f32[104,256]{1,0:T(8,128)S(1)}, u32[]{:S(2)}, u32[]{:S(2)}) %collective-permute-start.10) | collective-permute-done | bytes 106528 | tf_op jit(solution)/shard_map/ppermute | solution.py:672
  23.2 0.0 collective-permute-done.11.span_b
  23.2 0.3 %final_near.1.near = f32[1250,1,128]{2,1,0:T(1,128)S(1)} custom-call(f32[104,256]{1,0:T(8,128)S(1)} %collective-permute-done.10.span_a, f32[104,256]{1,0:T(8,128)S(1)} %collective-permute-done.11.span_b, f32[128,128]{1,0:T(8,128)S(1)} %collective-permute-done.9.pitch_a, f32[256,128]{1,0:T(8,128)S(1)} %get-tuple-element.55.inner, f32[1250,1,128]{2,1,0:T(1,128)S(1)} %last.1.before), custom_call_target="tpu_custom_call" | custom-call | flops 100000000 | bytes 1048576 | tf_op jit(solution)/shard_map/final_near/pallas_call | solution.py:648
  23.5 0.2 collective-permute-done.8.pitch_b
  23.6 1.1 %final.1 = f32[1250,1,128]{2,1,0:T(1,128)} custom-call(f32[8,128]{1,0:T(8,128)S(1)} %get-tuple-element.32.flags, f32[128,128]{1,0:T(8,128)S(1)} %collective-permute-done.8.pitch_b, f32[128,128]{1,0:T(8,128)S(1)} %collective-permute-done.9.pitch_a, f32[1250,1,128]{2,1,0:T(1,128)S(1)} %final_near.1.near), custom_call_target="tpu_custom_call" | custom-call | flops 100000000 | bytes 1048576 | tf_op jit(solution)/shard_map/final/pallas_call | solution.py:648
  (1 shorter events, 0.0 us)
Async XLA Ops:
  0.0 1.1 %copy-start.2 = (f32[5,5,5,5,2,1,128]{6,5,4,3,2,1,0:T(1,128)S(1)}, f32[5,5,5,5,2,1,128]{6,5,4,3,2,1,0:T(1,128)}, u32[]{:S(2)}) copy-start(f32[5,5,5,5,2,1,128]{6,5,4,3,2,1,0:T(1,128)} %param.5) | copy-start | bytes 1920004
  1.1 3.1 %copy-start.4 = (f32[5,5,5,2,1]{2,4,3,1,0:T(1,128)S(1)}, f32[5,5,5,2,1]{2,4,3,1,0:T(1,128)}, u32[]{:S(2)}) copy-start(f32[5,5,5,2,1]{2,4,3,1,0:T(1,128)} %param.6) | copy-start | bytes 3004
  1.1 7.8 %collective-permute-start.2 = (f32[104,256]{1,0:T(8,128)S(1)}, f32[104,256]{1,0:T(8,128)S(1)}, u32[]{:S(2)}, u32[]{:S(2)}) collective-permute-start(f32[104,256]{1,0:T(8,128)S(1)} %get-tuple-element.35), channel_id=1, source_target_pairs={{0,1},{1,0},{2,3},{3,2},{4,5},{5,4},{6,7},{7,6},{8,9},{9,8},{10,11... | collective-permute-start | bytes 319496 | tf_op jit(solution)/shard_map/ppermute | solution.py:672
  4.2 4.7 %collective-permute-start.3 = (f32[104,256]{1,0:T(8,128)S(1)}, f32[104,256]{1,0:T(8,128)S(1)}, u32[]{:S(2)}, u32[]{:S(2)}) collective-permute-start(f32[104,256]{1,0:T(8,128)S(1)} %get-tuple-element.36), channel_id=1, source_target_pairs={{0,4},{1,2},{2,1},{3,7},{4,0},{5,6},{6,5},{7,3},{8,12},{9,10},{10,... | collective-permute-start | bytes 319496 | tf_op jit(solution)/shard_map/ppermute | solution.py:672
  4.2 2.8 %copy-start.1 = (bf16[1792,640]{1,0:T(8,128)(2,1)S(1)}, bf16[1792,640]{1,0:T(8,128)(2,1)}, u32[]{:S(2)}) copy-start(bf16[1792,640]{1,0:T(8,128)(2,1)} %constant.4.clone.table) | copy-start | bytes 6881284
  4.2 2.8 %copy-start.3 = (f32[5,5,5,5,2,1,128]{6,5,4,3,2,1,0:T(1,128)S(1)}, f32[5,5,5,5,2,1,128]{6,5,4,3,2,1,0:T(1,128)}, u32[]{:S(2)}) copy-start(f32[5,5,5,5,2,1,128]{6,5,4,3,2,1,0:T(1,128)} %param.5) | copy-start | bytes 1920004
  4.2 2.8 %copy-start.5 = (s32[3]{0:T(128)S(1)}, s32[3]{0:T(128)}, u32[]{:S(2)}) copy-start(s32[3]{0:T(128)} %offsets.1) | copy-start | bytes 40
  4.4 4.6 %copy-start = (bf16[1312,640]{1,0:T(8,128)(2,1)S(1)}, bf16[1312,640]{1,0:T(8,128)(2,1)}, u32[]{:S(2)}) copy-start(bf16[1312,640]{1,0:T(8,128)(2,1)} %constant.5.clone.links) | copy-start | bytes 5038084
  4.4 4.9 %collective-permute-start = (f32[128,128]{1,0:T(8,128)S(1)}, f32[128,128]{1,0:T(8,128)S(1)}, u32[]{:S(2)}, u32[]{:S(2)}) collective-permute-start(f32[128,128]{1,0:T(8,128)S(1)} %get-tuple-element.33), channel_id=1, source_target_pairs={{0,28},{1,29},{2,30},{3,31},{4,8},{5,9},{6,10},{7,11},{8,4},{9,5},... | collective-permute-start | bytes 196616 | tf_op jit(solution)/shard_map/ppermute | solution.py:672
  7.0 1.9 %collective-permute-start.1 = (f32[128,128]{1,0:T(8,128)S(1)}, f32[128,128]{1,0:T(8,128)S(1)}, u32[]{:S(2)}, u32[]{:S(2)}) collective-permute-start(f32[128,128]{1,0:T(8,128)S(1)} %get-tuple-element.34), channel_id=1, source_target_pairs={{0,4},{1,5},{2,6},{3,7},{4,0},{5,1},{6,2},{7,3},{8,12},{9,13},{10,... | collective-permute-start | bytes 196616 | tf_op jit(solution)/shard_map/ppermute | solution.py:672
  9.6 6.8 %collective-permute-start.6 = (f32[104,256]{1,0:T(8,128)S(1)}, f32[104,256]{1,0:T(8,128)S(1)}, u32[]{:S(2)}, u32[]{:S(2)}) collective-permute-start(f32[104,256]{1,0:T(8,128)S(1)} %get-tuple-element.42), channel_id=1, source_target_pairs={{0,1},{1,0},{2,3},{3,2},{4,5},{5,4},{6,7},{7,6},{8,9},{9,8},{10,11... | collective-permute-start | bytes 319496 | tf_op jit(solution)/shard_map/ppermute | solution.py:672
  13.1 3.3 %collective-permute-start.7 = (f32[104,256]{1,0:T(8,128)S(1)}, f32[104,256]{1,0:T(8,128)S(1)}, u32[]{:S(2)}, u32[]{:S(2)}) collective-permute-start(f32[104,256]{1,0:T(8,128)S(1)} %get-tuple-element.43), channel_id=1, source_target_pairs={{0,4},{1,2},{2,1},{3,7},{4,0},{5,6},{6,5},{7,3},{8,12},{9,10},{10,... | collective-permute-start | bytes 319496 | tf_op jit(solution)/shard_map/ppermute | solution.py:672
  13.1 5.1 %collective-permute-start.4 = (f32[128,128]{1,0:T(8,128)S(1)}, f32[128,128]{1,0:T(8,128)S(1)}, u32[]{:S(2)}, u32[]{:S(2)}) collective-permute-start(f32[128,128]{1,0:T(8,128)S(1)} %get-tuple-element.40), channel_id=1, source_target_pairs={{0,28},{1,29},{2,30},{3,31},{4,8},{5,9},{6,10},{7,11},{8,4},{9,5},... | collective-permute-start | bytes 196616 | tf_op jit(solution)/shard_map/ppermute | solution.py:672
  14.3 2.1 %collective-permute-start.5 = (f32[128,128]{1,0:T(8,128)S(1)}, f32[128,128]{1,0:T(8,128)S(1)}, u32[]{:S(2)}, u32[]{:S(2)}) collective-permute-start(f32[128,128]{1,0:T(8,128)S(1)} %get-tuple-element.41), channel_id=1, source_target_pairs={{0,4},{1,5},{2,6},{3,7},{4,0},{5,1},{6,2},{7,3},{8,12},{9,13},{10,... | collective-permute-start | bytes 196616 | tf_op jit(solution)/shard_map/ppermute | solution.py:672
  18.4 4.8 %collective-permute-start.10 = (f32[104,256]{1,0:T(8,128)S(1)}, f32[104,256]{1,0:T(8,128)S(1)}, u32[]{:S(2)}, u32[]{:S(2)}) collective-permute-start(f32[104,256]{1,0:T(8,128)S(1)} %get-tuple-element.53), channel_id=1, source_target_pairs={{0,1},{1,0},{2,3},{3,2},{4,5},{5,4},{6,7},{7,6},{8,9},{9,8},{10,11... | collective-permute-start | bytes 319496 | tf_op jit(solution)/shard_map/ppermute | solution.py:672
  18.5 4.7 %collective-permute-start.11 = (f32[104,256]{1,0:T(8,128)S(1)}, f32[104,256]{1,0:T(8,128)S(1)}, u32[]{:S(2)}, u32[]{:S(2)}) collective-permute-start(f32[104,256]{1,0:T(8,128)S(1)} %get-tuple-element.54), channel_id=1, source_target_pairs={{0,4},{1,2},{2,1},{3,7},{4,0},{5,6},{6,5},{7,3},{8,12},{9,10},{10,... | collective-permute-start | bytes 319496 | tf_op jit(solution)/shard_map/ppermute | solution.py:672
  18.6 5.0 %collective-permute-start.8 = (f32[128,128]{1,0:T(8,128)S(1)}, f32[128,128]{1,0:T(8,128)S(1)}, u32[]{:S(2)}, u32[]{:S(2)}) collective-permute-start(f32[128,128]{1,0:T(8,128)S(1)} %get-tuple-element.51), channel_id=1, source_target_pairs={{0,28},{1,29},{2,30},{3,31},{4,8},{5,9},{6,10},{7,11},{8,4},{9,5},... | collective-permute-start | bytes 196616 | tf_op jit(solution)/shard_map/ppermute | solution.py:672
  20.2 1.5 %collective-permute-start.9 = (f32[128,128]{1,0:T(8,128)S(1)}, f32[128,128]{1,0:T(8,128)S(1)}, u32[]{:S(2)}, u32[]{:S(2)}) collective-permute-start(f32[128,128]{1,0:T(8,128)S(1)} %get-tuple-element.52), channel_id=1, source_target_pairs={{0,4},{1,5},{2,6},{3,7},{4,0},{5,1},{6,2},{7,3},{8,12},{9,13},{10,... | collective-permute-start | bytes 196616 | tf_op jit(solution)/shard_map/ppermute | solution.py:672

commit v11 on v10

--- a/solution.py
+++ b/solution.py
@@ -602,6 +602,19 @@
 
 
 def final_kernel(flags, pitch_b, pitch_a, near, out, result, faces, lifted, done):
+    copies = []
+
+    def send(origin, part):
+        grouped = (5, 5, 50, 1, LANES)
+        copy = pltpu.make_async_copy(
+            origin.reshape(*grouped).at[part], out.reshape(*grouped).at[part], done.at[len(copies)]
+        )
+        copy.start()
+        copies.append(copy)
+
+    odd = lax.axis_index("pitch") % 2
+    every, behind = (pl.ds(0, 5), pl.ds(1, 4))
+    send(near, (every, behind, pl.ds(10 - 10 * odd, 40)))
     flat = result.reshape(result.shape[0], LANES)
     flat[...] = near.reshape(near.shape[0], LANES)[...]
     pitch_odd, _ = parities()
@@ -630,11 +643,8 @@
         for v in range(5):
             add(v * 250 + e, 2, jnp.where(cols == 0, inlet[v], 0.0))
 
-    copies = []
-    for v in range(5):
-        part = pl.ds(v * 250, 250)
-        copies.append(pltpu.make_async_copy(result.at[part], out.at[part], done.at[v]))
-        copies[-1].start()
+    send(result, (every, pl.ds(0, 1), pl.ds(0, 50)))
+    send(result, (every, behind, pl.ds(40 * odd, 10)))
     for copy in copies:
         copy.wait()
 
@@ -763,7 +773,7 @@
             pltpu.VMEM(x.shape, F32),
             pltpu.VMEM((BLOCK + 2 * FACE_PAD, LANES), F32),
             pltpu.VMEM((BLOCK, LANES), F32),
-            pltpu.SemaphoreType.DMA((5,)),
+            pltpu.SemaphoreType.DMA((3,)),
         ],
         flops=10**8,
         out_spec=pl.BlockSpec(memory_space=pl.ANY),

time: 24.9 us -> 24.7 us (level)
  transfers between devices with their start and end apart: 12 -> 12, of which waited for: 3 -> 3; matrix products, arithmetic and copies ran while one was open for 0% -> 0% of each run, Pallas kernels for 26% -> 27%
where the time goes in v11:
time: 24.7 us; the launch traced here: 24.6 us
  starting transfers between devices  12.2 us (49%)
  Pallas kernels  7.94 us (32%)
  waiting for transfers between devices  3.11 us (13%)
  local copies, waits for them, and re-layouts  1.11 us (4%)
    ppermute x12, starting transfers between devices, swapped(): return lax.ppermute(value, ('pitch', 'span'), pairs)  12.2 us
    pallas_call x11, Pallas kernels, call(): pl.pallas_call(kernel, name=name, out_shape=[jax.ShapeDtypeStruct(shape,...  7.94 us
    ppermute x12, waiting for transfers between devices, swapped(): return lax.ppermute(value, ('pitch', 'span'), pairs)  3.11 us
    unnamed x12, local copies, waits for them, and re-layouts  1.11 us
  transfers between devices with their start and end apart: 12, of which 3 were waited for; matrix products, arithmetic and copies ran while one was open for 0% of the time, Pallas kernels for 27%

profile of v11, /device:TPU:0, one launch (start us, length us, event | category | flops | bytes accessed | tf_op | source)
XLA Modules:
  0.0 24.6 jit_solution(1557181095746655401)
XLA Ops:
  0.0 0.0 copy-start.2
  0.0 1.1 %copy-done.2 = f32[5,5,5,5,2,1,128]{6,5,4,3,2,1,0:T(1,128)S(1)} copy-done((f32[5,5,5,5,2,1,128]{6,5,4,3,2,1,0:T(1,128)S(1)}, f32[5,5,5,5,2,1,128]{6,5,4,3,2,1,0:T(1,128)}, u32[]{:S(2)}) %copy-start.2) | copy-done | bytes 640024
  1.1 0.0 copy-start.4
  1.1 3.1 %collective-permute-start.2 = (f32[104,256]{1,0:T(8,128)S(1)}, f32[104,256]{1,0:T(8,128)S(1)}, u32[]{:S(2)}, u32[]{:S(2)}) collective-permute-start(f32[104,256]{1,0:T(8,128)S(1)} %get-tuple-element.35), channel_id=1, source_target_pairs={{0,1},{1,0},{2,3},{3,2},{4,5},{5,4},{6,7},{7,6},{8,9},{9,8},{10,11... | collective-permute-start | bytes 319496 | tf_op jit(solution)/shard_map/ppermute | solution.py:682
  4.2 0.0 collective-permute-start.3
  4.2 0.0 copy-done.4
  4.2 0.0 copy-start.1
  4.2 0.0 copy-start.3
  4.2 0.0 copy-start.5
  4.3 0.1 begin_pitch.1
  4.4 0.0 copy-start
  4.4 2.6 %collective-permute-start = (f32[128,128]{1,0:T(8,128)S(1)}, f32[128,128]{1,0:T(8,128)S(1)}, u32[]{:S(2)}, u32[]{:S(2)}) collective-permute-start(f32[128,128]{1,0:T(8,128)S(1)} %get-tuple-element.33), channel_id=1, source_target_pairs={{0,28},{1,29},{2,30},{3,31},{4,8},{5,9},{6,10},{7,11},{8,4},{9,5},... | collective-permute-start | bytes 196616 | tf_op jit(solution)/shard_map/ppermute | solution.py:682
  7.0 0.0 collective-permute-start.1
  7.0 0.0 copy-done.1
  7.0 0.0 copy-done.3
  7.0 0.0 copy-done.5
  7.0 1.9 %first.1 = (f32[640,256]{1,0:T(8,128)S(1)}, f32[640,256]{1,0:T(8,128)S(1)}, f32[512,256]{1,0:T(8,128)S(1)}, f32[8,128]{1,0:T(8,128)S(1)}) custom-call(s32[3]{0:T(128)S(1)} %copy-done.5, f32[1250,1,128]{2,1,0:T(1,128)S(1)} %bitcast.9, bf16[1792,640]{1,0:T(8,128)(2,1)S(1)} %copy-done.1), custom_call_target="tpu_custom_call" | custom-call | flops 1000000000 | bytes 1048576 | tf_op jit(solution)/shard_map/first/pallas_call | solution.py:658
  8.9 0.0 collective-permute-done.1.pitch_a
  8.9 0.0 collective-permute-done.2.span_a
  8.9 0.0 collective-permute-done.3.span_b
  9.0 0.0 copy-done
  9.0 0.3 %near.2 = (f32[512,256]{1,0:T(8,128)S(1)}, bf16[512,256]{1,0:T(8,128)(2,1)S(1)}, bf16[512,256]{1,0:T(8,128)(2,1)S(1)}) custom-call(f32[104,256]{1,0:T(8,128)S(1)} %collective-permute-done.2.span_a, f32[104,256]{1,0:T(8,128)S(1)} %collective-permute-done.3.span_b, f32[128,128]{1,0:T(8,128)S(1)} %collective-permute-done.1.pitch_a, ...), custom_call_target="tpu_custom_call" | custom-call | flops 100000000 | bytes 1048576 | tf_op jit(solution)/shard_map/near/pallas_call | solution.py:658
  9.3 0.0 collective-permute-done.pitch_b
  9.3 0.2 far.2
  9.6 3.5 %collective-permute-start.6 = (f32[104,256]{1,0:T(8,128)S(1)}, f32[104,256]{1,0:T(8,128)S(1)}, u32[]{:S(2)}, u32[]{:S(2)}) collective-permute-start(f32[104,256]{1,0:T(8,128)S(1)} %get-tuple-element.42), channel_id=1, source_target_pairs={{0,1},{1,0},{2,3},{3,2},{4,5},{5,4},{6,7},{7,6},{8,9},{9,8},{10,11... | collective-permute-start | bytes 319496 | tf_op jit(solution)/shard_map/ppermute | solution.py:682
  13.1 0.0 collective-permute-start.7
  13.1 1.2 %collective-permute-start.4 = (f32[128,128]{1,0:T(8,128)S(1)}, f32[128,128]{1,0:T(8,128)S(1)}, u32[]{:S(2)}, u32[]{:S(2)}) collective-permute-start(f32[128,128]{1,0:T(8,128)S(1)} %get-tuple-element.40), channel_id=1, source_target_pairs={{0,28},{1,29},{2,30},{3,31},{4,8},{5,9},{6,10},{7,11},{8,4},{9,5},... | collective-permute-start | bytes 196616 | tf_op jit(solution)/shard_map/ppermute | solution.py:682
  14.3 0.0 collective-permute-start.5
  14.3 2.0 %later.1 = (f32[640,256]{1,0:T(8,128)S(1)}, f32[512,256]{1,0:T(8,128)S(1)}) custom-call(f32[640,256]{1,0:T(8,128)S(1)} %get-tuple-element.45.base, f32[640,256]{1,0:T(8,128)S(1)} %get-tuple-element.46.before, bf16[512,256]{1,0:T(8,128)(2,1)S(1)} %get-tuple-element.47.near_high, bf16[512,256]{1,0:T(8,128)(2,1)S(1)} %get-tuple-element.48.near_low, ...), custom_call_target="tpu_custom_call" | custom-call | flops 1000000000 | bytes 1048576 | tf_op jit(solution)/shard_map/later/pallas_call | solution.py:658
  16.4 0.0 collective-permute-done.5.pitch_a
  16.4 0.0 collective-permute-done.6.span_a
  16.4 0.0 collective-permute-done.7.span_b
  16.4 0.3 %near.3 = (f32[512,256]{1,0:T(8,128)S(1)}, bf16[512,256]{1,0:T(8,128)(2,1)S(1)}, bf16[512,256]{1,0:T(8,128)(2,1)S(1)}) custom-call(f32[104,256]{1,0:T(8,128)S(1)} %collective-permute-done.6.span_a, f32[104,256]{1,0:T(8,128)S(1)} %collective-permute-done.7.span_b, f32[128,128]{1,0:T(8,128)S(1)} %collective-permute-done.5.pitch_a, ...), custom_call_target="tpu_custom_call" | custom-call | flops 100000000 | bytes 1048576 | tf_op jit(solution)/shard_map/near/pallas_call | solution.py:658
  16.7 1.5 %collective-permute-done.4.pitch_b = f32[128,128]{1,0:T(8,128)S(1)} collective-permute-done((f32[128,128]{1,0:T(8,128)S(1)}, f32[128,128]{1,0:T(8,128)S(1)}, u32[]{:S(2)}, u32[]{:S(2)}) %collective-permute-start.4) | collective-permute-done | bytes 65568 | tf_op jit(solution)/shard_map/ppermute | solution.py:682
  18.2 0.2 far.3
  18.4 0.1 collective-permute-start.10
  18.5 0.1 collective-permute-start.11
  18.6 1.6 %collective-permute-start.8 = (f32[128,128]{1,0:T(8,128)S(1)}, f32[128,128]{1,0:T(8,128)S(1)}, u32[]{:S(2)}, u32[]{:S(2)}) collective-permute-start(f32[128,128]{1,0:T(8,128)S(1)} %get-tuple-element.51), channel_id=1, source_target_pairs={{0,28},{1,29},{2,30},{3,31},{4,8},{5,9},{6,10},{7,11},{8,4},{9,5},... | collective-permute-start | bytes 196616 | tf_op jit(solution)/shard_map/ppermute | solution.py:682
  20.2 0.0 collective-permute-start.9
  20.2 1.5 %last.1.before = f32[1250,1,128]{2,1,0:T(1,128)S(1)} custom-call(f32[640,256]{1,0:T(8,128)S(1)} %get-tuple-element.45.base, f32[640,256]{1,0:T(8,128)S(1)} %get-tuple-element.56.before, bf16[512,256]{1,0:T(8,128)(2,1)S(1)} %get-tuple-element.57.near_high, bf16[512,256]{1,0:T(8,128)(2,1)S(1)} %get-tuple-element.58.near_low, ...), custom_call_target="tpu_custom_call" | custom-call | flops 1000000000 | bytes 1048576 | tf_op jit(solution)/shard_map/last/pallas_call | solution.py:658
  21.7 0.0 collective-permute-done.9.pitch_a
  21.8 1.5 %collective-permute-done.10.span_a = f32[104,256]{1,0:T(8,128)S(1)} collective-permute-done((f32[104,256]{1,0:T(8,128)S(1)}, f32[104,256]{1,0:T(8,128)S(1)}, u32[]{:S(2)}, u32[]{:S(2)}) %collective-permute-start.10) | collective-permute-done | bytes 106528 | tf_op jit(solution)/shard_map/ppermute | solution.py:682
  23.2 0.0 collective-permute-done.11.span_b
  23.2 0.3 %final_near.1.near = f32[1250,1,128]{2,1,0:T(1,128)S(1)} custom-call(f32[104,256]{1,0:T(8,128)S(1)} %collective-permute-done.10.span_a, f32[104,256]{1,0:T(8,128)S(1)} %collective-permute-done.11.span_b, f32[128,128]{1,0:T(8,128)S(1)} %collective-permute-done.9.pitch_a, f32[256,128]{1,0:T(8,128)S(1)} %get-tuple-element.55.inner, f32[1250,1,128]{2,1,0:T(1,128)S(1)} %last.1.before), custom_call_target="tpu_custom_call" | custom-call | flops 100000000 | bytes 1048576 | tf_op jit(solution)/shard_map/final_near/pallas_call | solution.py:658
  23.5 0.2 collective-permute-done.8.pitch_b
  23.6 0.9 %final.1 = f32[1250,1,128]{2,1,0:T(1,128)} custom-call(f32[8,128]{1,0:T(8,128)S(1)} %get-tuple-element.32.flags, f32[128,128]{1,0:T(8,128)S(1)} %collective-permute-done.8.pitch_b, f32[128,128]{1,0:T(8,128)S(1)} %collective-permute-done.9.pitch_a, f32[1250,1,128]{2,1,0:T(1,128)S(1)} %final_near.1.near), custom_call_target="tpu_custom_call" | custom-call | flops 100000000 | bytes 1048576 | tf_op jit(solution)/shard_map/final/pallas_call | solution.py:658
  (1 shorter events, 0.0 us)
Async XLA Ops:
  0.0 1.1 %copy-start.2 = (f32[5,5,5,5,2,1,128]{6,5,4,3,2,1,0:T(1,128)S(1)}, f32[5,5,5,5,2,1,128]{6,5,4,3,2,1,0:T(1,128)}, u32[]{:S(2)}) copy-start(f32[5,5,5,5,2,1,128]{6,5,4,3,2,1,0:T(1,128)} %param.5) | copy-start | bytes 1920004
  1.1 3.1 %copy-start.4 = (f32[5,5,5,2,1]{2,4,3,1,0:T(1,128)S(1)}, f32[5,5,5,2,1]{2,4,3,1,0:T(1,128)}, u32[]{:S(2)}) copy-start(f32[5,5,5,2,1]{2,4,3,1,0:T(1,128)} %param.6) | copy-start | bytes 3004
  1.1 7.8 %collective-permute-start.2 = (f32[104,256]{1,0:T(8,128)S(1)}, f32[104,256]{1,0:T(8,128)S(1)}, u32[]{:S(2)}, u32[]{:S(2)}) collective-permute-start(f32[104,256]{1,0:T(8,128)S(1)} %get-tuple-element.35), channel_id=1, source_target_pairs={{0,1},{1,0},{2,3},{3,2},{4,5},{5,4},{6,7},{7,6},{8,9},{9,8},{10,11... | collective-permute-start | bytes 319496 | tf_op jit(solution)/shard_map/ppermute | solution.py:682
  4.2 4.7 %collective-permute-start.3 = (f32[104,256]{1,0:T(8,128)S(1)}, f32[104,256]{1,0:T(8,128)S(1)}, u32[]{:S(2)}, u32[]{:S(2)}) collective-permute-start(f32[104,256]{1,0:T(8,128)S(1)} %get-tuple-element.36), channel_id=1, source_target_pairs={{0,4},{1,2},{2,1},{3,7},{4,0},{5,6},{6,5},{7,3},{8,12},{9,10},{10,... | collective-permute-start | bytes 319496 | tf_op jit(solution)/shard_map/ppermute | solution.py:682
  4.2 2.8 %copy-start.1 = (bf16[1792,640]{1,0:T(8,128)(2,1)S(1)}, bf16[1792,640]{1,0:T(8,128)(2,1)}, u32[]{:S(2)}) copy-start(bf16[1792,640]{1,0:T(8,128)(2,1)} %constant.4.clone.table) | copy-start | bytes 6881284
  4.2 2.8 %copy-start.3 = (f32[5,5,5,5,2,1,128]{6,5,4,3,2,1,0:T(1,128)S(1)}, f32[5,5,5,5,2,1,128]{6,5,4,3,2,1,0:T(1,128)}, u32[]{:S(2)}) copy-start(f32[5,5,5,5,2,1,128]{6,5,4,3,2,1,0:T(1,128)} %param.5) | copy-start | bytes 1920004
  4.2 2.8 %copy-start.5 = (s32[3]{0:T(128)S(1)}, s32[3]{0:T(128)}, u32[]{:S(2)}) copy-start(s32[3]{0:T(128)} %offsets.1) | copy-start | bytes 40
  4.4 4.6 %copy-start = (bf16[1312,640]{1,0:T(8,128)(2,1)S(1)}, bf16[1312,640]{1,0:T(8,128)(2,1)}, u32[]{:S(2)}) copy-start(bf16[1312,640]{1,0:T(8,128)(2,1)} %constant.5.clone.links) | copy-start | bytes 5038084
  4.4 4.9 %collective-permute-start = (f32[128,128]{1,0:T(8,128)S(1)}, f32[128,128]{1,0:T(8,128)S(1)}, u32[]{:S(2)}, u32[]{:S(2)}) collective-permute-start(f32[128,128]{1,0:T(8,128)S(1)} %get-tuple-element.33), channel_id=1, source_target_pairs={{0,28},{1,29},{2,30},{3,31},{4,8},{5,9},{6,10},{7,11},{8,4},{9,5},... | collective-permute-start | bytes 196616 | tf_op jit(solution)/shard_map/ppermute | solution.py:682
  7.0 1.9 %collective-permute-start.1 = (f32[128,128]{1,0:T(8,128)S(1)}, f32[128,128]{1,0:T(8,128)S(1)}, u32[]{:S(2)}, u32[]{:S(2)}) collective-permute-start(f32[128,128]{1,0:T(8,128)S(1)} %get-tuple-element.34), channel_id=1, source_target_pairs={{0,4},{1,5},{2,6},{3,7},{4,0},{5,1},{6,2},{7,3},{8,12},{9,13},{10,... | collective-permute-start | bytes 196616 | tf_op jit(solution)/shard_map/ppermute | solution.py:682
  9.6 6.8 %collective-permute-start.6 = (f32[104,256]{1,0:T(8,128)S(1)}, f32[104,256]{1,0:T(8,128)S(1)}, u32[]{:S(2)}, u32[]{:S(2)}) collective-permute-start(f32[104,256]{1,0:T(8,128)S(1)} %get-tuple-element.42), channel_id=1, source_target_pairs={{0,1},{1,0},{2,3},{3,2},{4,5},{5,4},{6,7},{7,6},{8,9},{9,8},{10,11... | collective-permute-start | bytes 319496 | tf_op jit(solution)/shard_map/ppermute | solution.py:682
  13.1 3.3 %collective-permute-start.7 = (f32[104,256]{1,0:T(8,128)S(1)}, f32[104,256]{1,0:T(8,128)S(1)}, u32[]{:S(2)}, u32[]{:S(2)}) collective-permute-start(f32[104,256]{1,0:T(8,128)S(1)} %get-tuple-element.43), channel_id=1, source_target_pairs={{0,4},{1,2},{2,1},{3,7},{4,0},{5,6},{6,5},{7,3},{8,12},{9,10},{10,... | collective-permute-start | bytes 319496 | tf_op jit(solution)/shard_map/ppermute | solution.py:682
  13.1 5.1 %collective-permute-start.4 = (f32[128,128]{1,0:T(8,128)S(1)}, f32[128,128]{1,0:T(8,128)S(1)}, u32[]{:S(2)}, u32[]{:S(2)}) collective-permute-start(f32[128,128]{1,0:T(8,128)S(1)} %get-tuple-element.40), channel_id=1, source_target_pairs={{0,28},{1,29},{2,30},{3,31},{4,8},{5,9},{6,10},{7,11},{8,4},{9,5},... | collective-permute-start | bytes 196616 | tf_op jit(solution)/shard_map/ppermute | solution.py:682
  14.3 2.1 %collective-permute-start.5 = (f32[128,128]{1,0:T(8,128)S(1)}, f32[128,128]{1,0:T(8,128)S(1)}, u32[]{:S(2)}, u32[]{:S(2)}) collective-permute-start(f32[128,128]{1,0:T(8,128)S(1)} %get-tuple-element.41), channel_id=1, source_target_pairs={{0,4},{1,5},{2,6},{3,7},{4,0},{5,1},{6,2},{7,3},{8,12},{9,13},{10,... | collective-permute-start | bytes 196616 | tf_op jit(solution)/shard_map/ppermute | solution.py:682
  18.4 4.8 %collective-permute-start.10 = (f32[104,256]{1,0:T(8,128)S(1)}, f32[104,256]{1,0:T(8,128)S(1)}, u32[]{:S(2)}, u32[]{:S(2)}) collective-permute-start(f32[104,256]{1,0:T(8,128)S(1)} %get-tuple-element.53), channel_id=1, source_target_pairs={{0,1},{1,0},{2,3},{3,2},{4,5},{5,4},{6,7},{7,6},{8,9},{9,8},{10,11... | collective-permute-start | bytes 319496 | tf_op jit(solution)/shard_map/ppermute | solution.py:682
  18.5 4.7 %collective-permute-start.11 = (f32[104,256]{1,0:T(8,128)S(1)}, f32[104,256]{1,0:T(8,128)S(1)}, u32[]{:S(2)}, u32[]{:S(2)}) collective-permute-start(f32[104,256]{1,0:T(8,128)S(1)} %get-tuple-element.54), channel_id=1, source_target_pairs={{0,4},{1,2},{2,1},{3,7},{4,0},{5,6},{6,5},{7,3},{8,12},{9,10},{10,... | collective-permute-start | bytes 319496 | tf_op jit(solution)/shard_map/ppermute | solution.py:682
  18.6 5.0 %collective-permute-start.8 = (f32[128,128]{1,0:T(8,128)S(1)}, f32[128,128]{1,0:T(8,128)S(1)}, u32[]{:S(2)}, u32[]{:S(2)}) collective-permute-start(f32[128,128]{1,0:T(8,128)S(1)} %get-tuple-element.51), channel_id=1, source_target_pairs={{0,28},{1,29},{2,30},{3,31},{4,8},{5,9},{6,10},{7,11},{8,4},{9,5},... | collective-permute-start | bytes 196616 | tf_op jit(solution)/shard_map/ppermute | solution.py:682
  20.2 1.5 %collective-permute-start.9 = (f32[128,128]{1,0:T(8,128)S(1)}, f32[128,128]{1,0:T(8,128)S(1)}, u32[]{:S(2)}, u32[]{:S(2)}) collective-permute-start(f32[128,128]{1,0:T(8,128)S(1)} %get-tuple-element.52), channel_id=1, source_target_pairs={{0,4},{1,5},{2,6},{3,7},{4,0},{5,1},{6,2},{7,3},{8,12},{9,13},{10,... | collective-permute-start | bytes 196616 | tf_op jit(solution)/shard_map/ppermute | solution.py:682

commit v12 on v11

--- a/solution.py
+++ b/solution.py
@@ -428,6 +428,23 @@
         )
 
 
+def weights(table, choice, cols, lane):
+    total = jnp.zeros(choice.shape, jnp.float32)
+    for v in range(5):
+        values = [float(table[i, v]) for i in range(table.shape[0])]
+        if any(values):
+            factor = sum(
+                jnp.where(choice == i, value, 0.0) for i, value in enumerate(values) if value
+            )
+            total = total + jnp.where(cols == 25 * v + lane, factor, 0.0)
+    return total
+
+
+def inlet_column(part, row):
+    cols = lax.broadcasted_iota(jnp.int32, part.shape, 1)
+    return jnp.where(cols == 0, jnp.sum(part * row, axis=1, keepdims=True), 0.0)
+
+
 def far_lift(gain, pitch_b, faces):
     pitch_odd, _ = parities()
     faces[FACE_PAD : FACE_PAD + BLOCK] = pitch_b[...]
@@ -481,39 +498,23 @@
     cols = lax.broadcasted_iota(jnp.int32, (25, LANES), 1)
     node = sum((rows >= 5 * k).astype(jnp.int32) for k in range(1, 5))
     variable = rows - 5 * node
-    scale = gain * lift_factor(0)
-    inflow = half_flux(0, 1.0)
-
-    def weights(table, choice, lane):
-        total = jnp.zeros(choice.shape, jnp.float32)
-        for v in range(5):
-            values = [float(scale * table[i, v]) for i in range(table.shape[0])]
-            if any(values):
-                factor = sum(
-                    jnp.where(choice == i, value, 0.0) for i, value in enumerate(values) if value
-                )
-                total = total + jnp.where(cols[: choice.shape[0]] == 25 * v + lane, factor, 0.0)
-        return total
-
-    def column(part, row):
-        total = jnp.sum(part * row, axis=1, keepdims=True)
-        return jnp.where(cols[: part.shape[0]] == 0, total, 0.0)
+    inflow = gain * lift_factor(0) * half_flux(0, 1.0)
 
     pitch_parts = [
-        (block, weights(inflow, variable, 5 * p + node)) for block, p in ((0, 4), (1, 0))
+        (block, weights(inflow, variable, cols, 5 * p + node)) for block, p in ((0, 4), (1, 0))
     ]
     span_parts = []
     for block, s, sign in ((2, 4, 1.0), (3, 0, -1.0)):
         sent = half_flux(2, sign)[:4] @ inflow
         for c in range(4):
-            part = weights(sent[c : c + 1], rows[:5] * 0, 5 * rows[:5] + s)
+            part = weights(sent[c : c + 1], rows[:5] * 0, cols[:5], 5 * rows[:5] + s)
             span_parts.append((block * BLOCK + c * 25, part))
     for e in range(2):
         row = inlet_row(section, flags, wake, e)
         for block, part in pitch_parts:
-            inlets[e][pl.ds(block * BLOCK, 25, stride=5), :] = column(part, row)
+            inlets[e][pl.ds(block * BLOCK, 25, stride=5), :] = inlet_column(part, row)
         for start, part in span_parts:
-            inlets[e][start : start + 5] = column(part, row)
+            inlets[e][start : start + 5] = inlet_column(part, row)
 
     both = jnp.concatenate([traces[e][...] + inlets[e][...] for e in range(2)], axis=1)
     emit_span_faces(both[2 * BLOCK :], span_odd, next_span_a, next_span_b)
@@ -615,33 +616,30 @@
     odd = lax.axis_index("pitch") % 2
     every, behind = (pl.ds(0, 5), pl.ds(1, 4))
     send(near, (every, behind, pl.ds(10 - 10 * odd, 40)))
+    source = near.reshape(near.shape[0], LANES)
     flat = result.reshape(result.shape[0], LANES)
-    flat[...] = near.reshape(near.shape[0], LANES)[...]
+    flat[...] = source[...]
     pitch_odd, _ = parities()
     gain = GAIN[2]
-
-    def add(start, stride, values):
-        at = pl.ds(start, values.shape[0], stride=stride)
-        flat[at, :] = flat[at, :] + values
 
     lifted[...] = far_lift(gain, pitch_b, faces)
     for s in range(5):
         values = lifted[s * 25 : s * 25 + 25]
-        add(40 + 2 * s + 1, 50, jnp.where(pitch_odd, values, 0.0))
-        add(2 * s, 50, jnp.where(pitch_odd, 0.0, values))
+        for start, own in ((40 + 2 * s + 1, True), (2 * s, False)):
+            at = pl.ds(start, 25, stride=50)
+            added = jnp.where(pitch_odd, values, 0.0) if own else jnp.where(pitch_odd, 0.0, values)
+            flat[at, :] = source[at, :] + added
 
     wake = arrived_wake(pitch_a, pitch_b)
     rows = lax.broadcasted_iota(jnp.int32, (25, LANES), 0)
     cols = lax.broadcasted_iota(jnp.int32, (25, LANES), 1)
+    inflow = gain * lift_factor(0) * half_flux(0, 1.0)
+    parts = [weights(inflow[v : v + 1], rows * 0, cols, rows) for v in range(5)]
     for e in range(2):
         row = inlet_row(2, flags, wake, e)
-        columns = [
-            jnp.sum(jnp.where(cols == rows + 25 * v, row, 0.0), axis=1, keepdims=True)
-            for v in range(5)
-        ]
-        inlet = combine(gain * lift_factor(0) * half_flux(0, 1.0), columns)
         for v in range(5):
-            add(v * 250 + e, 2, jnp.where(cols == 0, inlet[v], 0.0))
+            at = pl.ds(v * 250 + e, 25, stride=2)
+            flat[at, :] = flat[at, :] + inlet_column(parts[v], row)
 
     send(result, (every, pl.ds(0, 1), pl.ds(0, 50)))
     send(result, (every, behind, pl.ds(40 * odd, 10)))

time: 24.7 us -> 24.7 us (level)
  no operation moved by 1% of the time
where the time goes in v12:
time: 24.7 us; the launch traced here: 24.6 us
  starting transfers between devices  12.2 us (49%)
  Pallas kernels  7.94 us (32%)
  waiting for transfers between devices  3.11 us (13%)
  local copies, waits for them, and re-layouts  1.11 us (4%)
    ppermute x12, starting transfers between devices, swapped(): return lax.ppermute(value, ('pitch', 'span'), pairs)  12.2 us
    pallas_call x11, Pallas kernels, call(): pl.pallas_call(kernel, name=name, out_shape=[jax.ShapeDtypeStruct(shape,...  7.94 us
    ppermute x12, waiting for transfers between devices, swapped(): return lax.ppermute(value, ('pitch', 'span'), pairs)  3.11 us
    unnamed x12, local copies, waits for them, and re-layouts  1.11 us
  transfers between devices with their start and end apart: 12, of which 3 were waited for; matrix products, arithmetic and copies ran while one was open for 0% of the time, Pallas kernels for 27%

profile of v12, /device:TPU:0, one launch (start us, length us, event | category | flops | bytes accessed | tf_op | source)
XLA Modules:
  0.0 24.6 jit_solution(14483667556576944143)
XLA Ops:
  0.0 0.0 copy-start.2
  0.0 1.1 %copy-done.2 = f32[5,5,5,5,2,1,128]{6,5,4,3,2,1,0:T(1,128)S(1)} copy-done((f32[5,5,5,5,2,1,128]{6,5,4,3,2,1,0:T(1,128)S(1)}, f32[5,5,5,5,2,1,128]{6,5,4,3,2,1,0:T(1,128)}, u32[]{:S(2)}) %copy-start.2) | copy-done | bytes 640024
  1.1 0.0 copy-start.4
  1.1 3.1 %collective-permute-start.2 = (f32[104,256]{1,0:T(8,128)S(1)}, f32[104,256]{1,0:T(8,128)S(1)}, u32[]{:S(2)}, u32[]{:S(2)}) collective-permute-start(f32[104,256]{1,0:T(8,128)S(1)} %get-tuple-element.35), channel_id=1, source_target_pairs={{0,1},{1,0},{2,3},{3,2},{4,5},{5,4},{6,7},{7,6},{8,9},{9,8},{10,11... | collective-permute-start | bytes 319496 | tf_op jit(solution)/shard_map/ppermute | solution.py:680
  4.2 0.0 collective-permute-start.3
  4.2 0.0 copy-done.4
  4.2 0.0 copy-start.1
  4.2 0.0 copy-start.3
  4.2 0.0 copy-start.5
  4.3 0.1 begin_pitch.1
  4.4 0.0 copy-start
  4.4 2.6 %collective-permute-start = (f32[128,128]{1,0:T(8,128)S(1)}, f32[128,128]{1,0:T(8,128)S(1)}, u32[]{:S(2)}, u32[]{:S(2)}) collective-permute-start(f32[128,128]{1,0:T(8,128)S(1)} %get-tuple-element.33), channel_id=1, source_target_pairs={{0,28},{1,29},{2,30},{3,31},{4,8},{5,9},{6,10},{7,11},{8,4},{9,5},... | collective-permute-start | bytes 196616 | tf_op jit(solution)/shard_map/ppermute | solution.py:680
  7.0 0.0 collective-permute-start.1
  7.0 0.0 copy-done.1
  7.0 0.0 copy-done.3
  7.0 0.0 copy-done.5
  7.0 1.9 %first.1 = (f32[640,256]{1,0:T(8,128)S(1)}, f32[640,256]{1,0:T(8,128)S(1)}, f32[512,256]{1,0:T(8,128)S(1)}, f32[8,128]{1,0:T(8,128)S(1)}) custom-call(s32[3]{0:T(128)S(1)} %copy-done.5, f32[1250,1,128]{2,1,0:T(1,128)S(1)} %bitcast.9, bf16[1792,640]{1,0:T(8,128)(2,1)S(1)} %copy-done.1), custom_call_target="tpu_custom_call" | custom-call | flops 1000000000 | bytes 1048576 | tf_op jit(solution)/shard_map/first/pallas_call | solution.py:656
  8.9 0.0 collective-permute-done.1.pitch_a
  8.9 0.0 collective-permute-done.2.span_a
  8.9 0.0 collective-permute-done.3.span_b
  9.0 0.0 copy-done
  9.0 0.3 %near.2 = (f32[512,256]{1,0:T(8,128)S(1)}, bf16[512,256]{1,0:T(8,128)(2,1)S(1)}, bf16[512,256]{1,0:T(8,128)(2,1)S(1)}) custom-call(f32[104,256]{1,0:T(8,128)S(1)} %collective-permute-done.2.span_a, f32[104,256]{1,0:T(8,128)S(1)} %collective-permute-done.3.span_b, f32[128,128]{1,0:T(8,128)S(1)} %collective-permute-done.1.pitch_a, ...), custom_call_target="tpu_custom_call" | custom-call | flops 100000000 | bytes 1048576 | tf_op jit(solution)/shard_map/near/pallas_call | solution.py:656
  9.3 0.0 collective-permute-done.pitch_b
  9.3 0.2 far.2
  9.6 3.5 %collective-permute-start.6 = (f32[104,256]{1,0:T(8,128)S(1)}, f32[104,256]{1,0:T(8,128)S(1)}, u32[]{:S(2)}, u32[]{:S(2)}) collective-permute-start(f32[104,256]{1,0:T(8,128)S(1)} %get-tuple-element.42), channel_id=1, source_target_pairs={{0,1},{1,0},{2,3},{3,2},{4,5},{5,4},{6,7},{7,6},{8,9},{9,8},{10,11... | collective-permute-start | bytes 319496 | tf_op jit(solution)/shard_map/ppermute | solution.py:680
  13.1 0.0 collective-permute-start.7
  13.1 1.2 %collective-permute-start.4 = (f32[128,128]{1,0:T(8,128)S(1)}, f32[128,128]{1,0:T(8,128)S(1)}, u32[]{:S(2)}, u32[]{:S(2)}) collective-permute-start(f32[128,128]{1,0:T(8,128)S(1)} %get-tuple-element.40), channel_id=1, source_target_pairs={{0,28},{1,29},{2,30},{3,31},{4,8},{5,9},{6,10},{7,11},{8,4},{9,5},... | collective-permute-start | bytes 196616 | tf_op jit(solution)/shard_map/ppermute | solution.py:680
  14.3 0.0 collective-permute-start.5
  14.3 2.0 %later.1 = (f32[640,256]{1,0:T(8,128)S(1)}, f32[512,256]{1,0:T(8,128)S(1)}) custom-call(f32[640,256]{1,0:T(8,128)S(1)} %get-tuple-element.45.base, f32[640,256]{1,0:T(8,128)S(1)} %get-tuple-element.46.before, bf16[512,256]{1,0:T(8,128)(2,1)S(1)} %get-tuple-element.47.near_high, bf16[512,256]{1,0:T(8,128)(2,1)S(1)} %get-tuple-element.48.near_low, ...), custom_call_target="tpu_custom_call" | custom-call | flops 1000000000 | bytes 1048576 | tf_op jit(solution)/shard_map/later/pallas_call | solution.py:656
  16.4 0.0 collective-permute-done.5.pitch_a
  16.4 0.0 collective-permute-done.6.span_a
  16.4 0.0 collective-permute-done.7.span_b
  16.4 0.3 %near.3 = (f32[512,256]{1,0:T(8,128)S(1)}, bf16[512,256]{1,0:T(8,128)(2,1)S(1)}, bf16[512,256]{1,0:T(8,128)(2,1)S(1)}) custom-call(f32[104,256]{1,0:T(8,128)S(1)} %collective-permute-done.6.span_a, f32[104,256]{1,0:T(8,128)S(1)} %collective-permute-done.7.span_b, f32[128,128]{1,0:T(8,128)S(1)} %collective-permute-done.5.pitch_a, ...), custom_call_target="tpu_custom_call" | custom-call | flops 100000000 | bytes 1048576 | tf_op jit(solution)/shard_map/near/pallas_call | solution.py:656
  16.7 1.5 %collective-permute-done.4.pitch_b = f32[128,128]{1,0:T(8,128)S(1)} collective-permute-done((f32[128,128]{1,0:T(8,128)S(1)}, f32[128,128]{1,0:T(8,128)S(1)}, u32[]{:S(2)}, u32[]{:S(2)}) %collective-permute-start.4) | collective-permute-done | bytes 65568 | tf_op jit(solution)/shard_map/ppermute | solution.py:680
  18.2 0.2 far.3
  18.4 0.1 collective-permute-start.10
  18.5 0.1 collective-permute-start.11
  18.6 1.6 %collective-permute-start.8 = (f32[128,128]{1,0:T(8,128)S(1)}, f32[128,128]{1,0:T(8,128)S(1)}, u32[]{:S(2)}, u32[]{:S(2)}) collective-permute-start(f32[128,128]{1,0:T(8,128)S(1)} %get-tuple-element.51), channel_id=1, source_target_pairs={{0,28},{1,29},{2,30},{3,31},{4,8},{5,9},{6,10},{7,11},{8,4},{9,5},... | collective-permute-start | bytes 196616 | tf_op jit(solution)/shard_map/ppermute | solution.py:680
  20.2 0.0 collective-permute-start.9
  20.2 1.5 %last.1.before = f32[1250,1,128]{2,1,0:T(1,128)S(1)} custom-call(f32[640,256]{1,0:T(8,128)S(1)} %get-tuple-element.45.base, f32[640,256]{1,0:T(8,128)S(1)} %get-tuple-element.56.before, bf16[512,256]{1,0:T(8,128)(2,1)S(1)} %get-tuple-element.57.near_high, bf16[512,256]{1,0:T(8,128)(2,1)S(1)} %get-tuple-element.58.near_low, ...), custom_call_target="tpu_custom_call" | custom-call | flops 1000000000 | bytes 1048576 | tf_op jit(solution)/shard_map/last/pallas_call | solution.py:656
  21.7 0.0 collective-permute-done.9.pitch_a
  21.8 1.5 %collective-permute-done.10.span_a = f32[104,256]{1,0:T(8,128)S(1)} collective-permute-done((f32[104,256]{1,0:T(8,128)S(1)}, f32[104,256]{1,0:T(8,128)S(1)}, u32[]{:S(2)}, u32[]{:S(2)}) %collective-permute-start.10) | collective-permute-done | bytes 106528 | tf_op jit(solution)/shard_map/ppermute | solution.py:680
  23.2 0.0 collective-permute-done.11.span_b
  23.2 0.3 %final_near.1.near = f32[1250,1,128]{2,1,0:T(1,128)S(1)} custom-call(f32[104,256]{1,0:T(8,128)S(1)} %collective-permute-done.10.span_a, f32[104,256]{1,0:T(8,128)S(1)} %collective-permute-done.11.span_b, f32[128,128]{1,0:T(8,128)S(1)} %collective-permute-done.9.pitch_a, f32[256,128]{1,0:T(8,128)S(1)} %get-tuple-element.55.inner, f32[1250,1,128]{2,1,0:T(1,128)S(1)} %last.1.before), custom_call_target="tpu_custom_call" | custom-call | flops 100000000 | bytes 1048576 | tf_op jit(solution)/shard_map/final_near/pallas_call | solution.py:656
  23.5 0.2 collective-permute-done.8.pitch_b
  23.6 0.9 %final.1 = f32[1250,1,128]{2,1,0:T(1,128)} custom-call(f32[8,128]{1,0:T(8,128)S(1)} %get-tuple-element.32.flags, f32[128,128]{1,0:T(8,128)S(1)} %collective-permute-done.8.pitch_b, f32[128,128]{1,0:T(8,128)S(1)} %collective-permute-done.9.pitch_a, f32[1250,1,128]{2,1,0:T(1,128)S(1)} %final_near.1.near), custom_call_target="tpu_custom_call" | custom-call | flops 100000000 | bytes 1048576 | tf_op jit(solution)/shard_map/final/pallas_call | solution.py:656
  (1 shorter events, 0.0 us)
Async XLA Ops:
  0.0 1.1 %copy-start.2 = (f32[5,5,5,5,2,1,128]{6,5,4,3,2,1,0:T(1,128)S(1)}, f32[5,5,5,5,2,1,128]{6,5,4,3,2,1,0:T(1,128)}, u32[]{:S(2)}) copy-start(f32[5,5,5,5,2,1,128]{6,5,4,3,2,1,0:T(1,128)} %param.5) | copy-start | bytes 1920004
  1.1 3.1 %copy-start.4 = (f32[5,5,5,2,1]{2,4,3,1,0:T(1,128)S(1)}, f32[5,5,5,2,1]{2,4,3,1,0:T(1,128)}, u32[]{:S(2)}) copy-start(f32[5,5,5,2,1]{2,4,3,1,0:T(1,128)} %param.6) | copy-start | bytes 3004
  1.1 7.8 %collective-permute-start.2 = (f32[104,256]{1,0:T(8,128)S(1)}, f32[104,256]{1,0:T(8,128)S(1)}, u32[]{:S(2)}, u32[]{:S(2)}) collective-permute-start(f32[104,256]{1,0:T(8,128)S(1)} %get-tuple-element.35), channel_id=1, source_target_pairs={{0,1},{1,0},{2,3},{3,2},{4,5},{5,4},{6,7},{7,6},{8,9},{9,8},{10,11... | collective-permute-start | bytes 319496 | tf_op jit(solution)/shard_map/ppermute | solution.py:680
  4.2 4.7 %collective-permute-start.3 = (f32[104,256]{1,0:T(8,128)S(1)}, f32[104,256]{1,0:T(8,128)S(1)}, u32[]{:S(2)}, u32[]{:S(2)}) collective-permute-start(f32[104,256]{1,0:T(8,128)S(1)} %get-tuple-element.36), channel_id=1, source_target_pairs={{0,4},{1,2},{2,1},{3,7},{4,0},{5,6},{6,5},{7,3},{8,12},{9,10},{10,... | collective-permute-start | bytes 319496 | tf_op jit(solution)/shard_map/ppermute | solution.py:680
  4.2 2.8 %copy-start.1 = (bf16[1792,640]{1,0:T(8,128)(2,1)S(1)}, bf16[1792,640]{1,0:T(8,128)(2,1)}, u32[]{:S(2)}) copy-start(bf16[1792,640]{1,0:T(8,128)(2,1)} %constant.4.clone.table) | copy-start | bytes 6881284
  4.2 2.8 %copy-start.3 = (f32[5,5,5,5,2,1,128]{6,5,4,3,2,1,0:T(1,128)S(1)}, f32[5,5,5,5,2,1,128]{6,5,4,3,2,1,0:T(1,128)}, u32[]{:S(2)}) copy-start(f32[5,5,5,5,2,1,128]{6,5,4,3,2,1,0:T(1,128)} %param.5) | copy-start | bytes 1920004
  4.2 2.8 %copy-start.5 = (s32[3]{0:T(128)S(1)}, s32[3]{0:T(128)}, u32[]{:S(2)}) copy-start(s32[3]{0:T(128)} %offsets.1) | copy-start | bytes 40
  4.4 4.6 %copy-start = (bf16[1312,640]{1,0:T(8,128)(2,1)S(1)}, bf16[1312,640]{1,0:T(8,128)(2,1)}, u32[]{:S(2)}) copy-start(bf16[1312,640]{1,0:T(8,128)(2,1)} %constant.5.clone.links) | copy-start | bytes 5038084
  4.4 4.9 %collective-permute-start = (f32[128,128]{1,0:T(8,128)S(1)}, f32[128,128]{1,0:T(8,128)S(1)}, u32[]{:S(2)}, u32[]{:S(2)}) collective-permute-start(f32[128,128]{1,0:T(8,128)S(1)} %get-tuple-element.33), channel_id=1, source_target_pairs={{0,28},{1,29},{2,30},{3,31},{4,8},{5,9},{6,10},{7,11},{8,4},{9,5},... | collective-permute-start | bytes 196616 | tf_op jit(solution)/shard_map/ppermute | solution.py:680
  7.0 1.9 %collective-permute-start.1 = (f32[128,128]{1,0:T(8,128)S(1)}, f32[128,128]{1,0:T(8,128)S(1)}, u32[]{:S(2)}, u32[]{:S(2)}) collective-permute-start(f32[128,128]{1,0:T(8,128)S(1)} %get-tuple-element.34), channel_id=1, source_target_pairs={{0,4},{1,5},{2,6},{3,7},{4,0},{5,1},{6,2},{7,3},{8,12},{9,13},{10,... | collective-permute-start | bytes 196616 | tf_op jit(solution)/shard_map/ppermute | solution.py:680
  9.6 6.8 %collective-permute-start.6 = (f32[104,256]{1,0:T(8,128)S(1)}, f32[104,256]{1,0:T(8,128)S(1)}, u32[]{:S(2)}, u32[]{:S(2)}) collective-permute-start(f32[104,256]{1,0:T(8,128)S(1)} %get-tuple-element.42), channel_id=1, source_target_pairs={{0,1},{1,0},{2,3},{3,2},{4,5},{5,4},{6,7},{7,6},{8,9},{9,8},{10,11... | collective-permute-start | bytes 319496 | tf_op jit(solution)/shard_map/ppermute | solution.py:680
  13.1 3.3 %collective-permute-start.7 = (f32[104,256]{1,0:T(8,128)S(1)}, f32[104,256]{1,0:T(8,128)S(1)}, u32[]{:S(2)}, u32[]{:S(2)}) collective-permute-start(f32[104,256]{1,0:T(8,128)S(1)} %get-tuple-element.43), channel_id=1, source_target_pairs={{0,4},{1,2},{2,1},{3,7},{4,0},{5,6},{6,5},{7,3},{8,12},{9,10},{10,... | collective-permute-start | bytes 319496 | tf_op jit(solution)/shard_map/ppermute | solution.py:680
  13.1 5.1 %collective-permute-start.4 = (f32[128,128]{1,0:T(8,128)S(1)}, f32[128,128]{1,0:T(8,128)S(1)}, u32[]{:S(2)}, u32[]{:S(2)}) collective-permute-start(f32[128,128]{1,0:T(8,128)S(1)} %get-tuple-element.40), channel_id=1, source_target_pairs={{0,28},{1,29},{2,30},{3,31},{4,8},{5,9},{6,10},{7,11},{8,4},{9,5},... | collective-permute-start | bytes 196616 | tf_op jit(solution)/shard_map/ppermute | solution.py:680
  14.3 2.1 %collective-permute-start.5 = (f32[128,128]{1,0:T(8,128)S(1)}, f32[128,128]{1,0:T(8,128)S(1)}, u32[]{:S(2)}, u32[]{:S(2)}) collective-permute-start(f32[128,128]{1,0:T(8,128)S(1)} %get-tuple-element.41), channel_id=1, source_target_pairs={{0,4},{1,5},{2,6},{3,7},{4,0},{5,1},{6,2},{7,3},{8,12},{9,13},{10,... | collective-permute-start | bytes 196616 | tf_op jit(solution)/shard_map/ppermute | solution.py:680
  18.4 4.8 %collective-permute-start.10 = (f32[104,256]{1,0:T(8,128)S(1)}, f32[104,256]{1,0:T(8,128)S(1)}, u32[]{:S(2)}, u32[]{:S(2)}) collective-permute-start(f32[104,256]{1,0:T(8,128)S(1)} %get-tuple-element.53), channel_id=1, source_target_pairs={{0,1},{1,0},{2,3},{3,2},{4,5},{5,4},{6,7},{7,6},{8,9},{9,8},{10,11... | collective-permute-start | bytes 319496 | tf_op jit(solution)/shard_map/ppermute | solution.py:680
  18.5 4.7 %collective-permute-start.11 = (f32[104,256]{1,0:T(8,128)S(1)}, f32[104,256]{1,0:T(8,128)S(1)}, u32[]{:S(2)}, u32[]{:S(2)}) collective-permute-start(f32[104,256]{1,0:T(8,128)S(1)} %get-tuple-element.54), channel_id=1, source_target_pairs={{0,4},{1,2},{2,1},{3,7},{4,0},{5,6},{6,5},{7,3},{8,12},{9,10},{10,... | collective-permute-start | bytes 319496 | tf_op jit(solution)/shard_map/ppermute | solution.py:680
  18.6 5.0 %collective-permute-start.8 = (f32[128,128]{1,0:T(8,128)S(1)}, f32[128,128]{1,0:T(8,128)S(1)}, u32[]{:S(2)}, u32[]{:S(2)}) collective-permute-start(f32[128,128]{1,0:T(8,128)S(1)} %get-tuple-element.51), channel_id=1, source_target_pairs={{0,28},{1,29},{2,30},{3,31},{4,8},{5,9},{6,10},{7,11},{8,4},{9,5},... | collective-permute-start | bytes 196616 | tf_op jit(solution)/shard_map/ppermute | solution.py:680
  20.2 1.5 %collective-permute-start.9 = (f32[128,128]{1,0:T(8,128)S(1)}, f32[128,128]{1,0:T(8,128)S(1)}, u32[]{:S(2)}, u32[]{:S(2)}) collective-permute-start(f32[128,128]{1,0:T(8,128)S(1)} %get-tuple-element.52), channel_id=1, source_target_pairs={{0,4},{1,5},{2,6},{3,7},{4,0},{5,1},{6,2},{7,3},{8,12},{9,13},{10,... | collective-permute-start | bytes 196616 | tf_op jit(solution)/shard_map/ppermute | solution.py:680

commit v13 on v12

--- a/solution.py
+++ b/solution.py
@@ -35,7 +35,7 @@
 LIFT_AT = TRACES
 INLET_AT = LIFT_AT + ROWS
 LANES = 128
-VMEM_LIMIT = 24 * 1024 * 1024
+VMEM_LIMIT = 8 * 1024 * 1024
 
 
 def derivative_table():

time: 24.7 us -> 24.7 us (level)
  no operation moved by 1% of the time
where the time goes in v13:
time: 24.7 us; the launch traced here: 24.6 us
  starting transfers between devices  12.2 us (49%)
  Pallas kernels  7.94 us (32%)
  waiting for transfers between devices  3.11 us (13%)
  local copies, waits for them, and re-layouts  1.11 us (4%)
    ppermute x12, starting transfers between devices, swapped(): return lax.ppermute(value, ('pitch', 'span'), pairs)  12.2 us
    pallas_call x11, Pallas kernels, call(): pl.pallas_call(kernel, name=name, out_shape=[jax.ShapeDtypeStruct(shape,...  7.94 us
    ppermute x12, waiting for transfers between devices, swapped(): return lax.ppermute(value, ('pitch', 'span'), pairs)  3.11 us
    unnamed x12, local copies, waits for them, and re-layouts  1.11 us
  transfers between devices with their start and end apart: 12, of which 3 were waited for; matrix products, arithmetic and copies ran while one was open for 0% of the time, Pallas kernels for 27%

profile of v13, /device:TPU:0, one launch (start us, length us, event | category | flops | bytes accessed | tf_op | source)
XLA Modules:
  0.0 24.6 jit_solution(8188429810753935613)
XLA Ops:
  0.0 0.0 copy-start.2
  0.0 1.1 %copy-done.2 = f32[5,5,5,5,2,1,128]{6,5,4,3,2,1,0:T(1,128)S(1)} copy-done((f32[5,5,5,5,2,1,128]{6,5,4,3,2,1,0:T(1,128)S(1)}, f32[5,5,5,5,2,1,128]{6,5,4,3,2,1,0:T(1,128)}, u32[]{:S(2)}) %copy-start.2) | copy-done | bytes 640024
  1.1 0.0 copy-start.4
  1.1 3.1 %collective-permute-start.2 = (f32[104,256]{1,0:T(8,128)S(1)}, f32[104,256]{1,0:T(8,128)S(1)}, u32[]{:S(2)}, u32[]{:S(2)}) collective-permute-start(f32[104,256]{1,0:T(8,128)S(1)} %get-tuple-element.35), channel_id=1, source_target_pairs={{0,1},{1,0},{2,3},{3,2},{4,5},{5,4},{6,7},{7,6},{8,9},{9,8},{10,11... | collective-permute-start | bytes 319496 | tf_op jit(solution)/shard_map/ppermute | solution.py:680
  4.2 0.0 collective-permute-start.3
  4.2 0.0 copy-done.4
  4.2 0.0 copy-start.1
  4.2 0.0 copy-start.3
  4.2 0.0 copy-start.5
  4.3 0.1 begin_pitch.1
  4.4 0.0 copy-start
  4.4 2.6 %collective-permute-start = (f32[128,128]{1,0:T(8,128)S(1)}, f32[128,128]{1,0:T(8,128)S(1)}, u32[]{:S(2)}, u32[]{:S(2)}) collective-permute-start(f32[128,128]{1,0:T(8,128)S(1)} %get-tuple-element.33), channel_id=1, source_target_pairs={{0,28},{1,29},{2,30},{3,31},{4,8},{5,9},{6,10},{7,11},{8,4},{9,5},... | collective-permute-start | bytes 196616 | tf_op jit(solution)/shard_map/ppermute | solution.py:680
  7.0 0.0 collective-permute-start.1
  7.0 0.0 copy-done.1
  7.0 0.0 copy-done.3
  7.0 0.0 copy-done.5
  7.0 1.9 %first.1 = (f32[640,256]{1,0:T(8,128)S(1)}, f32[640,256]{1,0:T(8,128)S(1)}, f32[512,256]{1,0:T(8,128)S(1)}, f32[8,128]{1,0:T(8,128)S(1)}) custom-call(s32[3]{0:T(128)S(1)} %copy-done.5, f32[1250,1,128]{2,1,0:T(1,128)S(1)} %bitcast.9, bf16[1792,640]{1,0:T(8,128)(2,1)S(1)} %copy-done.1), custom_call_target="tpu_custom_call" | custom-call | flops 1000000000 | bytes 1048576 | tf_op jit(solution)/shard_map/first/pallas_call | solution.py:656
  8.9 0.0 collective-permute-done.1.pitch_a
  8.9 0.0 collective-permute-done.2.span_a
  8.9 0.0 collective-permute-done.3.span_b
  9.0 0.0 copy-done
  9.0 0.3 %near.2 = (f32[512,256]{1,0:T(8,128)S(1)}, bf16[512,256]{1,0:T(8,128)(2,1)S(1)}, bf16[512,256]{1,0:T(8,128)(2,1)S(1)}) custom-call(f32[104,256]{1,0:T(8,128)S(1)} %collective-permute-done.2.span_a, f32[104,256]{1,0:T(8,128)S(1)} %collective-permute-done.3.span_b, f32[128,128]{1,0:T(8,128)S(1)} %collective-permute-done.1.pitch_a, ...), custom_call_target="tpu_custom_call" | custom-call | flops 100000000 | bytes 1048576 | tf_op jit(solution)/shard_map/near/pallas_call | solution.py:656
  9.3 0.0 collective-permute-done.pitch_b
  9.3 0.2 far.2
  9.6 3.5 %collective-permute-start.6 = (f32[104,256]{1,0:T(8,128)S(1)}, f32[104,256]{1,0:T(8,128)S(1)}, u32[]{:S(2)}, u32[]{:S(2)}) collective-permute-start(f32[104,256]{1,0:T(8,128)S(1)} %get-tuple-element.42), channel_id=1, source_target_pairs={{0,1},{1,0},{2,3},{3,2},{4,5},{5,4},{6,7},{7,6},{8,9},{9,8},{10,11... | collective-permute-start | bytes 319496 | tf_op jit(solution)/shard_map/ppermute | solution.py:680
  13.1 0.0 collective-permute-start.7
  13.1 1.2 %collective-permute-start.4 = (f32[128,128]{1,0:T(8,128)S(1)}, f32[128,128]{1,0:T(8,128)S(1)}, u32[]{:S(2)}, u32[]{:S(2)}) collective-permute-start(f32[128,128]{1,0:T(8,128)S(1)} %get-tuple-element.40), channel_id=1, source_target_pairs={{0,28},{1,29},{2,30},{3,31},{4,8},{5,9},{6,10},{7,11},{8,4},{9,5},... | collective-permute-start | bytes 196616 | tf_op jit(solution)/shard_map/ppermute | solution.py:680
  14.3 0.0 collective-permute-start.5
  14.3 2.0 %later.1 = (f32[640,256]{1,0:T(8,128)S(1)}, f32[512,256]{1,0:T(8,128)S(1)}) custom-call(f32[640,256]{1,0:T(8,128)S(1)} %get-tuple-element.45.base, f32[640,256]{1,0:T(8,128)S(1)} %get-tuple-element.46.before, bf16[512,256]{1,0:T(8,128)(2,1)S(1)} %get-tuple-element.47.near_high, bf16[512,256]{1,0:T(8,128)(2,1)S(1)} %get-tuple-element.48.near_low, ...), custom_call_target="tpu_custom_call" | custom-call | flops 1000000000 | bytes 1048576 | tf_op jit(solution)/shard_map/later/pallas_call | solution.py:656
  16.4 0.0 collective-permute-done.5.pitch_a
  16.4 0.0 collective-permute-done.6.span_a
  16.4 0.0 collective-permute-done.7.span_b
  16.4 0.3 %near.3 = (f32[512,256]{1,0:T(8,128)S(1)}, bf16[512,256]{1,0:T(8,128)(2,1)S(1)}, bf16[512,256]{1,0:T(8,128)(2,1)S(1)}) custom-call(f32[104,256]{1,0:T(8,128)S(1)} %collective-permute-done.6.span_a, f32[104,256]{1,0:T(8,128)S(1)} %collective-permute-done.7.span_b, f32[128,128]{1,0:T(8,128)S(1)} %collective-permute-done.5.pitch_a, ...), custom_call_target="tpu_custom_call" | custom-call | flops 100000000 | bytes 1048576 | tf_op jit(solution)/shard_map/near/pallas_call | solution.py:656
  16.7 1.5 %collective-permute-done.4.pitch_b = f32[128,128]{1,0:T(8,128)S(1)} collective-permute-done((f32[128,128]{1,0:T(8,128)S(1)}, f32[128,128]{1,0:T(8,128)S(1)}, u32[]{:S(2)}, u32[]{:S(2)}) %collective-permute-start.4) | collective-permute-done | bytes 65568 | tf_op jit(solution)/shard_map/ppermute | solution.py:680
  18.2 0.2 far.3
  18.4 0.1 collective-permute-start.10
  18.5 0.1 collective-permute-start.11
  18.6 1.6 %collective-permute-start.8 = (f32[128,128]{1,0:T(8,128)S(1)}, f32[128,128]{1,0:T(8,128)S(1)}, u32[]{:S(2)}, u32[]{:S(2)}) collective-permute-start(f32[128,128]{1,0:T(8,128)S(1)} %get-tuple-element.51), channel_id=1, source_target_pairs={{0,28},{1,29},{2,30},{3,31},{4,8},{5,9},{6,10},{7,11},{8,4},{9,5},... | collective-permute-start | bytes 196616 | tf_op jit(solution)/shard_map/ppermute | solution.py:680
  20.2 0.0 collective-permute-start.9
  20.2 1.5 %last.1.before = f32[1250,1,128]{2,1,0:T(1,128)S(1)} custom-call(f32[640,256]{1,0:T(8,128)S(1)} %get-tuple-element.45.base, f32[640,256]{1,0:T(8,128)S(1)} %get-tuple-element.56.before, bf16[512,256]{1,0:T(8,128)(2,1)S(1)} %get-tuple-element.57.near_high, bf16[512,256]{1,0:T(8,128)(2,1)S(1)} %get-tuple-element.58.near_low, ...), custom_call_target="tpu_custom_call" | custom-call | flops 1000000000 | bytes 1048576 | tf_op jit(solution)/shard_map/last/pallas_call | solution.py:656
  21.7 0.0 collective-permute-done.9.pitch_a
  21.8 1.5 %collective-permute-done.10.span_a = f32[104,256]{1,0:T(8,128)S(1)} collective-permute-done((f32[104,256]{1,0:T(8,128)S(1)}, f32[104,256]{1,0:T(8,128)S(1)}, u32[]{:S(2)}, u32[]{:S(2)}) %collective-permute-start.10) | collective-permute-done | bytes 106528 | tf_op jit(solution)/shard_map/ppermute | solution.py:680
  23.2 0.0 collective-permute-done.11.span_b
  23.2 0.3 %final_near.1.near = f32[1250,1,128]{2,1,0:T(1,128)S(1)} custom-call(f32[104,256]{1,0:T(8,128)S(1)} %collective-permute-done.10.span_a, f32[104,256]{1,0:T(8,128)S(1)} %collective-permute-done.11.span_b, f32[128,128]{1,0:T(8,128)S(1)} %collective-permute-done.9.pitch_a, f32[256,128]{1,0:T(8,128)S(1)} %get-tuple-element.55.inner, f32[1250,1,128]{2,1,0:T(1,128)S(1)} %last.1.before), custom_call_target="tpu_custom_call" | custom-call | flops 100000000 | bytes 1048576 | tf_op jit(solution)/shard_map/final_near/pallas_call | solution.py:656
  23.5 0.2 collective-permute-done.8.pitch_b
  23.6 0.9 %final.1 = f32[1250,1,128]{2,1,0:T(1,128)} custom-call(f32[8,128]{1,0:T(8,128)S(1)} %get-tuple-element.32.flags, f32[128,128]{1,0:T(8,128)S(1)} %collective-permute-done.8.pitch_b, f32[128,128]{1,0:T(8,128)S(1)} %collective-permute-done.9.pitch_a, f32[1250,1,128]{2,1,0:T(1,128)S(1)} %final_near.1.near), custom_call_target="tpu_custom_call" | custom-call | flops 100000000 | bytes 1048576 | tf_op jit(solution)/shard_map/final/pallas_call | solution.py:656
  (1 shorter events, 0.0 us)
Async XLA Ops:
  0.0 1.1 %copy-start.2 = (f32[5,5,5,5,2,1,128]{6,5,4,3,2,1,0:T(1,128)S(1)}, f32[5,5,5,5,2,1,128]{6,5,4,3,2,1,0:T(1,128)}, u32[]{:S(2)}) copy-start(f32[5,5,5,5,2,1,128]{6,5,4,3,2,1,0:T(1,128)} %param.5) | copy-start | bytes 1920004
  1.1 3.1 %copy-start.4 = (f32[5,5,5,2,1]{2,4,3,1,0:T(1,128)S(1)}, f32[5,5,5,2,1]{2,4,3,1,0:T(1,128)}, u32[]{:S(2)}) copy-start(f32[5,5,5,2,1]{2,4,3,1,0:T(1,128)} %param.6) | copy-start | bytes 3004
  1.1 7.8 %collective-permute-start.2 = (f32[104,256]{1,0:T(8,128)S(1)}, f32[104,256]{1,0:T(8,128)S(1)}, u32[]{:S(2)}, u32[]{:S(2)}) collective-permute-start(f32[104,256]{1,0:T(8,128)S(1)} %get-tuple-element.35), channel_id=1, source_target_pairs={{0,1},{1,0},{2,3},{3,2},{4,5},{5,4},{6,7},{7,6},{8,9},{9,8},{10,11... | collective-permute-start | bytes 319496 | tf_op jit(solution)/shard_map/ppermute | solution.py:680
  4.2 4.7 %collective-permute-start.3 = (f32[104,256]{1,0:T(8,128)S(1)}, f32[104,256]{1,0:T(8,128)S(1)}, u32[]{:S(2)}, u32[]{:S(2)}) collective-permute-start(f32[104,256]{1,0:T(8,128)S(1)} %get-tuple-element.36), channel_id=1, source_target_pairs={{0,4},{1,2},{2,1},{3,7},{4,0},{5,6},{6,5},{7,3},{8,12},{9,10},{10,... | collective-permute-start | bytes 319496 | tf_op jit(solution)/shard_map/ppermute | solution.py:680
  4.2 2.8 %copy-start.1 = (bf16[1792,640]{1,0:T(8,128)(2,1)S(1)}, bf16[1792,640]{1,0:T(8,128)(2,1)}, u32[]{:S(2)}) copy-start(bf16[1792,640]{1,0:T(8,128)(2,1)} %constant.4.clone.table) | copy-start | bytes 6881284
  4.2 2.8 %copy-start.3 = (f32[5,5,5,5,2,1,128]{6,5,4,3,2,1,0:T(1,128)S(1)}, f32[5,5,5,5,2,1,128]{6,5,4,3,2,1,0:T(1,128)}, u32[]{:S(2)}) copy-start(f32[5,5,5,5,2,1,128]{6,5,4,3,2,1,0:T(1,128)} %param.5) | copy-start | bytes 1920004
  4.2 2.8 %copy-start.5 = (s32[3]{0:T(128)S(1)}, s32[3]{0:T(128)}, u32[]{:S(2)}) copy-start(s32[3]{0:T(128)} %offsets.1) | copy-start | bytes 40
  4.4 4.6 %copy-start = (bf16[1312,640]{1,0:T(8,128)(2,1)S(1)}, bf16[1312,640]{1,0:T(8,128)(2,1)}, u32[]{:S(2)}) copy-start(bf16[1312,640]{1,0:T(8,128)(2,1)} %constant.5.clone.links) | copy-start | bytes 5038084
  4.4 4.9 %collective-permute-start = (f32[128,128]{1,0:T(8,128)S(1)}, f32[128,128]{1,0:T(8,128)S(1)}, u32[]{:S(2)}, u32[]{:S(2)}) collective-permute-start(f32[128,128]{1,0:T(8,128)S(1)} %get-tuple-element.33), channel_id=1, source_target_pairs={{0,28},{1,29},{2,30},{3,31},{4,8},{5,9},{6,10},{7,11},{8,4},{9,5},... | collective-permute-start | bytes 196616 | tf_op jit(solution)/shard_map/ppermute | solution.py:680
  7.0 1.9 %collective-permute-start.1 = (f32[128,128]{1,0:T(8,128)S(1)}, f32[128,128]{1,0:T(8,128)S(1)}, u32[]{:S(2)}, u32[]{:S(2)}) collective-permute-start(f32[128,128]{1,0:T(8,128)S(1)} %get-tuple-element.34), channel_id=1, source_target_pairs={{0,4},{1,5},{2,6},{3,7},{4,0},{5,1},{6,2},{7,3},{8,12},{9,13},{10,... | collective-permute-start | bytes 196616 | tf_op jit(solution)/shard_map/ppermute | solution.py:680
  9.6 6.8 %collective-permute-start.6 = (f32[104,256]{1,0:T(8,128)S(1)}, f32[104,256]{1,0:T(8,128)S(1)}, u32[]{:S(2)}, u32[]{:S(2)}) collective-permute-start(f32[104,256]{1,0:T(8,128)S(1)} %get-tuple-element.42), channel_id=1, source_target_pairs={{0,1},{1,0},{2,3},{3,2},{4,5},{5,4},{6,7},{7,6},{8,9},{9,8},{10,11... | collective-permute-start | bytes 319496 | tf_op jit(solution)/shard_map/ppermute | solution.py:680
  13.1 3.3 %collective-permute-start.7 = (f32[104,256]{1,0:T(8,128)S(1)}, f32[104,256]{1,0:T(8,128)S(1)}, u32[]{:S(2)}, u32[]{:S(2)}) collective-permute-start(f32[104,256]{1,0:T(8,128)S(1)} %get-tuple-element.43), channel_id=1, source_target_pairs={{0,4},{1,2},{2,1},{3,7},{4,0},{5,6},{6,5},{7,3},{8,12},{9,10},{10,... | collective-permute-start | bytes 319496 | tf_op jit(solution)/shard_map/ppermute | solution.py:680
  13.1 5.1 %collective-permute-start.4 = (f32[128,128]{1,0:T(8,128)S(1)}, f32[128,128]{1,0:T(8,128)S(1)}, u32[]{:S(2)}, u32[]{:S(2)}) collective-permute-start(f32[128,128]{1,0:T(8,128)S(1)} %get-tuple-element.40), channel_id=1, source_target_pairs={{0,28},{1,29},{2,30},{3,31},{4,8},{5,9},{6,10},{7,11},{8,4},{9,5},... | collective-permute-start | bytes 196616 | tf_op jit(solution)/shard_map/ppermute | solution.py:680
  14.3 2.1 %collective-permute-start.5 = (f32[128,128]{1,0:T(8,128)S(1)}, f32[128,128]{1,0:T(8,128)S(1)}, u32[]{:S(2)}, u32[]{:S(2)}) collective-permute-start(f32[128,128]{1,0:T(8,128)S(1)} %get-tuple-element.41), channel_id=1, source_target_pairs={{0,4},{1,5},{2,6},{3,7},{4,0},{5,1},{6,2},{7,3},{8,12},{9,13},{10,... | collective-permute-start | bytes 196616 | tf_op jit(solution)/shard_map/ppermute | solution.py:680
  18.4 4.8 %collective-permute-start.10 = (f32[104,256]{1,0:T(8,128)S(1)}, f32[104,256]{1,0:T(8,128)S(1)}, u32[]{:S(2)}, u32[]{:S(2)}) collective-permute-start(f32[104,256]{1,0:T(8,128)S(1)} %get-tuple-element.53), channel_id=1, source_target_pairs={{0,1},{1,0},{2,3},{3,2},{4,5},{5,4},{6,7},{7,6},{8,9},{9,8},{10,11... | collective-permute-start | bytes 319496 | tf_op jit(solution)/shard_map/ppermute | solution.py:680
  18.5 4.7 %collective-permute-start.11 = (f32[104,256]{1,0:T(8,128)S(1)}, f32[104,256]{1,0:T(8,128)S(1)}, u32[]{:S(2)}, u32[]{:S(2)}) collective-permute-start(f32[104,256]{1,0:T(8,128)S(1)} %get-tuple-element.54), channel_id=1, source_target_pairs={{0,4},{1,2},{2,1},{3,7},{4,0},{5,6},{6,5},{7,3},{8,12},{9,10},{10,... | collective-permute-start | bytes 319496 | tf_op jit(solution)/shard_map/ppermute | solution.py:680
  18.6 5.0 %collective-permute-start.8 = (f32[128,128]{1,0:T(8,128)S(1)}, f32[128,128]{1,0:T(8,128)S(1)}, u32[]{:S(2)}, u32[]{:S(2)}) collective-permute-start(f32[128,128]{1,0:T(8,128)S(1)} %get-tuple-element.51), channel_id=1, source_target_pairs={{0,28},{1,29},{2,30},{3,31},{4,8},{5,9},{6,10},{7,11},{8,4},{9,5},... | collective-permute-start | bytes 196616 | tf_op jit(solution)/shard_map/ppermute | solution.py:680
  20.2 1.5 %collective-permute-start.9 = (f32[128,128]{1,0:T(8,128)S(1)}, f32[128,128]{1,0:T(8,128)S(1)}, u32[]{:S(2)}, u32[]{:S(2)}) collective-permute-start(f32[128,128]{1,0:T(8,128)S(1)} %get-tuple-element.52), channel_id=1, source_target_pairs={{0,4},{1,5},{2,6},{3,7},{4,0},{5,1},{6,2},{7,3},{8,12},{9,13},{10,... | collective-permute-start | bytes 196616 | tf_op jit(solution)/shard_map/ppermute | solution.py:680
